TPU v7x, 512 devices: a whole 4x8x8 slice. The times are simulated.
512 devices in a mesh: row: 16 (over z, core), col: 32 (over x, y).
Axes of the slice: x: 4, y: 8, z: 8, core: 2. Of those that a mesh axis runs over, the one named last changes fastest.
Arguments:
- factor: float32 [2, 512, 24576], P(None, 'row', 'col'), may hold values from -0.0390625 to 0.0390625
- solved: float32 [1024, 24576], P('row', 'col'), may hold values from -6 to 6
- rhs_window: float32 [1024, 2, 512], P('col', None, 'row'), may hold values from -6 to 6
- inverses: float32 [2, 512, 512], replicated, as said below
- coupling: float32 [512, 512], replicated, may hold values from -0.25 to 0.25
Outputs:
- solution: float32 [1024, 2, 512], P('col', None, 'row')
- updated: float32 [1024, 24576], P('row', 'col')
Inputs may be any that keep to these rules, and one draw needn't show every extreme that they name: inverses[k] is lower triangular; its diagonal entries lie between 0.5 and 1.5.
All inputs are finite; a program needn't handle non-finite values.
Results may differ from a plain program's by a relative error of at most 0.00011.
Values sent between devices are 32-bit elements; how exact they have to be, the bound alone decides.
No kernel may reach another device: no remote copies, remote signals or barrier semaphores. Data moves between devices by JAX's collectives and lax.ppermute only.
A program may use at most 64 MiB of HBM per device.

v0:
```python
import jax
import jax.numpy as jnp
from jax import lax
from jax.sharding import PartitionSpec as P

precise = lax.Precision.HIGHEST


def panel_solve(residual, inverses, coupling):
    forward_lead = jnp.dot(residual[:, 0, :], inverses[0].T, precision=precise)
    forward_next = jnp.dot(
        residual[:, 1, :] - jnp.dot(forward_lead, coupling.T, precision=precise),
        inverses[1].T,
        precision=precise,
    )
    backward_next = jnp.dot(forward_next, inverses[1], precision=precise)
    backward_lead = jnp.dot(
        forward_lead - jnp.dot(backward_next, coupling, precision=precise),
        inverses[0],
        precision=precise,
    )
    return jnp.stack([backward_lead, backward_next], axis=1)


def shards(factor, solved, rhs_window, inverses, coupling):
    local_rows = factor.shape[1]
    row_rank = lax.axis_index("row")
    totals = jnp.einsum(
        "rj,kij->rki", lax.all_gather(solved, "row", axis=0, tiled=True), factor, precision=precise
    )
    shares = lax.psum_scatter(totals, "col", scatter_dimension=0, tiled=True)
    residual = lax.all_gather(rhs_window - shares, "row", axis=2, tiled=True)
    solution_all = panel_solve(residual, inverses, coupling)
    owned_block = lax.dynamic_slice_in_dim(solution_all, row_rank * local_rows, local_rows, 2)
    gathered = lax.all_gather(owned_block, "col", axis=0, tiled=True)
    correction = lax.psum_scatter(
        jnp.einsum("rki,kij->rj", gathered, factor, precision=precise),
        "row",
        scatter_dimension=0,
        tiled=True,
    )
    updated = solved - correction
    return (owned_block, updated)


def solution(mesh):
    in_specs = (P(None, "row", "col"), P("row", "col"), P("col", None, "row"), P(), P())
    out_specs = (P("col", None, "row"), P("row", "col"))
    return jax.shard_map(shards, mesh=mesh, in_specs=in_specs, out_specs=out_specs, check_vma=False)
```

profile of v0, /device:TPU:6, one launch (start us, length us, event | category | flops | bytes accessed | tf_op | source)
XLA Modules:
  0.0 429.6 jit_solution(7138031970386429290)
XLA Ops:
  7.2 0.0 copy-start
  7.2 0.0 all-gather.2.cloned.1.call-start
  7.2 0.7 all-gather.2.cloned.1.call-update
  7.9 0.0 copy-start.4
  7.9 0.0 reduce-scatter.3.cloned.1.call-start
  8.0 51.3 %all-gather.2.cloned.1.call-done = f32[1024,768]{1,0:T(8,128)} async-done(((f32[64,768]{1,0:T(8,128)}), f32[1024,768]{1,0:T(8,128)}) %all-gather.2.cloned.1.call-update) | async-done | bytes 3145744 | tf_op jit(solution)/shard_map/all_gather | solution.py:29
  59.2 5.0 %fusion = f32[1024,2,32]{2,0,1:T(8,128)} fusion(f32[2,32,768]{2,1,0:T(8,128)} %param.5, f32[1024,768]{1,0:T(8,128)} %all-gather.2.cloned.1.call-done), kind=kOutput, calls=%fused_computation | convolution fusion | flops 603979776 | bytes 3604480 | tf_op jit(solution)/shard_map/rj,kij->rki/dot_general | solution.py:28
  64.3 0.0 reduce-scatter.3.cloned.1.call-update
  64.3 0.0 reduce-scatter.5.cloned.1.call-start
  64.4 216.6 %reduce-scatter.3.cloned.1.call-done = f32[32,2,32]{2,0,1:T(8,128)} async-done(((f32[1024,2,32]{2,0,1:T(8,128)}), f32[32,2,32]{2,0,1:T(8,128)}) %reduce-scatter.3.cloned.1.call-update) | async-done | bytes 8208 | tf_op jit(solution)/shard_map/reduce_scatter | solution.py:31
  281.0 0.0 copy-done.4
  281.0 0.8 copy_subtract_fusion
  281.7 0.1 copy.10
  281.8 19.6 %all_gather.10 = f32[32,2,512]{0,1,2:T(2,128)S(1)} all-gather(f32[32,2,32]{0,1,2:T(2,128)S(1)} %copy.10), channel_id=1, replica_groups=mesh['row'=16,'col'=32] {'row'}, dimensions={2}, use_global_device_ids=true | all-gather | bytes 139264 | tf_op jit(solution)/shard_map/all_gather | solution.py:32
  301.4 0.4 fusion.14
  301.8 0.0 copy-done.1
  301.8 1.1 fusion.7
  302.9 0.0 copy-done
  302.9 1.0 convolution_subtract_fusion
  303.9 1.1 fusion.4
  305.0 0.7 fusion.2
  305.7 0.0 copy-start.2
  305.7 0.7 convolution_subtract_fusion.1
  306.5 0.7 convolution_bitcast_fusion.1
  307.2 0.1 fusion.13
  307.3 48.1 %all_gather.11 = f32[1024,2,32]{2,0,1:T(8,128)S(1)} all-gather(f32[32,2,32]{2,0,1:T(8,128)S(1)} %fusion.13), channel_id=1, replica_groups=mesh['row'=16,'col'=32] {'col'}, dimensions={0}, use_global_device_ids=true | all-gather | bytes 270336 | tf_op jit(solution)/shard_map/all_gather | solution.py:35
  355.4 0.0 copy-done.2
  355.4 4.3 %convolution_bitcast_fusion = f32[1024,768]{1,0:T(8,128)} fusion(f32[1024,2,32]{2,0,1:T(8,128)S(1)} %all_gather.11, f32[2,32,768]{2,1,0:T(8,128)S(1)} %copy-done.2), kind=kOutput, calls=%fused_computation.2 | convolution fusion | flops 603979776 | bytes 3604480 | tf_op jit(solution)/shard_map/rki,kij->rj/dot_general | solution.py:37
  359.7 0.0 reduce-scatter.5.cloned.1.call-update
  359.7 0.6 copy.11
  360.3 61.1 %reduce-scatter.5.cloned.1.call-done = f32[64,768]{1,0:T(8,128)} async-done(((f32[1024,768]{1,0:T(8,128)}), f32[64,768]{1,0:T(8,128)}) %reduce-scatter.5.cloned.1.call-update) | async-done | bytes 196624 | tf_op jit(solution)/shard_map/reduce_scatter | solution.py:36
  421.4 1.6 sub.15
  (3 shorter events, 0.0 us)
Async XLA Ops:
  7.2 295.8 %copy-start = (f32[512,512]{1,0:T(8,128)S(1)}, f32[512,512]{1,0:T(8,128)}, u32[]{:S(2)}) copy-start(f32[512,512]{1,0:T(8,128)} %param.9) | copy-start | bytes 3145732
  7.2 52.1 %all-gather.2.cloned.1.call-start = ((), (), s32[]{:S(2)}) async-start(), calls=%async_computation.2 | async-start | bytes 3342336 | tf_op jit(solution)/shard_map/all_gather | solution.py:29
  7.9 273.1 %copy-start.4 = (f32[32,2,32]{2,1,0:T(2,128)S(1)}, f32[32,2,32]{2,1,0:T(2,128)}, u32[]{:S(2)}) copy-start(f32[32,2,32]{2,1,0:T(2,128)} %param.7) | copy-start | bytes 24580
  7.9 273.0 %reduce-scatter.3.cloned.1.call-start = ((), (), s32[]{:S(2)}) async-start(), calls=%async_computation.3 | async-start | bytes 1081344 | tf_op jit(solution)/shard_map/reduce_scatter | solution.py:31
  64.3 237.5 %copy-start.1 = (f32[2,512,512]{2,1,0:T(8,128)S(1)}, f32[2,512,512]{2,1,0:T(8,128)}, u32[]{:S(2)}) copy-start(f32[2,512,512]{2,1,0:T(8,128)} %param.8) | copy-start | bytes 6291460
  64.3 357.1 %reduce-scatter.5.cloned.1.call-start = ((), (), s32[]{:S(2)}) async-start(), calls=%async_computation.4 | async-start | bytes 3342336 | tf_op jit(solution)/shard_map/reduce_scatter | solution.py:36
  305.7 49.6 %copy-start.2 = (f32[2,32,768]{2,1,0:T(8,128)S(1)}, f32[2,32,768]{2,1,0:T(8,128)}, u32[]{:S(2)}) copy-start(f32[2,32,768]{2,1,0:T(8,128)} %param.5) | copy-start | bytes 589828
  359.7 61.8 %copy-start.3 = (f32[64,768]{1,0:T(8,128)S(1)}, f32[64,768]{1,0:T(8,128)}, u32[]{:S(2)}) copy-start(f32[64,768]{1,0:T(8,128)} %param.6) | copy-start | bytes 589828
Sparse Core Ops, SparseCore 0:
  10.1 49.0 all-gather.1
  64.4 216.5 reduce-scatter.2
  359.8 61.5 reduce-scatter.4
where the time goes:
time: 430 us
  waiting for transfers between devices  330 us (77%)
  blocking collectives  67.7 us (16%)
  matrix products  14.6 us (3%)
  between operations  13.8 us (3%)
    reduce_scatter x1, waiting for transfers between devices, shards(): shares = lax.psum_scatter(totals, 'col', scatter_dimension=0, tiled=True)  217 us
    reduce_scatter x1, waiting for transfers between devices, shards(): lax.psum_scatter(jnp.einsum('rki,kij->rj', gathered, factor, precision=pr...  61.1 us
    all_gather x1, waiting for transfers between devices, shards(): lax.all_gather(solved, 'row', axis=0, tiled=True)  51.3 us
    all_gather x1, blocking collectives, shards(): gathered = lax.all_gather(owned_block, 'col', axis=0, tiled=True)  48.1 us
    all_gather x1, blocking collectives, shards(): residual = lax.all_gather(rhs_window - shares, 'row', axis=2, tiled=True)  19.6 us
  transfers between devices with their start and end apart: 3, of which 3 were waited for; matrix products, arithmetic and copies ran while one was open for 0% of the time, Pallas kernels for 0%

commit v1 on v0

v1 whole, which is shorter than its diff:
```python
import jax
import jax.numpy as jnp
from jax import lax
from jax.sharding import PartitionSpec as P

precise = lax.Precision.HIGHEST

PLANES = 8
CORES = 2
COLS = 32


def core_swap():
    return [(row, row ^ 1) for row in range(PLANES * CORES)]


def plane_shift(step):
    return [
        (plane * CORES + core, (plane + step) % PLANES * CORES + core)
        for plane in range(PLANES)
        for core in range(CORES)
    ]


def window_to_work():
    pairs = []
    for row in range(PLANES * CORES):
        plane, core = divmod(row, CORES)
        for col in range(COLS):
            rhs_row, half = divmod(col, 2)
            rhs_plane, rhs_core = divmod(rhs_row, CORES)
            target = (rhs_core * 2 + half) * PLANES + plane
            pairs.append((row * COLS + col, (rhs_plane * CORES + core) * COLS + target))
    return pairs


def work_to_window():
    return [
        (row * COLS + col, (col // 2) * COLS + 2 * row + col % 2)
        for row in range(PLANES * CORES)
        for col in range(COLS)
    ]


def panel_solve(lead, follow, inverses, coupling):
    forward_lead = jnp.dot(lead, inverses[0].T, precision=precise)
    forward_next = jnp.dot(
        follow - jnp.dot(forward_lead, coupling.T, precision=precise),
        inverses[1].T,
        precision=precise,
    )
    backward_next = jnp.dot(forward_next, inverses[1], precision=precise)
    backward_lead = jnp.dot(
        forward_lead - jnp.dot(backward_next, coupling, precision=precise),
        inverses[0],
        precision=precise,
    )
    return backward_lead, backward_next


def turn(blocks, start):
    twice = jnp.concatenate([blocks, blocks], axis=2)
    return lax.dynamic_slice_in_dim(twice, start, PLANES, 2)


def shards(factor, solved, rhs_window, inverses, coupling):
    rows, width = solved.shape
    part = factor.shape[1]
    row = lax.axis_index("row")
    col = lax.axis_index("col")
    plane, core = row // CORES, row % CORES

    window = lax.ppermute(rhs_window, ("row", "col"), window_to_work())
    own = factor.reshape(2 * part, width)
    behind1 = lax.ppermute(own, "row", plane_shift(1))
    ahead1 = lax.ppermute(own, "row", plane_shift(-1))
    behind2 = lax.ppermute(own, "row", plane_shift(2))
    ahead2 = lax.ppermute(own, "row", plane_shift(-2))
    solved_pair = jnp.concatenate([solved, lax.ppermute(solved, "row", core_swap())], axis=0)
    behind3 = lax.ppermute(behind2, "row", plane_shift(1))
    ahead3 = lax.ppermute(ahead2, "row", plane_shift(-1))
    across = jnp.concatenate(
        [
            lax.ppermute(ahead2[:part], "row", plane_shift(-2)),
            lax.ppermute(behind2[part:], "row", plane_shift(2)),
        ],
        axis=0,
    )
    panel = jnp.concatenate(
        [own, ahead1, ahead2, ahead3, across, behind3, behind2, behind1], axis=0
    )
    totals = jnp.einsum("rj,ij->ri", solved_pair, panel, precision=precise)
    panel_other = lax.ppermute(panel, "row", core_swap())

    rhs_core, rhs_half, rhs_plane = col // 16, col // 8 % 2, col % 8
    at = (
        (rhs_core ^ core) * rows + rhs_half * (rows // 2),
        (rhs_plane - plane) % PLANES * 2 * part,
    )
    block = window.reshape(rows // 2, 2 * part)
    totals = lax.dynamic_update_slice(
        totals, lax.dynamic_slice(totals, at, block.shape) - block, at
    )
    each = rows // COLS
    spread = lax.all_to_all(
        totals.reshape(2, COLS, each, -1), "col", split_axis=1, concat_axis=0, tiled=True
    )
    residual = -jnp.sum(spread.reshape(COLS, 2, each, -1), axis=0)
    other = lax.ppermute(residual[1], "row", core_swap())
    pair = jnp.stack([residual[0], other], axis=0).reshape(2, each, PLANES, 2, part)
    by_core = jnp.where(core == 0, pair, pair[::-1])
    whole = turn(by_core, PLANES - plane)
    whole = jnp.transpose(whole, (3, 1, 2, 0, 4)).reshape(2, each, -1)
    backward_lead, backward_next = panel_solve(whole[0], whole[1], inverses, coupling)
    found = jnp.stack([backward_lead, backward_next], axis=0)
    found = found.reshape(2, each, PLANES, CORES, part)
    found = turn(jnp.transpose(found, (3, 1, 2, 0, 4)), plane)
    found = jnp.where(core == 0, found, found[::-1])
    found = jnp.transpose(found, (1, 0, 2, 3, 4)).reshape(each, -1)
    gathered = lax.all_to_all(
        jnp.broadcast_to(found, (COLS,) + found.shape), "col", 0, 0, tiled=True
    ).reshape(rows, -1)

    out_row, out_half = col // 2, col % 2
    out_plane, out_core = out_row // CORES, out_row % CORES
    grid = gathered.reshape(rows, CORES * PLANES, 2, part)
    mine = lax.dynamic_slice(
        grid,
        (out_half * (rows // 2), (out_core ^ core) * PLANES + (out_plane - plane) % PLANES, 0, 0),
        (rows // 2, 1, 2, part),
    )
    owned = lax.ppermute(mine[:, 0], ("row", "col"), work_to_window())
    half = panel.shape[0]
    correction = jnp.dot(gathered[:, :half], panel, precision=precise)
    correction += jnp.dot(gathered[:, half:], panel_other, precision=precise)
    return owned, solved - correction


def solution(mesh):
    in_specs = (P(None, "row", "col"), P("row", "col"), P("col", None, "row"), P(), P())
    out_specs = (P("col", None, "row"), P("row", "col"))
    return jax.shard_map(shards, mesh=mesh, in_specs=in_specs, out_specs=out_specs, check_vma=False)
```

time: 430 us -> 143 us (0.33)
  the two profiles are of different devices: /device:TPU:6 before, /device:TPU:13 now
where the time goes in v1:
time: 143 us; the launch traced here: 142 us
  starting transfers between devices  74.8 us (52%)
  waiting for transfers between devices  31.9 us (22%)
  local copies, waits for them, and re-layouts  17.6 us (12%)
  matrix products  16.5 us (12%)
    ppermute x1, starting transfers between devices, shards(): ahead2 = lax.ppermute(own, 'row', plane_shift(-2))  10.8 us
    all_to_all x1, waiting for transfers between devices, shards(): lax.all_to_all(jnp.broadcast_to(found, (COLS,) + found.shape), 'col', 0,...  10.6 us
    all_to_all x1, starting transfers between devices, shards(): lax.all_to_all(totals.reshape(2, COLS, each, -1), 'col', split_axis=1, co...  9.16 us
    ppermute x1, starting transfers between devices, shards(): ahead3 = lax.ppermute(ahead2, 'row', plane_shift(-1))  8.73 us
    ppermute x1, waiting for transfers between devices, shards(): owned = lax.ppermute(mine[:, 0], ('row', 'col'), work_to_window())  8.22 us
    unnamed x18, local copies, waits for them, and re-layouts  7.02 us
    all_to_all x1, starting transfers between devices, shards(): lax.all_to_all(jnp.broadcast_to(found, (COLS,) + found.shape), 'col', 0,...  5.67 us
    ppermute x1, starting transfers between devices, shards(): ahead1 = lax.ppermute(own, 'row', plane_shift(-1))  5.48 us
  transfers between devices with their start and end apart: 15, of which 7 were waited for; matrix products, arithmetic and copies ran while one was open for 15% of the time, Pallas kernels for 0%

profile of v1, /device:TPU:13, one launch (start us, length us, event | category | flops | bytes accessed | tf_op | source)
XLA Modules:
  0.0 142.2 jit_solution(3914544680892895733)
XLA Ops:
  0.6 10.8 %collective-permute-start.2 = (f32[64,768]{1,0:T(8,128)}, f32[64,768]{1,0:T(8,128)S(1)}, u32[]{:S(2)}, u32[]{:S(2)}) collective-permute-start(f32[64,768]{1,0:T(8,128)} %bitcast.42), channel_id=1, source_target_pairs={{0,384},{32,416},{64,448},{96,480},{128,0},{160,32},{192,64},{224,... | collective-permute-start | bytes 589832 | tf_op jit(solution)/shard_map/ppermute | solution.py:78
  11.4 1.9 %collective-permute-start.5 = (f32[64,768]{1,0:T(8,128)}, f32[64,768]{1,0:T(8,128)S(1)}, u32[]{:S(2)}, u32[]{:S(2)}) collective-permute-start(f32[64,768]{1,0:T(8,128)} %bitcast.43), channel_id=1, source_target_pairs={{0,128},{32,160},{64,192},{96,224},{128,256},{160,288},{192,320},{... | collective-permute-start | bytes 589832 | tf_op jit(solution)/shard_map/ppermute | solution.py:77
  13.4 5.5 %collective-permute-start.1 = (f32[64,768]{1,0:T(8,128)}, f32[64,768]{1,0:T(8,128)S(1)}, u32[]{:S(2)}, u32[]{:S(2)}) collective-permute-start(f32[64,768]{1,0:T(8,128)} %bitcast.44), channel_id=1, source_target_pairs={{0,448},{32,480},{64,0},{96,32},{128,64},{160,96},{192,128},{224,1... | collective-permute-start | bytes 589832 | tf_op jit(solution)/shard_map/ppermute | solution.py:76
  18.9 1.9 %collective-permute-start.8 = (f32[64,768]{1,0:T(8,128)}, f32[64,768]{1,0:T(8,128)S(1)}, u32[]{:S(2)}, u32[]{:S(2)}) collective-permute-start(f32[64,768]{1,0:T(8,128)} %bitcast.45), channel_id=1, source_target_pairs={{0,64},{32,96},{64,128},{96,160},{128,192},{160,224},{192,256},{22... | collective-permute-start | bytes 589832 | tf_op jit(solution)/shard_map/ppermute | solution.py:75
  20.8 2.0 %collective-permute-start.9 = (f32[32,2,32]{2,1,0:T(2,128)}, f32[32,2,32]{2,1,0:T(2,128)S(1)}, u32[]{:S(2)}, u32[]{:S(2)}) collective-permute-start(f32[32,2,32]{2,1,0:T(2,128)} %param.7), channel_id=1, source_target_pairs={{0,0},{1,8},{2,16},{3,24},{4,64},{5,72},{6,80},{7,88},{8,128},{9,1... | collective-permute-start | bytes 24584 | tf_op jit(solution)/shard_map/ppermute | solution.py:73
  22.8 1.6 %constant_dynamic-update-slice_fusion.8 = f32[512,768]{1,0:T(8,128)} fusion(f32[64,768]{1,0:T(8,128)} %bitcast.46), kind=kLoop, calls=%fused_computation.43 | loop fusion | bytes 393216
  24.4 4.6 %collective-permute-done.9 = f32[32,2,32]{2,1,0:T(2,128)S(1)} collective-permute-done((f32[32,2,32]{2,1,0:T(2,128)}, f32[32,2,32]{2,1,0:T(2,128)S(1)}, u32[]{:S(2)}, u32[]{:S(2)}) %collective-permute-start.9) | collective-permute-done | bytes 8224 | tf_op jit(solution)/shard_map/ppermute | solution.py:73
  29.0 4.5 %collective-permute-start = (f32[64,768]{1,0:T(8,128)}, f32[64,768]{1,0:T(8,128)}, u32[]{:S(2)}, u32[]{:S(2)}) collective-permute-start(f32[64,768]{1,0:T(8,128)} %param.6), channel_id=1, source_target_pairs={{0,32},{32,0},{64,96},{96,64},{128,160},{160,128},{192,224},{224,1... | collective-permute-start | bytes 589832 | tf_op jit(solution)/shard_map/ppermute | solution.py:79
  33.6 5.3 %collective-permute-start.4 = (f32[32,768]{1,0:T(8,128)S(1)}, f32[32,768]{1,0:T(8,128)S(1)}, u32[]{:S(2)}, u32[]{:S(2)}) collective-permute-start(f32[32,768]{1,0:T(8,128)S(1)} %slice.44), channel_id=1, source_target_pairs={{0,384},{32,416},{64,448},{96,480},{128,0},{160,32},{192,64},{224,... | collective-permute-start | bytes 294920 | tf_op jit(solution)/shard_map/ppermute | solution.py:84
  39.0 1.9 %collective-permute-start.6 = (f32[32,768]{1,0:T(8,128)S(1)}, f32[32,768]{1,0:T(8,128)S(1)}, u32[]{:S(2)}, u32[]{:S(2)}) collective-permute-start(f32[32,768]{1,0:T(8,128)S(1)} %slice.45), channel_id=1, source_target_pairs={{0,128},{32,160},{64,192},{96,224},{128,256},{160,288},{192,320},{... | collective-permute-start | bytes 294920 | tf_op jit(solution)/shard_map/ppermute | solution.py:85
  40.9 8.7 %collective-permute-start.3 = (f32[64,768]{1,0:T(8,128)S(1)}, f32[64,768]{1,0:T(8,128)S(1)}, u32[]{:S(2)}, u32[]{:S(2)}) collective-permute-start(f32[64,768]{1,0:T(8,128)S(1)} %collective-permute-done.2), channel_id=1, source_target_pairs={{0,448},{32,480},{64,0},{96,32},{128,64},{160,96},{192,128},{224,1... | collective-permute-start | bytes 589832 | tf_op jit(solution)/shard_map/ppermute | solution.py:81
  51.1 2.3 %collective-permute-done.3 = f32[64,768]{1,0:T(8,128)S(1)} collective-permute-done((f32[64,768]{1,0:T(8,128)S(1)}, f32[64,768]{1,0:T(8,128)S(1)}, u32[]{:S(2)}, u32[]{:S(2)}) %collective-permute-start.3) | collective-permute-done | bytes 196640 | tf_op jit(solution)/shard_map/ppermute | solution.py:81
  53.4 2.0 %collective-permute-start.7 = (f32[64,768]{1,0:T(8,128)S(1)}, f32[64,768]{1,0:T(8,128)S(1)}, u32[]{:S(2)}, u32[]{:S(2)}) collective-permute-start(f32[64,768]{1,0:T(8,128)S(1)} %collective-permute-done.5), channel_id=1, source_target_pairs={{0,64},{32,96},{64,128},{96,160},{128,192},{160,224},{192,256},{22... | collective-permute-start | bytes 589832 | tf_op jit(solution)/shard_map/ppermute | solution.py:80
  57.4 5.1 %collective-permute-done.7 = f32[64,768]{1,0:T(8,128)S(1)} collective-permute-done((f32[64,768]{1,0:T(8,128)S(1)}, f32[64,768]{1,0:T(8,128)S(1)}, u32[]{:S(2)}, u32[]{:S(2)}) %collective-permute-start.7) | collective-permute-done | bytes 196640 | tf_op jit(solution)/shard_map/ppermute | solution.py:80
  64.5 3.4 %fusion.11 = f32[128,512]{1,0:T(8,128)S(1)} fusion(f32[512,768]{1,0:T(8,128)} %constant_dynamic-update-slice_fusion, f32[64,768]{1,0:T(8,128)} %collective-permute-done, f32[64,768]{1,0:T(8,128)S(1)} %copy-done.2), kind=kOutput, calls=%fused_computation.16 | convolution fusion | flops 604078080 | bytes 2228224 | tf_op jit(solution)/shard_map/rj,ij->ri/dot_general | solution.py:92
  68.0 1.1 dynamic_update_slice.3
  69.9 1.7 %copy.16 = f32[2,32,2,512]{3,2,0,1:T(2,128)} copy(f32[2,32,2,512]{3,2,1,0:T(2,128)} %reshape.42) | data formatting | bytes 524288 | tf_op jit(solution)/shard_map/reshape | solution.py:106
  71.6 9.2 %all-to-all-start = ((f32[2,32,2,512]{3,2,0,1:T(2,128)}), f32[2,32,2,512]{3,2,0,1:T(2,128)S(1)}, u32[]{:S(2)}, u32[]{:S(2)}) async-start(f32[2,32,2,512]{3,2,0,1:T(2,128)} %copy.16), calls=%async_computation | async-start | bytes 524288 | tf_op jit(solution)/shard_map/all_to_all | solution.py:105
  80.8 1.1 slice_bitcast_fusion
  81.9 2.6 %copy.21 = f32[512,512]{1,0:T(8,128)} copy(f32[512,512]{0,1:T(8,128)} %slice_bitcast_fusion) | data formatting | bytes 2097152 | tf_op jit(solution)/shard_map/dot_general | solution.py:53
  84.4 4.5 %collective-permute-start.12 = (f32[512,768]{1,0:T(8,128)}, f32[512,768]{1,0:T(8,128)}, u32[]{:S(2)}, u32[]{:S(2)}) collective-permute-start(f32[512,768]{1,0:T(8,128)} %constant_dynamic-update-slice_fusion), channel_id=1, source_target_pairs={{0,32},{32,0},{64,96},{96,64},{128,160},{160,128},{192,224},{224,1... | collective-permute-start | bytes 4718600 | tf_op jit(solution)/shard_map/ppermute | solution.py:93
  89.5 5.5 %collective-permute-start.10 = (f32[2,512]{1,0:T(2,128)S(1)}, f32[2,512]{1,0:T(2,128)S(1)}, u32[]{:S(2)}, u32[]{:S(2)}) collective-permute-start(f32[2,512]{1,0:T(2,128)S(1)} %get-tuple-element.4), channel_id=1, source_target_pairs={{0,32},{32,0},{64,96},{96,64},{128,160},{160,128},{192,224},{224,1... | collective-permute-start | bytes 12296 | tf_op jit(solution)/shard_map/ppermute | solution.py:109
  97.2 1.0 convolution_subtract_fusion.1
  98.1 1.0 fusion.4
  100.5 3.4 %convolution_bitcast_fusion = f32[1,2,8,2,32]{4,1,3,2,0:T(2,128)S(1)} fusion(f32[2,512,1,1]{1,0,3,2:T(2,128)S(1)} %fusion.1, f32[8,2,32,512]{3,2,1,0:T(8,128)} %bitcast.41), kind=kOutput, calls=%fused_computation.2 | convolution fusion | flops 6291456 | bytes 1056768 | tf_op jit(solution)/shard_map/dot_general | solution.py:53
  104.8 5.7 %all-to-all-start.1 = ((f32[32,2,1024]{2,1,0:T(2,128)}), f32[32,2,1024]{2,1,0:T(2,128)S(1)}, u32[]{:S(2)}, u32[]{:S(2)}) async-start(f32[32,2,1024]{2,1,0:T(2,128)} %broadcast_in_dim.3), calls=%async_computation.1 | async-start | bytes 524288 | tf_op jit(solution)/shard_map/all_to_all | solution.py:120
  110.6 10.6 %all-to-all-done.1 = f32[32,2,1024]{2,1,0:T(2,128)S(1)} async-done(((f32[32,2,1024]{2,1,0:T(2,128)}), f32[32,2,1024]{2,1,0:T(2,128)S(1)}, u32[]{:S(2)}, u32[]{:S(2)}) %all-to-all-start.1) | async-done | bytes 262176 | tf_op jit(solution)/shard_map/all_to_all | solution.py:120
  121.2 1.0 reshape_reshape.3
  122.2 5.4 %collective-permute-start.11 = (f32[32,2,32]{2,1,0:T(2,128)S(1)}, f32[32,2,32]{2,1,0:T(2,128)S(1)}, u32[]{:S(2)}, u32[]{:S(2)}) collective-permute-start(f32[32,2,32]{2,1,0:T(2,128)S(1)} %dynamic-slice_bitcast_fusion), channel_id=1, source_target_pairs={{0,0},{1,1},{2,32},{3,33},{4,64},{5,65},{6,96},{7,97},{8,128},{9,1... | collective-permute-start | bytes 24584 | tf_op jit(solution)/shard_map/ppermute | solution.py:132
  127.8 8.2 %collective-permute-done.11 = f32[32,2,32]{2,1,0:T(2,128)S(1)} collective-permute-done((f32[32,2,32]{2,1,0:T(2,128)S(1)}, f32[32,2,32]{2,1,0:T(2,128)S(1)}, u32[]{:S(2)}, u32[]{:S(2)}) %collective-permute-start.11) | collective-permute-done | bytes 8224 | tf_op jit(solution)/shard_map/ppermute | solution.py:132
  136.0 2.5 %fusion.15 = f32[64,768]{1,0:T(8,128)S(1)} fusion(f32[512,768]{1,0:T(8,128)} %collective-permute-done.12, f32[64,1024]{1,0:T(8,128)S(1)} %reshape.44), kind=kOutput, calls=%fused_computation.20 | convolution fusion | flops 301989888 | bytes 1900544 | tf_op jit(solution)/shard_map/dot_general | solution.py:135
  138.5 3.2 %fusion = f32[64,768]{1,0:T(8,128)} fusion(f32[64,768]{1,0:T(8,128)S(1)} %copy-done.3, f32[64,768]{1,0:T(8,128)S(1)} %fusion.15, f32[512,768]{1,0:T(8,128)} %constant_dynamic-update-slice_fusion, f32[64,1024]{1,0:T(8,128)S(1)} %reshape.44), kind=kOutput, calls=%fused_computation.1 | convolution fusion | flops 302088192 | bytes 2293760 | tf_op jit(solution)/shard_map/dot_general | solution.py:134
  (59 shorter events, 12.4 us)
Async XLA Ops:
  0.6 96.5 %copy-start = (f32[512,512]{1,0:T(8,128)S(1)}, f32[512,512]{1,0:T(8,128)}, u32[]{:S(2)}) copy-start(f32[512,512]{1,0:T(8,128)} %param.9) | copy-start | bytes 3145732
  0.6 33.0 %collective-permute-start.2 = (f32[64,768]{1,0:T(8,128)}, f32[64,768]{1,0:T(8,128)S(1)}, u32[]{:S(2)}, u32[]{:S(2)}) collective-permute-start(f32[64,768]{1,0:T(8,128)} %bitcast.42), channel_id=1, source_target_pairs={{0,384},{32,416},{64,448},{96,480},{128,0},{160,32},{192,64},{224,... | collective-permute-start | bytes 589832 | tf_op jit(solution)/shard_map/ppermute | solution.py:78
  11.4 27.5 %collective-permute-start.5 = (f32[64,768]{1,0:T(8,128)}, f32[64,768]{1,0:T(8,128)S(1)}, u32[]{:S(2)}, u32[]{:S(2)}) collective-permute-start(f32[64,768]{1,0:T(8,128)} %bitcast.43), channel_id=1, source_target_pairs={{0,128},{32,160},{64,192},{96,224},{128,256},{160,288},{192,320},{... | collective-permute-start | bytes 589832 | tf_op jit(solution)/shard_map/ppermute | solution.py:77
  13.4 27.6 %collective-permute-start.1 = (f32[64,768]{1,0:T(8,128)}, f32[64,768]{1,0:T(8,128)S(1)}, u32[]{:S(2)}, u32[]{:S(2)}) collective-permute-start(f32[64,768]{1,0:T(8,128)} %bitcast.44), channel_id=1, source_target_pairs={{0,448},{32,480},{64,0},{96,32},{128,64},{160,96},{192,128},{224,1... | collective-permute-start | bytes 589832 | tf_op jit(solution)/shard_map/ppermute | solution.py:76
  18.9 45.0 %collective-permute-start.8 = (f32[64,768]{1,0:T(8,128)}, f32[64,768]{1,0:T(8,128)S(1)}, u32[]{:S(2)}, u32[]{:S(2)}) collective-permute-start(f32[64,768]{1,0:T(8,128)} %bitcast.45), channel_id=1, source_target_pairs={{0,64},{32,96},{64,128},{96,160},{128,192},{160,224},{192,256},{22... | collective-permute-start | bytes 589832 | tf_op jit(solution)/shard_map/ppermute | solution.py:75
  20.8 8.2 %collective-permute-start.9 = (f32[32,2,32]{2,1,0:T(2,128)}, f32[32,2,32]{2,1,0:T(2,128)S(1)}, u32[]{:S(2)}, u32[]{:S(2)}) collective-permute-start(f32[32,2,32]{2,1,0:T(2,128)} %param.7), channel_id=1, source_target_pairs={{0,0},{1,8},{2,16},{3,24},{4,64},{5,72},{6,80},{7,88},{8,128},{9,1... | collective-permute-start | bytes 24584 | tf_op jit(solution)/shard_map/ppermute | solution.py:73
  29.0 35.5 %collective-permute-start = (f32[64,768]{1,0:T(8,128)}, f32[64,768]{1,0:T(8,128)}, u32[]{:S(2)}, u32[]{:S(2)}) collective-permute-start(f32[64,768]{1,0:T(8,128)} %param.6), channel_id=1, source_target_pairs={{0,32},{32,0},{64,96},{96,64},{128,160},{160,128},{192,224},{224,1... | collective-permute-start | bytes 589832 | tf_op jit(solution)/shard_map/ppermute | solution.py:79
  33.6 30.9 %copy-start.2 = (f32[64,768]{1,0:T(8,128)S(1)}, f32[64,768]{1,0:T(8,128)}, u32[]{:S(2)}) copy-start(f32[64,768]{1,0:T(8,128)} %param.6) | copy-start | bytes 589828
  33.6 22.4 %collective-permute-start.4 = (f32[32,768]{1,0:T(8,128)S(1)}, f32[32,768]{1,0:T(8,128)S(1)}, u32[]{:S(2)}, u32[]{:S(2)}) collective-permute-start(f32[32,768]{1,0:T(8,128)S(1)} %slice.44), channel_id=1, source_target_pairs={{0,384},{32,416},{64,448},{96,480},{128,0},{160,32},{192,64},{224,... | collective-permute-start | bytes 294920 | tf_op jit(solution)/shard_map/ppermute | solution.py:84
  39.0 17.7 %collective-permute-start.6 = (f32[32,768]{1,0:T(8,128)S(1)}, f32[32,768]{1,0:T(8,128)S(1)}, u32[]{:S(2)}, u32[]{:S(2)}) collective-permute-start(f32[32,768]{1,0:T(8,128)S(1)} %slice.45), channel_id=1, source_target_pairs={{0,128},{32,160},{64,192},{96,224},{128,256},{160,288},{192,320},{... | collective-permute-start | bytes 294920 | tf_op jit(solution)/shard_map/ppermute | solution.py:85
  40.9 12.4 %collective-permute-start.3 = (f32[64,768]{1,0:T(8,128)S(1)}, f32[64,768]{1,0:T(8,128)S(1)}, u32[]{:S(2)}, u32[]{:S(2)}) collective-permute-start(f32[64,768]{1,0:T(8,128)S(1)} %collective-permute-done.2), channel_id=1, source_target_pairs={{0,448},{32,480},{64,0},{96,32},{128,64},{160,96},{192,128},{224,1... | collective-permute-start | bytes 589832 | tf_op jit(solution)/shard_map/ppermute | solution.py:81
  53.4 9.1 %collective-permute-start.7 = (f32[64,768]{1,0:T(8,128)S(1)}, f32[64,768]{1,0:T(8,128)S(1)}, u32[]{:S(2)}, u32[]{:S(2)}) collective-permute-start(f32[64,768]{1,0:T(8,128)S(1)} %collective-permute-done.5), channel_id=1, source_target_pairs={{0,64},{32,96},{64,128},{96,160},{128,192},{160,224},{192,256},{22... | collective-permute-start | bytes 589832 | tf_op jit(solution)/shard_map/ppermute | solution.py:80
  64.5 16.3 %copy-start.1 = (f32[2,512,512]{2,1,0:T(8,128)S(1)}, f32[2,512,512]{2,1,0:T(8,128)}, u32[]{:S(2)}) copy-start(f32[2,512,512]{2,1,0:T(8,128)} %param.8) | copy-start | bytes 6291460
  71.6 17.7 %all-to-all-start = ((f32[2,32,2,512]{3,2,0,1:T(2,128)}), f32[2,32,2,512]{3,2,0,1:T(2,128)S(1)}, u32[]{:S(2)}, u32[]{:S(2)}) async-start(f32[2,32,2,512]{3,2,0,1:T(2,128)} %copy.16), calls=%async_computation | async-start | bytes 524288 | tf_op jit(solution)/shard_map/all_to_all | solution.py:105
  84.4 51.6 %collective-permute-start.12 = (f32[512,768]{1,0:T(8,128)}, f32[512,768]{1,0:T(8,128)}, u32[]{:S(2)}, u32[]{:S(2)}) collective-permute-start(f32[512,768]{1,0:T(8,128)} %constant_dynamic-update-slice_fusion), channel_id=1, source_target_pairs={{0,32},{32,0},{64,96},{96,64},{128,160},{160,128},{192,224},{224,1... | collective-permute-start | bytes 4718600 | tf_op jit(solution)/shard_map/ppermute | solution.py:93
  89.5 6.3 %collective-permute-start.10 = (f32[2,512]{1,0:T(2,128)S(1)}, f32[2,512]{1,0:T(2,128)S(1)}, u32[]{:S(2)}, u32[]{:S(2)}) collective-permute-start(f32[2,512]{1,0:T(2,128)S(1)} %get-tuple-element.4), channel_id=1, source_target_pairs={{0,32},{32,0},{64,96},{96,64},{128,160},{160,128},{192,224},{224,1... | collective-permute-start | bytes 12296 | tf_op jit(solution)/shard_map/ppermute | solution.py:109
  104.8 16.3 %all-to-all-start.1 = ((f32[32,2,1024]{2,1,0:T(2,128)}), f32[32,2,1024]{2,1,0:T(2,128)S(1)}, u32[]{:S(2)}, u32[]{:S(2)}) async-start(f32[32,2,1024]{2,1,0:T(2,128)} %broadcast_in_dim.3), calls=%async_computation.1 | async-start | bytes 524288 | tf_op jit(solution)/shard_map/all_to_all | solution.py:120
  122.1 16.3 %copy-start.3 = (f32[64,768]{1,0:T(8,128)S(1)}, f32[64,768]{1,0:T(8,128)}, u32[]{:S(2)}) copy-start(f32[64,768]{1,0:T(8,128)} %param.6) | copy-start | bytes 589828
  122.2 13.8 %collective-permute-start.11 = (f32[32,2,32]{2,1,0:T(2,128)S(1)}, f32[32,2,32]{2,1,0:T(2,128)S(1)}, u32[]{:S(2)}, u32[]{:S(2)}) collective-permute-start(f32[32,2,32]{2,1,0:T(2,128)S(1)} %dynamic-slice_bitcast_fusion), channel_id=1, source_target_pairs={{0,0},{1,1},{2,32},{3,33},{4,64},{5,65},{6,96},{7,97},{8,128},{9,1... | collective-permute-start | bytes 24584 | tf_op jit(solution)/shard_map/ppermute | solution.py:132

commit v2 on v1

--- a/solution.py
+++ b/solution.py
@@ -1,9 +1,12 @@
 import jax
 import jax.numpy as jnp
 from jax import lax
+from jax.experimental import pallas as pl
+from jax.experimental.pallas import tpu as pltpu
 from jax.sharding import PartitionSpec as P
 
 precise = lax.Precision.HIGHEST
+VMEM_BYTES = 32 * 1024 * 1024
 
 PLANES = 8
 CORES = 2
@@ -20,6 +23,11 @@
         for plane in range(PLANES)
         for core in range(CORES)
     ]
+
+
+def plane_groups():
+    size = CORES * COLS
+    return [list(range(plane * size, (plane + 1) * size)) for plane in range(PLANES)]
 
 
 def window_to_work():
@@ -42,6 +50,97 @@
     ]
 
 
+def halves(x):
+    high = x.astype(jnp.bfloat16)
+    return high, (x - high.astype(jnp.float32)).astype(jnp.bfloat16)
+
+
+def in_vmem():
+    return pl.BlockSpec(memory_space=pltpu.VMEM)
+
+
+def kernel_call(body, out_shape, in_specs, out_specs, flops=0, moved=0):
+    return pl.pallas_call(
+        body,
+        out_shape=out_shape,
+        in_specs=in_specs,
+        out_specs=out_specs,
+        compiler_params=pltpu.CompilerParams(vmem_limit_bytes=VMEM_BYTES),
+        cost_estimate=pl.CostEstimate(flops=flops, bytes_accessed=moved, transcendentals=0),
+    )
+
+
+def hold(values, arrivals):
+    def body(*refs):
+        count = len(values)
+        for source, target in zip(refs[:count], refs[count + len(arrivals) :]):
+            target[...] = source[...]
+
+    return kernel_call(
+        body,
+        [jax.ShapeDtypeStruct(v.shape, v.dtype) for v in values],
+        [in_vmem()] * len(values) + [pl.BlockSpec(memory_space=pl.ANY)] * len(arrivals),
+        [in_vmem()] * len(values),
+    )(*values, *arrivals)
+
+
+def rounded_dot(left, right, contract):
+    (left_up, left_down), (right_up, right_down) = left, right
+
+    def one(x, y):
+        return lax.dot_general(x, y, (contract, ((), ())), preferred_element_type=jnp.float32)
+
+    return one(left_up, right_up) + one(left_down, right_up) + one(left_up, right_down)
+
+
+def reduce_panel(solved_pair, placed, pieces):
+    rows, width = solved_pair.shape
+    unknowns = placed.shape[1]
+    each = rows // (CORES * COLS)
+
+    def body(solved_ref, placed_ref, *refs):
+        *piece_refs, out_ref, panel_ref = refs
+        at = 0
+        for ref in piece_refs:
+            panel_ref[at : at + ref.shape[0]] = ref[...]
+            at += ref.shape[0]
+        total = rounded_dot(halves(panel_ref[...]), halves(solved_ref[...]), ((1,), (1,)))
+        partial = placed_ref[...] - total.T
+        for member in range(CORES * COLS):
+            out_ref[member] = partial[member * each : (member + 1) * each]
+
+    return kernel_call(
+        body,
+        [
+            jax.ShapeDtypeStruct((CORES * COLS, each, unknowns), jnp.float32),
+            jax.ShapeDtypeStruct((unknowns, width), jnp.float32),
+        ],
+        [in_vmem()] * (2 + len(pieces)),
+        [in_vmem()] * 2,
+        flops=6 * rows * unknowns * width,
+        moved=8 * unknowns * width,
+    )(solved_pair, placed, *pieces)
+
+
+def correct(solved, found, panel, panel_other):
+    def body(solved_ref, found_ref, panel_ref, other_ref, out_ref):
+        half = panel_ref.shape[0]
+        contract = ((1,), (0,))
+        total = rounded_dot(halves(found_ref[:, :half]), halves(panel_ref[...]), contract)
+        total += rounded_dot(halves(found_ref[:, half:]), halves(other_ref[...]), contract)
+        out_ref[...] = solved_ref[...] - total
+
+    rows, width = solved.shape
+    return kernel_call(
+        body,
+        jax.ShapeDtypeStruct(solved.shape, solved.dtype),
+        [in_vmem()] * 4,
+        in_vmem(),
+        flops=36 * rows * found.shape[1] * width,
+        moved=4 * found.shape[1] * width,
+    )(solved, found, panel, panel_other)
+
+
 def panel_solve(lead, follow, inverses, coupling):
     forward_lead = jnp.dot(lead, inverses[0].T, precision=precise)
     forward_next = jnp.dot(
@@ -70,49 +169,47 @@
     col = lax.axis_index("col")
     plane, core = row // CORES, row % CORES
 
-    window = lax.ppermute(rhs_window, ("row", "col"), window_to_work())
     own = factor.reshape(2 * part, width)
+    behind2 = lax.ppermute(own, "row", plane_shift(2))
+    ahead2 = lax.ppermute(own, "row", plane_shift(-2))
     behind1 = lax.ppermute(own, "row", plane_shift(1))
     ahead1 = lax.ppermute(own, "row", plane_shift(-1))
-    behind2 = lax.ppermute(own, "row", plane_shift(2))
-    ahead2 = lax.ppermute(own, "row", plane_shift(-2))
-    solved_pair = jnp.concatenate([solved, lax.ppermute(solved, "row", core_swap())], axis=0)
     behind3 = lax.ppermute(behind2, "row", plane_shift(1))
     ahead3 = lax.ppermute(ahead2, "row", plane_shift(-1))
-    across = jnp.concatenate(
-        [
-            lax.ppermute(ahead2[:part], "row", plane_shift(-2)),
-            lax.ppermute(behind2[part:], "row", plane_shift(2)),
-        ],
-        axis=0,
-    )
-    panel = jnp.concatenate(
-        [own, ahead1, ahead2, ahead3, across, behind3, behind2, behind1], axis=0
-    )
-    totals = jnp.einsum("rj,ij->ri", solved_pair, panel, precision=precise)
+    across = [
+        lax.ppermute(ahead2[:part], "row", plane_shift(-2)),
+        lax.ppermute(behind2[part:], "row", plane_shift(2)),
+    ]
+    window = lax.ppermute(rhs_window, ("row", "col"), window_to_work())
+    (solved_held,) = hold((solved,), (behind1, ahead1))
+    solved_other = lax.ppermute(solved_held, "row", core_swap())
+    pair = jnp.stack([solved, solved_other], axis=0)
+    solved_pair = jnp.where(core == 0, pair, pair[::-1]).reshape(2 * rows, width)
+
+    rhs_core, rhs_half, rhs_plane = col // 16, col // 8 % 2, col % 8
+    block = window.reshape(rows // 2, 2 * part)
+    at = (rhs_core * rows + rhs_half * (rows // 2), (rhs_plane - plane) % PLANES * 2 * part)
+    placed = jnp.zeros((2 * rows, PLANES * 2 * part), jnp.float32)
+    placed = lax.dynamic_update_slice(placed, block, at)
+
+    pieces = [own, ahead1, ahead2, ahead3, *across, behind3, behind2, behind1]
+    partial, panel = reduce_panel(solved_pair, placed, pieces)
     panel_other = lax.ppermute(panel, "row", core_swap())
 
-    rhs_core, rhs_half, rhs_plane = col // 16, col // 8 % 2, col % 8
-    at = (
-        (rhs_core ^ core) * rows + rhs_half * (rows // 2),
-        (rhs_plane - plane) % PLANES * 2 * part,
-    )
-    block = window.reshape(rows // 2, 2 * part)
-    totals = lax.dynamic_update_slice(
-        totals, lax.dynamic_slice(totals, at, block.shape) - block, at
-    )
     each = rows // COLS
     spread = lax.all_to_all(
-        totals.reshape(2, COLS, each, -1), "col", split_axis=1, concat_axis=0, tiled=True
-    )
-    residual = -jnp.sum(spread.reshape(COLS, 2, each, -1), axis=0)
-    other = lax.ppermute(residual[1], "row", core_swap())
-    pair = jnp.stack([residual[0], other], axis=0).reshape(2, each, PLANES, 2, part)
-    by_core = jnp.where(core == 0, pair, pair[::-1])
-    whole = turn(by_core, PLANES - plane)
-    whole = jnp.transpose(whole, (3, 1, 2, 0, 4)).reshape(2, each, -1)
-    backward_lead, backward_next = panel_solve(whole[0], whole[1], inverses, coupling)
-    found = jnp.stack([backward_lead, backward_next], axis=0)
+        partial,
+        ("row", "col"),
+        0,
+        0,
+        axis_index_groups=plane_groups(),
+        tiled=True,
+    )
+    residual = jnp.sum(spread.reshape(CORES, COLS, each, -1), axis=1)
+    residual = turn(residual.reshape(CORES, each, PLANES, 2, part), PLANES - plane)
+    whole = jnp.transpose(residual, (3, 1, 2, 0, 4)).reshape(2, each, -1)
+    solved_panels = panel_solve(whole[0], whole[1], inverses, coupling)
+    found = jnp.stack(lax.optimization_barrier(solved_panels), axis=0)
     found = found.reshape(2, each, PLANES, CORES, part)
     found = turn(jnp.transpose(found, (3, 1, 2, 0, 4)), plane)
     found = jnp.where(core == 0, found, found[::-1])
@@ -130,10 +227,7 @@
         (rows // 2, 1, 2, part),
     )
     owned = lax.ppermute(mine[:, 0], ("row", "col"), work_to_window())
-    half = panel.shape[0]
-    correction = jnp.dot(gathered[:, :half], panel, precision=precise)
-    correction += jnp.dot(gathered[:, half:], panel_other, precision=precise)
-    return owned, solved - correction
+    return owned, correct(solved, gathered, panel, panel_other)
 
 
 def solution(mesh):

time: 143 us -> 134 us (0.937)
  the two profiles are of different devices: /device:TPU:13 before, /device:TPU:76 now
where the time goes in v2:
time: 134 us; the launch traced here: 133 us
  starting transfers between devices  74.4 us (56%)
  waiting for transfers between devices  38 us (28%)
  local copies, waits for them, and re-layouts  8.01 us (6%)
  matrix products  5.93 us (4%)
  Pallas kernels  4.63 us (3%)
    all_to_all x1, starting transfers between devices, shards(): lax.all_to_all(partial, ('row', 'col'), 0, 0, axis_index_groups=plane_gro...  17.7 us
    all_to_all x1, waiting for transfers between devices, shards(): lax.all_to_all(jnp.broadcast_to(found, (COLS,) + found.shape), 'col', 0,...  10.2 us
    ppermute x1, waiting for transfers between devices, shards(): owned = lax.ppermute(mine[:, 0], ('row', 'col'), work_to_window())  9.44 us
    all_to_all x1, waiting for transfers between devices, shards(): lax.all_to_all(partial, ('row', 'col'), 0, 0, axis_index_groups=plane_gro...  8.55 us
    all_to_all x1, starting transfers between devices, shards(): lax.all_to_all(jnp.broadcast_to(found, (COLS,) + found.shape), 'col', 0,...  7.63 us
    ppermute x1, waiting for transfers between devices, shards(): window = lax.ppermute(rhs_window, ('row', 'col'), window_to_work())  7.54 us
    ppermute x1, starting transfers between devices, shards(): behind2 = lax.ppermute(own, 'row', plane_shift(2))  7.3 us
    ppermute x1, starting transfers between devices, shards(): lax.ppermute(ahead2[:part], 'row', plane_shift(-2))  7.06 us
  transfers between devices with their start and end apart: 14, of which 6 were waited for; matrix products, arithmetic and copies ran while one was open for 9% of the time, Pallas kernels for 0%

profile of v2, /device:TPU:76, one launch (start us, length us, event | category | flops | bytes accessed | tf_op | source)
XLA Modules:
  0.0 133.4 jit_solution(10913398124585968150)
XLA Ops:
  0.6 2.1 %collective-permute-start.1 = (f32[64,768]{1,0:T(8,128)}, f32[64,768]{1,0:T(8,128)S(1)}, u32[]{:S(2)}, u32[]{:S(2)}) collective-permute-start(f32[64,768]{1,0:T(8,128)} %bitcast.34), channel_id=1, source_target_pairs={{0,448},{32,480},{64,0},{96,32},{128,64},{160,96},{192,128},{224,1... | collective-permute-start | bytes 589832 | tf_op jit(solution)/shard_map/ppermute | solution.py:176
  2.7 4.3 %collective-permute-start = (f32[64,768]{1,0:T(8,128)}, f32[64,768]{1,0:T(8,128)S(1)}, u32[]{:S(2)}, u32[]{:S(2)}) collective-permute-start(f32[64,768]{1,0:T(8,128)} %bitcast.35), channel_id=1, source_target_pairs={{0,64},{32,96},{64,128},{96,160},{128,192},{160,224},{192,256},{22... | collective-permute-start | bytes 589832 | tf_op jit(solution)/shard_map/ppermute | solution.py:175
  7.0 7.3 %collective-permute-start.7 = (f32[64,768]{1,0:T(8,128)}, f32[64,768]{1,0:T(8,128)S(1)}, u32[]{:S(2)}, u32[]{:S(2)}) collective-permute-start(f32[64,768]{1,0:T(8,128)} %bitcast.36), channel_id=1, source_target_pairs={{0,128},{32,160},{64,192},{96,224},{128,256},{160,288},{192,320},{... | collective-permute-start | bytes 589832 | tf_op jit(solution)/shard_map/ppermute | solution.py:173
  14.3 5.5 %collective-permute-start.4 = (f32[64,768]{1,0:T(8,128)}, f32[64,768]{1,0:T(8,128)S(1)}, u32[]{:S(2)}, u32[]{:S(2)}) collective-permute-start(f32[64,768]{1,0:T(8,128)} %bitcast.37), channel_id=1, source_target_pairs={{0,384},{32,416},{64,448},{96,480},{128,0},{160,32},{192,64},{224,... | collective-permute-start | bytes 589832 | tf_op jit(solution)/shard_map/ppermute | solution.py:174
  19.9 0.9 copy-done.1
  20.8 2.1 %collective-permute-start.2 = (f32[64,768]{1,0:T(8,128)S(1)}, f32[64,768]{1,0:T(8,128)S(1)}, u32[]{:S(2)}, u32[]{:S(2)}) collective-permute-start(f32[64,768]{1,0:T(8,128)S(1)} %shard_map.68), channel_id=1, source_target_pairs={{0,32},{32,0},{64,96},{96,64},{128,160},{160,128},{192,224},{224,1... | collective-permute-start | bytes 589832 | tf_op jit(solution)/shard_map/ppermute | solution.py:185
  22.8 3.9 %collective-permute-start.3 = (f32[32,2,32]{2,1,0:T(2,128)}, f32[32,2,32]{2,1,0:T(2,128)S(1)}, u32[]{:S(2)}, u32[]{:S(2)}) collective-permute-start(f32[32,2,32]{2,1,0:T(2,128)} %param.7), channel_id=1, source_target_pairs={{0,0},{1,8},{2,16},{3,24},{4,64},{5,72},{6,80},{7,88},{8,128},{9,1... | collective-permute-start | bytes 24584 | tf_op jit(solution)/shard_map/ppermute | solution.py:183
  26.8 7.5 %collective-permute-done.3 = f32[32,2,32]{2,1,0:T(2,128)S(1)} collective-permute-done((f32[32,2,32]{2,1,0:T(2,128)}, f32[32,2,32]{2,1,0:T(2,128)S(1)}, u32[]{:S(2)}, u32[]{:S(2)}) %collective-permute-start.3) | collective-permute-done | bytes 8224 | tf_op jit(solution)/shard_map/ppermute | solution.py:183
  34.5 0.9 dynamic_update_slice.3.placed_ref
  35.4 1.9 %collective-permute-start.8 = (f32[32,768]{1,0:T(8,128)S(1)}, f32[32,768]{1,0:T(8,128)S(1)}, u32[]{:S(2)}, u32[]{:S(2)}) collective-permute-start(f32[32,768]{1,0:T(8,128)S(1)} %slice.29), channel_id=1, source_target_pairs={{0,128},{32,160},{64,192},{96,224},{128,256},{160,288},{192,320},{... | collective-permute-start | bytes 294920 | tf_op jit(solution)/shard_map/ppermute | solution.py:181
  37.3 7.1 %collective-permute-start.6 = (f32[32,768]{1,0:T(8,128)S(1)}, f32[32,768]{1,0:T(8,128)S(1)}, u32[]{:S(2)}, u32[]{:S(2)}) collective-permute-start(f32[32,768]{1,0:T(8,128)S(1)} %slice.28), channel_id=1, source_target_pairs={{0,384},{32,416},{64,448},{96,480},{128,0},{160,32},{192,64},{224,... | collective-permute-start | bytes 294920 | tf_op jit(solution)/shard_map/ppermute | solution.py:180
  44.4 1.9 %collective-permute-start.9 = (f32[64,768]{1,0:T(8,128)S(1)}, f32[64,768]{1,0:T(8,128)S(1)}, u32[]{:S(2)}, u32[]{:S(2)}) collective-permute-start(f32[64,768]{1,0:T(8,128)S(1)} %collective-permute-done.7.refs_7_), channel_id=1, source_target_pairs={{0,64},{32,96},{64,128},{96,160},{128,192},{160,224},{192,256},{22... | collective-permute-start | bytes 589832 | tf_op jit(solution)/shard_map/ppermute | solution.py:177
  46.3 4.5 %collective-permute-start.5 = (f32[64,768]{1,0:T(8,128)S(1)}, f32[64,768]{1,0:T(8,128)S(1)}, u32[]{:S(2)}, u32[]{:S(2)}) collective-permute-start(f32[64,768]{1,0:T(8,128)S(1)} %collective-permute-done.4.refs_2_), channel_id=1, source_target_pairs={{0,448},{32,480},{64,0},{96,32},{128,64},{160,96},{192,128},{224,1... | collective-permute-start | bytes 589832 | tf_op jit(solution)/shard_map/ppermute | solution.py:178
  50.8 1.0 pad_maximum_fusion
  51.8 0.7 collective-permute-done.9.refs_6_
  52.5 1.6 %collective-permute-done.5.refs_3_ = f32[64,768]{1,0:T(8,128)S(1)} collective-permute-done((f32[64,768]{1,0:T(8,128)S(1)}, f32[64,768]{1,0:T(8,128)S(1)}, u32[]{:S(2)}, u32[]{:S(2)}) %collective-permute-start.5) | collective-permute-done | bytes 196640 | tf_op jit(solution)/shard_map/ppermute | solution.py:178
  54.1 1.6 %shard_map.69 = (f32[64,2,512]{2,1,0:T(2,128)}, f32[512,768]{1,0:T(8,128)S(1)}) custom-call(f32[128,768]{1,0:T(8,128)S(1)} %bitcast.32, f32[128,512]{1,0:T(8,128)S(1)} %dynamic_update_slice.3.placed_ref, f32[64,768]{1,0:T(8,128)S(1)} %bitcast.38, f32[64,768]{1,0:T(8,128)S(1)} %collective-permute-done.1.refs_2_.refs_1_, ...), custom_call_target="tpu_custom_call" | custom-call | flops 301989888 | bytes 3145728 | tf_op jit(solution)/shard_map/pallas_call | solution.py:112
  55.7 1.2 copy-done.4
  56.8 17.7 %all-to-all-start = ((f32[64,2,512]{2,1,0:T(2,128)}), f32[64,2,512]{2,1,0:T(2,128)S(1)}, u32[]{:S(2)}, u32[]{:S(2)}) async-start(f32[64,2,512]{2,1,0:T(2,128)} %get-tuple-element.6), calls=%async_computation | async-start | bytes 524288 | tf_op jit(solution)/shard_map/all_to_all | solution.py:200
  74.6 2.2 %collective-permute-start.11 = (f32[512,768]{1,0:T(8,128)}, f32[512,768]{1,0:T(8,128)}, u32[]{:S(2)}, u32[]{:S(2)}) collective-permute-start(f32[512,768]{1,0:T(8,128)} %copy-done.4), channel_id=1, source_target_pairs={{0,32},{32,0},{64,96},{96,64},{128,160},{160,128},{192,224},{224,1... | collective-permute-start | bytes 4718600 | tf_op jit(solution)/shard_map/ppermute | solution.py:197
  76.8 8.5 %all-to-all-done = f32[64,2,512]{2,1,0:T(2,128)S(1)} async-done(((f32[64,2,512]{2,1,0:T(2,128)}), f32[64,2,512]{2,1,0:T(2,128)S(1)}, u32[]{:S(2)}, u32[]{:S(2)}) %all-to-all-start) | async-done | bytes 262176 | tf_op jit(solution)/shard_map/all_to_all | solution.py:200
  85.8 2.2 %fusion.6 = f32[2,512]{1,0:T(2,128)S(1)} fusion(f32[2,512]{1,0:T(2,128)S(1)} %squeeze.17, f32[2,512,512]{2,1,0:T(8,128)} %param.8), kind=kOutput, calls=%fused_computation.8 | convolution fusion | flops 6291456 | bytes 1056768 | tf_op jit(solution)/shard_map/dot_general | solution.py:145
  88.0 1.0 convolution_subtract_fusion.1
  89.0 1.0 fusion.2
  92.3 0.8 broadcast_in_dim.7
  93.0 7.6 %all-to-all-start.1 = ((f32[32,2,1024]{2,1,0:T(2,128)}), f32[32,2,1024]{2,1,0:T(2,128)S(1)}, u32[]{:S(2)}, u32[]{:S(2)}) async-start(f32[32,2,1024]{2,1,0:T(2,128)} %broadcast_in_dim.7), calls=%async_computation.1 | async-start | bytes 524288 | tf_op jit(solution)/shard_map/all_to_all | solution.py:217
  100.8 10.2 %all-to-all-done.1 = f32[32,2,1024]{2,1,0:T(2,128)S(1)} async-done(((f32[32,2,1024]{2,1,0:T(2,128)}), f32[32,2,1024]{2,1,0:T(2,128)S(1)}, u32[]{:S(2)}, u32[]{:S(2)}) %all-to-all-start.1) | async-done | bytes 262176 | tf_op jit(solution)/shard_map/all_to_all | solution.py:217
  111.0 1.9 %reshape_reshape.3 = f32[64,16,2,32]{3,2,1,0:T(2,128)} reshape(f32[32,2,1024]{2,1,0:T(2,128)S(1)} %all-to-all-done.1) | data formatting | bytes 524288 | tf_op jit(solution)/shard_map/reshape;reshape | solution.py:223
  112.9 0.8 dynamic-slice_bitcast_fusion
  113.7 6.4 %collective-permute-start.10 = (f32[32,2,32]{2,1,0:T(2,128)S(1)}, f32[32,2,32]{2,1,0:T(2,128)S(1)}, u32[]{:S(2)}, u32[]{:S(2)}) collective-permute-start(f32[32,2,32]{2,1,0:T(2,128)S(1)} %dynamic-slice_bitcast_fusion), channel_id=1, source_target_pairs={{0,0},{1,1},{2,32},{3,33},{4,64},{5,65},{6,96},{7,97},{8,128},{9,1... | collective-permute-start | bytes 24584 | tf_op jit(solution)/shard_map/ppermute | solution.py:229
  120.2 9.4 %collective-permute-done.10 = f32[32,2,32]{2,1,0:T(2,128)S(1)} collective-permute-done((f32[32,2,32]{2,1,0:T(2,128)S(1)}, f32[32,2,32]{2,1,0:T(2,128)S(1)}, u32[]{:S(2)}, u32[]{:S(2)}) %collective-permute-start.10) | collective-permute-done | bytes 8224 | tf_op jit(solution)/shard_map/ppermute | solution.py:229
  129.7 3.0 %shard_map.70 = f32[64,768]{1,0:T(8,128)} custom-call(f32[64,768]{1,0:T(8,128)S(1)} %copy-done.2, f32[64,1024]{1,0:T(8,128)S(1)} %reshape.41.found_ref, f32[512,768]{1,0:T(8,128)S(1)} %copy-done.5, f32[512,768]{1,0:T(8,128)} %collective-permute-done.11.other_ref), custom_call_target="tpu_custom_call" | custom-call | flops 1811939328 | bytes 3145728 | tf_op jit(solution)/shard_map/pallas_call | solution.py:134
  (49 shorter events, 3.7 us)
Async XLA Ops:
  0.6 87.4 %copy-start = (f32[512,512]{1,0:T(8,128)S(1)}, f32[512,512]{1,0:T(8,128)}, u32[]{:S(2)}) copy-start(f32[512,512]{1,0:T(8,128)} %param.9) | copy-start | bytes 3145732
  0.6 19.2 %collective-permute-start.1 = (f32[64,768]{1,0:T(8,128)}, f32[64,768]{1,0:T(8,128)S(1)}, u32[]{:S(2)}, u32[]{:S(2)}) collective-permute-start(f32[64,768]{1,0:T(8,128)} %bitcast.34), channel_id=1, source_target_pairs={{0,448},{32,480},{64,0},{96,32},{128,64},{160,96},{192,128},{224,1... | collective-permute-start | bytes 589832 | tf_op jit(solution)/shard_map/ppermute | solution.py:176
  2.7 17.1 %collective-permute-start = (f32[64,768]{1,0:T(8,128)}, f32[64,768]{1,0:T(8,128)S(1)}, u32[]{:S(2)}, u32[]{:S(2)}) collective-permute-start(f32[64,768]{1,0:T(8,128)} %bitcast.35), channel_id=1, source_target_pairs={{0,64},{32,96},{64,128},{96,160},{128,192},{160,224},{192,256},{22... | collective-permute-start | bytes 589832 | tf_op jit(solution)/shard_map/ppermute | solution.py:175
  7.0 28.3 %collective-permute-start.7 = (f32[64,768]{1,0:T(8,128)}, f32[64,768]{1,0:T(8,128)S(1)}, u32[]{:S(2)}, u32[]{:S(2)}) collective-permute-start(f32[64,768]{1,0:T(8,128)} %bitcast.36), channel_id=1, source_target_pairs={{0,128},{32,160},{64,192},{96,224},{128,256},{160,288},{192,320},{... | collective-permute-start | bytes 589832 | tf_op jit(solution)/shard_map/ppermute | solution.py:173
  14.3 23.0 %collective-permute-start.4 = (f32[64,768]{1,0:T(8,128)}, f32[64,768]{1,0:T(8,128)S(1)}, u32[]{:S(2)}, u32[]{:S(2)}) collective-permute-start(f32[64,768]{1,0:T(8,128)} %bitcast.37), channel_id=1, source_target_pairs={{0,384},{32,416},{64,448},{96,480},{128,0},{160,32},{192,64},{224,... | collective-permute-start | bytes 589832 | tf_op jit(solution)/shard_map/ppermute | solution.py:174
  19.8 0.9 copy-start.1
  20.8 33.3 %copy-start.3 = (f32[2,32,768]{2,1,0:T(8,128)S(1)}, f32[2,32,768]{2,1,0:T(8,128)}, u32[]{:S(2)}) copy-start(f32[2,32,768]{2,1,0:T(8,128)} %param.5) | copy-start | bytes 589828
  20.8 30.0 %collective-permute-start.2 = (f32[64,768]{1,0:T(8,128)S(1)}, f32[64,768]{1,0:T(8,128)S(1)}, u32[]{:S(2)}, u32[]{:S(2)}) collective-permute-start(f32[64,768]{1,0:T(8,128)S(1)} %shard_map.68), channel_id=1, source_target_pairs={{0,32},{32,0},{64,96},{96,64},{128,160},{160,128},{192,224},{224,1... | collective-permute-start | bytes 589832 | tf_op jit(solution)/shard_map/ppermute | solution.py:185
  22.8 11.5 %collective-permute-start.3 = (f32[32,2,32]{2,1,0:T(2,128)}, f32[32,2,32]{2,1,0:T(2,128)S(1)}, u32[]{:S(2)}, u32[]{:S(2)}) collective-permute-start(f32[32,2,32]{2,1,0:T(2,128)} %param.7), channel_id=1, source_target_pairs={{0,0},{1,8},{2,16},{3,24},{4,64},{5,72},{6,80},{7,88},{8,128},{9,1... | collective-permute-start | bytes 24584 | tf_op jit(solution)/shard_map/ppermute | solution.py:183
  35.4 16.4 %collective-permute-start.8 = (f32[32,768]{1,0:T(8,128)S(1)}, f32[32,768]{1,0:T(8,128)S(1)}, u32[]{:S(2)}, u32[]{:S(2)}) collective-permute-start(f32[32,768]{1,0:T(8,128)S(1)} %slice.29), channel_id=1, source_target_pairs={{0,128},{32,160},{64,192},{96,224},{128,256},{160,288},{192,320},{... | collective-permute-start | bytes 294920 | tf_op jit(solution)/shard_map/ppermute | solution.py:181
  37.3 14.5 %collective-permute-start.6 = (f32[32,768]{1,0:T(8,128)S(1)}, f32[32,768]{1,0:T(8,128)S(1)}, u32[]{:S(2)}, u32[]{:S(2)}) collective-permute-start(f32[32,768]{1,0:T(8,128)S(1)} %slice.28), channel_id=1, source_target_pairs={{0,384},{32,416},{64,448},{96,480},{128,0},{160,32},{192,64},{224,... | collective-permute-start | bytes 294920 | tf_op jit(solution)/shard_map/ppermute | solution.py:180
  44.4 8.1 %collective-permute-start.9 = (f32[64,768]{1,0:T(8,128)S(1)}, f32[64,768]{1,0:T(8,128)S(1)}, u32[]{:S(2)}, u32[]{:S(2)}) collective-permute-start(f32[64,768]{1,0:T(8,128)S(1)} %collective-permute-done.7.refs_7_), channel_id=1, source_target_pairs={{0,64},{32,96},{64,128},{96,160},{128,192},{160,224},{192,256},{22... | collective-permute-start | bytes 589832 | tf_op jit(solution)/shard_map/ppermute | solution.py:177
  46.3 7.8 %collective-permute-start.5 = (f32[64,768]{1,0:T(8,128)S(1)}, f32[64,768]{1,0:T(8,128)S(1)}, u32[]{:S(2)}, u32[]{:S(2)}) collective-permute-start(f32[64,768]{1,0:T(8,128)S(1)} %collective-permute-done.4.refs_2_), channel_id=1, source_target_pairs={{0,448},{32,480},{64,0},{96,32},{128,64},{160,96},{192,128},{224,1... | collective-permute-start | bytes 589832 | tf_op jit(solution)/shard_map/ppermute | solution.py:178
  55.7 1.2 copy-start.4
  56.8 32.2 %copy-start.6 = (f32[2,512,512]{2,1,0:T(8,128)S(1)}, f32[2,512,512]{2,1,0:T(8,128)}, u32[]{:S(2)}) copy-start(f32[2,512,512]{2,1,0:T(8,128)} %param.8) | copy-start | bytes 6291460
  56.8 28.5 %all-to-all-start = ((f32[64,2,512]{2,1,0:T(2,128)}), f32[64,2,512]{2,1,0:T(2,128)S(1)}, u32[]{:S(2)}, u32[]{:S(2)}) async-start(f32[64,2,512]{2,1,0:T(2,128)} %get-tuple-element.6), calls=%async_computation | async-start | bytes 524288 | tf_op jit(solution)/shard_map/all_to_all | solution.py:200
  74.6 55.1 %collective-permute-start.11 = (f32[512,768]{1,0:T(8,128)}, f32[512,768]{1,0:T(8,128)}, u32[]{:S(2)}, u32[]{:S(2)}) collective-permute-start(f32[512,768]{1,0:T(8,128)} %copy-done.4), channel_id=1, source_target_pairs={{0,32},{32,0},{64,96},{96,64},{128,160},{160,128},{192,224},{224,1... | collective-permute-start | bytes 4718600 | tf_op jit(solution)/shard_map/ppermute | solution.py:197
  88.0 3.2 %copy-start.7 = (f32[2,512,512]{2,1,0:T(8,128)S(1)}, f32[2,512,512]{2,1,0:T(8,128)}, u32[]{:S(2)}) copy-start(f32[2,512,512]{2,1,0:T(8,128)} %param.8) | copy-start | bytes 6291460
  91.2 38.5 %copy-start.2 = (f32[64,768]{1,0:T(8,128)S(1)}, f32[64,768]{1,0:T(8,128)}, u32[]{:S(2)}) copy-start(f32[64,768]{1,0:T(8,128)} %solved_ref.1) | copy-start | bytes 589828
  91.2 38.5 %copy-start.5 = (f32[512,768]{1,0:T(8,128)S(1)}, f32[512,768]{1,0:T(8,128)}, u32[]{:S(2)}) copy-start(f32[512,768]{1,0:T(8,128)} %copy-done.4) | copy-start | bytes 4718596
  93.0 17.9 %all-to-all-start.1 = ((f32[32,2,1024]{2,1,0:T(2,128)}), f32[32,2,1024]{2,1,0:T(2,128)S(1)}, u32[]{:S(2)}, u32[]{:S(2)}) async-start(f32[32,2,1024]{2,1,0:T(2,128)} %broadcast_in_dim.7), calls=%async_computation.1 | async-start | bytes 524288 | tf_op jit(solution)/shard_map/all_to_all | solution.py:217
  113.7 16.0 %collective-permute-start.10 = (f32[32,2,32]{2,1,0:T(2,128)S(1)}, f32[32,2,32]{2,1,0:T(2,128)S(1)}, u32[]{:S(2)}, u32[]{:S(2)}) collective-permute-start(f32[32,2,32]{2,1,0:T(2,128)S(1)} %dynamic-slice_bitcast_fusion), channel_id=1, source_target_pairs={{0,0},{1,1},{2,32},{3,33},{4,64},{5,65},{6,96},{7,97},{8,128},{9,1... | collective-permute-start | bytes 24584 | tf_op jit(solution)/shard_map/ppermute | solution.py:229

commit v3 on v0

v3 whole, which is shorter than its diff:
```python
import jax
import jax.numpy as jnp
from jax import lax
from jax.experimental import pallas as pl
from jax.experimental.pallas import tpu as pltpu
from jax.sharding import PartitionSpec as P

PLANES = 8
CORES = 2
ROWS = PLANES * CORES
HALF_RING = ROWS // 2
COLS = 32
VMEM_BYTES = 16 * 1024 * 1024


def core_swap():
    return [(row, row ^ 1) for row in range(ROWS)]


def apart(step):
    return [
        (plane * CORES + core, (plane + (step, -step)[core]) % PLANES * CORES + core)
        for plane in range(PLANES)
        for core in range(CORES)
    ]


def ring_place(unknown_row, plane):
    return (unknown_row - CORES * plane + HALF_RING - 1) % ROWS


def window_to_work():
    pairs = []
    for row in range(ROWS):
        for col in range(COLS):
            rhs_row, half = divmod(col, 2)
            plane, rhs_core = divmod(rhs_row, CORES)
            keeper, slot = divmod(ring_place(row, plane), HALF_RING)
            target = (rhs_core * 2 + half) * HALF_RING + slot
            pairs.append((row * COLS + col, (plane * CORES + keeper) * COLS + target))
    return pairs


def work_to_window():
    return [
        (row * COLS + col, (col // 2) * COLS + 2 * row + col % 2)
        for row in range(ROWS)
        for col in range(COLS)
    ]


def halves(x):
    high = x.astype(jnp.bfloat16)
    return high, (x - high.astype(jnp.float32)).astype(jnp.bfloat16)


def rounded_dot(left, right, contract):
    (left_up, left_down), (right_up, right_down) = left, right

    def one(x, y):
        return lax.dot_general(x, y, (contract, ((), ())), preferred_element_type=jnp.float32)

    return one(left_up, right_up) + one(left_down, right_up) + one(left_up, right_down)


def in_vmem():
    return pl.BlockSpec(memory_space=pltpu.VMEM)


def kernel_call(body, out_shape, in_specs, out_specs, scratch=(), flops=0, moved=0):
    return pl.pallas_call(
        body,
        out_shape=out_shape,
        in_specs=in_specs,
        out_specs=out_specs,
        scratch_shapes=scratch,
        compiler_params=pltpu.CompilerParams(vmem_limit_bytes=VMEM_BYTES),
        cost_estimate=pl.CostEstimate(flops=flops, bytes_accessed=moved, transcendentals=0),
    )


def reduce_panel(places, solved, solved_other, window, pieces):
    rows, width = solved.shape
    unit = pieces[0].shape[0]
    unknowns = HALF_RING * unit
    each = rows // COLS

    def body(places_ref, solved_ref, other_ref, window_ref, *refs):
        own, one, two, three, four, out_ref, panel_out, panel, partial, sem = refs
        core = places_ref[0]

        def put(place, ref, at):
            start = pl.multiple_of(jnp.where(core == 0, HALF_RING - 1 - place, place) * unit, unit)
            panel[pl.ds(start, unit)] = ref[at * unit : (at + 1) * unit]

        put(0, own, 0)
        for step, ref in ((1, one), (2, two), (3, three)):
            put(2 * step, ref, 0)
            put(2 * step - 1, ref, 1)
        put(HALF_RING - 1, four, 0)
        copy = pltpu.make_async_copy(panel, panel_out, sem)
        copy.start()
        solved_pair = jnp.concatenate([solved_ref[...], other_ref[...]], axis=0)
        total = rounded_dot(halves(panel[...]), halves(solved_pair), ((1,), (1,)))
        partial[...] = -total.T
        lane = lax.broadcasted_iota(jnp.int32, (rows // 2, unknowns), 1)
        spread = jnp.concatenate([window_ref[...]] * HALF_RING, axis=1)
        first = pl.multiple_of(places_ref[1], rows // 2)
        partial[pl.ds(first, rows // 2)] += jnp.where(lane // unit == places_ref[2], spread, 0.0)
        for member in range(COLS):
            at = member * each
            out_ref[member, :each] = partial[at : at + each]
            out_ref[member, each:] = partial[rows + at : rows + at + each]
        copy.wait()

    return kernel_call(
        body,
        [
            jax.ShapeDtypeStruct((COLS, 2 * each, unknowns), jnp.float32),
            jax.ShapeDtypeStruct((unknowns, width), jnp.float32),
        ],
        [pl.BlockSpec(memory_space=pltpu.SMEM)] + [in_vmem()] * (3 + len(pieces)),
        [in_vmem(), pl.BlockSpec(memory_space=pltpu.MemorySpace.HBM)],
        scratch=[
            pltpu.VMEM((unknowns, width), jnp.float32),
            pltpu.VMEM((2 * rows, unknowns), jnp.float32),
            pltpu.SemaphoreType.DMA,
        ],
        flops=12 * rows * unknowns * width,
        moved=8 * unknowns * width,
    )(places, solved, solved_other, window, *pieces)


def panel_solve(residual, inverses, coupling):
    each, size = residual.shape[1:]
    deep = 16

    def body(residual_ref, inverses_ref, coupling_ref, out_ref, padded):
        def times(x, matrix, across):
            up, down = halves(x)
            contract = (((1,), (1 if across else 0,)), ((), ()))
            both = lax.dot_general(
                jnp.concatenate([up, down], axis=0),
                matrix[0],
                contract,
                preferred_element_type=jnp.float32,
            )
            rest = lax.dot_general(up, matrix[1], contract, preferred_element_type=jnp.float32)
            return both[:deep] + both[deep:] + rest

        padded[...] = jnp.zeros_like(padded)
        padded[0, :each] = residual_ref[0]
        padded[1, :each] = residual_ref[1]
        lead, follow, link = halves(inverses_ref[0]), halves(inverses_ref[1]), halves(coupling_ref[...])
        forward_lead = times(padded[0], lead, True)
        forward_next = times(padded[1] - times(forward_lead, link, True), follow, True)
        backward_next = times(forward_next, follow, False)
        backward_lead = times(forward_lead - times(backward_next, link, False), lead, False)
        out_ref[0] = backward_lead[:each]
        out_ref[1] = backward_next[:each]

    return kernel_call(
        body,
        jax.ShapeDtypeStruct(residual.shape, residual.dtype),
        [in_vmem()] * 3,
        in_vmem(),
        scratch=[pltpu.VMEM((2, deep, size), jnp.float32)],
        flops=36 * deep * size * size,
        moved=12 * size * size,
    )(residual, inverses, coupling)


def correct(solved, found, panel, panel_other):
    def body(solved_ref, found_ref, panel_ref, other_ref, out_ref):
        half = panel_ref.shape[0]
        contract = ((1,), (0,))
        total = rounded_dot(halves(found_ref[:, :half]), halves(panel_ref[...]), contract)
        total += rounded_dot(halves(found_ref[:, half:]), halves(other_ref[...]), contract)
        out_ref[...] = solved_ref[...] - total

    rows, width = solved.shape
    return kernel_call(
        body,
        jax.ShapeDtypeStruct(solved.shape, solved.dtype),
        [in_vmem()] * 4,
        in_vmem(),
        flops=36 * rows * found.shape[1] * width,
        moved=4 * found.shape[1] * width,
    )(solved, found, panel, panel_other)


def turn(blocks, start):
    twice = jnp.concatenate([blocks, blocks], axis=1)
    return lax.dynamic_slice_in_dim(twice, start, ROWS, 1)


def shards(factor, solved, rhs_window, inverses, coupling):
    rows, width = solved.shape
    part = factor.shape[1]
    row = lax.axis_index("row")
    col = lax.axis_index("col")
    plane, core = row // CORES, row % CORES

    own = factor.reshape(2 * part, width)
    both = jnp.concatenate([own, lax.ppermute(own, "row", core_swap())], axis=0)
    two = lax.ppermute(both, "row", apart(2))
    one = lax.ppermute(both, "row", apart(1))
    solved_other = lax.ppermute(solved, "row", core_swap())
    window = lax.ppermute(rhs_window, ("row", "col"), window_to_work())
    four = lax.ppermute(two[2 * part :], "row", apart(2))
    three = lax.ppermute(two, "row", apart(1))

    places = jnp.stack(
        [core, ((col // 16) ^ core) * rows + col // 8 % 2 * (rows // 2), col % 8]
    ).astype(jnp.int32)
    partial, panel = reduce_panel(
        places,
        solved,
        solved_other,
        window.reshape(rows // 2, 2 * part),
        [own, one, two, three, four],
    )
    panel_other = lax.ppermute(panel, "row", core_swap())

    each = rows // COLS
    spread = lax.all_to_all(partial, "col", 0, 0, tiled=True)
    residual = jnp.sum(spread, axis=0)
    residual_other = lax.ppermute(residual[each:], "row", core_swap())
    pair = jnp.stack([residual[:each], residual_other], axis=1)
    pair = jnp.where(core == 0, pair, pair[:, ::-1]).reshape(each, ROWS, 2, part)
    start = (HALF_RING - 1 - CORES * plane) % ROWS
    whole = jnp.transpose(turn(pair, start), (2, 0, 1, 3)).reshape(2, each, -1)
    found = panel_solve(whole, inverses, coupling).reshape(2, each, ROWS, part)
    found = turn(jnp.transpose(found, (1, 2, 0, 3)), (ROWS - start) % ROWS)
    found = found.reshape(each, CORES, -1)
    found = jnp.where(core == 0, found, found[:, ::-1]).reshape(each, -1)
    gathered = lax.all_to_all(
        jnp.broadcast_to(found, (COLS,) + found.shape), "col", 0, 0, tiled=True
    ).reshape(rows, -1)

    place = ring_place(col // 2, plane)
    slot = (place // HALF_RING ^ core) * HALF_RING + place % HALF_RING
    mine = lax.dynamic_slice(
        gathered, (col % 2 * (rows // 2), slot * 2 * part), (rows // 2, 2 * part)
    ).reshape(rows // 2, 2, part)
    owned = lax.ppermute(mine, ("row", "col"), work_to_window())
    return owned, correct(solved, gathered, panel, panel_other)


def solution(mesh):
    in_specs = (P(None, "row", "col"), P("row", "col"), P("col", None, "row"), P(), P())
    out_specs = (P("col", None, "row"), P("row", "col"))
    return jax.shard_map(shards, mesh=mesh, in_specs=in_specs, out_specs=out_specs, check_vma=False)
```

time: 430 us -> 120 us (0.28)
  the two profiles are of different devices: /device:TPU:6 before, /device:TPU:68 now
where the time goes in v3:
time: 120 us
  starting transfers between devices  51.8 us (43%)
  waiting for transfers between devices  49.3 us (41%)
  local copies, waits for them, and re-layouts  7.73 us (6%)
  Pallas kernels  7.27 us (6%)
  other arithmetic  2.6 us (2%)
    all_to_all x1, waiting for transfers between devices, shards(): lax.all_to_all(jnp.broadcast_to(found, (COLS,) + found.shape), 'col', 0,...  11 us
    ppermute x1, waiting for transfers between devices, shards(): window = lax.ppermute(rhs_window, ('row', 'col'), window_to_work())  10.9 us
    ppermute x1, waiting for transfers between devices, shards(): owned = lax.ppermute(mine, ('row', 'col'), work_to_window())  8.77 us
    ppermute x1, waiting for transfers between devices, shards(): two = lax.ppermute(both, 'row', apart(2))  8.6 us
    all_to_all x1, starting transfers between devices, shards(): spread = lax.all_to_all(partial, 'col', 0, 0, tiled=True)  7.61 us
    all_to_all x1, waiting for transfers between devices, shards(): spread = lax.all_to_all(partial, 'col', 0, 0, tiled=True)  7.36 us
    ppermute x1, starting transfers between devices, shards(): owned = lax.ppermute(mine, ('row', 'col'), work_to_window())  7.25 us
    all_to_all x1, starting transfers between devices, shards(): lax.all_to_all(jnp.broadcast_to(found, (COLS,) + found.shape), 'col', 0,...  6.17 us
  transfers between devices with their start and end apart: 12, of which 7 were waited for; matrix products, arithmetic and copies ran while one was open for 3% of the time, Pallas kernels for 1%

profile of v3, /device:TPU:68, one launch (start us, length us, event | category | flops | bytes accessed | tf_op | source)
XLA Modules:
  0.0 119.8 jit_solution(7258740442186900227)
XLA Ops:
  0.6 1.9 %collective-permute-start.2 = (f32[64,768]{1,0:T(8,128)}, f32[64,768]{1,0:T(8,128)S(1)}, u32[]{:S(2)}, u32[]{:S(2)}) collective-permute-start(f32[64,768]{1,0:T(8,128)} %bitcast.16), channel_id=1, source_target_pairs={{0,32},{32,0},{64,96},{96,64},{128,160},{160,128},{192,224},{224,1... | collective-permute-start | bytes 589832 | tf_op jit(solution)/shard_map/ppermute | solution.py:205
  2.6 1.6 %collective-permute-done.2 = f32[64,768]{1,0:T(8,128)S(1)} collective-permute-done((f32[64,768]{1,0:T(8,128)}, f32[64,768]{1,0:T(8,128)S(1)}, u32[]{:S(2)}, u32[]{:S(2)}) %collective-permute-start.2) | collective-permute-done | bytes 196640 | tf_op jit(solution)/shard_map/ppermute | solution.py:205
  4.2 1.7 %pad_maximum_fusion = f32[128,768]{1,0:T(8,128)} fusion(f32[64,768]{1,0:T(8,128)S(1)} %collective-permute-done.2, f32[64,768]{1,0:T(8,128)} %bitcast.17), kind=kLoop, calls=%fused_computation | loop fusion | flops 98304 | bytes 786432 | tf_op jit(solution)/shard_map/concatenate | solution.py:205
  5.9 6.1 %collective-permute-start.4 = (f32[128,768]{1,0:T(8,128)}, f32[128,768]{1,0:T(8,128)S(1)}, u32[]{:S(2)}, u32[]{:S(2)}) collective-permute-start(f32[128,768]{1,0:T(8,128)} %pad_maximum_fusion), channel_id=1, source_target_pairs={{0,128},{32,416},{64,192},{96,480},{128,256},{160,32},{192,320},{2... | collective-permute-start | bytes 1179656 | tf_op jit(solution)/shard_map/ppermute | solution.py:206
  12.0 5.5 %collective-permute-start.3 = (f32[128,768]{1,0:T(8,128)}, f32[128,768]{1,0:T(8,128)}, u32[]{:S(2)}, u32[]{:S(2)}) collective-permute-start(f32[128,768]{1,0:T(8,128)} %pad_maximum_fusion), channel_id=1, source_target_pairs={{0,64},{32,480},{64,128},{96,32},{128,192},{160,96},{192,256},{224... | collective-permute-start | bytes 1179656 | tf_op jit(solution)/shard_map/ppermute | solution.py:207
  17.5 8.6 %collective-permute-done.4.refs_2_ = f32[128,768]{1,0:T(8,128)S(1)} collective-permute-done((f32[128,768]{1,0:T(8,128)}, f32[128,768]{1,0:T(8,128)S(1)}, u32[]{:S(2)}, u32[]{:S(2)}) %collective-permute-start.4) | collective-permute-done | bytes 393248 | tf_op jit(solution)/shard_map/ppermute | solution.py:206
  26.1 1.9 %collective-permute-start.5 = (f32[128,768]{1,0:T(8,128)S(1)}, f32[128,768]{1,0:T(8,128)}, u32[]{:S(2)}, u32[]{:S(2)}) collective-permute-start(f32[128,768]{1,0:T(8,128)S(1)} %collective-permute-done.4.refs_2_), channel_id=1, source_target_pairs={{0,64},{32,480},{64,128},{96,32},{128,192},{160,96},{192,256},{224... | collective-permute-start | bytes 1179656 | tf_op jit(solution)/shard_map/ppermute | solution.py:211
  28.0 1.9 %collective-permute-start = (f32[64,768]{1,0:T(8,128)}, f32[64,768]{1,0:T(8,128)}, u32[]{:S(2)}, u32[]{:S(2)}) collective-permute-start(f32[64,768]{1,0:T(8,128)} %solved_ref.3), channel_id=1, source_target_pairs={{0,32},{32,0},{64,96},{96,64},{128,160},{160,128},{192,224},{224,1... | collective-permute-start | bytes 589832 | tf_op jit(solution)/shard_map/ppermute | solution.py:208
  29.9 0.7 slice.12
  30.6 5.7 %collective-permute-start.6 = (f32[64,768]{1,0:T(8,128)}, f32[64,768]{1,0:T(8,128)}, u32[]{:S(2)}, u32[]{:S(2)}) collective-permute-start(f32[64,768]{1,0:T(8,128)} %slice.12), channel_id=1, source_target_pairs={{0,128},{32,416},{64,192},{96,480},{128,256},{160,32},{192,320},{2... | collective-permute-start | bytes 589832 | tf_op jit(solution)/shard_map/ppermute | solution.py:210
  36.3 3.9 %collective-permute-start.1 = (f32[32,2,32]{2,1,0:T(2,128)}, f32[32,2,32]{2,1,0:T(2,128)S(1)}, u32[]{:S(2)}, u32[]{:S(2)}) collective-permute-start(f32[32,2,32]{2,1,0:T(2,128)} %param.7), channel_id=1, source_target_pairs={{0,7},{1,15},{2,23},{3,31},{4,69},{5,77},{6,85},{7,93},{8,131},{9,... | collective-permute-start | bytes 24584 | tf_op jit(solution)/shard_map/ppermute | solution.py:209
  40.3 0.7 pad_add_fusion.places_ref
  40.9 10.9 %collective-permute-done.1 = f32[32,2,32]{2,1,0:T(2,128)S(1)} collective-permute-done((f32[32,2,32]{2,1,0:T(2,128)}, f32[32,2,32]{2,1,0:T(2,128)S(1)}, u32[]{:S(2)}, u32[]{:S(2)}) %collective-permute-start.1) | collective-permute-done | bytes 8224 | tf_op jit(solution)/shard_map/ppermute | solution.py:209
  52.0 1.1 copy-done.2
  53.0 0.9 copy-done.4
  54.0 0.7 copy-done.6
  54.6 2.5 %shard_map.68 = (f32[32,4,512]{2,1,0:T(4,128)S(1)}, f32[512,768]{1,0:T(8,128)S(1)}) custom-call(s32[3]{0:T(128)S(1)} %copy-done.6, f32[64,768]{1,0:T(8,128)S(1)} %copy-done.4, f32[64,768]{1,0:T(8,128)} %collective-permute-done.other_ref, f32[32,64]{1,0:T(8,128)S(1)} %reshape.31.window_ref, f32[64,768]{1,0:T(8,128)S(1)} %bitcast.18, ...), custom_call_target="tpu_custom_call" | custom-call | flops 301989888 | bytes 3145728 | tf_op jit(solution)/shard_map/pallas_call | solution.py:116
  57.1 0.7 copy-done.3
  57.8 1.2 copy-done.7
  59.0 7.6 %all-to-all-start = ((f32[32,4,512]{2,1,0:T(4,128)}), f32[32,4,512]{2,1,0:T(4,128)S(1)}, u32[]{:S(2)}, u32[]{:S(2)}) async-start(f32[32,4,512]{2,1,0:T(4,128)} %copy-done.3), calls=%async_computation | async-start | bytes 524288 | tf_op jit(solution)/shard_map/all_to_all | solution.py:226
  66.6 1.9 %collective-permute-start.9 = (f32[512,768]{1,0:T(8,128)}, f32[512,768]{1,0:T(8,128)}, u32[]{:S(2)}, u32[]{:S(2)}) collective-permute-start(f32[512,768]{1,0:T(8,128)} %copy-done.7), channel_id=1, source_target_pairs={{0,32},{32,0},{64,96},{96,64},{128,160},{160,128},{192,224},{224,1... | collective-permute-start | bytes 4718600 | tf_op jit(solution)/shard_map/ppermute | solution.py:223
  68.5 7.4 %all-to-all-done = f32[32,4,512]{2,1,0:T(4,128)S(1)} async-done(((f32[32,4,512]{2,1,0:T(4,128)}), f32[32,4,512]{2,1,0:T(4,128)S(1)}, u32[]{:S(2)}, u32[]{:S(2)}) %all-to-all-start) | async-done | bytes 262176 | tf_op jit(solution)/shard_map/all_to_all | solution.py:226
  75.9 1.9 %collective-permute-start.7 = (f32[2,512]{1,0:T(2,128)S(1)}, f32[2,512]{1,0:T(2,128)S(1)}, u32[]{:S(2)}, u32[]{:S(2)}) collective-permute-start(f32[2,512]{1,0:T(2,128)S(1)} %get-tuple-element.7), channel_id=1, source_target_pairs={{0,32},{32,0},{64,96},{96,64},{128,160},{160,128},{192,224},{224,1... | collective-permute-start | bytes 12296 | tf_op jit(solution)/shard_map/ppermute | solution.py:228
  77.9 1.1 collective-permute-done.7
  79.5 1.8 %shard_map.69 = f32[2,2,512]{2,1,0:T(2,128)S(1)} custom-call(f32[2,2,512]{2,1,0:T(2,128)S(1)} %reshape.34.residual_ref, f32[2,512,512]{2,1,0:T(8,128)S(1)} %copy-done, f32[512,512]{1,0:T(8,128)S(1)} %copy-done.1), custom_call_target="tpu_custom_call" | custom-call | flops 150994944 | bytes 3145728 | tf_op jit(solution)/shard_map/pallas_call | solution.py:162
  81.7 0.8 broadcast_in_dim.3
  82.5 6.2 %all-to-all-start.1 = ((f32[32,2,1024]{2,1,0:T(2,128)}), f32[32,2,1024]{2,1,0:T(2,128)S(1)}, u32[]{:S(2)}, u32[]{:S(2)}) async-start(f32[32,2,1024]{2,1,0:T(2,128)} %broadcast_in_dim.3), calls=%async_computation.1 | async-start | bytes 524288 | tf_op jit(solution)/shard_map/all_to_all | solution.py:237
  88.7 11.0 %all-to-all-done.1 = f32[32,2,1024]{2,1,0:T(2,128)S(1)} async-done(((f32[32,2,1024]{2,1,0:T(2,128)}), f32[32,2,1024]{2,1,0:T(2,128)S(1)}, u32[]{:S(2)}, u32[]{:S(2)}) %all-to-all-start.1) | async-done | bytes 262176 | tf_op jit(solution)/shard_map/all_to_all | solution.py:237
  100.1 7.2 %collective-permute-start.8 = (f32[32,2,32]{2,1,0:T(2,128)S(1)}, f32[32,2,32]{2,1,0:T(2,128)S(1)}, u32[]{:S(2)}, u32[]{:S(2)}) collective-permute-start(f32[32,2,32]{2,1,0:T(2,128)S(1)} %reshape.39), channel_id=1, source_target_pairs={{0,0},{1,1},{2,32},{3,33},{4,64},{5,65},{6,96},{7,97},{8,128},{9,1... | collective-permute-start | bytes 24584 | tf_op jit(solution)/shard_map/ppermute | solution.py:246
  107.3 8.8 %collective-permute-done.8 = f32[32,2,32]{2,1,0:T(2,128)S(1)} collective-permute-done((f32[32,2,32]{2,1,0:T(2,128)S(1)}, f32[32,2,32]{2,1,0:T(2,128)S(1)}, u32[]{:S(2)}, u32[]{:S(2)}) %collective-permute-start.8) | collective-permute-done | bytes 8224 | tf_op jit(solution)/shard_map/ppermute | solution.py:246
  116.1 3.0 %shard_map.70 = f32[64,768]{1,0:T(8,128)} custom-call(f32[64,768]{1,0:T(8,128)S(1)} %copy-done.5, f32[64,1024]{1,0:T(8,128)S(1)} %reshape.38.found_ref, f32[512,768]{1,0:T(8,128)S(1)} %copy-done.8, f32[512,768]{1,0:T(8,128)} %collective-permute-done.9.other_ref), custom_call_target="tpu_custom_call" | custom-call | flops 1811939328 | bytes 3145728 | tf_op jit(solution)/shard_map/pallas_call | solution.py:182
  119.2 0.6 copy.15
  (40 shorter events, 1.4 us)
Async XLA Ops:
  0.6 3.5 %collective-permute-start.2 = (f32[64,768]{1,0:T(8,128)}, f32[64,768]{1,0:T(8,128)S(1)}, u32[]{:S(2)}, u32[]{:S(2)}) collective-permute-start(f32[64,768]{1,0:T(8,128)} %bitcast.16), channel_id=1, source_target_pairs={{0,32},{32,0},{64,96},{96,64},{128,160},{160,128},{192,224},{224,1... | collective-permute-start | bytes 589832 | tf_op jit(solution)/shard_map/ppermute | solution.py:205
  5.9 20.2 %collective-permute-start.4 = (f32[128,768]{1,0:T(8,128)}, f32[128,768]{1,0:T(8,128)S(1)}, u32[]{:S(2)}, u32[]{:S(2)}) collective-permute-start(f32[128,768]{1,0:T(8,128)} %pad_maximum_fusion), channel_id=1, source_target_pairs={{0,128},{32,416},{64,192},{96,480},{128,256},{160,32},{192,320},{2... | collective-permute-start | bytes 1179656 | tf_op jit(solution)/shard_map/ppermute | solution.py:206
  12.0 40.0 %collective-permute-start.3 = (f32[128,768]{1,0:T(8,128)}, f32[128,768]{1,0:T(8,128)}, u32[]{:S(2)}, u32[]{:S(2)}) collective-permute-start(f32[128,768]{1,0:T(8,128)} %pad_maximum_fusion), channel_id=1, source_target_pairs={{0,64},{32,480},{64,128},{96,32},{128,192},{160,96},{192,256},{224... | collective-permute-start | bytes 1179656 | tf_op jit(solution)/shard_map/ppermute | solution.py:207
  26.1 25.9 %collective-permute-start.5 = (f32[128,768]{1,0:T(8,128)S(1)}, f32[128,768]{1,0:T(8,128)}, u32[]{:S(2)}, u32[]{:S(2)}) collective-permute-start(f32[128,768]{1,0:T(8,128)S(1)} %collective-permute-done.4.refs_2_), channel_id=1, source_target_pairs={{0,64},{32,480},{64,128},{96,32},{128,192},{160,96},{192,256},{224... | collective-permute-start | bytes 1179656 | tf_op jit(solution)/shard_map/ppermute | solution.py:211
  28.0 23.9 %collective-permute-start = (f32[64,768]{1,0:T(8,128)}, f32[64,768]{1,0:T(8,128)}, u32[]{:S(2)}, u32[]{:S(2)}) collective-permute-start(f32[64,768]{1,0:T(8,128)} %solved_ref.3), channel_id=1, source_target_pairs={{0,32},{32,0},{64,96},{96,64},{128,160},{160,128},{192,224},{224,1... | collective-permute-start | bytes 589832 | tf_op jit(solution)/shard_map/ppermute | solution.py:208
  30.6 21.3 %collective-permute-start.6 = (f32[64,768]{1,0:T(8,128)}, f32[64,768]{1,0:T(8,128)}, u32[]{:S(2)}, u32[]{:S(2)}) collective-permute-start(f32[64,768]{1,0:T(8,128)} %slice.12), channel_id=1, source_target_pairs={{0,128},{32,416},{64,192},{96,480},{128,256},{160,32},{192,320},{2... | collective-permute-start | bytes 589832 | tf_op jit(solution)/shard_map/ppermute | solution.py:210
  36.3 15.5 %collective-permute-start.1 = (f32[32,2,32]{2,1,0:T(2,128)}, f32[32,2,32]{2,1,0:T(2,128)S(1)}, u32[]{:S(2)}, u32[]{:S(2)}) collective-permute-start(f32[32,2,32]{2,1,0:T(2,128)} %param.7), channel_id=1, source_target_pairs={{0,7},{1,15},{2,23},{3,31},{4,69},{5,77},{6,85},{7,93},{8,131},{9,... | collective-permute-start | bytes 24584 | tf_op jit(solution)/shard_map/ppermute | solution.py:209
  51.9 27.5 %copy-start = (f32[2,512,512]{2,1,0:T(8,128)S(1)}, f32[2,512,512]{2,1,0:T(8,128)}, u32[]{:S(2)}) copy-start(f32[2,512,512]{2,1,0:T(8,128)} %inverses_ref.1) | copy-start | bytes 6291460
  51.9 27.5 %copy-start.1 = (f32[512,512]{1,0:T(8,128)S(1)}, f32[512,512]{1,0:T(8,128)}, u32[]{:S(2)}) copy-start(f32[512,512]{1,0:T(8,128)} %coupling_ref.1) | copy-start | bytes 3145732
  52.0 1.1 copy-start.2
  53.0 0.9 copy-start.4
  54.0 0.7 copy-start.6
  57.1 0.7 copy-start.3
  57.8 1.2 copy-start.7
  59.0 16.9 %all-to-all-start = ((f32[32,4,512]{2,1,0:T(4,128)}), f32[32,4,512]{2,1,0:T(4,128)S(1)}, u32[]{:S(2)}, u32[]{:S(2)}) async-start(f32[32,4,512]{2,1,0:T(4,128)} %copy-done.3), calls=%async_computation | async-start | bytes 524288 | tf_op jit(solution)/shard_map/all_to_all | solution.py:226
  66.6 49.5 %collective-permute-start.9 = (f32[512,768]{1,0:T(8,128)}, f32[512,768]{1,0:T(8,128)}, u32[]{:S(2)}, u32[]{:S(2)}) collective-permute-start(f32[512,768]{1,0:T(8,128)} %copy-done.7), channel_id=1, source_target_pairs={{0,32},{32,0},{64,96},{96,64},{128,160},{160,128},{192,224},{224,1... | collective-permute-start | bytes 4718600 | tf_op jit(solution)/shard_map/ppermute | solution.py:223
  75.9 3.1 %collective-permute-start.7 = (f32[2,512]{1,0:T(2,128)S(1)}, f32[2,512]{1,0:T(2,128)S(1)}, u32[]{:S(2)}, u32[]{:S(2)}) collective-permute-start(f32[2,512]{1,0:T(2,128)S(1)} %get-tuple-element.7), channel_id=1, source_target_pairs={{0,32},{32,0},{64,96},{96,64},{128,160},{160,128},{192,224},{224,1... | collective-permute-start | bytes 12296 | tf_op jit(solution)/shard_map/ppermute | solution.py:228
  81.3 34.9 %copy-start.5 = (f32[64,768]{1,0:T(8,128)S(1)}, f32[64,768]{1,0:T(8,128)}, u32[]{:S(2)}) copy-start(f32[64,768]{1,0:T(8,128)} %solved_ref.3) | copy-start | bytes 589828
  81.3 34.9 %copy-start.8 = (f32[512,768]{1,0:T(8,128)S(1)}, f32[512,768]{1,0:T(8,128)}, u32[]{:S(2)}) copy-start(f32[512,768]{1,0:T(8,128)} %copy-done.7) | copy-start | bytes 4718596
  82.5 17.2 %all-to-all-start.1 = ((f32[32,2,1024]{2,1,0:T(2,128)}), f32[32,2,1024]{2,1,0:T(2,128)S(1)}, u32[]{:S(2)}, u32[]{:S(2)}) async-start(f32[32,2,1024]{2,1,0:T(2,128)} %broadcast_in_dim.3), calls=%async_computation.1 | async-start | bytes 524288 | tf_op jit(solution)/shard_map/all_to_all | solution.py:237
  100.1 16.0 %collective-permute-start.8 = (f32[32,2,32]{2,1,0:T(2,128)S(1)}, f32[32,2,32]{2,1,0:T(2,128)S(1)}, u32[]{:S(2)}, u32[]{:S(2)}) collective-permute-start(f32[32,2,32]{2,1,0:T(2,128)S(1)} %reshape.39), channel_id=1, source_target_pairs={{0,0},{1,1},{2,32},{3,33},{4,64},{5,65},{6,96},{7,97},{8,128},{9,1... | collective-permute-start | bytes 24584 | tf_op jit(solution)/shard_map/ppermute | solution.py:246

commit v4 on v3

v4 whole, which is shorter than its diff:
```python
import jax
import jax.numpy as jnp
from jax import lax
from jax.experimental import pallas as pl
from jax.experimental.pallas import tpu as pltpu
from jax.sharding import PartitionSpec as P

PLANES = 8
CORES = 2
ROWS = PLANES * CORES
HALF_RING = ROWS // 2
COLS = 32
MIB = 1024 * 1024


def core_swap():
    return [(row, row ^ 1) for row in range(ROWS)]


def apart(step):
    return [
        (plane * CORES + core, (plane + (step, -step)[core]) % PLANES * CORES + core)
        for plane in range(PLANES)
        for core in range(CORES)
    ]


def ring_place(unknown_row, plane):
    return (unknown_row - CORES * plane + HALF_RING - 1) % ROWS


def window_to_work():
    pairs = []
    for row in range(ROWS):
        for col in range(COLS):
            rhs_row, half = divmod(col, 2)
            plane, rhs_core = divmod(rhs_row, CORES)
            keeper, slot = divmod(ring_place(row, plane), HALF_RING)
            target = (rhs_core * 2 + half) * HALF_RING + slot
            pairs.append((row * COLS + col, (plane * CORES + keeper) * COLS + target))
    return pairs


def work_to_window():
    return [
        (row * COLS + col, (col // 2) * COLS + 2 * row + col % 2)
        for row in range(ROWS)
        for col in range(COLS)
    ]


def halves(x):
    high = x.astype(jnp.bfloat16)
    return high, (x - high.astype(jnp.float32)).astype(jnp.bfloat16)


def rounded_dot(left, right, contract):
    (left_up, left_down), (right_up, right_down) = left, right

    def one(x, y):
        return lax.dot_general(x, y, (contract, ((), ())), preferred_element_type=jnp.float32)

    return one(left_up, right_up) + one(left_down, right_up) + one(left_up, right_down)


def in_vmem():
    return pl.BlockSpec(memory_space=pltpu.VMEM)


def kernel_call(body, out_shape, in_specs, out_specs, scratch=(), mib=16, flops=0, moved=0):
    return pl.pallas_call(
        body,
        out_shape=out_shape,
        in_specs=in_specs,
        out_specs=out_specs,
        scratch_shapes=scratch,
        compiler_params=pltpu.CompilerParams(vmem_limit_bytes=mib * MIB),
        cost_estimate=pl.CostEstimate(flops=flops, bytes_accessed=moved, transcendentals=0),
    )


def position():
    row = lax.axis_index("row")
    return row // CORES, row % CORES


def anywhere():
    return pl.BlockSpec(memory_space=pl.ANY)


def join(one, two, arrivals=()):
    def body(one_ref, two_ref, *refs):
        out_ref, sems = refs[-2:]
        rows = one_ref.shape[0]
        first = pltpu.make_async_copy(one_ref, out_ref.at[:rows], sems.at[0])
        second = pltpu.make_async_copy(two_ref, out_ref.at[rows:], sems.at[1])
        first.start()
        second.start()
        first.wait()
        second.wait()

    shape = (one.shape[0] + two.shape[0], one.shape[1])
    return kernel_call(
        body,
        jax.ShapeDtypeStruct(shape, one.dtype),
        [anywhere()] * (2 + len(arrivals)),
        anywhere(),
        scratch=[pltpu.SemaphoreType.DMA((2,))],
        mib=2,
        moved=16 * one.size,
    )(one, two, *arrivals)


def second_half(both):
    def body(both_ref, out_ref, sem):
        copy = pltpu.make_async_copy(both_ref.at[out_ref.shape[0] :], out_ref, sem)
        copy.start()
        copy.wait()

    shape = (both.shape[0] // 2, both.shape[1])
    return kernel_call(
        body,
        jax.ShapeDtypeStruct(shape, both.dtype),
        [anywhere()],
        anywhere(),
        scratch=[pltpu.SemaphoreType.DMA],
        mib=2,
        moved=4 * both.size,
    )(both)


def reduce_panel(solved, solved_other, window, pieces):
    rows, width = solved.shape
    part = pieces[0].shape[0] // 2
    side = HALF_RING * part
    unknowns = 2 * side
    each = rows // COLS

    def body(solved_ref, other_ref, window_ref, *refs):
        own, one, two, three, four, out_ref, panel, partial = refs
        core, col = position()[1], lax.axis_index("col")

        def put(place, ref, at):
            first = jnp.where(core == 0, HALF_RING - 1 - place, place) * part
            for k in range(2):
                start = pl.multiple_of(first + k * side, part)
                panel[pl.ds(start, part)] = ref[(2 * at + k) * part : (2 * at + k + 1) * part]

        put(0, own, 0)
        for step, ref in ((1, one), (2, two), (3, three)):
            put(2 * step, ref, 0)
            put(2 * step - 1, ref, 1)
        put(HALF_RING - 1, four, 0)
        solved_pair = jnp.concatenate([solved_ref[...], other_ref[...]], axis=0)
        total = rounded_dot(halves(panel[...]), halves(solved_pair), ((1,), (1,)))
        partial[...] = -total.T
        spread = jnp.concatenate(
            [jnp.concatenate([window_ref[:, k]] * HALF_RING, axis=1) for k in range(2)], axis=1
        )
        lane = lax.broadcasted_iota(jnp.int32, spread.shape, 1)
        slot = lane % side // part
        first = ((col // (2 * HALF_RING)) ^ core) * rows + col // HALF_RING % 2 * (rows // 2)
        first = pl.multiple_of(first, rows // 2)
        partial[pl.ds(first, rows // 2)] += jnp.where(slot == col % HALF_RING, spread, 0.0)
        for member in range(COLS):
            at = member * each
            out_ref[member, :each] = partial[at : at + each]
            out_ref[member, each:] = partial[rows + at : rows + at + each]

    return kernel_call(
        body,
        [
            jax.ShapeDtypeStruct((COLS, 2 * each, unknowns), jnp.float32),
            jax.ShapeDtypeStruct((unknowns, width), jnp.float32),
        ],
        [in_vmem()] * (3 + len(pieces)),
        [in_vmem()] * 2,
        scratch=[pltpu.VMEM((2 * rows, unknowns), jnp.float32)],
        mib=32,
        flops=12 * rows * unknowns * width,
        moved=8 * unknowns * width,
    )(solved, solved_other, window, *pieces)


def panel_solve(residual, residual_other, inverses, coupling):
    each, size = residual.shape
    side = size // 2
    part = side // HALF_RING
    deep = 16

    def body(residual_ref, other_ref, inverses_ref, coupling_ref, out_ref, padded):
        plane, core = position()
        first = (CORES * plane + HALF_RING + 1 + core * HALF_RING) % ROWS

        def times(x, matrix, across):
            up, down = halves(x)
            contract = (((1,), (1 if across else 0,)), ((), ()))
            both = lax.dot_general(
                jnp.concatenate([up, down], axis=0),
                matrix[0],
                contract,
                preferred_element_type=jnp.float32,
            )
            rest = lax.dot_general(up, matrix[1], contract, preferred_element_type=jnp.float32)
            return both[:deep] + both[deep:] + rest

        padded[...] = jnp.zeros_like(padded)
        for k in range(2):
            padded[k, :each, :side] = residual_ref[:, k * side : (k + 1) * side]
            padded[k, :each, side:] = other_ref[:, k * side : (k + 1) * side]
        turned = [pltpu.roll(padded[k], first * part, 1) for k in range(2)]
        lead, follow, link = halves(inverses_ref[0]), halves(inverses_ref[1]), halves(coupling_ref[...])
        forward_lead = times(turned[0], lead, True)
        forward_next = times(turned[1] - times(forward_lead, link, True), follow, True)
        backward_next = times(forward_next, follow, False)
        backward_lead = times(forward_lead - times(backward_next, link, False), lead, False)
        back = (ROWS - first) % ROWS
        for k, found in enumerate((backward_lead, backward_next)):
            found = pltpu.roll(found, back * part, 1)[:each]
            out_ref[:, k * side : (k + 1) * side] = found[:, :side]
            out_ref[:, size + k * side : size + (k + 1) * side] = found[:, side:]

    return kernel_call(
        body,
        jax.ShapeDtypeStruct((each, 2 * size), residual.dtype),
        [in_vmem()] * 4,
        in_vmem(),
        scratch=[pltpu.VMEM((2, deep, size), jnp.float32)],
        flops=36 * deep * size * size,
        moved=12 * size * size,
    )(residual, residual_other, inverses, coupling)


def correct(solved, found, panel, panel_other):
    rows, width = solved.shape
    size = panel.shape[0]
    side = size // 2
    part = side // HALF_RING

    def body(solved_ref, found_ref, panel_ref, other_ref, out_ref, owned_ref):
        (plane, core), col = position(), lax.axis_index("col")
        total = jnp.zeros((rows, width), jnp.float32)
        for start, ref in ((0, panel_ref), (size, other_ref)):
            up, down = halves(found_ref[:, start : start + size])
            panel_up, panel_down = halves(ref[...])
            both = jnp.dot(
                jnp.concatenate([up, down], axis=0), panel_up, preferred_element_type=jnp.float32
            )
            rest = jnp.dot(up, panel_down, preferred_element_type=jnp.float32)
            total += both[:rows] + both[rows:] + rest
        out_ref[...] = solved_ref[...] - total
        place = (col // 2 - CORES * plane + ROWS + HALF_RING - 1) % ROWS
        keeper = (place // HALF_RING) ^ core
        first = pl.multiple_of(col % 2 * (rows // 2), rows // 2)
        back = (HALF_RING - place % HALF_RING) % HALF_RING
        for k in range(2):
            start = pl.multiple_of(keeper * size + k * side, side)
            block = found_ref[pl.ds(first, rows // 2), pl.ds(start, side)]
            owned_ref[:, k] = pltpu.roll(block, back * part, 1)[:, :part]

    return kernel_call(
        body,
        [
            jax.ShapeDtypeStruct(solved.shape, solved.dtype),
            jax.ShapeDtypeStruct((rows // 2, 2, part), solved.dtype),
        ],
        [in_vmem()] * 4,
        [in_vmem()] * 2,
        flops=36 * rows * found.shape[1] * width,
        moved=4 * found.shape[1] * width,
    )(solved, found, panel, panel_other)


def shards(factor, solved, rhs_window, inverses, coupling):
    rows, width = solved.shape
    part = factor.shape[1]

    own = factor.reshape(2 * part, width)
    other = lax.ppermute(own, "row", core_swap())
    two = lax.ppermute(join(own, other), "row", apart(2))
    solved_other = lax.ppermute(solved, "row", core_swap())
    window = lax.ppermute(rhs_window, ("row", "col"), window_to_work())
    one = lax.ppermute(join(own, other, (solved_other, window)), "row", apart(1))
    three = lax.ppermute(two, "row", apart(1))
    four = lax.ppermute(second_half(two), "row", apart(2))

    partial, panel = reduce_panel(
        solved, solved_other, window, [own, one, two, three, four]
    )
    panel_other = lax.ppermute(panel, "row", core_swap())

    each = rows // COLS
    residual = jnp.sum(lax.all_to_all(partial, "col", 0, 0, tiled=True), axis=0)
    residual_other = lax.ppermute(residual[each:], "row", core_swap())
    found = panel_solve(residual[:each], residual_other, inverses, coupling)
    gathered = lax.all_to_all(
        jnp.broadcast_to(found, (COLS,) + found.shape), "col", 0, 0, tiled=True
    ).reshape(rows, -1)
    updated, mine = correct(solved, gathered, panel, panel_other)
    owned = lax.ppermute(mine, ("row", "col"), work_to_window())
    return owned, updated


def solution(mesh):
    in_specs = (P(None, "row", "col"), P("row", "col"), P("col", None, "row"), P(), P())
    out_specs = (P("col", None, "row"), P("row", "col"))
    return jax.shard_map(shards, mesh=mesh, in_specs=in_specs, out_specs=out_specs, check_vma=False)
```

time: 120 us -> 120 us (level)
  blocking collectives: 0 us -> 37.3 us
  starting transfers between devices: 51.8 us -> 34.2 us
  waiting for transfers between devices: 49.3 us -> 36.2 us
  local copies, waits for them, and re-layouts: 7.73 us -> 1.83 us
  other arithmetic: 2.6 us -> 1.01 us
  Pallas kernels: 7.27 us -> 8.5 us
    all_to_all x0 -> x2, blocking collectives: none -> 37.3 us  [the longest x1 20.3 us: shards(): residual = jnp.sum(lax.all_to_all(partial, 'col', 0, 0, tiled=True), axis=0)]
    all_to_all x2 -> x0, waiting for transfers between devices: 18.3 us -> none  [the longest x1 11 us: shards(): lax.all_to_all(jnp.broadcast_to(found, (COLS,) + found.shape), 'col', 0,...]
    all_to_all x2 -> x0, starting transfers between devices: 13.8 us -> none  [the longest x1 7.61 us: shards(): spread = lax.all_to_all(partial, 'col', 0, 0, tiled=True)]
    ppermute x4, starting transfers between devices: 19.1 us -> 12.6 us  [the longest x1 6.09 us: shards(): two = lax.ppermute(join(own, other), 'row', apart(2))]
    ppermute x1, starting transfers between devices: 1.92 us -> 5.72 us  [shards(): solved_other = lax.ppermute(solved, 'row', core_swap())]
    unnamed x20 -> x11, local copies, waits for them, and re-layouts: 5.15 us -> 1.56 us
    ppermute x4, waiting for transfers between devices: 10.2 us -> 13.6 us  [the longest x1 8.81 us: shards(): four = lax.ppermute(second_half(two), 'row', apart(2))]
    concatenate x2 -> x0, other arithmetic: 1.78 us -> none  [the longest x1 1.71 us: shards(): both = jnp.concatenate([own, lax.ppermute(own, 'row', core_swap())], axis=0)]
  transfers between devices with their start and end apart: 12 -> 10, of which waited for: 7 -> 6; matrix products, arithmetic and copies ran while one was open for 3% -> 1% of each run, Pallas kernels for 1% -> 2%
where the time goes in v4:
time: 120 us
  blocking collectives  37.3 us (31%)
  waiting for transfers between devices  36.2 us (30%)
  starting transfers between devices  34.2 us (29%)
  Pallas kernels  8.5 us (7%)
  local copies, waits for them, and re-layouts  1.83 us (2%)
    all_to_all x1, blocking collectives, shards(): residual = jnp.sum(lax.all_to_all(partial, 'col', 0, 0, tiled=True), axis=0)  20.3 us
    all_to_all x1, blocking collectives, shards(): lax.all_to_all(jnp.broadcast_to(found, (COLS,) + found.shape), 'col', 0,...  17 us
    ppermute x1, waiting for transfers between devices, shards(): window = lax.ppermute(rhs_window, ('row', 'col'), window_to_work())  11.1 us
    ppermute x1, waiting for transfers between devices, shards(): owned = lax.ppermute(mine, ('row', 'col'), work_to_window())  10.4 us
    ppermute x1, waiting for transfers between devices, shards(): four = lax.ppermute(second_half(two), 'row', apart(2))  8.81 us
    ppermute x1, starting transfers between devices, shards(): two = lax.ppermute(join(own, other), 'row', apart(2))  6.09 us
    ppermute x1, starting transfers between devices, shards(): solved_other = lax.ppermute(solved, 'row', core_swap())  5.72 us
    ppermute x1, starting transfers between devices, shards(): owned = lax.ppermute(mine, ('row', 'col'), work_to_window())  5.64 us
  transfers between devices with their start and end apart: 10, of which 6 were waited for; matrix products, arithmetic and copies ran while one was open for 1% of the time, Pallas kernels for 2%

profile of v4, /device:TPU:68, one launch (start us, length us, event | category | flops | bytes accessed | tf_op | source)
XLA Modules:
  0.0 119.7 jit_solution(10907680053447491112)
XLA Ops:
  0.6 1.9 %collective-permute-start.2 = (f32[64,768]{1,0:T(8,128)}, f32[64,768]{1,0:T(8,128)S(1)}, u32[]{:S(2)}, u32[]{:S(2)}) collective-permute-start(f32[64,768]{1,0:T(8,128)} %bitcast.1), channel_id=1, source_target_pairs={{0,32},{32,0},{64,96},{96,64},{128,160},{160,128},{192,224},{224,1... | collective-permute-start | bytes 589832 | tf_op jit(solution)/shard_map/ppermute | solution.py:279
  2.6 1.6 %collective-permute-done.2.two_ref = f32[64,768]{1,0:T(8,128)S(1)} collective-permute-done((f32[64,768]{1,0:T(8,128)}, f32[64,768]{1,0:T(8,128)S(1)}, u32[]{:S(2)}, u32[]{:S(2)}) %collective-permute-start.2) | collective-permute-done | bytes 196640 | tf_op jit(solution)/shard_map/ppermute | solution.py:279
  4.2 0.9 copy-done.1
  5.1 0.5 shard_map.69
  5.6 6.1 %collective-permute-start.4 = (f32[128,768]{1,0:T(8,128)S(1)}, f32[128,768]{1,0:T(8,128)S(1)}, u32[]{:S(2)}, u32[]{:S(2)}) collective-permute-start(f32[128,768]{1,0:T(8,128)S(1)} %shard_map.69), channel_id=1, source_target_pairs={{0,128},{32,416},{64,192},{96,480},{128,256},{160,32},{192,320},{2... | collective-permute-start | bytes 1179656 | tf_op jit(solution)/shard_map/ppermute | solution.py:280
  11.7 5.7 %collective-permute-start = (f32[64,768]{1,0:T(8,128)}, f32[64,768]{1,0:T(8,128)S(1)}, u32[]{:S(2)}, u32[]{:S(2)}) collective-permute-start(f32[64,768]{1,0:T(8,128)} %solved_ref.3), channel_id=1, source_target_pairs={{0,32},{32,0},{64,96},{96,64},{128,160},{160,128},{192,224},{224,1... | collective-permute-start | bytes 589832 | tf_op jit(solution)/shard_map/ppermute | solution.py:281
  17.4 4.5 %collective-permute-start.1 = (f32[32,2,32]{2,1,0:T(2,128)}, f32[32,2,32]{2,1,0:T(2,128)S(1)}, u32[]{:S(2)}, u32[]{:S(2)}) collective-permute-start(f32[32,2,32]{2,1,0:T(2,128)} %param.7), channel_id=1, source_target_pairs={{0,7},{1,15},{2,23},{3,31},{4,69},{5,77},{6,85},{7,93},{8,131},{9,... | collective-permute-start | bytes 24584 | tf_op jit(solution)/shard_map/ppermute | solution.py:282
  21.9 11.1 %collective-permute-done.1.refs_1_.window_ref = f32[32,2,32]{2,1,0:T(2,128)S(1)} collective-permute-done((f32[32,2,32]{2,1,0:T(2,128)}, f32[32,2,32]{2,1,0:T(2,128)S(1)}, u32[]{:S(2)}, u32[]{:S(2)}) %collective-permute-start.1) | collective-permute-done | bytes 8224 | tf_op jit(solution)/shard_map/ppermute | solution.py:282
  33.0 0.5 shard_map.68
  33.5 0.0 copy-start
  33.6 0.0 copy-start.3
  33.6 2.2 %collective-permute-start.3 = (f32[128,768]{1,0:T(8,128)S(1)}, f32[128,768]{1,0:T(8,128)S(1)}, u32[]{:S(2)}, u32[]{:S(2)}) collective-permute-start(f32[128,768]{1,0:T(8,128)S(1)} %shard_map.68), channel_id=1, source_target_pairs={{0,64},{32,480},{64,128},{96,32},{128,192},{160,96},{192,256},{224... | collective-permute-start | bytes 1179656 | tf_op jit(solution)/shard_map/ppermute | solution.py:283
  35.8 0.0 collective-permute-done.4.both_ref.refs_2_
  35.8 1.9 %collective-permute-start.5 = (f32[128,768]{1,0:T(8,128)S(1)}, f32[128,768]{1,0:T(8,128)S(1)}, u32[]{:S(2)}, u32[]{:S(2)}) collective-permute-start(f32[128,768]{1,0:T(8,128)S(1)} %collective-permute-done.4.both_ref.refs_2_), channel_id=1, source_target_pairs={{0,64},{32,480},{64,128},{96,32},{128,192},{160,96},{192,256},{224... | collective-permute-start | bytes 1179656 | tf_op jit(solution)/shard_map/ppermute | solution.py:284
  37.7 0.3 shard_map.70
  38.0 2.4 %collective-permute-start.6 = (f32[64,768]{1,0:T(8,128)S(1)}, f32[64,768]{1,0:T(8,128)S(1)}, u32[]{:S(2)}, u32[]{:S(2)}) collective-permute-start(f32[64,768]{1,0:T(8,128)S(1)} %shard_map.70), channel_id=1, source_target_pairs={{0,128},{32,416},{64,192},{96,480},{128,256},{160,32},{192,320},{2... | collective-permute-start | bytes 589832 | tf_op jit(solution)/shard_map/ppermute | solution.py:285
  40.4 3.1 %collective-permute-done.3.refs_1_ = f32[128,768]{1,0:T(8,128)S(1)} collective-permute-done((f32[128,768]{1,0:T(8,128)S(1)}, f32[128,768]{1,0:T(8,128)S(1)}, u32[]{:S(2)}, u32[]{:S(2)}) %collective-permute-start.3) | collective-permute-done | bytes 393248 | tf_op jit(solution)/shard_map/ppermute | solution.py:283
  43.5 8.8 %collective-permute-done.6.refs_4_ = f32[64,768]{1,0:T(8,128)S(1)} collective-permute-done((f32[64,768]{1,0:T(8,128)S(1)}, f32[64,768]{1,0:T(8,128)S(1)}, u32[]{:S(2)}, u32[]{:S(2)}) %collective-permute-start.6) | collective-permute-done | bytes 196640 | tf_op jit(solution)/shard_map/ppermute | solution.py:285
  52.3 2.2 %shard_map.71 = (f32[32,4,512]{2,1,0:T(4,128)S(1)}, f32[512,768]{1,0:T(8,128)}) custom-call(f32[64,768]{1,0:T(8,128)S(1)} %copy-done.4, f32[64,768]{1,0:T(8,128)S(1)} %collective-permute-done.refs_0_.other_ref, f32[32,2,32]{2,1,0:T(2,128)S(1)} %collective-permute-done.1.refs_1_.window_ref, f32[64,768]{1,0:T(8,128)S(1)} %bitcast.4, ...), custom_call_target="tpu_custom_call" | custom-call | flops 301989888 | bytes 3145728 | tf_op jit(solution)/shard_map/pallas_call | solution.py:170
  54.5 1.9 %collective-permute-start.8 = (f32[512,768]{1,0:T(8,128)}, f32[512,768]{1,0:T(8,128)}, u32[]{:S(2)}, u32[]{:S(2)}) collective-permute-start(f32[512,768]{1,0:T(8,128)} %get-tuple-element.7.panel_ref), channel_id=1, source_target_pairs={{0,32},{32,0},{64,96},{96,64},{128,160},{160,128},{192,224},{224,1... | collective-permute-start | bytes 4718600 | tf_op jit(solution)/shard_map/ppermute | solution.py:290
  56.4 20.3 %all_to_all.10 = f32[32,4,512]{2,1,0:T(4,128)} all-to-all(f32[32,4,512]{2,1,0:T(4,128)S(1)} %get-tuple-element.6), channel_id=1, replica_groups=mesh['row'=16,'col'=32] {'col'}, dimensions={0} | all-to-all | bytes 524288 | tf_op jit(solution)/shard_map/all_to_all | solution.py:293
  76.7 1.0 reduce_sum.9
  77.7 1.9 %collective-permute-start.7 = (f32[2,512]{1,0:T(2,128)S(1)}, f32[2,512]{1,0:T(2,128)S(1)}, u32[]{:S(2)}, u32[]{:S(2)}) collective-permute-start(f32[2,512]{1,0:T(2,128)S(1)} %get-tuple-element.10), channel_id=1, source_target_pairs={{0,32},{32,0},{64,96},{96,64},{128,160},{160,128},{192,224},{224,1... | collective-permute-start | bytes 12296 | tf_op jit(solution)/shard_map/ppermute | solution.py:294
  79.6 1.1 collective-permute-done.7.other_ref
  80.8 1.9 %shard_map.72 = f32[2,1024]{1,0:T(2,128)S(1)} custom-call(f32[2,512]{1,0:T(2,128)S(1)} %get-tuple-element.11.residual_ref, f32[2,512]{1,0:T(2,128)S(1)} %collective-permute-done.7.other_ref, f32[2,512,512]{2,1,0:T(8,128)S(1)} %copy-done, f32[512,512]{1,0:T(8,128)S(1)} %copy-done.3), custom_call_target="tpu_custom_call" | custom-call | flops 150994944 | bytes 3145728 | tf_op jit(solution)/shard_map/pallas_call | solution.py:223
  82.7 0.1 broadcast_in_dim.3
  82.8 17.0 %all_to_all.11 = f32[32,2,1024]{2,1,0:T(2,128)S(1)} all-to-all(f32[32,2,1024]{2,1,0:T(2,128)S(1)} %broadcast_in_dim.3), channel_id=1, replica_groups=mesh['row'=16,'col'=32] {'col'}, dimensions={0} | all-to-all | bytes 524288 | tf_op jit(solution)/shard_map/all_to_all | solution.py:296
  99.7 0.2 reshape.11.found_ref
  99.9 3.2 %shard_map.73 = (f32[64,768]{1,0:T(8,128)}, f32[32,2,32]{2,1,0:T(2,128)S(1)}) custom-call(f32[64,768]{1,0:T(8,128)S(1)} %copy-done.4, f32[64,1024]{1,0:T(8,128)S(1)} %reshape.11.found_ref, f32[512,768]{1,0:T(8,128)} %get-tuple-element.7.panel_ref, f32[512,768]{1,0:T(8,128)} %collective-permute-done.8.other_ref), custom_call_target="tpu_custom_call" | custom-call | flops 1811939328 | bytes 3145728 | tf_op jit(solution)/shard_map/pallas_call | solution.py:261
  103.1 5.6 %collective-permute-start.9 = (f32[32,2,32]{2,1,0:T(2,128)S(1)}, f32[32,2,32]{2,1,0:T(2,128)S(1)}, u32[]{:S(2)}, u32[]{:S(2)}) collective-permute-start(f32[32,2,32]{2,1,0:T(2,128)S(1)} %get-tuple-element.8), channel_id=1, source_target_pairs={{0,0},{1,1},{2,32},{3,33},{4,64},{5,65},{6,96},{7,97},{8,128},{9,1... | collective-permute-start | bytes 24584 | tf_op jit(solution)/shard_map/ppermute | solution.py:300
  108.7 10.4 %collective-permute-done.9 = f32[32,2,32]{2,1,0:T(2,128)S(1)} collective-permute-done((f32[32,2,32]{2,1,0:T(2,128)S(1)}, f32[32,2,32]{2,1,0:T(2,128)S(1)}, u32[]{:S(2)}, u32[]{:S(2)}) %collective-permute-start.9) | collective-permute-done | bytes 8224 | tf_op jit(solution)/shard_map/ppermute | solution.py:300
  119.1 0.6 copy.8
  (11 shorter events, 0.0 us)
Async XLA Ops:
  0.6 3.5 %collective-permute-start.2 = (f32[64,768]{1,0:T(8,128)}, f32[64,768]{1,0:T(8,128)S(1)}, u32[]{:S(2)}, u32[]{:S(2)}) collective-permute-start(f32[64,768]{1,0:T(8,128)} %bitcast.1), channel_id=1, source_target_pairs={{0,32},{32,0},{64,96},{96,64},{128,160},{160,128},{192,224},{224,1... | collective-permute-start | bytes 589832 | tf_op jit(solution)/shard_map/ppermute | solution.py:279
  4.2 0.9 copy-start.1
  5.1 47.2 %copy-start.2 = (f32[2,32,768]{2,1,0:T(8,128)S(1)}, f32[2,32,768]{2,1,0:T(8,128)}, u32[]{:S(2)}) copy-start(f32[2,32,768]{2,1,0:T(8,128)} %param.5) | copy-start | bytes 589828
  5.1 47.2 %copy-start.4 = (f32[64,768]{1,0:T(8,128)S(1)}, f32[64,768]{1,0:T(8,128)}, u32[]{:S(2)}) copy-start(f32[64,768]{1,0:T(8,128)} %solved_ref.3) | copy-start | bytes 589828
  5.6 30.1 %collective-permute-start.4 = (f32[128,768]{1,0:T(8,128)S(1)}, f32[128,768]{1,0:T(8,128)S(1)}, u32[]{:S(2)}, u32[]{:S(2)}) collective-permute-start(f32[128,768]{1,0:T(8,128)S(1)} %shard_map.69), channel_id=1, source_target_pairs={{0,128},{32,416},{64,192},{96,480},{128,256},{160,32},{192,320},{2... | collective-permute-start | bytes 1179656 | tf_op jit(solution)/shard_map/ppermute | solution.py:280
  11.7 21.3 %collective-permute-start = (f32[64,768]{1,0:T(8,128)}, f32[64,768]{1,0:T(8,128)S(1)}, u32[]{:S(2)}, u32[]{:S(2)}) collective-permute-start(f32[64,768]{1,0:T(8,128)} %solved_ref.3), channel_id=1, source_target_pairs={{0,32},{32,0},{64,96},{96,64},{128,160},{160,128},{192,224},{224,1... | collective-permute-start | bytes 589832 | tf_op jit(solution)/shard_map/ppermute | solution.py:281
  17.4 15.6 %collective-permute-start.1 = (f32[32,2,32]{2,1,0:T(2,128)}, f32[32,2,32]{2,1,0:T(2,128)S(1)}, u32[]{:S(2)}, u32[]{:S(2)}) collective-permute-start(f32[32,2,32]{2,1,0:T(2,128)} %param.7), channel_id=1, source_target_pairs={{0,7},{1,15},{2,23},{3,31},{4,69},{5,77},{6,85},{7,93},{8,131},{9,... | collective-permute-start | bytes 24584 | tf_op jit(solution)/shard_map/ppermute | solution.py:282
  33.5 47.2 %copy-start = (f32[2,512,512]{2,1,0:T(8,128)S(1)}, f32[2,512,512]{2,1,0:T(8,128)}, u32[]{:S(2)}) copy-start(f32[2,512,512]{2,1,0:T(8,128)} %inverses_ref.1) | copy-start | bytes 6291460
  33.6 47.2 %copy-start.3 = (f32[512,512]{1,0:T(8,128)S(1)}, f32[512,512]{1,0:T(8,128)}, u32[]{:S(2)}) copy-start(f32[512,512]{1,0:T(8,128)} %coupling_ref.1) | copy-start | bytes 3145732
  33.6 9.9 %collective-permute-start.3 = (f32[128,768]{1,0:T(8,128)S(1)}, f32[128,768]{1,0:T(8,128)S(1)}, u32[]{:S(2)}, u32[]{:S(2)}) collective-permute-start(f32[128,768]{1,0:T(8,128)S(1)} %shard_map.68), channel_id=1, source_target_pairs={{0,64},{32,480},{64,128},{96,32},{128,192},{160,96},{192,256},{224... | collective-permute-start | bytes 1179656 | tf_op jit(solution)/shard_map/ppermute | solution.py:283
  35.8 16.5 %collective-permute-start.5 = (f32[128,768]{1,0:T(8,128)S(1)}, f32[128,768]{1,0:T(8,128)S(1)}, u32[]{:S(2)}, u32[]{:S(2)}) collective-permute-start(f32[128,768]{1,0:T(8,128)S(1)} %collective-permute-done.4.both_ref.refs_2_), channel_id=1, source_target_pairs={{0,64},{32,480},{64,128},{96,32},{128,192},{160,96},{192,256},{224... | collective-permute-start | bytes 1179656 | tf_op jit(solution)/shard_map/ppermute | solution.py:284
  38.0 14.3 %collective-permute-start.6 = (f32[64,768]{1,0:T(8,128)S(1)}, f32[64,768]{1,0:T(8,128)S(1)}, u32[]{:S(2)}, u32[]{:S(2)}) collective-permute-start(f32[64,768]{1,0:T(8,128)S(1)} %shard_map.70), channel_id=1, source_target_pairs={{0,128},{32,416},{64,192},{96,480},{128,256},{160,32},{192,320},{2... | collective-permute-start | bytes 589832 | tf_op jit(solution)/shard_map/ppermute | solution.py:285
  54.5 45.4 %collective-permute-start.8 = (f32[512,768]{1,0:T(8,128)}, f32[512,768]{1,0:T(8,128)}, u32[]{:S(2)}, u32[]{:S(2)}) collective-permute-start(f32[512,768]{1,0:T(8,128)} %get-tuple-element.7.panel_ref), channel_id=1, source_target_pairs={{0,32},{32,0},{64,96},{96,64},{128,160},{160,128},{192,224},{224,1... | collective-permute-start | bytes 4718600 | tf_op jit(solution)/shard_map/ppermute | solution.py:290
  77.7 3.1 %collective-permute-start.7 = (f32[2,512]{1,0:T(2,128)S(1)}, f32[2,512]{1,0:T(2,128)S(1)}, u32[]{:S(2)}, u32[]{:S(2)}) collective-permute-start(f32[2,512]{1,0:T(2,128)S(1)} %get-tuple-element.10), channel_id=1, source_target_pairs={{0,32},{32,0},{64,96},{96,64},{128,160},{160,128},{192,224},{224,1... | collective-permute-start | bytes 12296 | tf_op jit(solution)/shard_map/ppermute | solution.py:294
  103.1 16.0 %collective-permute-start.9 = (f32[32,2,32]{2,1,0:T(2,128)S(1)}, f32[32,2,32]{2,1,0:T(2,128)S(1)}, u32[]{:S(2)}, u32[]{:S(2)}) collective-permute-start(f32[32,2,32]{2,1,0:T(2,128)S(1)} %get-tuple-element.8), channel_id=1, source_target_pairs={{0,0},{1,1},{2,32},{3,33},{4,64},{5,65},{6,96},{7,97},{8,128},{9,1... | collective-permute-start | bytes 24584 | tf_op jit(solution)/shard_map/ppermute | solution.py:300

commit v5 on v4

--- a/solution.py
+++ b/solution.py
@@ -88,9 +88,8 @@
     return pl.BlockSpec(memory_space=pl.ANY)
 
 
-def join(one, two, arrivals=()):
-    def body(one_ref, two_ref, *refs):
-        out_ref, sems = refs[-2:]
+def join(one, two):
+    def body(one_ref, two_ref, out_ref, sems):
         rows = one_ref.shape[0]
         first = pltpu.make_async_copy(one_ref, out_ref.at[:rows], sems.at[0])
         second = pltpu.make_async_copy(two_ref, out_ref.at[rows:], sems.at[1])
@@ -103,30 +102,26 @@
     return kernel_call(
         body,
         jax.ShapeDtypeStruct(shape, one.dtype),
-        [anywhere()] * (2 + len(arrivals)),
+        [anywhere()] * 2,
         anywhere(),
         scratch=[pltpu.SemaphoreType.DMA((2,))],
         mib=2,
         moved=16 * one.size,
-    )(one, two, *arrivals)
-
-
-def second_half(both):
-    def body(both_ref, out_ref, sem):
-        copy = pltpu.make_async_copy(both_ref.at[out_ref.shape[0] :], out_ref, sem)
-        copy.start()
-        copy.wait()
-
-    shape = (both.shape[0] // 2, both.shape[1])
-    return kernel_call(
-        body,
-        jax.ShapeDtypeStruct(shape, both.dtype),
-        [anywhere()],
-        anywhere(),
-        scratch=[pltpu.SemaphoreType.DMA],
-        mib=2,
-        moved=4 * both.size,
-    )(both)
+    )(one, two)
+
+
+def after(block, arrivals):
+    def body(*refs):
+        del refs
+
+    return pl.pallas_call(
+        body,
+        out_shape=jax.ShapeDtypeStruct(block.shape, block.dtype),
+        in_specs=[anywhere()] * (1 + len(arrivals)),
+        out_specs=anywhere(),
+        input_output_aliases={0: 0},
+        compiler_params=pltpu.CompilerParams(vmem_limit_bytes=MIB),
+    )(block, *arrivals)
 
 
 def reduce_panel(solved, solved_other, window, pieces):
@@ -137,7 +132,7 @@
     each = rows // COLS
 
     def body(solved_ref, other_ref, window_ref, *refs):
-        own, one, two, three, four, out_ref, panel, partial = refs
+        own, one, *pairs, four, out_ref, panel, partial = refs
         core, col = position()[1], lax.axis_index("col")
 
         def put(place, ref, at):
@@ -147,9 +142,10 @@
                 panel[pl.ds(start, part)] = ref[(2 * at + k) * part : (2 * at + k + 1) * part]
 
         put(0, own, 0)
-        for step, ref in ((1, one), (2, two), (3, three)):
-            put(2 * step, ref, 0)
-            put(2 * step - 1, ref, 1)
+        put(2, one, 0)
+        put(1, one, 1)
+        for place, ref in zip((4, 3, 6, 5), pairs):
+            put(place, ref, 0)
         put(HALF_RING - 1, four, 0)
         solved_pair = jnp.concatenate([solved_ref[...], other_ref[...]], axis=0)
         total = rounded_dot(halves(panel[...]), halves(solved_pair), ((1,), (1,)))
@@ -276,16 +272,22 @@
     part = factor.shape[1]
 
     own = factor.reshape(2 * part, width)
+    two_own = lax.ppermute(own, "row", apart(2))
     other = lax.ppermute(own, "row", core_swap())
-    two = lax.ppermute(join(own, other), "row", apart(2))
+    two_other = lax.ppermute(other, "row", apart(2))
+    one = lax.ppermute(join(own, other), "row", apart(1))
+    three_own = lax.ppermute(two_own, "row", apart(1))
     solved_other = lax.ppermute(solved, "row", core_swap())
     window = lax.ppermute(rhs_window, ("row", "col"), window_to_work())
-    one = lax.ppermute(join(own, other, (solved_other, window)), "row", apart(1))
-    three = lax.ppermute(two, "row", apart(1))
-    four = lax.ppermute(second_half(two), "row", apart(2))
+    two_other = after(two_other, (solved_other, window))
+    four = lax.ppermute(two_other, "row", apart(2))
+    three_other = lax.ppermute(two_other, "row", apart(1))
 
     partial, panel = reduce_panel(
-        solved, solved_other, window, [own, one, two, three, four]
+        solved,
+        solved_other,
+        window,
+        [own, one, two_own, two_other, three_own, three_other, four],
     )
     panel_other = lax.ppermute(panel, "row", core_swap())
 

time: 120 us -> 117 us (0.975)
  waiting for transfers between devices: 36.2 us -> 24.2 us
  starting transfers between devices: 34.2 us -> 43.9 us
  local copies, waits for them, and re-layouts: 1.83 us -> 3.67 us
    ppermute x4 -> x6, starting transfers between devices: 12.6 us -> 20.3 us  [the longest x1 6.09 us: shards(): two_own = lax.ppermute(own, 'row', apart(2))]
    ppermute x1, waiting for transfers between devices: 11.1 us -> 6.53 us  [shards(): window = lax.ppermute(rhs_window, ('row', 'col'), window_to_work())]
    ppermute x4 -> x6, waiting for transfers between devices: 11.9 us -> 7.74 us  [the longest x1 6.19 us: shards(): four = lax.ppermute(two_other, 'row', apart(2))]
    unnamed x11 -> x13, local copies, waits for them, and re-layouts: 1.56 us -> 3.41 us
    ppermute x1, waiting for transfers between devices: 1.62 us -> 0.01 us  [shards(): other = lax.ppermute(own, 'row', core_swap())]
    ppermute x1, starting transfers between devices: 5.64 us -> 7.22 us  [shards(): owned = lax.ppermute(mine, ('row', 'col'), work_to_window())]
    ppermute x1, waiting for transfers between devices: 10.4 us -> 8.79 us  [shards(): owned = lax.ppermute(mine, ('row', 'col'), work_to_window())]
  transfers between devices with their start and end apart: 10 -> 12, of which waited for: 6 -> 5; matrix products, arithmetic and copies ran while one was open for 1% -> 0% of each run, Pallas kernels for 2% -> 2%
where the time goes in v5:
time: 117 us; the launch traced here: 116 us
  starting transfers between devices  43.9 us (38%)
  blocking collectives  36.1 us (31%)
  waiting for transfers between devices  24.2 us (21%)
  Pallas kernels  7.71 us (7%)
  local copies, waits for them, and re-layouts  3.67 us (3%)
    all_to_all x1, blocking collectives, shards(): residual = jnp.sum(lax.all_to_all(partial, 'col', 0, 0, tiled=True), axis=0)  19.1 us
    all_to_all x1, blocking collectives, shards(): lax.all_to_all(jnp.broadcast_to(found, (COLS,) + found.shape), 'col', 0,...  17 us
    ppermute x1, waiting for transfers between devices, shards(): owned = lax.ppermute(mine, ('row', 'col'), work_to_window())  8.79 us
    ppermute x1, starting transfers between devices, shards(): owned = lax.ppermute(mine, ('row', 'col'), work_to_window())  7.22 us
    ppermute x1, waiting for transfers between devices, shards(): window = lax.ppermute(rhs_window, ('row', 'col'), window_to_work())  6.53 us
    ppermute x1, waiting for transfers between devices, shards(): four = lax.ppermute(two_other, 'row', apart(2))  6.19 us
    ppermute x1, starting transfers between devices, shards(): two_own = lax.ppermute(own, 'row', apart(2))  6.09 us
    ppermute x1, starting transfers between devices, shards(): solved_other = lax.ppermute(solved, 'row', core_swap())  6.08 us
  transfers between devices with their start and end apart: 12, of which 5 were waited for; matrix products, arithmetic and copies ran while one was open for 0% of the time, Pallas kernels for 2%

profile of v5, /device:TPU:68, one launch (start us, length us, event | category | flops | bytes accessed | tf_op | source)
XLA Modules:
  0.0 116.5 jit_solution(14106123388410402094)
XLA Ops:
  0.6 1.9 %collective-permute-start.2 = (f32[64,768]{1,0:T(8,128)}, f32[64,768]{1,0:T(8,128)S(1)}, u32[]{:S(2)}, u32[]{:S(2)}) collective-permute-start(f32[64,768]{1,0:T(8,128)} %bitcast.1), channel_id=1, source_target_pairs={{0,32},{32,0},{64,96},{96,64},{128,160},{160,128},{192,224},{224,1... | collective-permute-start | bytes 589832 | tf_op jit(solution)/shard_map/ppermute | solution.py:276
  2.6 6.1 %collective-permute-start.4 = (f32[64,768]{1,0:T(8,128)}, f32[64,768]{1,0:T(8,128)S(1)}, u32[]{:S(2)}, u32[]{:S(2)}) collective-permute-start(f32[64,768]{1,0:T(8,128)} %bitcast.2), channel_id=1, source_target_pairs={{0,128},{32,416},{64,192},{96,480},{128,256},{160,32},{192,320},{2... | collective-permute-start | bytes 589832 | tf_op jit(solution)/shard_map/ppermute | solution.py:275
  8.7 6.1 %collective-permute-start = (f32[64,768]{1,0:T(8,128)}, f32[64,768]{1,0:T(8,128)S(1)}, u32[]{:S(2)}, u32[]{:S(2)}) collective-permute-start(f32[64,768]{1,0:T(8,128)} %solved_ref.3), channel_id=1, source_target_pairs={{0,32},{32,0},{64,96},{96,64},{128,160},{160,128},{192,224},{224,1... | collective-permute-start | bytes 589832 | tf_op jit(solution)/shard_map/ppermute | solution.py:280
  14.8 2.2 %collective-permute-start.5 = (f32[64,768]{1,0:T(8,128)S(1)}, f32[64,768]{1,0:T(8,128)S(1)}, u32[]{:S(2)}, u32[]{:S(2)}) collective-permute-start(f32[64,768]{1,0:T(8,128)S(1)} %collective-permute-done.2.two_ref), channel_id=1, source_target_pairs={{0,128},{32,416},{64,192},{96,480},{128,256},{160,32},{192,320},{2... | collective-permute-start | bytes 589832 | tf_op jit(solution)/shard_map/ppermute | solution.py:277
  17.0 0.0 copy-start.2
  17.0 0.9 copy-done.2
  17.9 0.5 shard_map.68
  18.4 0.0 copy-start.1
  18.5 3.6 %collective-permute-start.3 = (f32[128,768]{1,0:T(8,128)S(1)}, f32[128,768]{1,0:T(8,128)S(1)}, u32[]{:S(2)}, u32[]{:S(2)}) collective-permute-start(f32[128,768]{1,0:T(8,128)S(1)} %shard_map.68), channel_id=1, source_target_pairs={{0,64},{32,480},{64,128},{96,32},{128,192},{160,96},{192,256},{224... | collective-permute-start | bytes 1179656 | tf_op jit(solution)/shard_map/ppermute | solution.py:278
  22.1 4.5 %collective-permute-start.1 = (f32[32,2,32]{2,1,0:T(2,128)}, f32[32,2,32]{2,1,0:T(2,128)S(1)}, u32[]{:S(2)}, u32[]{:S(2)}) collective-permute-start(f32[32,2,32]{2,1,0:T(2,128)} %param.7), channel_id=1, source_target_pairs={{0,7},{1,15},{2,23},{3,31},{4,69},{5,77},{6,85},{7,93},{8,131},{9,... | collective-permute-start | bytes 24584 | tf_op jit(solution)/shard_map/ppermute | solution.py:281
  26.7 4.5 %collective-permute-start.6 = (f32[64,768]{1,0:T(8,128)S(1)}, f32[64,768]{1,0:T(8,128)S(1)}, u32[]{:S(2)}, u32[]{:S(2)}) collective-permute-start(f32[64,768]{1,0:T(8,128)S(1)} %collective-permute-done.4.refs_2_), channel_id=1, source_target_pairs={{0,64},{32,480},{64,128},{96,32},{128,192},{160,96},{192,256},{224... | collective-permute-start | bytes 589832 | tf_op jit(solution)/shard_map/ppermute | solution.py:279
  31.2 6.5 %collective-permute-done.1.refs_2_.window_ref = f32[32,2,32]{2,1,0:T(2,128)S(1)} collective-permute-done((f32[32,2,32]{2,1,0:T(2,128)}, f32[32,2,32]{2,1,0:T(2,128)S(1)}, u32[]{:S(2)}, u32[]{:S(2)}) %collective-permute-start.1) | collective-permute-done | bytes 8224 | tf_op jit(solution)/shard_map/ppermute | solution.py:281
  37.7 1.9 %collective-permute-start.8 = (f32[64,768]{1,0:T(8,128)S(1)}, f32[64,768]{1,0:T(8,128)S(1)}, u32[]{:S(2)}, u32[]{:S(2)}) collective-permute-start(f32[64,768]{1,0:T(8,128)S(1)} %shard_map.69.refs_3_), channel_id=1, source_target_pairs={{0,128},{32,416},{64,192},{96,480},{128,256},{160,32},{192,320},{2... | collective-permute-start | bytes 589832 | tf_op jit(solution)/shard_map/ppermute | solution.py:283
  39.6 1.9 %collective-permute-start.7 = (f32[64,768]{1,0:T(8,128)S(1)}, f32[64,768]{1,0:T(8,128)S(1)}, u32[]{:S(2)}, u32[]{:S(2)}) collective-permute-start(f32[64,768]{1,0:T(8,128)S(1)} %shard_map.69.refs_3_), channel_id=1, source_target_pairs={{0,64},{32,480},{64,128},{96,32},{128,192},{160,96},{192,256},{224... | collective-permute-start | bytes 589832 | tf_op jit(solution)/shard_map/ppermute | solution.py:284
  41.6 6.2 %collective-permute-done.8.refs_6_ = f32[64,768]{1,0:T(8,128)S(1)} collective-permute-done((f32[64,768]{1,0:T(8,128)S(1)}, f32[64,768]{1,0:T(8,128)S(1)}, u32[]{:S(2)}, u32[]{:S(2)}) %collective-permute-start.8) | collective-permute-done | bytes 196640 | tf_op jit(solution)/shard_map/ppermute | solution.py:283
  47.8 1.5 %collective-permute-done.7.refs_5_ = f32[64,768]{1,0:T(8,128)S(1)} collective-permute-done((f32[64,768]{1,0:T(8,128)S(1)}, f32[64,768]{1,0:T(8,128)S(1)}, u32[]{:S(2)}, u32[]{:S(2)}) %collective-permute-start.7) | collective-permute-done | bytes 196640 | tf_op jit(solution)/shard_map/ppermute | solution.py:284
  49.3 0.9 copy-done.3
  50.2 0.9 copy-done.4
  51.2 2.2 %shard_map.70 = (f32[32,4,512]{2,1,0:T(4,128)S(1)}, f32[512,768]{1,0:T(8,128)}) custom-call(f32[64,768]{1,0:T(8,128)S(1)} %copy-done.4, f32[64,768]{1,0:T(8,128)S(1)} %collective-permute-done.refs_1_.other_ref, f32[32,2,32]{2,1,0:T(2,128)S(1)} %collective-permute-done.1.refs_2_.window_ref, f32[64,768]{1,0:T(8,128)S(1)} %bitcast.4, ...), custom_call_target="tpu_custom_call" | custom-call | flops 301989888 | bytes 3145728 | tf_op jit(solution)/shard_map/pallas_call | solution.py:166
  53.3 1.9 %collective-permute-start.10 = (f32[512,768]{1,0:T(8,128)}, f32[512,768]{1,0:T(8,128)}, u32[]{:S(2)}, u32[]{:S(2)}) collective-permute-start(f32[512,768]{1,0:T(8,128)} %get-tuple-element.7.panel_ref), channel_id=1, source_target_pairs={{0,32},{32,0},{64,96},{96,64},{128,160},{160,128},{192,224},{224,1... | collective-permute-start | bytes 4718600 | tf_op jit(solution)/shard_map/ppermute | solution.py:292
  55.2 19.1 %all_to_all.10 = f32[32,4,512]{2,1,0:T(4,128)S(1)} all-to-all(f32[32,4,512]{2,1,0:T(4,128)S(1)} %get-tuple-element.6), channel_id=1, replica_groups=mesh['row'=16,'col'=32] {'col'}, dimensions={0} | all-to-all | bytes 524288 | tf_op jit(solution)/shard_map/all_to_all | solution.py:295
  74.4 0.1 reduce_sum.9
  74.5 1.9 %collective-permute-start.9 = (f32[2,512]{1,0:T(2,128)S(1)}, f32[2,512]{1,0:T(2,128)S(1)}, u32[]{:S(2)}, u32[]{:S(2)}) collective-permute-start(f32[2,512]{1,0:T(2,128)S(1)} %get-tuple-element.10), channel_id=1, source_target_pairs={{0,32},{32,0},{64,96},{96,64},{128,160},{160,128},{192,224},{224,1... | collective-permute-start | bytes 12296 | tf_op jit(solution)/shard_map/ppermute | solution.py:296
  76.4 1.1 collective-permute-done.9.other_ref
  77.5 1.9 %shard_map.71 = f32[2,1024]{1,0:T(2,128)S(1)} custom-call(f32[2,512]{1,0:T(2,128)S(1)} %get-tuple-element.11.residual_ref, f32[2,512]{1,0:T(2,128)S(1)} %collective-permute-done.9.other_ref, f32[2,512,512]{2,1,0:T(8,128)S(1)} %copy-done, f32[512,512]{1,0:T(8,128)S(1)} %copy-done.1), custom_call_target="tpu_custom_call" | custom-call | flops 150994944 | bytes 3145728 | tf_op jit(solution)/shard_map/pallas_call | solution.py:219
  79.4 0.1 broadcast_in_dim.3
  79.5 17.0 %all_to_all.11 = f32[32,2,1024]{2,1,0:T(2,128)S(1)} all-to-all(f32[32,2,1024]{2,1,0:T(2,128)S(1)} %broadcast_in_dim.3), channel_id=1, replica_groups=mesh['row'=16,'col'=32] {'col'}, dimensions={0} | all-to-all | bytes 524288 | tf_op jit(solution)/shard_map/all_to_all | solution.py:298
  96.4 0.2 reshape.11.found_ref
  96.6 3.2 %shard_map.72 = (f32[64,768]{1,0:T(8,128)}, f32[32,2,32]{2,1,0:T(2,128)S(1)}) custom-call(f32[64,768]{1,0:T(8,128)S(1)} %copy-done.5, f32[64,1024]{1,0:T(8,128)S(1)} %reshape.11.found_ref, f32[512,768]{1,0:T(8,128)} %get-tuple-element.7.panel_ref, f32[512,768]{1,0:T(8,128)} %collective-permute-done.10.other_ref), custom_call_target="tpu_custom_call" | custom-call | flops 1811939328 | bytes 3145728 | tf_op jit(solution)/shard_map/pallas_call | solution.py:257
  99.8 7.2 %collective-permute-start.11 = (f32[32,2,32]{2,1,0:T(2,128)S(1)}, f32[32,2,32]{2,1,0:T(2,128)S(1)}, u32[]{:S(2)}, u32[]{:S(2)}) collective-permute-start(f32[32,2,32]{2,1,0:T(2,128)S(1)} %get-tuple-element.8), channel_id=1, source_target_pairs={{0,0},{1,1},{2,32},{3,33},{4,64},{5,65},{6,96},{7,97},{8,128},{9,1... | collective-permute-start | bytes 24584 | tf_op jit(solution)/shard_map/ppermute | solution.py:302
  107.1 8.8 %collective-permute-done.11 = f32[32,2,32]{2,1,0:T(2,128)S(1)} collective-permute-done((f32[32,2,32]{2,1,0:T(2,128)S(1)}, f32[32,2,32]{2,1,0:T(2,128)S(1)}, u32[]{:S(2)}, u32[]{:S(2)}) %collective-permute-start.11) | collective-permute-done | bytes 8224 | tf_op jit(solution)/shard_map/ppermute | solution.py:302
  115.8 0.6 copy.10
  (16 shorter events, 0.0 us)
Async XLA Ops:
  0.6 14.1 %collective-permute-start.2 = (f32[64,768]{1,0:T(8,128)}, f32[64,768]{1,0:T(8,128)S(1)}, u32[]{:S(2)}, u32[]{:S(2)}) collective-permute-start(f32[64,768]{1,0:T(8,128)} %bitcast.1), channel_id=1, source_target_pairs={{0,32},{32,0},{64,96},{96,64},{128,160},{160,128},{192,224},{224,1... | collective-permute-start | bytes 589832 | tf_op jit(solution)/shard_map/ppermute | solution.py:276
  2.6 24.1 %collective-permute-start.4 = (f32[64,768]{1,0:T(8,128)}, f32[64,768]{1,0:T(8,128)S(1)}, u32[]{:S(2)}, u32[]{:S(2)}) collective-permute-start(f32[64,768]{1,0:T(8,128)} %bitcast.2), channel_id=1, source_target_pairs={{0,128},{32,416},{64,192},{96,480},{128,256},{160,32},{192,320},{2... | collective-permute-start | bytes 589832 | tf_op jit(solution)/shard_map/ppermute | solution.py:275
  8.7 29.0 %collective-permute-start = (f32[64,768]{1,0:T(8,128)}, f32[64,768]{1,0:T(8,128)S(1)}, u32[]{:S(2)}, u32[]{:S(2)}) collective-permute-start(f32[64,768]{1,0:T(8,128)} %solved_ref.3), channel_id=1, source_target_pairs={{0,32},{32,0},{64,96},{96,64},{128,160},{160,128},{192,224},{224,1... | collective-permute-start | bytes 589832 | tf_op jit(solution)/shard_map/ppermute | solution.py:280
  14.8 22.9 %collective-permute-start.5 = (f32[64,768]{1,0:T(8,128)S(1)}, f32[64,768]{1,0:T(8,128)S(1)}, u32[]{:S(2)}, u32[]{:S(2)}) collective-permute-start(f32[64,768]{1,0:T(8,128)S(1)} %collective-permute-done.2.two_ref), channel_id=1, source_target_pairs={{0,128},{32,416},{64,192},{96,480},{128,256},{160,32},{192,320},{2... | collective-permute-start | bytes 589832 | tf_op jit(solution)/shard_map/ppermute | solution.py:277
  17.0 0.9 copy-start.2
  18.4 59.1 %copy-start = (f32[2,512,512]{2,1,0:T(8,128)S(1)}, f32[2,512,512]{2,1,0:T(8,128)}, u32[]{:S(2)}) copy-start(f32[2,512,512]{2,1,0:T(8,128)} %inverses_ref.1) | copy-start | bytes 6291460
  18.4 59.1 %copy-start.1 = (f32[512,512]{1,0:T(8,128)S(1)}, f32[512,512]{1,0:T(8,128)}, u32[]{:S(2)}) copy-start(f32[512,512]{1,0:T(8,128)} %coupling_ref.1) | copy-start | bytes 3145732
  18.5 30.8 %collective-permute-start.3 = (f32[128,768]{1,0:T(8,128)S(1)}, f32[128,768]{1,0:T(8,128)S(1)}, u32[]{:S(2)}, u32[]{:S(2)}) collective-permute-start(f32[128,768]{1,0:T(8,128)S(1)} %shard_map.68), channel_id=1, source_target_pairs={{0,64},{32,480},{64,128},{96,32},{128,192},{160,96},{192,256},{224... | collective-permute-start | bytes 1179656 | tf_op jit(solution)/shard_map/ppermute | solution.py:278
  22.1 15.6 %collective-permute-start.1 = (f32[32,2,32]{2,1,0:T(2,128)}, f32[32,2,32]{2,1,0:T(2,128)S(1)}, u32[]{:S(2)}, u32[]{:S(2)}) collective-permute-start(f32[32,2,32]{2,1,0:T(2,128)} %param.7), channel_id=1, source_target_pairs={{0,7},{1,15},{2,23},{3,31},{4,69},{5,77},{6,85},{7,93},{8,131},{9,... | collective-permute-start | bytes 24584 | tf_op jit(solution)/shard_map/ppermute | solution.py:281
  26.7 14.9 %collective-permute-start.6 = (f32[64,768]{1,0:T(8,128)S(1)}, f32[64,768]{1,0:T(8,128)S(1)}, u32[]{:S(2)}, u32[]{:S(2)}) collective-permute-start(f32[64,768]{1,0:T(8,128)S(1)} %collective-permute-done.4.refs_2_), channel_id=1, source_target_pairs={{0,64},{32,480},{64,128},{96,32},{128,192},{160,96},{192,256},{224... | collective-permute-start | bytes 589832 | tf_op jit(solution)/shard_map/ppermute | solution.py:279
  37.7 10.1 %collective-permute-start.8 = (f32[64,768]{1,0:T(8,128)S(1)}, f32[64,768]{1,0:T(8,128)S(1)}, u32[]{:S(2)}, u32[]{:S(2)}) collective-permute-start(f32[64,768]{1,0:T(8,128)S(1)} %shard_map.69.refs_3_), channel_id=1, source_target_pairs={{0,128},{32,416},{64,192},{96,480},{128,256},{160,32},{192,320},{2... | collective-permute-start | bytes 589832 | tf_op jit(solution)/shard_map/ppermute | solution.py:283
  39.6 9.7 %collective-permute-start.7 = (f32[64,768]{1,0:T(8,128)S(1)}, f32[64,768]{1,0:T(8,128)S(1)}, u32[]{:S(2)}, u32[]{:S(2)}) collective-permute-start(f32[64,768]{1,0:T(8,128)S(1)} %shard_map.69.refs_3_), channel_id=1, source_target_pairs={{0,64},{32,480},{64,128},{96,32},{128,192},{160,96},{192,256},{224... | collective-permute-start | bytes 589832 | tf_op jit(solution)/shard_map/ppermute | solution.py:284
  49.3 0.9 copy-start.3
  50.2 0.9 copy-start.4
  53.3 43.3 %collective-permute-start.10 = (f32[512,768]{1,0:T(8,128)}, f32[512,768]{1,0:T(8,128)}, u32[]{:S(2)}, u32[]{:S(2)}) collective-permute-start(f32[512,768]{1,0:T(8,128)} %get-tuple-element.7.panel_ref), channel_id=1, source_target_pairs={{0,32},{32,0},{64,96},{96,64},{128,160},{160,128},{192,224},{224,1... | collective-permute-start | bytes 4718600 | tf_op jit(solution)/shard_map/ppermute | solution.py:292
  74.5 3.1 %collective-permute-start.9 = (f32[2,512]{1,0:T(2,128)S(1)}, f32[2,512]{1,0:T(2,128)S(1)}, u32[]{:S(2)}, u32[]{:S(2)}) collective-permute-start(f32[2,512]{1,0:T(2,128)S(1)} %get-tuple-element.10), channel_id=1, source_target_pairs={{0,32},{32,0},{64,96},{96,64},{128,160},{160,128},{192,224},{224,1... | collective-permute-start | bytes 12296 | tf_op jit(solution)/shard_map/ppermute | solution.py:296
  77.5 19.1 %copy-start.5 = (f32[64,768]{1,0:T(8,128)S(1)}, f32[64,768]{1,0:T(8,128)}, u32[]{:S(2)}) copy-start(f32[64,768]{1,0:T(8,128)} %solved_ref.3) | copy-start | bytes 589828
  99.8 16.0 %collective-permute-start.11 = (f32[32,2,32]{2,1,0:T(2,128)S(1)}, f32[32,2,32]{2,1,0:T(2,128)S(1)}, u32[]{:S(2)}, u32[]{:S(2)}) collective-permute-start(f32[32,2,32]{2,1,0:T(2,128)S(1)} %get-tuple-element.8), channel_id=1, source_target_pairs={{0,0},{1,1},{2,32},{3,33},{4,64},{5,65},{6,96},{7,97},{8,128},{9,1... | collective-permute-start | bytes 24584 | tf_op jit(solution)/shard_map/ppermute | solution.py:302

commit v6 on v5

--- a/solution.py
+++ b/solution.py
@@ -10,6 +10,7 @@
 ROWS = PLANES * CORES
 HALF_RING = ROWS // 2
 COLS = 32
+TAIL = 8
 MIB = 1024 * 1024
 
 
@@ -23,22 +24,6 @@
         for plane in range(PLANES)
         for core in range(CORES)
     ]
-
-
-def ring_place(unknown_row, plane):
-    return (unknown_row - CORES * plane + HALF_RING - 1) % ROWS
-
-
-def window_to_work():
-    pairs = []
-    for row in range(ROWS):
-        for col in range(COLS):
-            rhs_row, half = divmod(col, 2)
-            plane, rhs_core = divmod(rhs_row, CORES)
-            keeper, slot = divmod(ring_place(row, plane), HALF_RING)
-            target = (rhs_core * 2 + half) * HALF_RING + slot
-            pairs.append((row * COLS + col, (plane * CORES + keeper) * COLS + target))
-    return pairs
 
 
 def work_to_window():
@@ -88,26 +73,54 @@
     return pl.BlockSpec(memory_space=pl.ANY)
 
 
-def join(one, two):
-    def body(one_ref, two_ref, out_ref, sems):
+def with_window(block, rhs_window):
+    rows, width = block.shape
+
+    def body(block_ref, window_ref, out_ref):
+        out_ref[:rows] = block_ref[...]
+        out_ref[rows:] = jnp.zeros((TAIL, width), jnp.float32)
+        count, _, part = window_ref.shape
+        for k in range(2):
+            turned = window_ref[:, k].T
+            for g in range(part // TAIL):
+                at = (k * (part // TAIL) + g) * count
+                out_ref[rows:, at : at + count] = turned[g * TAIL : (g + 1) * TAIL]
+
+    return kernel_call(
+        body,
+        jax.ShapeDtypeStruct((rows + TAIL, width), block.dtype),
+        [in_vmem()] * 2,
+        in_vmem(),
+        moved=8 * block.size,
+    )(block, rhs_window)
+
+
+def join(one, two, three):
+    def body(one_ref, two_ref, three_ref, out_ref, copy_ref, sems):
         rows = one_ref.shape[0]
-        first = pltpu.make_async_copy(one_ref, out_ref.at[:rows], sems.at[0])
-        second = pltpu.make_async_copy(two_ref, out_ref.at[rows:], sems.at[1])
-        first.start()
-        second.start()
-        first.wait()
-        second.wait()
+        copies = [
+            pltpu.make_async_copy(one_ref, out_ref.at[:rows], sems.at[0]),
+            pltpu.make_async_copy(two_ref, out_ref.at[rows:], sems.at[1]),
+            pltpu.make_async_copy(three_ref, copy_ref, sems.at[2]),
+        ]
+        for copy in copies:
+            copy.start()
+        for copy in copies:
+            copy.wait()
 
     shape = (one.shape[0] + two.shape[0], one.shape[1])
     return kernel_call(
         body,
-        jax.ShapeDtypeStruct(shape, one.dtype),
+        [
+            jax.ShapeDtypeStruct(shape, one.dtype),
+            jax.ShapeDtypeStruct(three.shape, three.dtype),
+        ],
+        [anywhere()] * 3,
         [anywhere()] * 2,
-        anywhere(),
-        scratch=[pltpu.SemaphoreType.DMA((2,))],
+        scratch=[pltpu.SemaphoreType.DMA((3,))],
         mib=2,
-        moved=16 * one.size,
-    )(one, two)
+        moved=24 * one.size,
+    )(one, two, three)
 
 
 def after(block, arrivals):
@@ -124,40 +137,43 @@
     )(block, *arrivals)
 
 
-def reduce_panel(solved, solved_other, window, pieces):
+def reduce_panel(solved, solved_other, both, one, others):
     rows, width = solved.shape
-    part = pieces[0].shape[0] // 2
+    block = both.shape[0] // 2
+    part = (block - TAIL) // 2
     side = HALF_RING * part
     unknowns = 2 * side
     each = rows // COLS
-
-    def body(solved_ref, other_ref, window_ref, *refs):
-        own, one, *pairs, four, out_ref, panel, partial = refs
-        core, col = position()[1], lax.axis_index("col")
+    count = rows // 2
+
+    def body(solved_ref, other_ref, both_ref, one_ref, *refs):
+        *block_refs, out_ref, panel, window, partial = refs
+        (plane, core), col = position(), lax.axis_index("col")
 
         def put(place, ref, at):
+            base = at * block
             first = jnp.where(core == 0, HALF_RING - 1 - place, place) * part
             for k in range(2):
                 start = pl.multiple_of(first + k * side, part)
-                panel[pl.ds(start, part)] = ref[(2 * at + k) * part : (2 * at + k + 1) * part]
-
-        put(0, own, 0)
-        put(2, one, 0)
-        put(1, one, 1)
-        for place, ref in zip((4, 3, 6, 5), pairs):
+                panel[pl.ds(start, part)] = ref[base + k * part : base + (k + 1) * part]
+                for g in range(part // TAIL):
+                    lanes = (k * (part // TAIL) + g) * count
+                    window[pl.ds(start + g * TAIL, TAIL)] = ref[
+                        base + 2 * part : base + block, lanes : lanes + count
+                    ]
+
+        put(0, both_ref, 0)
+        put(2, one_ref, 0)
+        put(1, one_ref, 1)
+        for place, ref in zip((4, 3, 6, 5, 7), block_refs):
             put(place, ref, 0)
-        put(HALF_RING - 1, four, 0)
         solved_pair = jnp.concatenate([solved_ref[...], other_ref[...]], axis=0)
         total = rounded_dot(halves(panel[...]), halves(solved_pair), ((1,), (1,)))
-        partial[...] = -total.T
-        spread = jnp.concatenate(
-            [jnp.concatenate([window_ref[:, k]] * HALF_RING, axis=1) for k in range(2)], axis=1
-        )
+        spread = jnp.concatenate([window[...]] * (2 * rows // count), axis=1)
         lane = lax.broadcasted_iota(jnp.int32, spread.shape, 1)
-        slot = lane % side // part
-        first = ((col // (2 * HALF_RING)) ^ core) * rows + col // HALF_RING % 2 * (rows // 2)
-        first = pl.multiple_of(first, rows // 2)
-        partial[pl.ds(first, rows // 2)] += jnp.where(slot == col % HALF_RING, spread, 0.0)
+        mine = 2 * ((col // 2 % CORES) ^ core) + col % 2
+        mine = jnp.where(plane == col // (2 * CORES), mine, -1)
+        partial[...] = (jnp.where(lane // count == mine, spread, 0.0) - total).T
         for member in range(COLS):
             at = member * each
             out_ref[member, :each] = partial[at : at + each]
@@ -169,13 +185,16 @@
             jax.ShapeDtypeStruct((COLS, 2 * each, unknowns), jnp.float32),
             jax.ShapeDtypeStruct((unknowns, width), jnp.float32),
         ],
-        [in_vmem()] * (3 + len(pieces)),
+        [in_vmem()] * (4 + len(others)),
         [in_vmem()] * 2,
-        scratch=[pltpu.VMEM((2 * rows, unknowns), jnp.float32)],
+        scratch=[
+            pltpu.VMEM((unknowns, count), jnp.float32),
+            pltpu.VMEM((2 * rows, unknowns), jnp.float32),
+        ],
         mib=32,
         flops=12 * rows * unknowns * width,
         moved=8 * unknowns * width,
-    )(solved, solved_other, window, *pieces)
+    )(solved, solved_other, both, one, *others)
 
 
 def panel_solve(residual, residual_other, inverses, coupling):
@@ -271,24 +290,21 @@
     rows, width = solved.shape
     part = factor.shape[1]
 
-    own = factor.reshape(2 * part, width)
+    own = with_window(factor.reshape(2 * part, width), rhs_window)
     two_own = lax.ppermute(own, "row", apart(2))
     other = lax.ppermute(own, "row", core_swap())
     two_other = lax.ppermute(other, "row", apart(2))
-    one = lax.ppermute(join(own, other), "row", apart(1))
+    both, solved_own = join(own, other, solved)
+    one = lax.ppermute(both, "row", apart(1))
     three_own = lax.ppermute(two_own, "row", apart(1))
     solved_other = lax.ppermute(solved, "row", core_swap())
-    window = lax.ppermute(rhs_window, ("row", "col"), window_to_work())
-    two_other = after(two_other, (solved_other, window))
+    two_other = after(two_other, (solved_other,))
     four = lax.ppermute(two_other, "row", apart(2))
     three_other = lax.ppermute(two_other, "row", apart(1))
-
     partial, panel = reduce_panel(
-        solved,
-        solved_other,
-        window,
-        [own, one, two_own, two_other, three_own, three_other, four],
+        solved_own, solved_other, both, one, [two_own, two_other, three_own, three_other, four]
     )
+
     panel_other = lax.ppermute(panel, "row", core_swap())
 
     each = rows // COLS

time: 117 us -> 109 us (0.932)
  waiting for transfers between devices: 24.2 us -> 18.6 us
  starting transfers between devices: 43.9 us -> 39.6 us
  blocking collectives: 36.1 us -> 38.4 us
    ppermute x2 -> x1, waiting for transfers between devices: 6.53 us -> 0.01 us  [shards(): one = lax.ppermute(both, 'row', apart(1))]
    ppermute x2 -> x1, starting transfers between devices: 8.17 us -> 3.38 us  [shards(): one = lax.ppermute(both, 'row', apart(1))]
    ppermute x1, starting transfers between devices: 6.08 us -> 1.92 us  [shards(): solved_other = lax.ppermute(solved, 'row', core_swap())]
    ppermute x1, starting transfers between devices: 2.25 us -> 6.4 us  [shards(): two_other = lax.ppermute(other, 'row', apart(2))]
    ppermute x1, starting transfers between devices: 1.92 us -> 4.23 us  [shards(): four = lax.ppermute(two_other, 'row', apart(2))]
    all_to_all x1, blocking collectives: 19.1 us -> 21.4 us  [shards(): residual = jnp.sum(lax.all_to_all(partial, 'col', 0, 0, tiled=True), axis=0)]
  transfers between devices with their start and end apart: 12 -> 11, of which waited for: 5 -> 4; matrix products, arithmetic and copies ran while one was open for 0% -> 0% of each run, Pallas kernels for 2% -> 2%
where the time goes in v6:
time: 109 us
  starting transfers between devices  39.6 us (36%)
  blocking collectives  38.4 us (35%)
  waiting for transfers between devices  18.6 us (17%)
  Pallas kernels  7.63 us (7%)
  local copies, waits for them, and re-layouts  3.49 us (3%)
    all_to_all x1, blocking collectives, shards(): residual = jnp.sum(lax.all_to_all(partial, 'col', 0, 0, tiled=True), axis=0)  21.4 us
    all_to_all x1, blocking collectives, shards(): lax.all_to_all(jnp.broadcast_to(found, (COLS,) + found.shape), 'col', 0,...  17 us
    ppermute x1, waiting for transfers between devices, shards(): owned = lax.ppermute(mine, ('row', 'col'), work_to_window())  9.51 us
    ppermute x1, starting transfers between devices, shards(): owned = lax.ppermute(mine, ('row', 'col'), work_to_window())  6.49 us
    ppermute x1, starting transfers between devices, shards(): two_other = lax.ppermute(other, 'row', apart(2))  6.4 us
    ppermute x1, waiting for transfers between devices, shards(): four = lax.ppermute(two_other, 'row', apart(2))  6.23 us
    ppermute x1, starting transfers between devices, shards(): two_own = lax.ppermute(own, 'row', apart(2))  6.09 us
    ppermute x1, starting transfers between devices, shards(): four = lax.ppermute(two_other, 'row', apart(2))  4.23 us
  transfers between devices with their start and end apart: 11, of which 4 were waited for; matrix products, arithmetic and copies ran while one was open for 0% of the time, Pallas kernels for 2%

profile of v6, /device:TPU:68, one launch (start us, length us, event | category | flops | bytes accessed | tf_op | source)
XLA Modules:
  0.0 108.5 jit_solution(6664579785660413195)
XLA Ops:
  0.6 0.9 copy-done.2
  1.6 0.8 copy-done.5
  2.3 0.2 shard_map.68.one_ref
  2.5 1.9 %collective-permute-start = (f32[72,768]{1,0:T(8,128)S(1)}, f32[72,768]{1,0:T(8,128)S(1)}, u32[]{:S(2)}, u32[]{:S(2)}) collective-permute-start(f32[72,768]{1,0:T(8,128)S(1)} %shard_map.68.one_ref), channel_id=1, source_target_pairs={{0,32},{32,0},{64,96},{96,64},{128,160},{160,128},{192,224},{224,1... | collective-permute-start | bytes 663560 | tf_op jit(solution)/shard_map/ppermute | solution.py:295
  4.4 6.1 %collective-permute-start.3 = (f32[72,768]{1,0:T(8,128)S(1)}, f32[72,768]{1,0:T(8,128)S(1)}, u32[]{:S(2)}, u32[]{:S(2)}) collective-permute-start(f32[72,768]{1,0:T(8,128)S(1)} %shard_map.68.one_ref), channel_id=1, source_target_pairs={{0,128},{32,416},{64,192},{96,480},{128,256},{160,32},{192,320},{2... | collective-permute-start | bytes 663560 | tf_op jit(solution)/shard_map/ppermute | solution.py:294
  10.5 0.0 collective-permute-done.two_ref
  10.5 6.4 %collective-permute-start.4 = (f32[72,768]{1,0:T(8,128)S(1)}, f32[72,768]{1,0:T(8,128)S(1)}, u32[]{:S(2)}, u32[]{:S(2)}) collective-permute-start(f32[72,768]{1,0:T(8,128)S(1)} %collective-permute-done.two_ref), channel_id=1, source_target_pairs={{0,128},{32,416},{64,192},{96,480},{128,256},{160,32},{192,320},{2... | collective-permute-start | bytes 663560 | tf_op jit(solution)/shard_map/ppermute | solution.py:296
  16.9 0.0 copy-start.3
  16.9 0.9 copy-done.3
  17.8 0.8 shard_map.69
  18.7 3.4 %collective-permute-start.2 = (f32[144,768]{1,0:T(8,128)S(1)}, f32[144,768]{1,0:T(8,128)S(1)}, u32[]{:S(2)}, u32[]{:S(2)}) collective-permute-start(f32[144,768]{1,0:T(8,128)S(1)} %get-tuple-element.9.both_ref), channel_id=1, source_target_pairs={{0,64},{32,480},{64,128},{96,32},{128,192},{160,96},{192,256},{224... | collective-permute-start | bytes 1327112 | tf_op jit(solution)/shard_map/ppermute | solution.py:298
  22.1 1.9 %collective-permute-start.1 = (f32[64,768]{1,0:T(8,128)S(1)}, f32[64,768]{1,0:T(8,128)S(1)}, u32[]{:S(2)}, u32[]{:S(2)}) collective-permute-start(f32[64,768]{1,0:T(8,128)S(1)} %copy-done.3), channel_id=1, source_target_pairs={{0,32},{32,0},{64,96},{96,64},{128,160},{160,128},{192,224},{224,1... | collective-permute-start | bytes 589832 | tf_op jit(solution)/shard_map/ppermute | solution.py:300
  24.0 3.4 %collective-permute-start.5 = (f32[72,768]{1,0:T(8,128)S(1)}, f32[72,768]{1,0:T(8,128)S(1)}, u32[]{:S(2)}, u32[]{:S(2)}) collective-permute-start(f32[72,768]{1,0:T(8,128)S(1)} %collective-permute-done.3.refs_0_), channel_id=1, source_target_pairs={{0,64},{32,480},{64,128},{96,32},{128,192},{160,96},{192,256},{224... | collective-permute-start | bytes 663560 | tf_op jit(solution)/shard_map/ppermute | solution.py:299
  27.4 4.2 %collective-permute-start.7 = (f32[72,768]{1,0:T(8,128)S(1)}, f32[72,768]{1,0:T(8,128)S(1)}, u32[]{:S(2)}, u32[]{:S(2)}) collective-permute-start(f32[72,768]{1,0:T(8,128)S(1)} %shard_map.70.refs_1_), channel_id=1, source_target_pairs={{0,128},{32,416},{64,192},{96,480},{128,256},{160,32},{192,320},{2... | collective-permute-start | bytes 663560 | tf_op jit(solution)/shard_map/ppermute | solution.py:302
  31.6 1.9 %collective-permute-start.6 = (f32[72,768]{1,0:T(8,128)S(1)}, f32[72,768]{1,0:T(8,128)S(1)}, u32[]{:S(2)}, u32[]{:S(2)}) collective-permute-start(f32[72,768]{1,0:T(8,128)S(1)} %shard_map.70.refs_1_), channel_id=1, source_target_pairs={{0,64},{32,480},{64,128},{96,32},{128,192},{160,96},{192,256},{224... | collective-permute-start | bytes 663560 | tf_op jit(solution)/shard_map/ppermute | solution.py:303
  33.6 6.2 %collective-permute-done.7.refs_4_ = f32[72,768]{1,0:T(8,128)S(1)} collective-permute-done((f32[72,768]{1,0:T(8,128)S(1)}, f32[72,768]{1,0:T(8,128)S(1)}, u32[]{:S(2)}, u32[]{:S(2)}) %collective-permute-start.7) | collective-permute-done | bytes 221216 | tf_op jit(solution)/shard_map/ppermute | solution.py:302
  39.8 1.7 %collective-permute-done.6.refs_3_ = f32[72,768]{1,0:T(8,128)S(1)} collective-permute-done((f32[72,768]{1,0:T(8,128)S(1)}, f32[72,768]{1,0:T(8,128)S(1)}, u32[]{:S(2)}, u32[]{:S(2)}) %collective-permute-start.6) | collective-permute-done | bytes 221216 | tf_op jit(solution)/shard_map/ppermute | solution.py:303
  41.5 1.6 %shard_map.71 = (f32[32,4,512]{2,1,0:T(4,128)S(1)}, f32[512,768]{1,0:T(8,128)}) custom-call(f32[64,768]{1,0:T(8,128)S(1)} %get-tuple-element.8.solved_ref, f32[64,768]{1,0:T(8,128)S(1)} %collective-permute-done.1.refs_1_.other_ref, f32[144,768]{1,0:T(8,128)S(1)} %get-tuple-element.9.both_ref, f32[144,768]{1,0:T(8,128)S(1)} %collective-permute-done.2.one_ref, ...), custom_call_target="tpu_custom_call" | custom-call | flops 301989888 | bytes 3145728 | tf_op jit(solution)/shard_map/pallas_call | solution.py:182
  43.1 1.9 %collective-permute-start.9 = (f32[512,768]{1,0:T(8,128)}, f32[512,768]{1,0:T(8,128)}, u32[]{:S(2)}, u32[]{:S(2)}) collective-permute-start(f32[512,768]{1,0:T(8,128)} %get-tuple-element.11.panel_ref), channel_id=1, source_target_pairs={{0,32},{32,0},{64,96},{96,64},{128,160},{160,128},{192,224},{224,1... | collective-permute-start | bytes 4718600 | tf_op jit(solution)/shard_map/ppermute | solution.py:308
  45.0 21.4 %all_to_all.10 = f32[32,4,512]{2,1,0:T(4,128)S(1)} all-to-all(f32[32,4,512]{2,1,0:T(4,128)S(1)} %get-tuple-element.10), channel_id=1, replica_groups=mesh['row'=16,'col'=32] {'col'}, dimensions={0} | all-to-all | bytes 524288 | tf_op jit(solution)/shard_map/all_to_all | solution.py:311
  66.4 0.1 reduce_sum.9
  66.5 1.9 %collective-permute-start.8 = (f32[2,512]{1,0:T(2,128)S(1)}, f32[2,512]{1,0:T(2,128)S(1)}, u32[]{:S(2)}, u32[]{:S(2)}) collective-permute-start(f32[2,512]{1,0:T(2,128)S(1)} %get-tuple-element.14), channel_id=1, source_target_pairs={{0,32},{32,0},{64,96},{96,64},{128,160},{160,128},{192,224},{224,1... | collective-permute-start | bytes 12296 | tf_op jit(solution)/shard_map/ppermute | solution.py:312
  68.4 1.1 %collective-permute-done.8.other_ref = f32[2,512]{1,0:T(2,128)S(1)} collective-permute-done((f32[2,512]{1,0:T(2,128)S(1)}, f32[2,512]{1,0:T(2,128)S(1)}, u32[]{:S(2)}, u32[]{:S(2)}) %collective-permute-start.8) | collective-permute-done | bytes 4128 | tf_op jit(solution)/shard_map/ppermute | solution.py:312
  69.6 1.9 %shard_map.72 = f32[2,1024]{1,0:T(2,128)S(1)} custom-call(f32[2,512]{1,0:T(2,128)S(1)} %get-tuple-element.15.residual_ref, f32[2,512]{1,0:T(2,128)S(1)} %collective-permute-done.8.other_ref, f32[2,512,512]{2,1,0:T(8,128)S(1)} %copy-done, f32[512,512]{1,0:T(8,128)S(1)} %copy-done.1), custom_call_target="tpu_custom_call" | custom-call | flops 150994944 | bytes 3145728 | tf_op jit(solution)/shard_map/pallas_call | solution.py:238
  71.5 0.1 broadcast_in_dim.3
  71.5 17.0 %all_to_all.11 = f32[32,2,1024]{2,1,0:T(2,128)S(1)} all-to-all(f32[32,2,1024]{2,1,0:T(2,128)S(1)} %broadcast_in_dim.3), channel_id=1, replica_groups=mesh['row'=16,'col'=32] {'col'}, dimensions={0} | all-to-all | bytes 524288 | tf_op jit(solution)/shard_map/all_to_all | solution.py:314
  88.5 0.2 reshape.11.found_ref
  88.7 0.0 collective-permute-done.9.other_ref
  88.7 3.2 %shard_map.73 = (f32[64,768]{1,0:T(8,128)}, f32[32,2,32]{2,1,0:T(2,128)S(1)}) custom-call(f32[64,768]{1,0:T(8,128)S(1)} %copy-done.4, f32[64,1024]{1,0:T(8,128)S(1)} %reshape.11.found_ref, f32[512,768]{1,0:T(8,128)} %get-tuple-element.11.panel_ref, f32[512,768]{1,0:T(8,128)} %collective-permute-done.9.other_ref), custom_call_target="tpu_custom_call" | custom-call | flops 1811939328 | bytes 3145728 | tf_op jit(solution)/shard_map/pallas_call | solution.py:276
  91.9 6.5 %collective-permute-start.10 = (f32[32,2,32]{2,1,0:T(2,128)S(1)}, f32[32,2,32]{2,1,0:T(2,128)S(1)}, u32[]{:S(2)}, u32[]{:S(2)}) collective-permute-start(f32[32,2,32]{2,1,0:T(2,128)S(1)} %get-tuple-element.12), channel_id=1, source_target_pairs={{0,0},{1,1},{2,32},{3,33},{4,64},{5,65},{6,96},{7,97},{8,128},{9,1... | collective-permute-start | bytes 24584 | tf_op jit(solution)/shard_map/ppermute | solution.py:318
  98.4 9.5 %collective-permute-done.10 = f32[32,2,32]{2,1,0:T(2,128)S(1)} collective-permute-done((f32[32,2,32]{2,1,0:T(2,128)S(1)}, f32[32,2,32]{2,1,0:T(2,128)S(1)}, u32[]{:S(2)}, u32[]{:S(2)}) %collective-permute-start.10) | collective-permute-done | bytes 8224 | tf_op jit(solution)/shard_map/ppermute | solution.py:318
  107.9 0.6 copy.10
  (15 shorter events, 0.0 us)
Async XLA Ops:
  0.6 0.9 copy-start.2
  1.6 0.8 copy-start.5
  2.5 8.0 %collective-permute-start = (f32[72,768]{1,0:T(8,128)S(1)}, f32[72,768]{1,0:T(8,128)S(1)}, u32[]{:S(2)}, u32[]{:S(2)}) collective-permute-start(f32[72,768]{1,0:T(8,128)S(1)} %shard_map.68.one_ref), channel_id=1, source_target_pairs={{0,32},{32,0},{64,96},{96,64},{128,160},{160,128},{192,224},{224,1... | collective-permute-start | bytes 663560 | tf_op jit(solution)/shard_map/ppermute | solution.py:295
  4.4 19.6 %collective-permute-start.3 = (f32[72,768]{1,0:T(8,128)S(1)}, f32[72,768]{1,0:T(8,128)S(1)}, u32[]{:S(2)}, u32[]{:S(2)}) collective-permute-start(f32[72,768]{1,0:T(8,128)S(1)} %shard_map.68.one_ref), channel_id=1, source_target_pairs={{0,128},{32,416},{64,192},{96,480},{128,256},{160,32},{192,320},{2... | collective-permute-start | bytes 663560 | tf_op jit(solution)/shard_map/ppermute | solution.py:294
  10.5 16.9 %collective-permute-start.4 = (f32[72,768]{1,0:T(8,128)S(1)}, f32[72,768]{1,0:T(8,128)S(1)}, u32[]{:S(2)}, u32[]{:S(2)}) collective-permute-start(f32[72,768]{1,0:T(8,128)S(1)} %collective-permute-done.two_ref), channel_id=1, source_target_pairs={{0,128},{32,416},{64,192},{96,480},{128,256},{160,32},{192,320},{2... | collective-permute-start | bytes 663560 | tf_op jit(solution)/shard_map/ppermute | solution.py:296
  16.9 0.9 copy-start.3
  18.7 22.8 %collective-permute-start.2 = (f32[144,768]{1,0:T(8,128)S(1)}, f32[144,768]{1,0:T(8,128)S(1)}, u32[]{:S(2)}, u32[]{:S(2)}) collective-permute-start(f32[144,768]{1,0:T(8,128)S(1)} %get-tuple-element.9.both_ref), channel_id=1, source_target_pairs={{0,64},{32,480},{64,128},{96,32},{128,192},{160,96},{192,256},{224... | collective-permute-start | bytes 1327112 | tf_op jit(solution)/shard_map/ppermute | solution.py:298
  22.1 5.3 %collective-permute-start.1 = (f32[64,768]{1,0:T(8,128)S(1)}, f32[64,768]{1,0:T(8,128)S(1)}, u32[]{:S(2)}, u32[]{:S(2)}) collective-permute-start(f32[64,768]{1,0:T(8,128)S(1)} %copy-done.3), channel_id=1, source_target_pairs={{0,32},{32,0},{64,96},{96,64},{128,160},{160,128},{192,224},{224,1... | collective-permute-start | bytes 589832 | tf_op jit(solution)/shard_map/ppermute | solution.py:300
  24.0 9.6 %collective-permute-start.5 = (f32[72,768]{1,0:T(8,128)S(1)}, f32[72,768]{1,0:T(8,128)S(1)}, u32[]{:S(2)}, u32[]{:S(2)}) collective-permute-start(f32[72,768]{1,0:T(8,128)S(1)} %collective-permute-done.3.refs_0_), channel_id=1, source_target_pairs={{0,64},{32,480},{64,128},{96,32},{128,192},{160,96},{192,256},{224... | collective-permute-start | bytes 663560 | tf_op jit(solution)/shard_map/ppermute | solution.py:299
  27.4 12.4 %collective-permute-start.7 = (f32[72,768]{1,0:T(8,128)S(1)}, f32[72,768]{1,0:T(8,128)S(1)}, u32[]{:S(2)}, u32[]{:S(2)}) collective-permute-start(f32[72,768]{1,0:T(8,128)S(1)} %shard_map.70.refs_1_), channel_id=1, source_target_pairs={{0,128},{32,416},{64,192},{96,480},{128,256},{160,32},{192,320},{2... | collective-permute-start | bytes 663560 | tf_op jit(solution)/shard_map/ppermute | solution.py:302
  31.6 9.8 %collective-permute-start.6 = (f32[72,768]{1,0:T(8,128)S(1)}, f32[72,768]{1,0:T(8,128)S(1)}, u32[]{:S(2)}, u32[]{:S(2)}) collective-permute-start(f32[72,768]{1,0:T(8,128)S(1)} %shard_map.70.refs_1_), channel_id=1, source_target_pairs={{0,64},{32,480},{64,128},{96,32},{128,192},{160,96},{192,256},{224... | collective-permute-start | bytes 663560 | tf_op jit(solution)/shard_map/ppermute | solution.py:303
  41.5 28.1 %copy-start = (f32[2,512,512]{2,1,0:T(8,128)S(1)}, f32[2,512,512]{2,1,0:T(8,128)}, u32[]{:S(2)}) copy-start(f32[2,512,512]{2,1,0:T(8,128)} %inverses_ref.1) | copy-start | bytes 6291460
  41.5 28.1 %copy-start.1 = (f32[512,512]{1,0:T(8,128)S(1)}, f32[512,512]{1,0:T(8,128)}, u32[]{:S(2)}) copy-start(f32[512,512]{1,0:T(8,128)} %coupling_ref.1) | copy-start | bytes 3145732
  43.1 45.6 %collective-permute-start.9 = (f32[512,768]{1,0:T(8,128)}, f32[512,768]{1,0:T(8,128)}, u32[]{:S(2)}, u32[]{:S(2)}) collective-permute-start(f32[512,768]{1,0:T(8,128)} %get-tuple-element.11.panel_ref), channel_id=1, source_target_pairs={{0,32},{32,0},{64,96},{96,64},{128,160},{160,128},{192,224},{224,1... | collective-permute-start | bytes 4718600 | tf_op jit(solution)/shard_map/ppermute | solution.py:308
  66.5 3.1 %collective-permute-start.8 = (f32[2,512]{1,0:T(2,128)S(1)}, f32[2,512]{1,0:T(2,128)S(1)}, u32[]{:S(2)}, u32[]{:S(2)}) collective-permute-start(f32[2,512]{1,0:T(2,128)S(1)} %get-tuple-element.14), channel_id=1, source_target_pairs={{0,32},{32,0},{64,96},{96,64},{128,160},{160,128},{192,224},{224,1... | collective-permute-start | bytes 12296 | tf_op jit(solution)/shard_map/ppermute | solution.py:312
  69.6 19.1 %copy-start.4 = (f32[64,768]{1,0:T(8,128)S(1)}, f32[64,768]{1,0:T(8,128)}, u32[]{:S(2)}) copy-start(f32[64,768]{1,0:T(8,128)} %solved_ref.1) | copy-start | bytes 589828
  91.9 16.0 %collective-permute-start.10 = (f32[32,2,32]{2,1,0:T(2,128)S(1)}, f32[32,2,32]{2,1,0:T(2,128)S(1)}, u32[]{:S(2)}, u32[]{:S(2)}) collective-permute-start(f32[32,2,32]{2,1,0:T(2,128)S(1)} %get-tuple-element.12), channel_id=1, source_target_pairs={{0,0},{1,1},{2,32},{3,33},{4,64},{5,65},{6,96},{7,97},{8,128},{9,1... | collective-permute-start | bytes 24584 | tf_op jit(solution)/shard_map/ppermute | solution.py:318

commit v7 on v6

--- a/solution.py
+++ b/solution.py
@@ -11,6 +11,7 @@
 HALF_RING = ROWS // 2
 COLS = 32
 TAIL = 8
+LANES = 256
 MIB = 1024 * 1024
 
 
@@ -73,81 +74,75 @@
     return pl.BlockSpec(memory_space=pl.ANY)
 
 
-def with_window(block, rhs_window):
-    rows, width = block.shape
-
-    def body(block_ref, window_ref, out_ref):
-        out_ref[:rows] = block_ref[...]
-        out_ref[rows:] = jnp.zeros((TAIL, width), jnp.float32)
-        count, _, part = window_ref.shape
-        for k in range(2):
+def in_hbm():
+    return pl.BlockSpec(memory_space=pltpu.MemorySpace.HBM)
+
+
+def with_window(factor, rhs_window):
+    panels, part, width = factor.shape
+    rows = panels * part
+    groups = width // LANES
+
+    def body(factor_ref, window_ref, out_ref):
+        count = window_ref.shape[0]
+        for k in range(panels):
             turned = window_ref[:, k].T
             for g in range(part // TAIL):
                 at = (k * (part // TAIL) + g) * count
-                out_ref[rows:, at : at + count] = turned[g * TAIL : (g + 1) * TAIL]
-
-    return kernel_call(
-        body,
-        jax.ShapeDtypeStruct((rows + TAIL, width), block.dtype),
+                out_ref[groups * rows :, at : at + count] = turned[g * TAIL : (g + 1) * TAIL]
+            for g in range(groups):
+                at = g * rows + k * part
+                out_ref[at : at + part] = factor_ref[k, :, g * LANES : (g + 1) * LANES]
+
+    return kernel_call(
+        body,
+        jax.ShapeDtypeStruct((groups * rows + TAIL, LANES), factor.dtype),
         [in_vmem()] * 2,
         in_vmem(),
-        moved=8 * block.size,
-    )(block, rhs_window)
-
-
-def join(one, two, three):
-    def body(one_ref, two_ref, three_ref, out_ref, copy_ref, sems):
+        mib=56,
+        moved=8 * factor.size,
+    )(factor, rhs_window)
+
+
+def join(one, two, arrivals=()):
+    def body(one_ref, two_ref, *refs):
+        out_ref, sems = refs[-2:]
         rows = one_ref.shape[0]
-        copies = [
-            pltpu.make_async_copy(one_ref, out_ref.at[:rows], sems.at[0]),
-            pltpu.make_async_copy(two_ref, out_ref.at[rows:], sems.at[1]),
-            pltpu.make_async_copy(three_ref, copy_ref, sems.at[2]),
-        ]
-        for copy in copies:
-            copy.start()
-        for copy in copies:
-            copy.wait()
+        first = pltpu.make_async_copy(one_ref, out_ref.at[:rows], sems.at[0])
+        second = pltpu.make_async_copy(two_ref, out_ref.at[rows:], sems.at[1])
+        first.start()
+        second.start()
+        first.wait()
+        second.wait()
 
     shape = (one.shape[0] + two.shape[0], one.shape[1])
     return kernel_call(
         body,
-        [
-            jax.ShapeDtypeStruct(shape, one.dtype),
-            jax.ShapeDtypeStruct(three.shape, three.dtype),
-        ],
-        [anywhere()] * 3,
-        [anywhere()] * 2,
-        scratch=[pltpu.SemaphoreType.DMA((3,))],
+        jax.ShapeDtypeStruct(shape, one.dtype),
+        [anywhere()] * (2 + len(arrivals)),
+        anywhere(),
+        scratch=[pltpu.SemaphoreType.DMA((2,))],
         mib=2,
-        moved=24 * one.size,
-    )(one, two, three)
-
-
-def after(block, arrivals):
-    def body(*refs):
-        del refs
-
-    return pl.pallas_call(
-        body,
-        out_shape=jax.ShapeDtypeStruct(block.shape, block.dtype),
-        in_specs=[anywhere()] * (1 + len(arrivals)),
-        out_specs=anywhere(),
-        input_output_aliases={0: 0},
-        compiler_params=pltpu.CompilerParams(vmem_limit_bytes=MIB),
-    )(block, *arrivals)
-
-
-def reduce_panel(solved, solved_other, both, one, others):
+        moved=16 * one.size,
+    )(one, two, *arrivals)
+
+
+def anywhere():
+    return pl.BlockSpec(memory_space=pl.ANY)
+
+
+def reduce_panel(solved, solved_other, pairs, last):
     rows, width = solved.shape
-    block = both.shape[0] // 2
-    part = (block - TAIL) // 2
+    groups = width // LANES
+    block = last.shape[0]
+    part = (block - TAIL) // (2 * groups)
     side = HALF_RING * part
     unknowns = 2 * side
     each = rows // COLS
     count = rows // 2
 
-    def body(solved_ref, other_ref, both_ref, one_ref, *refs):
-        *block_refs, out_ref, panel, window, partial = refs
+    def body(solved_ref, other_ref, *refs):
+        *pair_refs, last_ref, out_ref, panel, window, partial = refs
         (plane, core), col = position(), lax.axis_index("col")
 
         def put(place, ref, at):
@@ -155,18 +150,20 @@
             first = jnp.where(core == 0, HALF_RING - 1 - place, place) * part
             for k in range(2):
                 start = pl.multiple_of(first + k * side, part)
-                panel[pl.ds(start, part)] = ref[base + k * part : base + (k + 1) * part]
+                for g in range(groups):
+                    row = base + (2 * g + k) * part
+                    panel[pl.ds(start, part), g * LANES : (g + 1) * LANES] = ref[row : row + part]
                 for g in range(part // TAIL):
                     lanes = (k * (part // TAIL) + g) * count
                     window[pl.ds(start + g * TAIL, TAIL)] = ref[
-                        base + 2 * part : base + block, lanes : lanes + count
+                        base + block - TAIL : base + block, lanes : lanes + count
                     ]
 
-        put(0, both_ref, 0)
-        put(2, one_ref, 0)
-        put(1, one_ref, 1)
-        for place, ref in zip((4, 3, 6, 5, 7), block_refs):
-            put(place, ref, 0)
+        put(0, pair_refs[0], 0)
+        for step, ref in enumerate(pair_refs[1:], start=1):
+            put(2 * step, ref, 0)
+            put(2 * step - 1, ref, 1)
+        put(HALF_RING - 1, last_ref, 0)
         solved_pair = jnp.concatenate([solved_ref[...], other_ref[...]], axis=0)
         total = rounded_dot(halves(panel[...]), halves(solved_pair), ((1,), (1,)))
         spread = jnp.concatenate([window[...]] * (2 * rows // count), axis=1)
@@ -185,7 +182,7 @@
             jax.ShapeDtypeStruct((COLS, 2 * each, unknowns), jnp.float32),
             jax.ShapeDtypeStruct((unknowns, width), jnp.float32),
         ],
-        [in_vmem()] * (4 + len(others)),
+        [in_vmem()] * (3 + len(pairs)),
         [in_vmem()] * 2,
         scratch=[
             pltpu.VMEM((unknowns, count), jnp.float32),
@@ -194,7 +191,7 @@
         mib=32,
         flops=12 * rows * unknowns * width,
         moved=8 * unknowns * width,
-    )(solved, solved_other, both, one, *others)
+    )(solved, solved_other, *pairs, last)
 
 
 def panel_solve(residual, residual_other, inverses, coupling):
@@ -252,12 +249,23 @@
     side = size // 2
     part = side // HALF_RING
 
-    def body(solved_ref, found_ref, panel_ref, other_ref, out_ref, owned_ref):
+    chunk = size // 2
+
+    def body(solved_ref, found_ref, panel_ref, other_ref, out_ref, owned_ref, held, sems):
         (plane, core), col = position(), lax.axis_index("col")
+        copies = [
+            pltpu.make_async_copy(ref.at[at : at + chunk], held.at[i], sems.at[i])
+            for i, (ref, at) in enumerate(
+                (ref, at) for ref in (panel_ref, other_ref) for at in range(0, size, chunk)
+            )
+        ]
+        for copy in copies:
+            copy.start()
         total = jnp.zeros((rows, width), jnp.float32)
-        for start, ref in ((0, panel_ref), (size, other_ref)):
-            up, down = halves(found_ref[:, start : start + size])
-            panel_up, panel_down = halves(ref[...])
+        for i, copy in enumerate(copies):
+            up, down = halves(found_ref[:, i * chunk : (i + 1) * chunk])
+            copy.wait()
+            panel_up, panel_down = halves(held[i])
             both = jnp.dot(
                 jnp.concatenate([up, down], axis=0), panel_up, preferred_element_type=jnp.float32
             )
@@ -279,31 +287,30 @@
             jax.ShapeDtypeStruct(solved.shape, solved.dtype),
             jax.ShapeDtypeStruct((rows // 2, 2, part), solved.dtype),
         ],
-        [in_vmem()] * 4,
+        [in_vmem()] * 2 + [in_hbm()] * 2,
         [in_vmem()] * 2,
+        scratch=[
+            pltpu.VMEM((2 * size // chunk, chunk, width), jnp.float32),
+            pltpu.SemaphoreType.DMA((2 * size // chunk,)),
+        ],
         flops=36 * rows * found.shape[1] * width,
         moved=4 * found.shape[1] * width,
     )(solved, found, panel, panel_other)
 
 
 def shards(factor, solved, rhs_window, inverses, coupling):
-    rows, width = solved.shape
-    part = factor.shape[1]
-
-    own = with_window(factor.reshape(2 * part, width), rhs_window)
+    rows = solved.shape[0]
+    own = with_window(factor, rhs_window)
+    other = lax.ppermute(own, "row", core_swap())
     two_own = lax.ppermute(own, "row", apart(2))
-    other = lax.ppermute(own, "row", core_swap())
     two_other = lax.ppermute(other, "row", apart(2))
-    both, solved_own = join(own, other, solved)
+    both = join(own, other)
     one = lax.ppermute(both, "row", apart(1))
-    three_own = lax.ppermute(two_own, "row", apart(1))
     solved_other = lax.ppermute(solved, "row", core_swap())
-    two_other = after(two_other, (solved_other,))
     four = lax.ppermute(two_other, "row", apart(2))
-    three_other = lax.ppermute(two_other, "row", apart(1))
-    partial, panel = reduce_panel(
-        solved_own, solved_other, both, one, [two_own, two_other, three_own, three_other, four]
-    )
+    two = join(two_own, two_other, (solved_other,))
+    three = lax.ppermute(two, "row", apart(1))
+    partial, panel = reduce_panel(solved, solved_other, [both, one, two, three], four)
 
     panel_other = lax.ppermute(panel, "row", core_swap())
 

time: 109 us -> 108 us (level)
  the two profiles are of different devices: /device:TPU:68 before, /device:TPU:13 now
where the time goes in v7:
time: 108 us
  starting transfers between devices  41.4 us (38%)
  blocking collectives  36.1 us (33%)
  waiting for transfers between devices  17.7 us (16%)
  Pallas kernels  9.15 us (8%)
  local copies, waits for them, and re-layouts  1.82 us (2%)
    all_to_all x1, blocking collectives, shards(): residual = jnp.sum(lax.all_to_all(partial, 'col', 0, 0, tiled=True), axis=0)  20.1 us
    all_to_all x1, blocking collectives, shards(): lax.all_to_all(jnp.broadcast_to(found, (COLS,) + found.shape), 'col', 0,...  16 us
    ppermute x1, starting transfers between devices, shards(): two_own = lax.ppermute(own, 'row', apart(2))  10.7 us
    ppermute x1, waiting for transfers between devices, shards(): owned = lax.ppermute(mine, ('row', 'col'), work_to_window())  8.44 us
    ppermute x1, waiting for transfers between devices, shards(): four = lax.ppermute(two_other, 'row', apart(2))  7.05 us
    ppermute x1, starting transfers between devices, shards(): owned = lax.ppermute(mine, ('row', 'col'), work_to_window())  5.42 us
    ppermute x1, starting transfers between devices, shards(): panel_other = lax.ppermute(panel, 'row', core_swap())  4.99 us
    ppermute x1, starting transfers between devices, shards(): four = lax.ppermute(two_other, 'row', apart(2))  4.12 us
  transfers between devices with their start and end apart: 10, of which 4 were waited for; matrix products, arithmetic and copies ran while one was open for 1% of the time, Pallas kernels for 3%

profile of v7, /device:TPU:13, one launch (start us, length us, event | category | flops | bytes accessed | tf_op | source)
XLA Modules:
  0.0 108.0 jit_solution(8612231848978664137)
XLA Ops:
  0.6 0.0 copy-start.3
  0.6 1.8 %shard_map.68.one_ref = f32[200,256]{1,0:T(8,128)} custom-call(f32[2,32,768]{2,1,0:T(8,128)} %factor_ref.1, f32[32,2,32]{2,1,0:T(2,128)} %window_ref.1), custom_call_target="tpu_custom_call" | custom-call | bytes 393216 | tf_op jit(solution)/shard_map/pallas_call | solution.py:97
  2.5 2.6 %collective-permute-start.1 = (f32[200,256]{1,0:T(8,128)}, f32[200,256]{1,0:T(8,128)S(1)}, u32[]{:S(2)}, u32[]{:S(2)}) collective-permute-start(f32[200,256]{1,0:T(8,128)} %shard_map.68.one_ref), channel_id=1, source_target_pairs={{0,32},{32,0},{64,96},{96,64},{128,160},{160,128},{192,224},{224,1... | collective-permute-start | bytes 614408 | tf_op jit(solution)/shard_map/ppermute | solution.py:304
  5.0 10.7 %collective-permute-start.3 = (f32[200,256]{1,0:T(8,128)}, f32[200,256]{1,0:T(8,128)S(1)}, u32[]{:S(2)}, u32[]{:S(2)}) collective-permute-start(f32[200,256]{1,0:T(8,128)} %shard_map.68.one_ref), channel_id=1, source_target_pairs={{0,128},{32,416},{64,192},{96,480},{128,256},{160,32},{192,320},{2... | collective-permute-start | bytes 614408 | tf_op jit(solution)/shard_map/ppermute | solution.py:305
  15.7 0.0 collective-permute-done.1.two_ref
  15.7 2.2 %collective-permute-start.4 = (f32[200,256]{1,0:T(8,128)S(1)}, f32[200,256]{1,0:T(8,128)S(1)}, u32[]{:S(2)}, u32[]{:S(2)}) collective-permute-start(f32[200,256]{1,0:T(8,128)S(1)} %collective-permute-done.1.two_ref), channel_id=1, source_target_pairs={{0,128},{32,416},{64,192},{96,480},{128,256},{160,32},{192,320},{2... | collective-permute-start | bytes 614408 | tf_op jit(solution)/shard_map/ppermute | solution.py:306
  17.9 2.5 %collective-permute-start = (f32[64,768]{1,0:T(8,128)}, f32[64,768]{1,0:T(8,128)S(1)}, u32[]{:S(2)}, u32[]{:S(2)}) collective-permute-start(f32[64,768]{1,0:T(8,128)} %solved_ref.3), channel_id=1, source_target_pairs={{0,32},{32,0},{64,96},{96,64},{128,160},{160,128},{192,224},{224,1... | collective-permute-start | bytes 589832 | tf_op jit(solution)/shard_map/ppermute | solution.py:309
  20.4 0.9 copy-done.2
  21.3 0.5 shard_map.69.refs_0_
  21.8 1.9 %collective-permute-start.2 = (f32[400,256]{1,0:T(8,128)S(1)}, f32[400,256]{1,0:T(8,128)S(1)}, u32[]{:S(2)}, u32[]{:S(2)}) collective-permute-start(f32[400,256]{1,0:T(8,128)S(1)} %shard_map.69.refs_0_), channel_id=1, source_target_pairs={{0,64},{32,480},{64,128},{96,32},{128,192},{160,96},{192,256},{224... | collective-permute-start | bytes 1228808 | tf_op jit(solution)/shard_map/ppermute | solution.py:308
  23.8 0.0 collective-permute-done.3.one_ref
  23.8 1.4 %collective-permute-done.4.two_ref = f32[200,256]{1,0:T(8,128)S(1)} collective-permute-done((f32[200,256]{1,0:T(8,128)S(1)}, f32[200,256]{1,0:T(8,128)S(1)}, u32[]{:S(2)}, u32[]{:S(2)}) %collective-permute-start.4) | collective-permute-done | bytes 204832 | tf_op jit(solution)/shard_map/ppermute | solution.py:306
  25.2 0.5 shard_map.70.refs_2_
  25.7 0.0 copy-start
  25.7 3.9 %collective-permute-start.5 = (f32[400,256]{1,0:T(8,128)S(1)}, f32[400,256]{1,0:T(8,128)S(1)}, u32[]{:S(2)}, u32[]{:S(2)}) collective-permute-start(f32[400,256]{1,0:T(8,128)S(1)} %shard_map.70.refs_2_), channel_id=1, source_target_pairs={{0,64},{32,480},{64,128},{96,32},{128,192},{160,96},{192,256},{224... | collective-permute-start | bytes 1228808 | tf_op jit(solution)/shard_map/ppermute | solution.py:312
  29.6 4.1 %collective-permute-start.6 = (f32[200,256]{1,0:T(8,128)S(1)}, f32[200,256]{1,0:T(8,128)S(1)}, u32[]{:S(2)}, u32[]{:S(2)}) collective-permute-start(f32[200,256]{1,0:T(8,128)S(1)} %collective-permute-done.4.two_ref), channel_id=1, source_target_pairs={{0,128},{32,416},{64,192},{96,480},{128,256},{160,32},{192,320},{2... | collective-permute-start | bytes 614408 | tf_op jit(solution)/shard_map/ppermute | solution.py:310
  33.8 7.1 %collective-permute-done.6.refs_4_ = f32[200,256]{1,0:T(8,128)S(1)} collective-permute-done((f32[200,256]{1,0:T(8,128)S(1)}, f32[200,256]{1,0:T(8,128)S(1)}, u32[]{:S(2)}, u32[]{:S(2)}) %collective-permute-start.6) | collective-permute-done | bytes 204832 | tf_op jit(solution)/shard_map/ppermute | solution.py:310
  40.8 0.0 collective-permute-done.2.refs_1_
  40.8 1.6 %shard_map.71 = (f32[32,4,512]{2,1,0:T(4,128)S(1)}, f32[512,768]{1,0:T(8,128)}) custom-call(f32[64,768]{1,0:T(8,128)S(1)} %copy-done.3, f32[64,768]{1,0:T(8,128)S(1)} %collective-permute-done.refs_0_.other_ref, f32[400,256]{1,0:T(8,128)S(1)} %shard_map.69.refs_0_, f32[400,256]{1,0:T(8,128)S(1)} %collective-permute-done.2.refs_1_, ...), custom_call_target="tpu_custom_call" | custom-call | flops 301989888 | bytes 3145728 | tf_op jit(solution)/shard_map/pallas_call | solution.py:179
  42.4 5.0 %collective-permute-start.8 = (f32[512,768]{1,0:T(8,128)}, f32[512,768]{1,0:T(8,128)}, u32[]{:S(2)}, u32[]{:S(2)}) collective-permute-start(f32[512,768]{1,0:T(8,128)} %get-tuple-element.7.panel_ref), channel_id=1, source_target_pairs={{0,32},{32,0},{64,96},{96,64},{128,160},{160,128},{192,224},{224,1... | collective-permute-start | bytes 4718600 | tf_op jit(solution)/shard_map/ppermute | solution.py:315
  47.4 20.1 %all_to_all.10 = f32[32,4,512]{2,1,0:T(4,128)} all-to-all(f32[32,4,512]{2,1,0:T(4,128)S(1)} %get-tuple-element.6), channel_id=1, replica_groups=mesh['row'=16,'col'=32] {'col'}, dimensions={0} | all-to-all | bytes 524288 | tf_op jit(solution)/shard_map/all_to_all | solution.py:318
  67.5 1.0 reduce_sum.9
  68.6 3.1 %collective-permute-start.7 = (f32[2,512]{1,0:T(2,128)S(1)}, f32[2,512]{1,0:T(2,128)S(1)}, u32[]{:S(2)}, u32[]{:S(2)}) collective-permute-start(f32[2,512]{1,0:T(2,128)S(1)} %get-tuple-element.10), channel_id=1, source_target_pairs={{0,32},{32,0},{64,96},{96,64},{128,160},{160,128},{192,224},{224,1... | collective-permute-start | bytes 12296 | tf_op jit(solution)/shard_map/ppermute | solution.py:319
  71.7 0.8 collective-permute-done.7.other_ref
  72.5 1.9 %shard_map.72 = f32[2,1024]{1,0:T(2,128)S(1)} custom-call(f32[2,512]{1,0:T(2,128)S(1)} %get-tuple-element.11.residual_ref, f32[2,512]{1,0:T(2,128)S(1)} %collective-permute-done.7.other_ref, f32[2,512,512]{2,1,0:T(8,128)S(1)} %copy-done, f32[512,512]{1,0:T(8,128)S(1)} %copy-done.1), custom_call_target="tpu_custom_call" | custom-call | flops 150994944 | bytes 3145728 | tf_op jit(solution)/shard_map/pallas_call | solution.py:235
  74.4 0.1 broadcast_in_dim.3
  74.4 16.0 %all_to_all.11 = f32[32,2,1024]{2,1,0:T(2,128)S(1)} all-to-all(f32[32,2,1024]{2,1,0:T(2,128)S(1)} %broadcast_in_dim.3), channel_id=1, replica_groups=mesh['row'=16,'col'=32] {'col'}, dimensions={0} | all-to-all | bytes 524288 | tf_op jit(solution)/shard_map/all_to_all | solution.py:321
  90.4 0.2 reshape.7.found_ref
  90.6 2.8 %shard_map.73 = (f32[64,768]{1,0:T(8,128)}, f32[32,2,32]{2,1,0:T(2,128)S(1)}) custom-call(f32[64,768]{1,0:T(8,128)S(1)} %copy-done.3, f32[64,1024]{1,0:T(8,128)S(1)} %reshape.7.found_ref, f32[512,768]{1,0:T(8,128)} %get-tuple-element.7.panel_ref, f32[512,768]{1,0:T(8,128)} %collective-permute-done.8.other_ref), custom_call_target="tpu_custom_call" | custom-call | flops 1811939328 | bytes 3145728 | tf_op jit(solution)/shard_map/pallas_call | solution.py:284
  93.5 5.4 %collective-permute-start.9 = (f32[32,2,32]{2,1,0:T(2,128)S(1)}, f32[32,2,32]{2,1,0:T(2,128)S(1)}, u32[]{:S(2)}, u32[]{:S(2)}) collective-permute-start(f32[32,2,32]{2,1,0:T(2,128)S(1)} %get-tuple-element.8), channel_id=1, source_target_pairs={{0,0},{1,1},{2,32},{3,33},{4,64},{5,65},{6,96},{7,97},{8,128},{9,1... | collective-permute-start | bytes 24584 | tf_op jit(solution)/shard_map/ppermute | solution.py:325
  98.9 8.4 %collective-permute-done.9 = f32[32,2,32]{2,1,0:T(2,128)S(1)} collective-permute-done((f32[32,2,32]{2,1,0:T(2,128)S(1)}, f32[32,2,32]{2,1,0:T(2,128)S(1)}, u32[]{:S(2)}, u32[]{:S(2)}) %collective-permute-start.9) | collective-permute-done | bytes 8224 | tf_op jit(solution)/shard_map/ppermute | solution.py:325
  107.4 0.6 copy.8
  (9 shorter events, 0.0 us)
Async XLA Ops:
  0.6 40.2 %copy-start.3 = (f32[64,768]{1,0:T(8,128)S(1)}, f32[64,768]{1,0:T(8,128)}, u32[]{:S(2)}) copy-start(f32[64,768]{1,0:T(8,128)} %solved_ref.3) | copy-start | bytes 589828
  2.5 13.2 %collective-permute-start.1 = (f32[200,256]{1,0:T(8,128)}, f32[200,256]{1,0:T(8,128)S(1)}, u32[]{:S(2)}, u32[]{:S(2)}) collective-permute-start(f32[200,256]{1,0:T(8,128)} %shard_map.68.one_ref), channel_id=1, source_target_pairs={{0,32},{32,0},{64,96},{96,64},{128,160},{160,128},{192,224},{224,1... | collective-permute-start | bytes 614408 | tf_op jit(solution)/shard_map/ppermute | solution.py:304
  5.0 18.7 %collective-permute-start.3 = (f32[200,256]{1,0:T(8,128)}, f32[200,256]{1,0:T(8,128)S(1)}, u32[]{:S(2)}, u32[]{:S(2)}) collective-permute-start(f32[200,256]{1,0:T(8,128)} %shard_map.68.one_ref), channel_id=1, source_target_pairs={{0,128},{32,416},{64,192},{96,480},{128,256},{160,32},{192,320},{2... | collective-permute-start | bytes 614408 | tf_op jit(solution)/shard_map/ppermute | solution.py:305
  15.7 9.5 %collective-permute-start.4 = (f32[200,256]{1,0:T(8,128)S(1)}, f32[200,256]{1,0:T(8,128)S(1)}, u32[]{:S(2)}, u32[]{:S(2)}) collective-permute-start(f32[200,256]{1,0:T(8,128)S(1)} %collective-permute-done.1.two_ref), channel_id=1, source_target_pairs={{0,128},{32,416},{64,192},{96,480},{128,256},{160,32},{192,320},{2... | collective-permute-start | bytes 614408 | tf_op jit(solution)/shard_map/ppermute | solution.py:306
  17.9 5.9 %collective-permute-start = (f32[64,768]{1,0:T(8,128)}, f32[64,768]{1,0:T(8,128)S(1)}, u32[]{:S(2)}, u32[]{:S(2)}) collective-permute-start(f32[64,768]{1,0:T(8,128)} %solved_ref.3), channel_id=1, source_target_pairs={{0,32},{32,0},{64,96},{96,64},{128,160},{160,128},{192,224},{224,1... | collective-permute-start | bytes 589832 | tf_op jit(solution)/shard_map/ppermute | solution.py:309
  20.4 0.9 copy-start.2
  21.8 19.0 %collective-permute-start.2 = (f32[400,256]{1,0:T(8,128)S(1)}, f32[400,256]{1,0:T(8,128)S(1)}, u32[]{:S(2)}, u32[]{:S(2)}) collective-permute-start(f32[400,256]{1,0:T(8,128)S(1)} %shard_map.69.refs_0_), channel_id=1, source_target_pairs={{0,64},{32,480},{64,128},{96,32},{128,192},{160,96},{192,256},{224... | collective-permute-start | bytes 1228808 | tf_op jit(solution)/shard_map/ppermute | solution.py:308
  25.2 47.3 %copy-start.1 = (f32[512,512]{1,0:T(8,128)S(1)}, f32[512,512]{1,0:T(8,128)}, u32[]{:S(2)}) copy-start(f32[512,512]{1,0:T(8,128)} %coupling_ref.1) | copy-start | bytes 3145732
  25.7 46.8 %copy-start = (f32[2,512,512]{2,1,0:T(8,128)S(1)}, f32[2,512,512]{2,1,0:T(8,128)}, u32[]{:S(2)}) copy-start(f32[2,512,512]{2,1,0:T(8,128)} %inverses_ref.1) | copy-start | bytes 6291460
  25.7 15.1 %collective-permute-start.5 = (f32[400,256]{1,0:T(8,128)S(1)}, f32[400,256]{1,0:T(8,128)S(1)}, u32[]{:S(2)}, u32[]{:S(2)}) collective-permute-start(f32[400,256]{1,0:T(8,128)S(1)} %shard_map.70.refs_2_), channel_id=1, source_target_pairs={{0,64},{32,480},{64,128},{96,32},{128,192},{160,96},{192,256},{224... | collective-permute-start | bytes 1228808 | tf_op jit(solution)/shard_map/ppermute | solution.py:312
  29.6 11.2 %collective-permute-start.6 = (f32[200,256]{1,0:T(8,128)S(1)}, f32[200,256]{1,0:T(8,128)S(1)}, u32[]{:S(2)}, u32[]{:S(2)}) collective-permute-start(f32[200,256]{1,0:T(8,128)S(1)} %collective-permute-done.4.two_ref), channel_id=1, source_target_pairs={{0,128},{32,416},{64,192},{96,480},{128,256},{160,32},{192,320},{2... | collective-permute-start | bytes 614408 | tf_op jit(solution)/shard_map/ppermute | solution.py:310
  42.4 48.2 %collective-permute-start.8 = (f32[512,768]{1,0:T(8,128)}, f32[512,768]{1,0:T(8,128)}, u32[]{:S(2)}, u32[]{:S(2)}) collective-permute-start(f32[512,768]{1,0:T(8,128)} %get-tuple-element.7.panel_ref), channel_id=1, source_target_pairs={{0,32},{32,0},{64,96},{96,64},{128,160},{160,128},{192,224},{224,1... | collective-permute-start | bytes 4718600 | tf_op jit(solution)/shard_map/ppermute | solution.py:315
  68.6 3.9 %collective-permute-start.7 = (f32[2,512]{1,0:T(2,128)S(1)}, f32[2,512]{1,0:T(2,128)S(1)}, u32[]{:S(2)}, u32[]{:S(2)}) collective-permute-start(f32[2,512]{1,0:T(2,128)S(1)} %get-tuple-element.10), channel_id=1, source_target_pairs={{0,32},{32,0},{64,96},{96,64},{128,160},{160,128},{192,224},{224,1... | collective-permute-start | bytes 12296 | tf_op jit(solution)/shard_map/ppermute | solution.py:319
  93.5 13.9 %collective-permute-start.9 = (f32[32,2,32]{2,1,0:T(2,128)S(1)}, f32[32,2,32]{2,1,0:T(2,128)S(1)}, u32[]{:S(2)}, u32[]{:S(2)}) collective-permute-start(f32[32,2,32]{2,1,0:T(2,128)S(1)} %get-tuple-element.8), channel_id=1, source_target_pairs={{0,0},{1,1},{2,32},{3,33},{4,64},{5,65},{6,96},{7,97},{8,128},{9,1... | collective-permute-start | bytes 24584 | tf_op jit(solution)/shard_map/ppermute | solution.py:325

commit v8 on v7

--- a/solution.py
+++ b/solution.py
@@ -12,6 +12,7 @@
 COLS = 32
 TAIL = 8
 LANES = 256
+DEPTH = 256
 MIB = 1024 * 1024
 
 
@@ -194,13 +195,13 @@
     )(solved, solved_other, *pairs, last)
 
 
-def panel_solve(residual, residual_other, inverses, coupling):
+def panel_solve(residual, residual_other, inverses, coupling, arrival):
     each, size = residual.shape
     side = size // 2
     part = side // HALF_RING
     deep = 16
 
-    def body(residual_ref, other_ref, inverses_ref, coupling_ref, out_ref, padded):
+    def body(residual_ref, other_ref, inverses_ref, coupling_ref, _, out_ref, padded):
         plane, core = position()
         first = (CORES * plane + HALF_RING + 1 + core * HALF_RING) % ROWS
 
@@ -235,43 +236,59 @@
     return kernel_call(
         body,
         jax.ShapeDtypeStruct((each, 2 * size), residual.dtype),
-        [in_vmem()] * 4,
+        [in_vmem()] * 4 + [anywhere()],
         in_vmem(),
         scratch=[pltpu.VMEM((2, deep, size), jnp.float32)],
         flops=36 * deep * size * size,
         moved=12 * size * size,
-    )(residual, residual_other, inverses, coupling)
-
-
-def correct(solved, found, panel, panel_other):
-    rows, width = solved.shape
-    size = panel.shape[0]
-    side = size // 2
-    part = side // HALF_RING
-
-    chunk = size // 2
-
-    def body(solved_ref, found_ref, panel_ref, other_ref, out_ref, owned_ref, held, sems):
-        (plane, core), col = position(), lax.axis_index("col")
+    )(residual, residual_other, inverses, coupling, arrival)
+
+
+def correct(values, found, parts):
+    rows, width = values.shape
+
+    def body(values_ref, found_ref, *refs):
+        *panel_refs, out_ref, held, sems = refs
         copies = [
-            pltpu.make_async_copy(ref.at[at : at + chunk], held.at[i], sems.at[i])
-            for i, (ref, at) in enumerate(
-                (ref, at) for ref in (panel_ref, other_ref) for at in range(0, size, chunk)
-            )
+            pltpu.make_async_copy(ref.at[first : first + DEPTH], held.at[i], sems.at[i])
+            for i, (ref, (_, first, _)) in enumerate(zip(panel_refs, parts))
         ]
         for copy in copies:
             copy.start()
-        total = jnp.zeros((rows, width), jnp.float32)
-        for i, copy in enumerate(copies):
-            up, down = halves(found_ref[:, i * chunk : (i + 1) * chunk])
+        total = values_ref[...]
+        for i, (copy, (_, _, at)) in enumerate(zip(copies, parts)):
+            up, down = halves(found_ref[:, at : at + DEPTH])
             copy.wait()
             panel_up, panel_down = halves(held[i])
             both = jnp.dot(
                 jnp.concatenate([up, down], axis=0), panel_up, preferred_element_type=jnp.float32
             )
             rest = jnp.dot(up, panel_down, preferred_element_type=jnp.float32)
-            total += both[:rows] + both[rows:] + rest
-        out_ref[...] = solved_ref[...] - total
+            total -= both[:rows] + both[rows:] + rest
+        out_ref[...] = total
+
+    count = len(parts)
+    return kernel_call(
+        body,
+        jax.ShapeDtypeStruct(values.shape, values.dtype),
+        [in_vmem()] * 2 + [in_hbm()] * count,
+        in_vmem(),
+        scratch=[
+            pltpu.VMEM((count, DEPTH, width), jnp.float32),
+            pltpu.SemaphoreType.DMA((count,)),
+        ],
+        flops=18 * rows * count * DEPTH * width,
+        moved=4 * count * DEPTH * width,
+    )(values, found, *(panel for panel, _, _ in parts))
+
+
+def cut(found, part):
+    rows, width = found.shape
+    size = width // 2
+    side = size // 2
+
+    def body(found_ref, owned_ref):
+        (plane, core), col = position(), lax.axis_index("col")
         place = (col // 2 - CORES * plane + ROWS + HALF_RING - 1) % ROWS
         keeper = (place // HALF_RING) ^ core
         first = pl.multiple_of(col % 2 * (rows // 2), rows // 2)
@@ -279,23 +296,15 @@
         for k in range(2):
             start = pl.multiple_of(keeper * size + k * side, side)
             block = found_ref[pl.ds(first, rows // 2), pl.ds(start, side)]
-            owned_ref[:, k] = pltpu.roll(block, back * part, 1)[:, :part]
-
-    return kernel_call(
-        body,
-        [
-            jax.ShapeDtypeStruct(solved.shape, solved.dtype),
-            jax.ShapeDtypeStruct((rows // 2, 2, part), solved.dtype),
-        ],
-        [in_vmem()] * 2 + [in_hbm()] * 2,
-        [in_vmem()] * 2,
-        scratch=[
-            pltpu.VMEM((2 * size // chunk, chunk, width), jnp.float32),
-            pltpu.SemaphoreType.DMA((2 * size // chunk,)),
-        ],
-        flops=36 * rows * found.shape[1] * width,
-        moved=4 * found.shape[1] * width,
-    )(solved, found, panel, panel_other)
+            owned_ref[:, k] = pltpu.roll(block, back * part, 1)[:, : owned_ref.shape[2]]
+
+    return kernel_call(
+        body,
+        jax.ShapeDtypeStruct((rows // 2, 2, part), found.dtype),
+        [in_vmem()],
+        in_vmem(),
+        moved=4 * rows * part,
+    )(found)
 
 
 def shards(factor, solved, rhs_window, inverses, coupling):
@@ -317,13 +326,19 @@
     each = rows // COLS
     residual = jnp.sum(lax.all_to_all(partial, "col", 0, 0, tiled=True), axis=0)
     residual_other = lax.ppermute(residual[each:], "row", core_swap())
-    found = panel_solve(residual[:each], residual_other, inverses, coupling)
+    found = panel_solve(residual[:each], residual_other, inverses, coupling, panel_other)
     gathered = lax.all_to_all(
         jnp.broadcast_to(found, (COLS,) + found.shape), "col", 0, 0, tiled=True
     ).reshape(rows, -1)
-    updated, mine = correct(solved, gathered, panel, panel_other)
-    owned = lax.ppermute(mine, ("row", "col"), work_to_window())
-    return owned, updated
+    part = rhs_window.shape[2]
+    owned = lax.ppermute(cut(gathered, part), ("row", "col"), work_to_window())
+    size = panel.shape[0]
+    parts = [
+        (block, first, start + first)
+        for block, start in ((panel, 0), (panel_other, size))
+        for first in range(0, size, DEPTH)
+    ]
+    return owned, correct(solved, gathered, parts)
 
 
 def solution(mesh):

time: 108 us -> 108 us (level)
  local copies, waits for them, and re-layouts: 1.82 us -> 6.5 us
  waiting for transfers between devices: 17.7 us -> 14.7 us
  Pallas kernels: 9.15 us -> 8.01 us
    unnamed x9 -> x11, local copies, waits for them, and re-layouts: 1.55 us -> 5.28 us
    ppermute x1, waiting for transfers between devices: 8.44 us -> 5.41 us  [shards(): owned = lax.ppermute(cut(gathered, part), ('row', 'col'), work_to_window())]
    pallas_call x1 -> x2, Pallas kernels: 2.84 us -> 2.22 us  [the longest x1 2.09 us: correct(): kernel_call(body, jax.ShapeDtypeStruct(values.shape, values.dtype), [in_v...]
  transfers between devices with their start and end apart: 10 -> 10, of which waited for: 4 -> 4; matrix products, arithmetic and copies ran while one was open for 1% -> 0% of each run, Pallas kernels for 3% -> 3%
where the time goes in v8:
time: 108 us; the launch traced here: 107 us
  starting transfers between devices  41.2 us (38%)
  blocking collectives  36.1 us (33%)
  waiting for transfers between devices  14.7 us (14%)
  Pallas kernels  8.01 us (7%)
  local copies, waits for them, and re-layouts  6.5 us (6%)
    all_to_all x1, blocking collectives, shards(): residual = jnp.sum(lax.all_to_all(partial, 'col', 0, 0, tiled=True), axis=0)  20 us
    all_to_all x1, blocking collectives, shards(): lax.all_to_all(jnp.broadcast_to(found, (COLS,) + found.shape), 'col', 0,...  16.1 us
    ppermute x1, starting transfers between devices, shards(): two_own = lax.ppermute(own, 'row', apart(2))  10.7 us
    ppermute x1, waiting for transfers between devices, shards(): four = lax.ppermute(two_other, 'row', apart(2))  7.05 us
    ppermute x1, starting transfers between devices, shards(): owned = lax.ppermute(cut(gathered, part), ('row', 'col'), work_to_window())  5.42 us
    ppermute x1, waiting for transfers between devices, shards(): owned = lax.ppermute(cut(gathered, part), ('row', 'col'), work_to_window())  5.41 us
    unnamed x11, local copies, waits for them, and re-layouts  5.28 us
    ppermute x1, starting transfers between devices, shards(): panel_other = lax.ppermute(panel, 'row', core_swap())  5 us
  transfers between devices with their start and end apart: 10, of which 4 were waited for; matrix products, arithmetic and copies ran while one was open for 0% of the time, Pallas kernels for 3%

profile of v8, /device:TPU:13, one launch (start us, length us, event | category | flops | bytes accessed | tf_op | source)
XLA Modules:
  0.0 107.4 jit_solution(13458974557496428778)
XLA Ops:
  0.6 0.0 copy-start.3
  0.6 1.8 %shard_map.68.one_ref = f32[200,256]{1,0:T(8,128)} custom-call(f32[2,32,768]{2,1,0:T(8,128)} %factor_ref.1, f32[32,2,32]{2,1,0:T(2,128)} %window_ref.1), custom_call_target="tpu_custom_call" | custom-call | bytes 393216 | tf_op jit(solution)/shard_map/pallas_call | solution.py:98
  2.5 2.6 %collective-permute-start.1 = (f32[200,256]{1,0:T(8,128)}, f32[200,256]{1,0:T(8,128)S(1)}, u32[]{:S(2)}, u32[]{:S(2)}) collective-permute-start(f32[200,256]{1,0:T(8,128)} %shard_map.68.one_ref), channel_id=1, source_target_pairs={{0,32},{32,0},{64,96},{96,64},{128,160},{160,128},{192,224},{224,1... | collective-permute-start | bytes 614408 | tf_op jit(solution)/shard_map/ppermute | solution.py:313
  5.0 10.7 %collective-permute-start.3 = (f32[200,256]{1,0:T(8,128)}, f32[200,256]{1,0:T(8,128)S(1)}, u32[]{:S(2)}, u32[]{:S(2)}) collective-permute-start(f32[200,256]{1,0:T(8,128)} %shard_map.68.one_ref), channel_id=1, source_target_pairs={{0,128},{32,416},{64,192},{96,480},{128,256},{160,32},{192,320},{2... | collective-permute-start | bytes 614408 | tf_op jit(solution)/shard_map/ppermute | solution.py:314
  15.7 2.2 %collective-permute-start.4 = (f32[200,256]{1,0:T(8,128)S(1)}, f32[200,256]{1,0:T(8,128)S(1)}, u32[]{:S(2)}, u32[]{:S(2)}) collective-permute-start(f32[200,256]{1,0:T(8,128)S(1)} %collective-permute-done.1.two_ref), channel_id=1, source_target_pairs={{0,128},{32,416},{64,192},{96,480},{128,256},{160,32},{192,320},{2... | collective-permute-start | bytes 614408 | tf_op jit(solution)/shard_map/ppermute | solution.py:315
  17.9 2.5 %collective-permute-start = (f32[64,768]{1,0:T(8,128)}, f32[64,768]{1,0:T(8,128)S(1)}, u32[]{:S(2)}, u32[]{:S(2)}) collective-permute-start(f32[64,768]{1,0:T(8,128)} %values_ref.1), channel_id=1, source_target_pairs={{0,32},{32,0},{64,96},{96,64},{128,160},{160,128},{192,224},{224,1... | collective-permute-start | bytes 589832 | tf_op jit(solution)/shard_map/ppermute | solution.py:318
  20.4 0.9 copy-done.2
  21.3 0.5 shard_map.69.refs_0_
  21.8 1.9 %collective-permute-start.2 = (f32[400,256]{1,0:T(8,128)S(1)}, f32[400,256]{1,0:T(8,128)S(1)}, u32[]{:S(2)}, u32[]{:S(2)}) collective-permute-start(f32[400,256]{1,0:T(8,128)S(1)} %shard_map.69.refs_0_), channel_id=1, source_target_pairs={{0,64},{32,480},{64,128},{96,32},{128,192},{160,96},{192,256},{224... | collective-permute-start | bytes 1228808 | tf_op jit(solution)/shard_map/ppermute | solution.py:317
  23.8 1.4 %collective-permute-done.4.two_ref = f32[200,256]{1,0:T(8,128)S(1)} collective-permute-done((f32[200,256]{1,0:T(8,128)S(1)}, f32[200,256]{1,0:T(8,128)S(1)}, u32[]{:S(2)}, u32[]{:S(2)}) %collective-permute-start.4) | collective-permute-done | bytes 204832 | tf_op jit(solution)/shard_map/ppermute | solution.py:315
  25.2 0.5 shard_map.70.refs_2_
  25.7 3.8 %collective-permute-start.5 = (f32[400,256]{1,0:T(8,128)S(1)}, f32[400,256]{1,0:T(8,128)S(1)}, u32[]{:S(2)}, u32[]{:S(2)}) collective-permute-start(f32[400,256]{1,0:T(8,128)S(1)} %shard_map.70.refs_2_), channel_id=1, source_target_pairs={{0,64},{32,480},{64,128},{96,32},{128,192},{160,96},{192,256},{224... | collective-permute-start | bytes 1228808 | tf_op jit(solution)/shard_map/ppermute | solution.py:321
  29.5 4.1 %collective-permute-start.6 = (f32[200,256]{1,0:T(8,128)S(1)}, f32[200,256]{1,0:T(8,128)S(1)}, u32[]{:S(2)}, u32[]{:S(2)}) collective-permute-start(f32[200,256]{1,0:T(8,128)S(1)} %collective-permute-done.4.two_ref), channel_id=1, source_target_pairs={{0,128},{32,416},{64,192},{96,480},{128,256},{160,32},{192,320},{2... | collective-permute-start | bytes 614408 | tf_op jit(solution)/shard_map/ppermute | solution.py:319
  33.6 7.1 %collective-permute-done.6.refs_4_ = f32[200,256]{1,0:T(8,128)S(1)} collective-permute-done((f32[200,256]{1,0:T(8,128)S(1)}, f32[200,256]{1,0:T(8,128)S(1)}, u32[]{:S(2)}, u32[]{:S(2)}) %collective-permute-start.6) | collective-permute-done | bytes 204832 | tf_op jit(solution)/shard_map/ppermute | solution.py:319
  40.7 1.1 shard_map.71
  41.8 5.0 %collective-permute-start.8 = (f32[512,768]{1,0:T(8,128)S(1)}, f32[512,768]{1,0:T(8,128)S(1)}, u32[]{:S(2)}, u32[]{:S(2)}) collective-permute-start(f32[512,768]{1,0:T(8,128)S(1)} %get-tuple-element.5.refs_0_.refs_1_), channel_id=1, source_target_pairs={{0,32},{32,0},{64,96},{96,64},{128,160},{160,128},{192,224},{224,1... | collective-permute-start | bytes 4718600 | tf_op jit(solution)/shard_map/ppermute | solution.py:324
  46.8 20.0 %all_to_all.10 = f32[32,4,512]{2,1,0:T(4,128)S(1)} all-to-all(f32[32,4,512]{2,1,0:T(4,128)S(1)} %get-tuple-element.4), channel_id=1, replica_groups=mesh['row'=16,'col'=32] {'col'}, dimensions={0} | all-to-all | bytes 524288 | tf_op jit(solution)/shard_map/all_to_all | solution.py:327
  66.8 0.1 reduce_sum.9
  66.9 3.1 %collective-permute-start.7 = (f32[2,512]{1,0:T(2,128)S(1)}, f32[2,512]{1,0:T(2,128)S(1)}, u32[]{:S(2)}, u32[]{:S(2)}) collective-permute-start(f32[2,512]{1,0:T(2,128)S(1)} %get-tuple-element.6), channel_id=1, source_target_pairs={{0,32},{32,0},{64,96},{96,64},{128,160},{160,128},{192,224},{224,1... | collective-permute-start | bytes 12296 | tf_op jit(solution)/shard_map/ppermute | solution.py:328
  70.0 0.8 collective-permute-done.7.other_ref
  70.8 1.6 %copy-done = f32[2,512,512]{2,1,0:T(8,128)S(1)} copy-done((f32[2,512,512]{2,1,0:T(8,128)S(1)}, f32[2,512,512]{2,1,0:T(8,128)}, u32[]{:S(2)}) %copy-start) | copy-done | bytes 2097176
  72.4 1.2 %copy-done.1 = f32[512,512]{1,0:T(8,128)S(1)} copy-done((f32[512,512]{1,0:T(8,128)S(1)}, f32[512,512]{1,0:T(8,128)}, u32[]{:S(2)}) %copy-start.1) | copy-done | bytes 1048600
  73.6 1.9 %shard_map.72 = f32[2,1024]{1,0:T(2,128)S(1)} custom-call(f32[2,512]{1,0:T(2,128)S(1)} %get-tuple-element.7.residual_ref, f32[2,512]{1,0:T(2,128)S(1)} %collective-permute-done.7.other_ref, f32[2,512,512]{2,1,0:T(8,128)S(1)} %copy-done, f32[512,512]{1,0:T(8,128)S(1)} %copy-done.1, f32[512,768]{1,0:T(8,128)S(1)} %collective-permute-done.8._.refs_2_.refs_3_), custom_call_target="tpu_custom_call" | custom-call | flops 150994944 | bytes 3145728 | tf_op jit(solution)/shard_map/pallas_call | solution.py:236
  75.5 0.1 broadcast_in_dim.3
  75.6 16.1 %all_to_all.11 = f32[32,2,1024]{2,1,0:T(2,128)} all-to-all(f32[32,2,1024]{2,1,0:T(2,128)S(1)} %broadcast_in_dim.3), channel_id=1, replica_groups=mesh['row'=16,'col'=32] {'col'}, dimensions={0} | all-to-all | bytes 524288 | tf_op jit(solution)/shard_map/all_to_all | solution.py:330
  91.7 1.1 %reshape.7.found_ref = f32[64,1024]{1,0:T(8,128)S(1)} reshape(f32[32,2,1024]{2,1,0:T(2,128)} %all_to_all.11) | data formatting | bytes 524288 | tf_op jit(solution)/shard_map/reshape | solution.py:332
  92.8 0.1 shard_map.73
  92.9 5.4 %collective-permute-start.9 = (f32[32,2,32]{2,1,0:T(2,128)S(1)}, f32[32,2,32]{2,1,0:T(2,128)S(1)}, u32[]{:S(2)}, u32[]{:S(2)}) collective-permute-start(f32[32,2,32]{2,1,0:T(2,128)S(1)} %shard_map.73), channel_id=1, source_target_pairs={{0,0},{1,1},{2,32},{3,33},{4,64},{5,65},{6,96},{7,97},{8,128},{9,1... | collective-permute-start | bytes 24584 | tf_op jit(solution)/shard_map/ppermute | solution.py:334
  98.4 0.9 copy-done.4
  99.3 2.1 %shard_map.74 = f32[64,768]{1,0:T(8,128)} custom-call(f32[64,768]{1,0:T(8,128)S(1)} %copy-done.4, f32[64,1024]{1,0:T(8,128)S(1)} %reshape.7.found_ref, f32[512,768]{1,0:T(8,128)S(1)} %get-tuple-element.5.refs_0_.refs_1_, f32[512,768]{1,0:T(8,128)S(1)} %get-tuple-element.5.refs_0_.refs_1_, f32[512,768]{1,0:T(8,128)S(1)} %collective-permute-done.8._.refs_2_.refs_3_, ...), custom_call_target="tpu_custom_call" | custom-call | flops 905969664 | bytes 3145728 | tf_op jit(solution)/shard_map/pallas_call | solution.py:271
  101.4 5.4 %collective-permute-done.9 = f32[32,2,32]{2,1,0:T(2,128)S(1)} collective-permute-done((f32[32,2,32]{2,1,0:T(2,128)S(1)}, f32[32,2,32]{2,1,0:T(2,128)S(1)}, u32[]{:S(2)}, u32[]{:S(2)}) %collective-permute-start.9) | collective-permute-done | bytes 8224 | tf_op jit(solution)/shard_map/ppermute | solution.py:334
  106.8 0.6 copy.8
  (12 shorter events, 0.0 us)
Async XLA Ops:
  0.6 40.1 %copy-start.3 = (f32[64,768]{1,0:T(8,128)S(1)}, f32[64,768]{1,0:T(8,128)}, u32[]{:S(2)}) copy-start(f32[64,768]{1,0:T(8,128)} %values_ref.1) | copy-start | bytes 589828
  2.5 13.2 %collective-permute-start.1 = (f32[200,256]{1,0:T(8,128)}, f32[200,256]{1,0:T(8,128)S(1)}, u32[]{:S(2)}, u32[]{:S(2)}) collective-permute-start(f32[200,256]{1,0:T(8,128)} %shard_map.68.one_ref), channel_id=1, source_target_pairs={{0,32},{32,0},{64,96},{96,64},{128,160},{160,128},{192,224},{224,1... | collective-permute-start | bytes 614408 | tf_op jit(solution)/shard_map/ppermute | solution.py:313
  5.0 18.7 %collective-permute-start.3 = (f32[200,256]{1,0:T(8,128)}, f32[200,256]{1,0:T(8,128)S(1)}, u32[]{:S(2)}, u32[]{:S(2)}) collective-permute-start(f32[200,256]{1,0:T(8,128)} %shard_map.68.one_ref), channel_id=1, source_target_pairs={{0,128},{32,416},{64,192},{96,480},{128,256},{160,32},{192,320},{2... | collective-permute-start | bytes 614408 | tf_op jit(solution)/shard_map/ppermute | solution.py:314
  15.7 9.5 %collective-permute-start.4 = (f32[200,256]{1,0:T(8,128)S(1)}, f32[200,256]{1,0:T(8,128)S(1)}, u32[]{:S(2)}, u32[]{:S(2)}) collective-permute-start(f32[200,256]{1,0:T(8,128)S(1)} %collective-permute-done.1.two_ref), channel_id=1, source_target_pairs={{0,128},{32,416},{64,192},{96,480},{128,256},{160,32},{192,320},{2... | collective-permute-start | bytes 614408 | tf_op jit(solution)/shard_map/ppermute | solution.py:315
  17.9 5.9 %collective-permute-start = (f32[64,768]{1,0:T(8,128)}, f32[64,768]{1,0:T(8,128)S(1)}, u32[]{:S(2)}, u32[]{:S(2)}) collective-permute-start(f32[64,768]{1,0:T(8,128)} %values_ref.1), channel_id=1, source_target_pairs={{0,32},{32,0},{64,96},{96,64},{128,160},{160,128},{192,224},{224,1... | collective-permute-start | bytes 589832 | tf_op jit(solution)/shard_map/ppermute | solution.py:318
  20.4 0.9 copy-start.2
  21.8 18.8 %collective-permute-start.2 = (f32[400,256]{1,0:T(8,128)S(1)}, f32[400,256]{1,0:T(8,128)S(1)}, u32[]{:S(2)}, u32[]{:S(2)}) collective-permute-start(f32[400,256]{1,0:T(8,128)S(1)} %shard_map.69.refs_0_), channel_id=1, source_target_pairs={{0,64},{32,480},{64,128},{96,32},{128,192},{160,96},{192,256},{224... | collective-permute-start | bytes 1228808 | tf_op jit(solution)/shard_map/ppermute | solution.py:317
  25.7 15.0 %collective-permute-start.5 = (f32[400,256]{1,0:T(8,128)S(1)}, f32[400,256]{1,0:T(8,128)S(1)}, u32[]{:S(2)}, u32[]{:S(2)}) collective-permute-start(f32[400,256]{1,0:T(8,128)S(1)} %shard_map.70.refs_2_), channel_id=1, source_target_pairs={{0,64},{32,480},{64,128},{96,32},{128,192},{160,96},{192,256},{224... | collective-permute-start | bytes 1228808 | tf_op jit(solution)/shard_map/ppermute | solution.py:321
  29.5 11.2 %collective-permute-start.6 = (f32[200,256]{1,0:T(8,128)S(1)}, f32[200,256]{1,0:T(8,128)S(1)}, u32[]{:S(2)}, u32[]{:S(2)}) collective-permute-start(f32[200,256]{1,0:T(8,128)S(1)} %collective-permute-done.4.two_ref), channel_id=1, source_target_pairs={{0,128},{32,416},{64,192},{96,480},{128,256},{160,32},{192,320},{2... | collective-permute-start | bytes 614408 | tf_op jit(solution)/shard_map/ppermute | solution.py:319
  41.8 29.0 %collective-permute-start.8 = (f32[512,768]{1,0:T(8,128)S(1)}, f32[512,768]{1,0:T(8,128)S(1)}, u32[]{:S(2)}, u32[]{:S(2)}) collective-permute-start(f32[512,768]{1,0:T(8,128)S(1)} %get-tuple-element.5.refs_0_.refs_1_), channel_id=1, source_target_pairs={{0,32},{32,0},{64,96},{96,64},{128,160},{160,128},{192,224},{224,1... | collective-permute-start | bytes 4718600 | tf_op jit(solution)/shard_map/ppermute | solution.py:324
  66.9 3.9 %collective-permute-start.7 = (f32[2,512]{1,0:T(2,128)S(1)}, f32[2,512]{1,0:T(2,128)S(1)}, u32[]{:S(2)}, u32[]{:S(2)}) collective-permute-start(f32[2,512]{1,0:T(2,128)S(1)} %get-tuple-element.6), channel_id=1, source_target_pairs={{0,32},{32,0},{64,96},{96,64},{128,160},{160,128},{192,224},{224,1... | collective-permute-start | bytes 12296 | tf_op jit(solution)/shard_map/ppermute | solution.py:328
  70.8 1.6 %copy-start = (f32[2,512,512]{2,1,0:T(8,128)S(1)}, f32[2,512,512]{2,1,0:T(8,128)}, u32[]{:S(2)}) copy-start(f32[2,512,512]{2,1,0:T(8,128)} %inverses_ref.1) | copy-start | bytes 6291460
  72.4 1.2 %copy-start.1 = (f32[512,512]{1,0:T(8,128)S(1)}, f32[512,512]{1,0:T(8,128)}, u32[]{:S(2)}) copy-start(f32[512,512]{1,0:T(8,128)} %coupling_ref.1) | copy-start | bytes 3145732
  92.9 13.9 %collective-permute-start.9 = (f32[32,2,32]{2,1,0:T(2,128)S(1)}, f32[32,2,32]{2,1,0:T(2,128)S(1)}, u32[]{:S(2)}, u32[]{:S(2)}) collective-permute-start(f32[32,2,32]{2,1,0:T(2,128)S(1)} %shard_map.73), channel_id=1, source_target_pairs={{0,0},{1,1},{2,32},{3,33},{4,64},{5,65},{6,96},{7,97},{8,128},{9,1... | collective-permute-start | bytes 24584 | tf_op jit(solution)/shard_map/ppermute | solution.py:334
  98.4 0.9 copy-start.4

commit v9 on v8

--- a/solution.py
+++ b/solution.py
@@ -100,7 +100,7 @@
         jax.ShapeDtypeStruct((groups * rows + TAIL, LANES), factor.dtype),
         [in_vmem()] * 2,
         in_vmem(),
-        mib=56,
+        mib=16,
         moved=8 * factor.size,
     )(factor, rhs_window)
 
@@ -189,7 +189,7 @@
             pltpu.VMEM((unknowns, count), jnp.float32),
             pltpu.VMEM((2 * rows, unknowns), jnp.float32),
         ],
-        mib=32,
+        mib=24,
         flops=12 * rows * unknowns * width,
         moved=8 * unknowns * width,
     )(solved, solved_other, *pairs, last)

time: 108 us -> 108 us (level)
  Pallas kernels: 8.01 us -> 6.39 us
    pallas_call x1, Pallas kernels: 1.81 us -> 0.16 us  [with_window(): kernel_call(body, jax.ShapeDtypeStruct((groups * rows + TAIL, LANES), fac...]
    unnamed x11 -> x13, local copies, waits for them, and re-layouts: 5.28 us -> 6.08 us
where the time goes in v9:
time: 108 us; the launch traced here: 107 us
  starting transfers between devices  41.1 us (38%)
  blocking collectives  36.1 us (33%)
  waiting for transfers between devices  15.3 us (14%)
  local copies, waits for them, and re-layouts  7.29 us (7%)
  Pallas kernels  6.39 us (6%)
    all_to_all x1, blocking collectives, shards(): residual = jnp.sum(lax.all_to_all(partial, 'col', 0, 0, tiled=True), axis=0)  20 us
    all_to_all x1, blocking collectives, shards(): lax.all_to_all(jnp.broadcast_to(found, (COLS,) + found.shape), 'col', 0,...  16.1 us
    ppermute x1, starting transfers between devices, shards(): two_own = lax.ppermute(own, 'row', apart(2))  10.7 us
    ppermute x1, waiting for transfers between devices, shards(): four = lax.ppermute(two_other, 'row', apart(2))  7.26 us
    unnamed x13, local copies, waits for them, and re-layouts  6.08 us
    ppermute x1, starting transfers between devices, shards(): owned = lax.ppermute(cut(gathered, part), ('row', 'col'), work_to_window())  5.51 us
    ppermute x1, waiting for transfers between devices, shards(): owned = lax.ppermute(cut(gathered, part), ('row', 'col'), work_to_window())  5.18 us
    ppermute x1, starting transfers between devices, shards(): panel_other = lax.ppermute(panel, 'row', core_swap())  4.79 us
  transfers between devices with their start and end apart: 10, of which 4 were waited for; matrix products, arithmetic and copies ran while one was open for 0% of the time, Pallas kernels for 3%

profile of v9, /device:TPU:13, one launch (start us, length us, event | category | flops | bytes accessed | tf_op | source)
XLA Modules:
  0.0 107.1 jit_solution(14131707328141147029)
XLA Ops:
  0.7 1.0 copy-done.4
  1.6 0.8 copy-done.5
  2.4 0.2 shard_map.68.one_ref
  2.5 2.6 %collective-permute-start.1 = (f32[200,256]{1,0:T(8,128)S(1)}, f32[200,256]{1,0:T(8,128)S(1)}, u32[]{:S(2)}, u32[]{:S(2)}) collective-permute-start(f32[200,256]{1,0:T(8,128)S(1)} %shard_map.68.one_ref), channel_id=1, source_target_pairs={{0,32},{32,0},{64,96},{96,64},{128,160},{160,128},{192,224},{224,1... | collective-permute-start | bytes 614408 | tf_op jit(solution)/shard_map/ppermute | solution.py:313
  5.1 10.7 %collective-permute-start.3 = (f32[200,256]{1,0:T(8,128)S(1)}, f32[200,256]{1,0:T(8,128)S(1)}, u32[]{:S(2)}, u32[]{:S(2)}) collective-permute-start(f32[200,256]{1,0:T(8,128)S(1)} %shard_map.68.one_ref), channel_id=1, source_target_pairs={{0,128},{32,416},{64,192},{96,480},{128,256},{160,32},{192,320},{2... | collective-permute-start | bytes 614408 | tf_op jit(solution)/shard_map/ppermute | solution.py:314
  15.8 2.2 %collective-permute-start.4 = (f32[200,256]{1,0:T(8,128)S(1)}, f32[200,256]{1,0:T(8,128)S(1)}, u32[]{:S(2)}, u32[]{:S(2)}) collective-permute-start(f32[200,256]{1,0:T(8,128)S(1)} %collective-permute-done.1.two_ref), channel_id=1, source_target_pairs={{0,128},{32,416},{64,192},{96,480},{128,256},{160,32},{192,320},{2... | collective-permute-start | bytes 614408 | tf_op jit(solution)/shard_map/ppermute | solution.py:315
  18.0 2.5 %collective-permute-start = (f32[64,768]{1,0:T(8,128)}, f32[64,768]{1,0:T(8,128)S(1)}, u32[]{:S(2)}, u32[]{:S(2)}) collective-permute-start(f32[64,768]{1,0:T(8,128)} %values_ref.1), channel_id=1, source_target_pairs={{0,32},{32,0},{64,96},{96,64},{128,160},{160,128},{192,224},{224,1... | collective-permute-start | bytes 589832 | tf_op jit(solution)/shard_map/ppermute | solution.py:318
  20.5 0.5 shard_map.69.refs_0_
  21.0 1.9 %collective-permute-start.2 = (f32[400,256]{1,0:T(8,128)S(1)}, f32[400,256]{1,0:T(8,128)S(1)}, u32[]{:S(2)}, u32[]{:S(2)}) collective-permute-start(f32[400,256]{1,0:T(8,128)S(1)} %shard_map.69.refs_0_), channel_id=1, source_target_pairs={{0,64},{32,480},{64,128},{96,32},{128,192},{160,96},{192,256},{224... | collective-permute-start | bytes 1228808 | tf_op jit(solution)/shard_map/ppermute | solution.py:317
  23.0 2.1 %collective-permute-done.4.two_ref = f32[200,256]{1,0:T(8,128)S(1)} collective-permute-done((f32[200,256]{1,0:T(8,128)S(1)}, f32[200,256]{1,0:T(8,128)S(1)}, u32[]{:S(2)}, u32[]{:S(2)}) %collective-permute-start.4) | collective-permute-done | bytes 204832 | tf_op jit(solution)/shard_map/ppermute | solution.py:315
  25.0 0.5 shard_map.70.refs_2_
  25.6 3.8 %collective-permute-start.5 = (f32[400,256]{1,0:T(8,128)S(1)}, f32[400,256]{1,0:T(8,128)S(1)}, u32[]{:S(2)}, u32[]{:S(2)}) collective-permute-start(f32[400,256]{1,0:T(8,128)S(1)} %shard_map.70.refs_2_), channel_id=1, source_target_pairs={{0,64},{32,480},{64,128},{96,32},{128,192},{160,96},{192,256},{224... | collective-permute-start | bytes 1228808 | tf_op jit(solution)/shard_map/ppermute | solution.py:321
  29.4 4.1 %collective-permute-start.6 = (f32[200,256]{1,0:T(8,128)S(1)}, f32[200,256]{1,0:T(8,128)S(1)}, u32[]{:S(2)}, u32[]{:S(2)}) collective-permute-start(f32[200,256]{1,0:T(8,128)S(1)} %collective-permute-done.4.two_ref), channel_id=1, source_target_pairs={{0,128},{32,416},{64,192},{96,480},{128,256},{160,32},{192,320},{2... | collective-permute-start | bytes 614408 | tf_op jit(solution)/shard_map/ppermute | solution.py:319
  33.5 7.3 %collective-permute-done.6.refs_4_ = f32[200,256]{1,0:T(8,128)S(1)} collective-permute-done((f32[200,256]{1,0:T(8,128)S(1)}, f32[200,256]{1,0:T(8,128)S(1)}, u32[]{:S(2)}, u32[]{:S(2)}) %collective-permute-start.6) | collective-permute-done | bytes 204832 | tf_op jit(solution)/shard_map/ppermute | solution.py:319
  40.8 1.1 shard_map.71
  41.8 4.8 %collective-permute-start.8 = (f32[512,768]{1,0:T(8,128)S(1)}, f32[512,768]{1,0:T(8,128)S(1)}, u32[]{:S(2)}, u32[]{:S(2)}) collective-permute-start(f32[512,768]{1,0:T(8,128)S(1)} %get-tuple-element.5.refs_0_.refs_1_), channel_id=1, source_target_pairs={{0,32},{32,0},{64,96},{96,64},{128,160},{160,128},{192,224},{224,1... | collective-permute-start | bytes 4718600 | tf_op jit(solution)/shard_map/ppermute | solution.py:324
  46.6 20.0 %all_to_all.10 = f32[32,4,512]{2,1,0:T(4,128)S(1)} all-to-all(f32[32,4,512]{2,1,0:T(4,128)S(1)} %get-tuple-element.4), channel_id=1, replica_groups=mesh['row'=16,'col'=32] {'col'}, dimensions={0} | all-to-all | bytes 524288 | tf_op jit(solution)/shard_map/all_to_all | solution.py:327
  66.6 0.1 reduce_sum.9
  66.7 3.1 %collective-permute-start.7 = (f32[2,512]{1,0:T(2,128)S(1)}, f32[2,512]{1,0:T(2,128)S(1)}, u32[]{:S(2)}, u32[]{:S(2)}) collective-permute-start(f32[2,512]{1,0:T(2,128)S(1)} %get-tuple-element.6), channel_id=1, source_target_pairs={{0,32},{32,0},{64,96},{96,64},{128,160},{160,128},{192,224},{224,1... | collective-permute-start | bytes 12296 | tf_op jit(solution)/shard_map/ppermute | solution.py:328
  69.8 0.8 collective-permute-done.7.other_ref
  70.6 1.6 %copy-done = f32[2,512,512]{2,1,0:T(8,128)S(1)} copy-done((f32[2,512,512]{2,1,0:T(8,128)S(1)}, f32[2,512,512]{2,1,0:T(8,128)}, u32[]{:S(2)}) %copy-start) | copy-done | bytes 2097176
  72.2 1.2 %copy-done.1 = f32[512,512]{1,0:T(8,128)S(1)} copy-done((f32[512,512]{1,0:T(8,128)S(1)}, f32[512,512]{1,0:T(8,128)}, u32[]{:S(2)}) %copy-start.1) | copy-done | bytes 1048600
  73.5 1.9 %shard_map.72 = f32[2,1024]{1,0:T(2,128)S(1)} custom-call(f32[2,512]{1,0:T(2,128)S(1)} %get-tuple-element.7.residual_ref, f32[2,512]{1,0:T(2,128)S(1)} %collective-permute-done.7.other_ref, f32[2,512,512]{2,1,0:T(8,128)S(1)} %copy-done, f32[512,512]{1,0:T(8,128)S(1)} %copy-done.1, f32[512,768]{1,0:T(8,128)S(1)} %collective-permute-done.8._.refs_2_.refs_3_), custom_call_target="tpu_custom_call" | custom-call | flops 150994944 | bytes 3145728 | tf_op jit(solution)/shard_map/pallas_call | solution.py:236
  75.3 0.1 broadcast_in_dim.3
  75.4 16.1 %all_to_all.11 = f32[32,2,1024]{2,1,0:T(2,128)} all-to-all(f32[32,2,1024]{2,1,0:T(2,128)S(1)} %broadcast_in_dim.3), channel_id=1, replica_groups=mesh['row'=16,'col'=32] {'col'}, dimensions={0} | all-to-all | bytes 524288 | tf_op jit(solution)/shard_map/all_to_all | solution.py:330
  91.5 1.1 %reshape.7.found_ref = f32[64,1024]{1,0:T(8,128)S(1)} reshape(f32[32,2,1024]{2,1,0:T(2,128)} %all_to_all.11) | data formatting | bytes 524288 | tf_op jit(solution)/shard_map/reshape | solution.py:332
  92.7 0.1 shard_map.73
  92.8 5.5 %collective-permute-start.9 = (f32[32,2,32]{2,1,0:T(2,128)S(1)}, f32[32,2,32]{2,1,0:T(2,128)S(1)}, u32[]{:S(2)}, u32[]{:S(2)}) collective-permute-start(f32[32,2,32]{2,1,0:T(2,128)S(1)} %shard_map.73), channel_id=1, source_target_pairs={{0,0},{1,1},{2,32},{3,33},{4,64},{5,65},{6,96},{7,97},{8,128},{9,1... | collective-permute-start | bytes 24584 | tf_op jit(solution)/shard_map/ppermute | solution.py:334
  98.3 0.9 copy-done.3
  99.2 2.1 %shard_map.74 = f32[64,768]{1,0:T(8,128)} custom-call(f32[64,768]{1,0:T(8,128)S(1)} %copy-done.3, f32[64,1024]{1,0:T(8,128)S(1)} %reshape.7.found_ref, f32[512,768]{1,0:T(8,128)S(1)} %get-tuple-element.5.refs_0_.refs_1_, f32[512,768]{1,0:T(8,128)S(1)} %get-tuple-element.5.refs_0_.refs_1_, f32[512,768]{1,0:T(8,128)S(1)} %collective-permute-done.8._.refs_2_.refs_3_, ...), custom_call_target="tpu_custom_call" | custom-call | flops 905969664 | bytes 3145728 | tf_op jit(solution)/shard_map/pallas_call | solution.py:271
  101.3 5.2 %collective-permute-done.9 = f32[32,2,32]{2,1,0:T(2,128)S(1)} collective-permute-done((f32[32,2,32]{2,1,0:T(2,128)S(1)}, f32[32,2,32]{2,1,0:T(2,128)S(1)}, u32[]{:S(2)}, u32[]{:S(2)}) %collective-permute-start.9) | collective-permute-done | bytes 8224 | tf_op jit(solution)/shard_map/ppermute | solution.py:334
  106.5 0.6 copy.8
  (14 shorter events, 0.0 us)
Async XLA Ops:
  0.6 40.1 %copy-start.2 = (f32[64,768]{1,0:T(8,128)S(1)}, f32[64,768]{1,0:T(8,128)}, u32[]{:S(2)}) copy-start(f32[64,768]{1,0:T(8,128)} %values_ref.1) | copy-start | bytes 589828
  0.6 1.0 copy-start.4
  1.6 0.8 copy-start.5
  2.5 13.2 %collective-permute-start.1 = (f32[200,256]{1,0:T(8,128)S(1)}, f32[200,256]{1,0:T(8,128)S(1)}, u32[]{:S(2)}, u32[]{:S(2)}) collective-permute-start(f32[200,256]{1,0:T(8,128)S(1)} %shard_map.68.one_ref), channel_id=1, source_target_pairs={{0,32},{32,0},{64,96},{96,64},{128,160},{160,128},{192,224},{224,1... | collective-permute-start | bytes 614408 | tf_op jit(solution)/shard_map/ppermute | solution.py:313
  5.1 17.8 %collective-permute-start.3 = (f32[200,256]{1,0:T(8,128)S(1)}, f32[200,256]{1,0:T(8,128)S(1)}, u32[]{:S(2)}, u32[]{:S(2)}) collective-permute-start(f32[200,256]{1,0:T(8,128)S(1)} %shard_map.68.one_ref), channel_id=1, source_target_pairs={{0,128},{32,416},{64,192},{96,480},{128,256},{160,32},{192,320},{2... | collective-permute-start | bytes 614408 | tf_op jit(solution)/shard_map/ppermute | solution.py:314
  15.8 9.3 %collective-permute-start.4 = (f32[200,256]{1,0:T(8,128)S(1)}, f32[200,256]{1,0:T(8,128)S(1)}, u32[]{:S(2)}, u32[]{:S(2)}) collective-permute-start(f32[200,256]{1,0:T(8,128)S(1)} %collective-permute-done.1.two_ref), channel_id=1, source_target_pairs={{0,128},{32,416},{64,192},{96,480},{128,256},{160,32},{192,320},{2... | collective-permute-start | bytes 614408 | tf_op jit(solution)/shard_map/ppermute | solution.py:315
  18.0 5.0 %collective-permute-start = (f32[64,768]{1,0:T(8,128)}, f32[64,768]{1,0:T(8,128)S(1)}, u32[]{:S(2)}, u32[]{:S(2)}) collective-permute-start(f32[64,768]{1,0:T(8,128)} %values_ref.1), channel_id=1, source_target_pairs={{0,32},{32,0},{64,96},{96,64},{128,160},{160,128},{192,224},{224,1... | collective-permute-start | bytes 589832 | tf_op jit(solution)/shard_map/ppermute | solution.py:318
  21.0 19.7 %collective-permute-start.2 = (f32[400,256]{1,0:T(8,128)S(1)}, f32[400,256]{1,0:T(8,128)S(1)}, u32[]{:S(2)}, u32[]{:S(2)}) collective-permute-start(f32[400,256]{1,0:T(8,128)S(1)} %shard_map.69.refs_0_), channel_id=1, source_target_pairs={{0,64},{32,480},{64,128},{96,32},{128,192},{160,96},{192,256},{224... | collective-permute-start | bytes 1228808 | tf_op jit(solution)/shard_map/ppermute | solution.py:317
  25.6 15.2 %collective-permute-start.5 = (f32[400,256]{1,0:T(8,128)S(1)}, f32[400,256]{1,0:T(8,128)S(1)}, u32[]{:S(2)}, u32[]{:S(2)}) collective-permute-start(f32[400,256]{1,0:T(8,128)S(1)} %shard_map.70.refs_2_), channel_id=1, source_target_pairs={{0,64},{32,480},{64,128},{96,32},{128,192},{160,96},{192,256},{224... | collective-permute-start | bytes 1228808 | tf_op jit(solution)/shard_map/ppermute | solution.py:321
  29.4 11.4 %collective-permute-start.6 = (f32[200,256]{1,0:T(8,128)S(1)}, f32[200,256]{1,0:T(8,128)S(1)}, u32[]{:S(2)}, u32[]{:S(2)}) collective-permute-start(f32[200,256]{1,0:T(8,128)S(1)} %collective-permute-done.4.two_ref), channel_id=1, source_target_pairs={{0,128},{32,416},{64,192},{96,480},{128,256},{160,32},{192,320},{2... | collective-permute-start | bytes 614408 | tf_op jit(solution)/shard_map/ppermute | solution.py:319
  41.8 28.8 %collective-permute-start.8 = (f32[512,768]{1,0:T(8,128)S(1)}, f32[512,768]{1,0:T(8,128)S(1)}, u32[]{:S(2)}, u32[]{:S(2)}) collective-permute-start(f32[512,768]{1,0:T(8,128)S(1)} %get-tuple-element.5.refs_0_.refs_1_), channel_id=1, source_target_pairs={{0,32},{32,0},{64,96},{96,64},{128,160},{160,128},{192,224},{224,1... | collective-permute-start | bytes 4718600 | tf_op jit(solution)/shard_map/ppermute | solution.py:324
  66.7 3.9 %collective-permute-start.7 = (f32[2,512]{1,0:T(2,128)S(1)}, f32[2,512]{1,0:T(2,128)S(1)}, u32[]{:S(2)}, u32[]{:S(2)}) collective-permute-start(f32[2,512]{1,0:T(2,128)S(1)} %get-tuple-element.6), channel_id=1, source_target_pairs={{0,32},{32,0},{64,96},{96,64},{128,160},{160,128},{192,224},{224,1... | collective-permute-start | bytes 12296 | tf_op jit(solution)/shard_map/ppermute | solution.py:328
  70.6 1.6 %copy-start = (f32[2,512,512]{2,1,0:T(8,128)S(1)}, f32[2,512,512]{2,1,0:T(8,128)}, u32[]{:S(2)}) copy-start(f32[2,512,512]{2,1,0:T(8,128)} %inverses_ref.1) | copy-start | bytes 6291460
  72.2 1.2 %copy-start.1 = (f32[512,512]{1,0:T(8,128)S(1)}, f32[512,512]{1,0:T(8,128)}, u32[]{:S(2)}) copy-start(f32[512,512]{1,0:T(8,128)} %coupling_ref.1) | copy-start | bytes 3145732
  92.8 13.7 %collective-permute-start.9 = (f32[32,2,32]{2,1,0:T(2,128)S(1)}, f32[32,2,32]{2,1,0:T(2,128)S(1)}, u32[]{:S(2)}, u32[]{:S(2)}) collective-permute-start(f32[32,2,32]{2,1,0:T(2,128)S(1)} %shard_map.73), channel_id=1, source_target_pairs={{0,0},{1,1},{2,32},{3,33},{4,64},{5,65},{6,96},{7,97},{8,128},{9,1... | collective-permute-start | bytes 24584 | tf_op jit(solution)/shard_map/ppermute | solution.py:334
  98.3 0.9 copy-start.3

commit v10 on v9

--- a/solution.py
+++ b/solution.py
@@ -236,7 +236,7 @@
     return kernel_call(
         body,
         jax.ShapeDtypeStruct((each, 2 * size), residual.dtype),
-        [in_vmem()] * 4 + [anywhere()],
+        [in_vmem()] * 5,
         in_vmem(),
         scratch=[pltpu.VMEM((2, deep, size), jnp.float32)],
         flops=36 * deep * size * size,
@@ -326,7 +326,7 @@
     each = rows // COLS
     residual = jnp.sum(lax.all_to_all(partial, "col", 0, 0, tiled=True), axis=0)
     residual_other = lax.ppermute(residual[each:], "row", core_swap())
-    found = panel_solve(residual[:each], residual_other, inverses, coupling, panel_other)
+    found = panel_solve(residual[:each], residual_other, inverses, coupling, panel_other[:8, :128])
     gathered = lax.all_to_all(
         jnp.broadcast_to(found, (COLS,) + found.shape), "col", 0, 0, tiled=True
     ).reshape(rows, -1)

time: 108 us -> 108 us (level)
  no operation moved by 1% of the time
where the time goes in v10:
time: 108 us; the launch traced here: 107 us
  starting transfers between devices  41.1 us (38%)
  blocking collectives  36.1 us (33%)
  waiting for transfers between devices  15.3 us (14%)
  local copies, waits for them, and re-layouts  7.29 us (7%)
  Pallas kernels  6.42 us (6%)
    all_to_all x1, blocking collectives, shards(): residual = jnp.sum(lax.all_to_all(partial, 'col', 0, 0, tiled=True), axis=0)  20 us
    all_to_all x1, blocking collectives, shards(): lax.all_to_all(jnp.broadcast_to(found, (COLS,) + found.shape), 'col', 0,...  16.1 us
    ppermute x1, starting transfers between devices, shards(): two_own = lax.ppermute(own, 'row', apart(2))  10.7 us
    ppermute x1, waiting for transfers between devices, shards(): four = lax.ppermute(two_other, 'row', apart(2))  7.26 us
    unnamed x13, local copies, waits for them, and re-layouts  6.07 us
    ppermute x1, starting transfers between devices, shards(): owned = lax.ppermute(cut(gathered, part), ('row', 'col'), work_to_window())  5.51 us
    ppermute x1, waiting for transfers between devices, shards(): owned = lax.ppermute(cut(gathered, part), ('row', 'col'), work_to_window())  5.18 us
    ppermute x1, starting transfers between devices, shards(): panel_other = lax.ppermute(panel, 'row', core_swap())  4.79 us
  transfers between devices with their start and end apart: 10, of which 4 were waited for; matrix products, arithmetic and copies ran while one was open for 0% of the time, Pallas kernels for 3%

profile of v10, /device:TPU:13, one launch (start us, length us, event | category | flops | bytes accessed | tf_op | source)
XLA Modules:
  0.0 107.2 jit_solution(6786884568056302492)
XLA Ops:
  0.7 1.0 copy-done.4
  1.6 0.8 copy-done.5
  2.4 0.2 shard_map.68.one_ref
  2.5 2.6 %collective-permute-start.1 = (f32[200,256]{1,0:T(8,128)S(1)}, f32[200,256]{1,0:T(8,128)S(1)}, u32[]{:S(2)}, u32[]{:S(2)}) collective-permute-start(f32[200,256]{1,0:T(8,128)S(1)} %shard_map.68.one_ref), channel_id=1, source_target_pairs={{0,32},{32,0},{64,96},{96,64},{128,160},{160,128},{192,224},{224,1... | collective-permute-start | bytes 614408 | tf_op jit(solution)/shard_map/ppermute | solution.py:313
  5.1 10.7 %collective-permute-start.3 = (f32[200,256]{1,0:T(8,128)S(1)}, f32[200,256]{1,0:T(8,128)S(1)}, u32[]{:S(2)}, u32[]{:S(2)}) collective-permute-start(f32[200,256]{1,0:T(8,128)S(1)} %shard_map.68.one_ref), channel_id=1, source_target_pairs={{0,128},{32,416},{64,192},{96,480},{128,256},{160,32},{192,320},{2... | collective-permute-start | bytes 614408 | tf_op jit(solution)/shard_map/ppermute | solution.py:314
  15.8 2.2 %collective-permute-start.4 = (f32[200,256]{1,0:T(8,128)S(1)}, f32[200,256]{1,0:T(8,128)S(1)}, u32[]{:S(2)}, u32[]{:S(2)}) collective-permute-start(f32[200,256]{1,0:T(8,128)S(1)} %collective-permute-done.1.two_ref), channel_id=1, source_target_pairs={{0,128},{32,416},{64,192},{96,480},{128,256},{160,32},{192,320},{2... | collective-permute-start | bytes 614408 | tf_op jit(solution)/shard_map/ppermute | solution.py:315
  18.0 2.5 %collective-permute-start = (f32[64,768]{1,0:T(8,128)}, f32[64,768]{1,0:T(8,128)S(1)}, u32[]{:S(2)}, u32[]{:S(2)}) collective-permute-start(f32[64,768]{1,0:T(8,128)} %values_ref.1), channel_id=1, source_target_pairs={{0,32},{32,0},{64,96},{96,64},{128,160},{160,128},{192,224},{224,1... | collective-permute-start | bytes 589832 | tf_op jit(solution)/shard_map/ppermute | solution.py:318
  20.5 0.5 shard_map.69.refs_0_
  21.0 1.9 %collective-permute-start.2 = (f32[400,256]{1,0:T(8,128)S(1)}, f32[400,256]{1,0:T(8,128)S(1)}, u32[]{:S(2)}, u32[]{:S(2)}) collective-permute-start(f32[400,256]{1,0:T(8,128)S(1)} %shard_map.69.refs_0_), channel_id=1, source_target_pairs={{0,64},{32,480},{64,128},{96,32},{128,192},{160,96},{192,256},{224... | collective-permute-start | bytes 1228808 | tf_op jit(solution)/shard_map/ppermute | solution.py:317
  23.0 2.1 %collective-permute-done.4.two_ref = f32[200,256]{1,0:T(8,128)S(1)} collective-permute-done((f32[200,256]{1,0:T(8,128)S(1)}, f32[200,256]{1,0:T(8,128)S(1)}, u32[]{:S(2)}, u32[]{:S(2)}) %collective-permute-start.4) | collective-permute-done | bytes 204832 | tf_op jit(solution)/shard_map/ppermute | solution.py:315
  25.0 0.5 shard_map.70.refs_2_
  25.6 3.8 %collective-permute-start.5 = (f32[400,256]{1,0:T(8,128)S(1)}, f32[400,256]{1,0:T(8,128)S(1)}, u32[]{:S(2)}, u32[]{:S(2)}) collective-permute-start(f32[400,256]{1,0:T(8,128)S(1)} %shard_map.70.refs_2_), channel_id=1, source_target_pairs={{0,64},{32,480},{64,128},{96,32},{128,192},{160,96},{192,256},{224... | collective-permute-start | bytes 1228808 | tf_op jit(solution)/shard_map/ppermute | solution.py:321
  29.4 4.1 %collective-permute-start.6 = (f32[200,256]{1,0:T(8,128)S(1)}, f32[200,256]{1,0:T(8,128)S(1)}, u32[]{:S(2)}, u32[]{:S(2)}) collective-permute-start(f32[200,256]{1,0:T(8,128)S(1)} %collective-permute-done.4.two_ref), channel_id=1, source_target_pairs={{0,128},{32,416},{64,192},{96,480},{128,256},{160,32},{192,320},{2... | collective-permute-start | bytes 614408 | tf_op jit(solution)/shard_map/ppermute | solution.py:319
  33.5 7.3 %collective-permute-done.6.refs_4_ = f32[200,256]{1,0:T(8,128)S(1)} collective-permute-done((f32[200,256]{1,0:T(8,128)S(1)}, f32[200,256]{1,0:T(8,128)S(1)}, u32[]{:S(2)}, u32[]{:S(2)}) %collective-permute-start.6) | collective-permute-done | bytes 204832 | tf_op jit(solution)/shard_map/ppermute | solution.py:319
  40.8 1.1 shard_map.71
  41.8 4.8 %collective-permute-start.8 = (f32[512,768]{1,0:T(8,128)S(1)}, f32[512,768]{1,0:T(8,128)S(1)}, u32[]{:S(2)}, u32[]{:S(2)}) collective-permute-start(f32[512,768]{1,0:T(8,128)S(1)} %get-tuple-element.5.refs_0_.refs_1_), channel_id=1, source_target_pairs={{0,32},{32,0},{64,96},{96,64},{128,160},{160,128},{192,224},{224,1... | collective-permute-start | bytes 4718600 | tf_op jit(solution)/shard_map/ppermute | solution.py:324
  46.6 20.0 %all_to_all.10 = f32[32,4,512]{2,1,0:T(4,128)S(1)} all-to-all(f32[32,4,512]{2,1,0:T(4,128)S(1)} %get-tuple-element.4), channel_id=1, replica_groups=mesh['row'=16,'col'=32] {'col'}, dimensions={0} | all-to-all | bytes 524288 | tf_op jit(solution)/shard_map/all_to_all | solution.py:327
  66.6 0.1 reduce_sum.9
  66.7 3.1 %collective-permute-start.7 = (f32[2,512]{1,0:T(2,128)S(1)}, f32[2,512]{1,0:T(2,128)S(1)}, u32[]{:S(2)}, u32[]{:S(2)}) collective-permute-start(f32[2,512]{1,0:T(2,128)S(1)} %get-tuple-element.6), channel_id=1, source_target_pairs={{0,32},{32,0},{64,96},{96,64},{128,160},{160,128},{192,224},{224,1... | collective-permute-start | bytes 12296 | tf_op jit(solution)/shard_map/ppermute | solution.py:328
  69.9 0.8 collective-permute-done.7.other_ref
  70.6 1.6 %copy-done = f32[2,512,512]{2,1,0:T(8,128)S(1)} copy-done((f32[2,512,512]{2,1,0:T(8,128)S(1)}, f32[2,512,512]{2,1,0:T(8,128)}, u32[]{:S(2)}) %copy-start) | copy-done | bytes 2097176
  72.2 1.2 %copy-done.1 = f32[512,512]{1,0:T(8,128)S(1)} copy-done((f32[512,512]{1,0:T(8,128)S(1)}, f32[512,512]{1,0:T(8,128)}, u32[]{:S(2)}) %copy-start.1) | copy-done | bytes 1048600
  73.4 1.9 %shard_map.72 = f32[2,1024]{1,0:T(2,128)S(1)} custom-call(f32[2,512]{1,0:T(2,128)S(1)} %get-tuple-element.7.residual_ref, f32[2,512]{1,0:T(2,128)S(1)} %collective-permute-done.7.other_ref, f32[2,512,512]{2,1,0:T(8,128)S(1)} %copy-done, f32[512,512]{1,0:T(8,128)S(1)} %copy-done.1, f32[8,128]{1,0:T(8,128)S(1)} %slice.14._), custom_call_target="tpu_custom_call" | custom-call | flops 150994944 | bytes 3145728 | tf_op jit(solution)/shard_map/pallas_call | solution.py:236
  75.4 0.1 broadcast_in_dim.3
  75.5 16.1 %all_to_all.11 = f32[32,2,1024]{2,1,0:T(2,128)} all-to-all(f32[32,2,1024]{2,1,0:T(2,128)S(1)} %broadcast_in_dim.3), channel_id=1, replica_groups=mesh['row'=16,'col'=32] {'col'}, dimensions={0} | all-to-all | bytes 524288 | tf_op jit(solution)/shard_map/all_to_all | solution.py:330
  91.6 1.1 %reshape.7.found_ref = f32[64,1024]{1,0:T(8,128)S(1)} reshape(f32[32,2,1024]{2,1,0:T(2,128)} %all_to_all.11) | data formatting | bytes 524288 | tf_op jit(solution)/shard_map/reshape | solution.py:332
  92.7 0.1 shard_map.73
  92.8 5.5 %collective-permute-start.9 = (f32[32,2,32]{2,1,0:T(2,128)S(1)}, f32[32,2,32]{2,1,0:T(2,128)S(1)}, u32[]{:S(2)}, u32[]{:S(2)}) collective-permute-start(f32[32,2,32]{2,1,0:T(2,128)S(1)} %shard_map.73), channel_id=1, source_target_pairs={{0,0},{1,1},{2,32},{3,33},{4,64},{5,65},{6,96},{7,97},{8,128},{9,1... | collective-permute-start | bytes 24584 | tf_op jit(solution)/shard_map/ppermute | solution.py:334
  98.3 0.9 copy-done.3
  99.3 2.1 %shard_map.74 = f32[64,768]{1,0:T(8,128)} custom-call(f32[64,768]{1,0:T(8,128)S(1)} %copy-done.3, f32[64,1024]{1,0:T(8,128)S(1)} %reshape.7.found_ref, f32[512,768]{1,0:T(8,128)S(1)} %get-tuple-element.5.refs_0_.refs_1_, f32[512,768]{1,0:T(8,128)S(1)} %get-tuple-element.5.refs_0_.refs_1_, f32[512,768]{1,0:T(8,128)S(1)} %collective-permute-done.8.refs_2_.refs_3_, ...), custom_call_target="tpu_custom_call" | custom-call | flops 905969664 | bytes 3145728 | tf_op jit(solution)/shard_map/pallas_call | solution.py:271
  101.4 5.2 %collective-permute-done.9 = f32[32,2,32]{2,1,0:T(2,128)S(1)} collective-permute-done((f32[32,2,32]{2,1,0:T(2,128)S(1)}, f32[32,2,32]{2,1,0:T(2,128)S(1)}, u32[]{:S(2)}, u32[]{:S(2)}) %collective-permute-start.9) | collective-permute-done | bytes 8224 | tf_op jit(solution)/shard_map/ppermute | solution.py:334
  106.5 0.6 copy.8
  (15 shorter events, 0.0 us)
Async XLA Ops:
  0.6 40.1 %copy-start.2 = (f32[64,768]{1,0:T(8,128)S(1)}, f32[64,768]{1,0:T(8,128)}, u32[]{:S(2)}) copy-start(f32[64,768]{1,0:T(8,128)} %values_ref.1) | copy-start | bytes 589828
  0.6 1.0 copy-start.4
  1.6 0.8 copy-start.5
  2.5 13.2 %collective-permute-start.1 = (f32[200,256]{1,0:T(8,128)S(1)}, f32[200,256]{1,0:T(8,128)S(1)}, u32[]{:S(2)}, u32[]{:S(2)}) collective-permute-start(f32[200,256]{1,0:T(8,128)S(1)} %shard_map.68.one_ref), channel_id=1, source_target_pairs={{0,32},{32,0},{64,96},{96,64},{128,160},{160,128},{192,224},{224,1... | collective-permute-start | bytes 614408 | tf_op jit(solution)/shard_map/ppermute | solution.py:313
  5.1 17.8 %collective-permute-start.3 = (f32[200,256]{1,0:T(8,128)S(1)}, f32[200,256]{1,0:T(8,128)S(1)}, u32[]{:S(2)}, u32[]{:S(2)}) collective-permute-start(f32[200,256]{1,0:T(8,128)S(1)} %shard_map.68.one_ref), channel_id=1, source_target_pairs={{0,128},{32,416},{64,192},{96,480},{128,256},{160,32},{192,320},{2... | collective-permute-start | bytes 614408 | tf_op jit(solution)/shard_map/ppermute | solution.py:314
  15.8 9.3 %collective-permute-start.4 = (f32[200,256]{1,0:T(8,128)S(1)}, f32[200,256]{1,0:T(8,128)S(1)}, u32[]{:S(2)}, u32[]{:S(2)}) collective-permute-start(f32[200,256]{1,0:T(8,128)S(1)} %collective-permute-done.1.two_ref), channel_id=1, source_target_pairs={{0,128},{32,416},{64,192},{96,480},{128,256},{160,32},{192,320},{2... | collective-permute-start | bytes 614408 | tf_op jit(solution)/shard_map/ppermute | solution.py:315
  18.0 5.0 %collective-permute-start = (f32[64,768]{1,0:T(8,128)}, f32[64,768]{1,0:T(8,128)S(1)}, u32[]{:S(2)}, u32[]{:S(2)}) collective-permute-start(f32[64,768]{1,0:T(8,128)} %values_ref.1), channel_id=1, source_target_pairs={{0,32},{32,0},{64,96},{96,64},{128,160},{160,128},{192,224},{224,1... | collective-permute-start | bytes 589832 | tf_op jit(solution)/shard_map/ppermute | solution.py:318
  21.0 19.7 %collective-permute-start.2 = (f32[400,256]{1,0:T(8,128)S(1)}, f32[400,256]{1,0:T(8,128)S(1)}, u32[]{:S(2)}, u32[]{:S(2)}) collective-permute-start(f32[400,256]{1,0:T(8,128)S(1)} %shard_map.69.refs_0_), channel_id=1, source_target_pairs={{0,64},{32,480},{64,128},{96,32},{128,192},{160,96},{192,256},{224... | collective-permute-start | bytes 1228808 | tf_op jit(solution)/shard_map/ppermute | solution.py:317
  25.6 15.2 %collective-permute-start.5 = (f32[400,256]{1,0:T(8,128)S(1)}, f32[400,256]{1,0:T(8,128)S(1)}, u32[]{:S(2)}, u32[]{:S(2)}) collective-permute-start(f32[400,256]{1,0:T(8,128)S(1)} %shard_map.70.refs_2_), channel_id=1, source_target_pairs={{0,64},{32,480},{64,128},{96,32},{128,192},{160,96},{192,256},{224... | collective-permute-start | bytes 1228808 | tf_op jit(solution)/shard_map/ppermute | solution.py:321
  29.4 11.4 %collective-permute-start.6 = (f32[200,256]{1,0:T(8,128)S(1)}, f32[200,256]{1,0:T(8,128)S(1)}, u32[]{:S(2)}, u32[]{:S(2)}) collective-permute-start(f32[200,256]{1,0:T(8,128)S(1)} %collective-permute-done.4.two_ref), channel_id=1, source_target_pairs={{0,128},{32,416},{64,192},{96,480},{128,256},{160,32},{192,320},{2... | collective-permute-start | bytes 614408 | tf_op jit(solution)/shard_map/ppermute | solution.py:319
  41.8 28.0 %collective-permute-start.8 = (f32[512,768]{1,0:T(8,128)S(1)}, f32[512,768]{1,0:T(8,128)S(1)}, u32[]{:S(2)}, u32[]{:S(2)}) collective-permute-start(f32[512,768]{1,0:T(8,128)S(1)} %get-tuple-element.5.refs_0_.refs_1_), channel_id=1, source_target_pairs={{0,32},{32,0},{64,96},{96,64},{128,160},{160,128},{192,224},{224,1... | collective-permute-start | bytes 4718600 | tf_op jit(solution)/shard_map/ppermute | solution.py:324
  66.7 3.9 %collective-permute-start.7 = (f32[2,512]{1,0:T(2,128)S(1)}, f32[2,512]{1,0:T(2,128)S(1)}, u32[]{:S(2)}, u32[]{:S(2)}) collective-permute-start(f32[2,512]{1,0:T(2,128)S(1)} %get-tuple-element.6), channel_id=1, source_target_pairs={{0,32},{32,0},{64,96},{96,64},{128,160},{160,128},{192,224},{224,1... | collective-permute-start | bytes 12296 | tf_op jit(solution)/shard_map/ppermute | solution.py:328
  70.6 1.6 %copy-start = (f32[2,512,512]{2,1,0:T(8,128)S(1)}, f32[2,512,512]{2,1,0:T(8,128)}, u32[]{:S(2)}) copy-start(f32[2,512,512]{2,1,0:T(8,128)} %inverses_ref.1) | copy-start | bytes 6291460
  72.2 1.2 %copy-start.1 = (f32[512,512]{1,0:T(8,128)S(1)}, f32[512,512]{1,0:T(8,128)}, u32[]{:S(2)}) copy-start(f32[512,512]{1,0:T(8,128)} %coupling_ref.1) | copy-start | bytes 3145732
  92.8 13.7 %collective-permute-start.9 = (f32[32,2,32]{2,1,0:T(2,128)S(1)}, f32[32,2,32]{2,1,0:T(2,128)S(1)}, u32[]{:S(2)}, u32[]{:S(2)}) collective-permute-start(f32[32,2,32]{2,1,0:T(2,128)S(1)} %shard_map.73), channel_id=1, source_target_pairs={{0,0},{1,1},{2,32},{3,33},{4,64},{5,65},{6,96},{7,97},{8,128},{9,1... | collective-permute-start | bytes 24584 | tf_op jit(solution)/shard_map/ppermute | solution.py:334
  98.3 0.9 copy-start.3

commit v11 on v10

--- a/solution.py
+++ b/solution.py
@@ -189,7 +189,7 @@
             pltpu.VMEM((unknowns, count), jnp.float32),
             pltpu.VMEM((2 * rows, unknowns), jnp.float32),
         ],
-        mib=24,
+        mib=32,
         flops=12 * rows * unknowns * width,
         moved=8 * unknowns * width,
     )(solved, solved_other, *pairs, last)

time: 108 us -> 108 us (level)
  no operation moved by 1% of the time
where the time goes in v11:
time: 108 us; the launch traced here: 107 us
  starting transfers between devices  41.1 us (38%)
  blocking collectives  36.1 us (33%)
  waiting for transfers between devices  15.3 us (14%)
  local copies, waits for them, and re-layouts  7.29 us (7%)
  Pallas kernels  6.42 us (6%)
    all_to_all x1, blocking collectives, shards(): residual = jnp.sum(lax.all_to_all(partial, 'col', 0, 0, tiled=True), axis=0)  20 us
    all_to_all x1, blocking collectives, shards(): lax.all_to_all(jnp.broadcast_to(found, (COLS,) + found.shape), 'col', 0,...  16.1 us
    ppermute x1, starting transfers between devices, shards(): two_own = lax.ppermute(own, 'row', apart(2))  10.7 us
    ppermute x1, waiting for transfers between devices, shards(): four = lax.ppermute(two_other, 'row', apart(2))  7.26 us
    unnamed x13, local copies, waits for them, and re-layouts  6.07 us
    ppermute x1, starting transfers between devices, shards(): owned = lax.ppermute(cut(gathered, part), ('row', 'col'), work_to_window())  5.51 us
    ppermute x1, waiting for transfers between devices, shards(): owned = lax.ppermute(cut(gathered, part), ('row', 'col'), work_to_window())  5.18 us
    ppermute x1, starting transfers between devices, shards(): panel_other = lax.ppermute(panel, 'row', core_swap())  4.79 us
  transfers between devices with their start and end apart: 10, of which 4 were waited for; matrix products, arithmetic and copies ran while one was open for 0% of the time, Pallas kernels for 3%

profile of v11, /device:TPU:13, one launch (start us, length us, event | category | flops | bytes accessed | tf_op | source)
XLA Modules:
  0.0 107.2 jit_solution(11887686208177562209)
XLA Ops:
  0.7 1.0 copy-done.4
  1.6 0.8 copy-done.5
  2.4 0.2 shard_map.68.one_ref
  2.5 2.6 %collective-permute-start.1 = (f32[200,256]{1,0:T(8,128)S(1)}, f32[200,256]{1,0:T(8,128)S(1)}, u32[]{:S(2)}, u32[]{:S(2)}) collective-permute-start(f32[200,256]{1,0:T(8,128)S(1)} %shard_map.68.one_ref), channel_id=1, source_target_pairs={{0,32},{32,0},{64,96},{96,64},{128,160},{160,128},{192,224},{224,1... | collective-permute-start | bytes 614408 | tf_op jit(solution)/shard_map/ppermute | solution.py:313
  5.1 10.7 %collective-permute-start.3 = (f32[200,256]{1,0:T(8,128)S(1)}, f32[200,256]{1,0:T(8,128)S(1)}, u32[]{:S(2)}, u32[]{:S(2)}) collective-permute-start(f32[200,256]{1,0:T(8,128)S(1)} %shard_map.68.one_ref), channel_id=1, source_target_pairs={{0,128},{32,416},{64,192},{96,480},{128,256},{160,32},{192,320},{2... | collective-permute-start | bytes 614408 | tf_op jit(solution)/shard_map/ppermute | solution.py:314
  15.8 2.2 %collective-permute-start.4 = (f32[200,256]{1,0:T(8,128)S(1)}, f32[200,256]{1,0:T(8,128)S(1)}, u32[]{:S(2)}, u32[]{:S(2)}) collective-permute-start(f32[200,256]{1,0:T(8,128)S(1)} %collective-permute-done.1.two_ref), channel_id=1, source_target_pairs={{0,128},{32,416},{64,192},{96,480},{128,256},{160,32},{192,320},{2... | collective-permute-start | bytes 614408 | tf_op jit(solution)/shard_map/ppermute | solution.py:315
  18.0 2.5 %collective-permute-start = (f32[64,768]{1,0:T(8,128)}, f32[64,768]{1,0:T(8,128)S(1)}, u32[]{:S(2)}, u32[]{:S(2)}) collective-permute-start(f32[64,768]{1,0:T(8,128)} %values_ref.1), channel_id=1, source_target_pairs={{0,32},{32,0},{64,96},{96,64},{128,160},{160,128},{192,224},{224,1... | collective-permute-start | bytes 589832 | tf_op jit(solution)/shard_map/ppermute | solution.py:318
  20.5 0.5 shard_map.69.refs_0_
  21.0 1.9 %collective-permute-start.2 = (f32[400,256]{1,0:T(8,128)S(1)}, f32[400,256]{1,0:T(8,128)S(1)}, u32[]{:S(2)}, u32[]{:S(2)}) collective-permute-start(f32[400,256]{1,0:T(8,128)S(1)} %shard_map.69.refs_0_), channel_id=1, source_target_pairs={{0,64},{32,480},{64,128},{96,32},{128,192},{160,96},{192,256},{224... | collective-permute-start | bytes 1228808 | tf_op jit(solution)/shard_map/ppermute | solution.py:317
  23.0 2.1 %collective-permute-done.4.two_ref = f32[200,256]{1,0:T(8,128)S(1)} collective-permute-done((f32[200,256]{1,0:T(8,128)S(1)}, f32[200,256]{1,0:T(8,128)S(1)}, u32[]{:S(2)}, u32[]{:S(2)}) %collective-permute-start.4) | collective-permute-done | bytes 204832 | tf_op jit(solution)/shard_map/ppermute | solution.py:315
  25.0 0.5 shard_map.70.refs_2_
  25.6 3.8 %collective-permute-start.5 = (f32[400,256]{1,0:T(8,128)S(1)}, f32[400,256]{1,0:T(8,128)S(1)}, u32[]{:S(2)}, u32[]{:S(2)}) collective-permute-start(f32[400,256]{1,0:T(8,128)S(1)} %shard_map.70.refs_2_), channel_id=1, source_target_pairs={{0,64},{32,480},{64,128},{96,32},{128,192},{160,96},{192,256},{224... | collective-permute-start | bytes 1228808 | tf_op jit(solution)/shard_map/ppermute | solution.py:321
  29.4 4.1 %collective-permute-start.6 = (f32[200,256]{1,0:T(8,128)S(1)}, f32[200,256]{1,0:T(8,128)S(1)}, u32[]{:S(2)}, u32[]{:S(2)}) collective-permute-start(f32[200,256]{1,0:T(8,128)S(1)} %collective-permute-done.4.two_ref), channel_id=1, source_target_pairs={{0,128},{32,416},{64,192},{96,480},{128,256},{160,32},{192,320},{2... | collective-permute-start | bytes 614408 | tf_op jit(solution)/shard_map/ppermute | solution.py:319
  33.5 7.3 %collective-permute-done.6.refs_4_ = f32[200,256]{1,0:T(8,128)S(1)} collective-permute-done((f32[200,256]{1,0:T(8,128)S(1)}, f32[200,256]{1,0:T(8,128)S(1)}, u32[]{:S(2)}, u32[]{:S(2)}) %collective-permute-start.6) | collective-permute-done | bytes 204832 | tf_op jit(solution)/shard_map/ppermute | solution.py:319
  40.8 1.1 shard_map.71
  41.8 4.8 %collective-permute-start.8 = (f32[512,768]{1,0:T(8,128)S(1)}, f32[512,768]{1,0:T(8,128)S(1)}, u32[]{:S(2)}, u32[]{:S(2)}) collective-permute-start(f32[512,768]{1,0:T(8,128)S(1)} %get-tuple-element.5.refs_0_.refs_1_), channel_id=1, source_target_pairs={{0,32},{32,0},{64,96},{96,64},{128,160},{160,128},{192,224},{224,1... | collective-permute-start | bytes 4718600 | tf_op jit(solution)/shard_map/ppermute | solution.py:324
  46.6 20.0 %all_to_all.10 = f32[32,4,512]{2,1,0:T(4,128)S(1)} all-to-all(f32[32,4,512]{2,1,0:T(4,128)S(1)} %get-tuple-element.4), channel_id=1, replica_groups=mesh['row'=16,'col'=32] {'col'}, dimensions={0} | all-to-all | bytes 524288 | tf_op jit(solution)/shard_map/all_to_all | solution.py:327
  66.6 0.1 reduce_sum.9
  66.7 3.1 %collective-permute-start.7 = (f32[2,512]{1,0:T(2,128)S(1)}, f32[2,512]{1,0:T(2,128)S(1)}, u32[]{:S(2)}, u32[]{:S(2)}) collective-permute-start(f32[2,512]{1,0:T(2,128)S(1)} %get-tuple-element.6), channel_id=1, source_target_pairs={{0,32},{32,0},{64,96},{96,64},{128,160},{160,128},{192,224},{224,1... | collective-permute-start | bytes 12296 | tf_op jit(solution)/shard_map/ppermute | solution.py:328
  69.9 0.8 collective-permute-done.7.other_ref
  70.6 1.6 %copy-done = f32[2,512,512]{2,1,0:T(8,128)S(1)} copy-done((f32[2,512,512]{2,1,0:T(8,128)S(1)}, f32[2,512,512]{2,1,0:T(8,128)}, u32[]{:S(2)}) %copy-start) | copy-done | bytes 2097176
  72.2 1.2 %copy-done.1 = f32[512,512]{1,0:T(8,128)S(1)} copy-done((f32[512,512]{1,0:T(8,128)S(1)}, f32[512,512]{1,0:T(8,128)}, u32[]{:S(2)}) %copy-start.1) | copy-done | bytes 1048600
  73.4 1.9 %shard_map.72 = f32[2,1024]{1,0:T(2,128)S(1)} custom-call(f32[2,512]{1,0:T(2,128)S(1)} %get-tuple-element.7.residual_ref, f32[2,512]{1,0:T(2,128)S(1)} %collective-permute-done.7.other_ref, f32[2,512,512]{2,1,0:T(8,128)S(1)} %copy-done, f32[512,512]{1,0:T(8,128)S(1)} %copy-done.1, f32[8,128]{1,0:T(8,128)S(1)} %slice.14._), custom_call_target="tpu_custom_call" | custom-call | flops 150994944 | bytes 3145728 | tf_op jit(solution)/shard_map/pallas_call | solution.py:236
  75.4 0.1 broadcast_in_dim.3
  75.5 16.1 %all_to_all.11 = f32[32,2,1024]{2,1,0:T(2,128)} all-to-all(f32[32,2,1024]{2,1,0:T(2,128)S(1)} %broadcast_in_dim.3), channel_id=1, replica_groups=mesh['row'=16,'col'=32] {'col'}, dimensions={0} | all-to-all | bytes 524288 | tf_op jit(solution)/shard_map/all_to_all | solution.py:330
  91.6 1.1 %reshape.7.found_ref = f32[64,1024]{1,0:T(8,128)S(1)} reshape(f32[32,2,1024]{2,1,0:T(2,128)} %all_to_all.11) | data formatting | bytes 524288 | tf_op jit(solution)/shard_map/reshape | solution.py:332
  92.7 0.1 shard_map.73
  92.8 5.5 %collective-permute-start.9 = (f32[32,2,32]{2,1,0:T(2,128)S(1)}, f32[32,2,32]{2,1,0:T(2,128)S(1)}, u32[]{:S(2)}, u32[]{:S(2)}) collective-permute-start(f32[32,2,32]{2,1,0:T(2,128)S(1)} %shard_map.73), channel_id=1, source_target_pairs={{0,0},{1,1},{2,32},{3,33},{4,64},{5,65},{6,96},{7,97},{8,128},{9,1... | collective-permute-start | bytes 24584 | tf_op jit(solution)/shard_map/ppermute | solution.py:334
  98.3 0.9 copy-done.3
  99.3 2.1 %shard_map.74 = f32[64,768]{1,0:T(8,128)} custom-call(f32[64,768]{1,0:T(8,128)S(1)} %copy-done.3, f32[64,1024]{1,0:T(8,128)S(1)} %reshape.7.found_ref, f32[512,768]{1,0:T(8,128)S(1)} %get-tuple-element.5.refs_0_.refs_1_, f32[512,768]{1,0:T(8,128)S(1)} %get-tuple-element.5.refs_0_.refs_1_, f32[512,768]{1,0:T(8,128)S(1)} %collective-permute-done.8.refs_2_.refs_3_, ...), custom_call_target="tpu_custom_call" | custom-call | flops 905969664 | bytes 3145728 | tf_op jit(solution)/shard_map/pallas_call | solution.py:271
  101.4 5.2 %collective-permute-done.9 = f32[32,2,32]{2,1,0:T(2,128)S(1)} collective-permute-done((f32[32,2,32]{2,1,0:T(2,128)S(1)}, f32[32,2,32]{2,1,0:T(2,128)S(1)}, u32[]{:S(2)}, u32[]{:S(2)}) %collective-permute-start.9) | collective-permute-done | bytes 8224 | tf_op jit(solution)/shard_map/ppermute | solution.py:334
  106.5 0.6 copy.8
  (15 shorter events, 0.0 us)
Async XLA Ops:
  0.6 40.1 %copy-start.2 = (f32[64,768]{1,0:T(8,128)S(1)}, f32[64,768]{1,0:T(8,128)}, u32[]{:S(2)}) copy-start(f32[64,768]{1,0:T(8,128)} %values_ref.1) | copy-start | bytes 589828
  0.6 1.0 copy-start.4
  1.6 0.8 copy-start.5
  2.5 13.2 %collective-permute-start.1 = (f32[200,256]{1,0:T(8,128)S(1)}, f32[200,256]{1,0:T(8,128)S(1)}, u32[]{:S(2)}, u32[]{:S(2)}) collective-permute-start(f32[200,256]{1,0:T(8,128)S(1)} %shard_map.68.one_ref), channel_id=1, source_target_pairs={{0,32},{32,0},{64,96},{96,64},{128,160},{160,128},{192,224},{224,1... | collective-permute-start | bytes 614408 | tf_op jit(solution)/shard_map/ppermute | solution.py:313
  5.1 17.8 %collective-permute-start.3 = (f32[200,256]{1,0:T(8,128)S(1)}, f32[200,256]{1,0:T(8,128)S(1)}, u32[]{:S(2)}, u32[]{:S(2)}) collective-permute-start(f32[200,256]{1,0:T(8,128)S(1)} %shard_map.68.one_ref), channel_id=1, source_target_pairs={{0,128},{32,416},{64,192},{96,480},{128,256},{160,32},{192,320},{2... | collective-permute-start | bytes 614408 | tf_op jit(solution)/shard_map/ppermute | solution.py:314
  15.8 9.3 %collective-permute-start.4 = (f32[200,256]{1,0:T(8,128)S(1)}, f32[200,256]{1,0:T(8,128)S(1)}, u32[]{:S(2)}, u32[]{:S(2)}) collective-permute-start(f32[200,256]{1,0:T(8,128)S(1)} %collective-permute-done.1.two_ref), channel_id=1, source_target_pairs={{0,128},{32,416},{64,192},{96,480},{128,256},{160,32},{192,320},{2... | collective-permute-start | bytes 614408 | tf_op jit(solution)/shard_map/ppermute | solution.py:315
  18.0 5.0 %collective-permute-start = (f32[64,768]{1,0:T(8,128)}, f32[64,768]{1,0:T(8,128)S(1)}, u32[]{:S(2)}, u32[]{:S(2)}) collective-permute-start(f32[64,768]{1,0:T(8,128)} %values_ref.1), channel_id=1, source_target_pairs={{0,32},{32,0},{64,96},{96,64},{128,160},{160,128},{192,224},{224,1... | collective-permute-start | bytes 589832 | tf_op jit(solution)/shard_map/ppermute | solution.py:318
  21.0 19.7 %collective-permute-start.2 = (f32[400,256]{1,0:T(8,128)S(1)}, f32[400,256]{1,0:T(8,128)S(1)}, u32[]{:S(2)}, u32[]{:S(2)}) collective-permute-start(f32[400,256]{1,0:T(8,128)S(1)} %shard_map.69.refs_0_), channel_id=1, source_target_pairs={{0,64},{32,480},{64,128},{96,32},{128,192},{160,96},{192,256},{224... | collective-permute-start | bytes 1228808 | tf_op jit(solution)/shard_map/ppermute | solution.py:317
  25.6 15.2 %collective-permute-start.5 = (f32[400,256]{1,0:T(8,128)S(1)}, f32[400,256]{1,0:T(8,128)S(1)}, u32[]{:S(2)}, u32[]{:S(2)}) collective-permute-start(f32[400,256]{1,0:T(8,128)S(1)} %shard_map.70.refs_2_), channel_id=1, source_target_pairs={{0,64},{32,480},{64,128},{96,32},{128,192},{160,96},{192,256},{224... | collective-permute-start | bytes 1228808 | tf_op jit(solution)/shard_map/ppermute | solution.py:321
  29.4 11.4 %collective-permute-start.6 = (f32[200,256]{1,0:T(8,128)S(1)}, f32[200,256]{1,0:T(8,128)S(1)}, u32[]{:S(2)}, u32[]{:S(2)}) collective-permute-start(f32[200,256]{1,0:T(8,128)S(1)} %collective-permute-done.4.two_ref), channel_id=1, source_target_pairs={{0,128},{32,416},{64,192},{96,480},{128,256},{160,32},{192,320},{2... | collective-permute-start | bytes 614408 | tf_op jit(solution)/shard_map/ppermute | solution.py:319
  41.8 28.0 %collective-permute-start.8 = (f32[512,768]{1,0:T(8,128)S(1)}, f32[512,768]{1,0:T(8,128)S(1)}, u32[]{:S(2)}, u32[]{:S(2)}) collective-permute-start(f32[512,768]{1,0:T(8,128)S(1)} %get-tuple-element.5.refs_0_.refs_1_), channel_id=1, source_target_pairs={{0,32},{32,0},{64,96},{96,64},{128,160},{160,128},{192,224},{224,1... | collective-permute-start | bytes 4718600 | tf_op jit(solution)/shard_map/ppermute | solution.py:324
  66.7 3.9 %collective-permute-start.7 = (f32[2,512]{1,0:T(2,128)S(1)}, f32[2,512]{1,0:T(2,128)S(1)}, u32[]{:S(2)}, u32[]{:S(2)}) collective-permute-start(f32[2,512]{1,0:T(2,128)S(1)} %get-tuple-element.6), channel_id=1, source_target_pairs={{0,32},{32,0},{64,96},{96,64},{128,160},{160,128},{192,224},{224,1... | collective-permute-start | bytes 12296 | tf_op jit(solution)/shard_map/ppermute | solution.py:328
  70.6 1.6 %copy-start = (f32[2,512,512]{2,1,0:T(8,128)S(1)}, f32[2,512,512]{2,1,0:T(8,128)}, u32[]{:S(2)}) copy-start(f32[2,512,512]{2,1,0:T(8,128)} %inverses_ref.1) | copy-start | bytes 6291460
  72.2 1.2 %copy-start.1 = (f32[512,512]{1,0:T(8,128)S(1)}, f32[512,512]{1,0:T(8,128)}, u32[]{:S(2)}) copy-start(f32[512,512]{1,0:T(8,128)} %coupling_ref.1) | copy-start | bytes 3145732
  92.8 13.7 %collective-permute-start.9 = (f32[32,2,32]{2,1,0:T(2,128)S(1)}, f32[32,2,32]{2,1,0:T(2,128)S(1)}, u32[]{:S(2)}, u32[]{:S(2)}) collective-permute-start(f32[32,2,32]{2,1,0:T(2,128)S(1)} %shard_map.73), channel_id=1, source_target_pairs={{0,0},{1,1},{2,32},{3,33},{4,64},{5,65},{6,96},{7,97},{8,128},{9,1... | collective-permute-start | bytes 24584 | tf_op jit(solution)/shard_map/ppermute | solution.py:334
  98.3 0.9 copy-start.3

commit v12 on v11

--- a/solution.py
+++ b/solution.py
@@ -12,7 +12,6 @@
 COLS = 32
 TAIL = 8
 LANES = 256
-DEPTH = 256
 MIB = 1024 * 1024
 
 
@@ -244,42 +243,44 @@
     )(residual, residual_other, inverses, coupling, arrival)
 
 
-def correct(values, found, parts):
-    rows, width = values.shape
-
-    def body(values_ref, found_ref, *refs):
-        *panel_refs, out_ref, held, sems = refs
+def correct(solved, found, panel, panel_other):
+    rows, width = solved.shape
+    size = panel.shape[0]
+    chunk = size // 2
+
+    def body(solved_ref, found_ref, panel_ref, other_ref, out_ref, held, sems):
         copies = [
-            pltpu.make_async_copy(ref.at[first : first + DEPTH], held.at[i], sems.at[i])
-            for i, (ref, (_, first, _)) in enumerate(zip(panel_refs, parts))
+            pltpu.make_async_copy(ref.at[at : at + chunk], held.at[i], sems.at[i])
+            for i, (ref, at) in enumerate(
+                (ref, at) for ref in (panel_ref, other_ref) for at in range(0, size, chunk)
+            )
         ]
         for copy in copies:
             copy.start()
-        total = values_ref[...]
-        for i, (copy, (_, _, at)) in enumerate(zip(copies, parts)):
-            up, down = halves(found_ref[:, at : at + DEPTH])
+        total = jnp.zeros((rows, width), jnp.float32)
+        for i, copy in enumerate(copies):
+            up, down = halves(found_ref[:, i * chunk : (i + 1) * chunk])
             copy.wait()
             panel_up, panel_down = halves(held[i])
             both = jnp.dot(
                 jnp.concatenate([up, down], axis=0), panel_up, preferred_element_type=jnp.float32
             )
             rest = jnp.dot(up, panel_down, preferred_element_type=jnp.float32)
-            total -= both[:rows] + both[rows:] + rest
-        out_ref[...] = total
-
-    count = len(parts)
-    return kernel_call(
-        body,
-        jax.ShapeDtypeStruct(values.shape, values.dtype),
-        [in_vmem()] * 2 + [in_hbm()] * count,
+            total += both[:rows] + both[rows:] + rest
+        out_ref[...] = solved_ref[...] - total
+
+    return kernel_call(
+        body,
+        jax.ShapeDtypeStruct(solved.shape, solved.dtype),
+        [in_vmem()] * 2 + [in_hbm()] * 2,
         in_vmem(),
         scratch=[
-            pltpu.VMEM((count, DEPTH, width), jnp.float32),
-            pltpu.SemaphoreType.DMA((count,)),
+            pltpu.VMEM((2 * size // chunk, chunk, width), jnp.float32),
+            pltpu.SemaphoreType.DMA((2 * size // chunk,)),
         ],
-        flops=18 * rows * count * DEPTH * width,
-        moved=4 * count * DEPTH * width,
-    )(values, found, *(panel for panel, _, _ in parts))
+        flops=36 * rows * found.shape[1] * width,
+        moved=4 * found.shape[1] * width,
+    )(solved, found, panel, panel_other)
 
 
 def cut(found, part):
@@ -332,13 +333,7 @@
     ).reshape(rows, -1)
     part = rhs_window.shape[2]
     owned = lax.ppermute(cut(gathered, part), ("row", "col"), work_to_window())
-    size = panel.shape[0]
-    parts = [
-        (block, first, start + first)
-        for block, start in ((panel, 0), (panel_other, size))
-        for first in range(0, size, DEPTH)
-    ]
-    return owned, correct(solved, gathered, parts)
+    return owned, correct(solved, gathered, panel, panel_other)
 
 
 def solution(mesh):

time: 108 us -> 106 us (0.981)
  local copies, waits for them, and re-layouts: 7.29 us -> 3.3 us
  Pallas kernels: 6.42 us -> 7.66 us
    unnamed x13 -> x11, local copies, waits for them, and re-layouts: 6.07 us -> 2.35 us
  transfers between devices with their start and end apart: 10 -> 10, of which waited for: 4 -> 4; matrix products, arithmetic and copies ran while one was open for 0% -> 2% of each run, Pallas kernels for 3% -> 4%
where the time goes in v12:
time: 106 us; the launch traced here: 105 us
  starting transfers between devices  41.2 us (39%)
  blocking collectives  36.1 us (34%)
  waiting for transfers between devices  14.8 us (14%)
  Pallas kernels  7.66 us (7%)
  local copies, waits for them, and re-layouts  3.3 us (3%)
    all_to_all x1, blocking collectives, shards(): residual = jnp.sum(lax.all_to_all(partial, 'col', 0, 0, tiled=True), axis=0)  20.1 us
    all_to_all x1, blocking collectives, shards(): lax.all_to_all(jnp.broadcast_to(found, (COLS,) + found.shape), 'col', 0,...  16 us
    ppermute x1, starting transfers between devices, shards(): two_own = lax.ppermute(own, 'row', apart(2))  10.7 us
    ppermute x1, waiting for transfers between devices, shards(): four = lax.ppermute(two_other, 'row', apart(2))  7.26 us
    ppermute x1, starting transfers between devices, shards(): owned = lax.ppermute(cut(gathered, part), ('row', 'col'), work_to_window())  5.5 us
    ppermute x1, waiting for transfers between devices, shards(): owned = lax.ppermute(cut(gathered, part), ('row', 'col'), work_to_window())  5.37 us
    ppermute x1, starting transfers between devices, shards(): panel_other = lax.ppermute(panel, 'row', core_swap())  4.78 us
    ppermute x1, starting transfers between devices, shards(): four = lax.ppermute(two_other, 'row', apart(2))  4.12 us
  transfers between devices with their start and end apart: 10, of which 4 were waited for; matrix products, arithmetic and copies ran while one was open for 2% of the time, Pallas kernels for 4%

profile of v12, /device:TPU:13, one launch (start us, length us, event | category | flops | bytes accessed | tf_op | source)
XLA Modules:
  0.0 105.0 jit_solution(1159185188713161202)
XLA Ops:
  0.6 0.0 copy-start.2
  0.7 1.0 copy-done.3
  1.6 0.8 copy-done.4
  2.4 0.2 shard_map.68.one_ref
  2.5 2.6 %collective-permute-start.1 = (f32[200,256]{1,0:T(8,128)S(1)}, f32[200,256]{1,0:T(8,128)S(1)}, u32[]{:S(2)}, u32[]{:S(2)}) collective-permute-start(f32[200,256]{1,0:T(8,128)S(1)} %shard_map.68.one_ref), channel_id=1, source_target_pairs={{0,32},{32,0},{64,96},{96,64},{128,160},{160,128},{192,224},{224,1... | collective-permute-start | bytes 614408 | tf_op jit(solution)/shard_map/ppermute | solution.py:314
  5.1 10.7 %collective-permute-start.3 = (f32[200,256]{1,0:T(8,128)S(1)}, f32[200,256]{1,0:T(8,128)S(1)}, u32[]{:S(2)}, u32[]{:S(2)}) collective-permute-start(f32[200,256]{1,0:T(8,128)S(1)} %shard_map.68.one_ref), channel_id=1, source_target_pairs={{0,128},{32,416},{64,192},{96,480},{128,256},{160,32},{192,320},{2... | collective-permute-start | bytes 614408 | tf_op jit(solution)/shard_map/ppermute | solution.py:315
  15.8 2.2 %collective-permute-start.4 = (f32[200,256]{1,0:T(8,128)S(1)}, f32[200,256]{1,0:T(8,128)S(1)}, u32[]{:S(2)}, u32[]{:S(2)}) collective-permute-start(f32[200,256]{1,0:T(8,128)S(1)} %collective-permute-done.1.two_ref), channel_id=1, source_target_pairs={{0,128},{32,416},{64,192},{96,480},{128,256},{160,32},{192,320},{2... | collective-permute-start | bytes 614408 | tf_op jit(solution)/shard_map/ppermute | solution.py:316
  18.0 2.5 %collective-permute-start = (f32[64,768]{1,0:T(8,128)}, f32[64,768]{1,0:T(8,128)S(1)}, u32[]{:S(2)}, u32[]{:S(2)}) collective-permute-start(f32[64,768]{1,0:T(8,128)} %solved_ref.3), channel_id=1, source_target_pairs={{0,32},{32,0},{64,96},{96,64},{128,160},{160,128},{192,224},{224,1... | collective-permute-start | bytes 589832 | tf_op jit(solution)/shard_map/ppermute | solution.py:319
  20.5 0.5 shard_map.69.refs_0_
  21.0 1.9 %collective-permute-start.2 = (f32[400,256]{1,0:T(8,128)S(1)}, f32[400,256]{1,0:T(8,128)S(1)}, u32[]{:S(2)}, u32[]{:S(2)}) collective-permute-start(f32[400,256]{1,0:T(8,128)S(1)} %shard_map.69.refs_0_), channel_id=1, source_target_pairs={{0,64},{32,480},{64,128},{96,32},{128,192},{160,96},{192,256},{224... | collective-permute-start | bytes 1228808 | tf_op jit(solution)/shard_map/ppermute | solution.py:318
  23.0 2.1 %collective-permute-done.4.two_ref = f32[200,256]{1,0:T(8,128)S(1)} collective-permute-done((f32[200,256]{1,0:T(8,128)S(1)}, f32[200,256]{1,0:T(8,128)S(1)}, u32[]{:S(2)}, u32[]{:S(2)}) %collective-permute-start.4) | collective-permute-done | bytes 204832 | tf_op jit(solution)/shard_map/ppermute | solution.py:316
  25.0 0.5 shard_map.70.refs_2_
  25.6 0.0 copy-start
  25.6 3.9 %collective-permute-start.5 = (f32[400,256]{1,0:T(8,128)S(1)}, f32[400,256]{1,0:T(8,128)S(1)}, u32[]{:S(2)}, u32[]{:S(2)}) collective-permute-start(f32[400,256]{1,0:T(8,128)S(1)} %shard_map.70.refs_2_), channel_id=1, source_target_pairs={{0,64},{32,480},{64,128},{96,32},{128,192},{160,96},{192,256},{224... | collective-permute-start | bytes 1228808 | tf_op jit(solution)/shard_map/ppermute | solution.py:322
  29.5 4.1 %collective-permute-start.6 = (f32[200,256]{1,0:T(8,128)S(1)}, f32[200,256]{1,0:T(8,128)S(1)}, u32[]{:S(2)}, u32[]{:S(2)}) collective-permute-start(f32[200,256]{1,0:T(8,128)S(1)} %collective-permute-done.4.two_ref), channel_id=1, source_target_pairs={{0,128},{32,416},{64,192},{96,480},{128,256},{160,32},{192,320},{2... | collective-permute-start | bytes 614408 | tf_op jit(solution)/shard_map/ppermute | solution.py:320
  33.6 7.3 %collective-permute-done.6.refs_4_ = f32[200,256]{1,0:T(8,128)S(1)} collective-permute-done((f32[200,256]{1,0:T(8,128)S(1)}, f32[200,256]{1,0:T(8,128)S(1)}, u32[]{:S(2)}, u32[]{:S(2)}) %collective-permute-start.6) | collective-permute-done | bytes 204832 | tf_op jit(solution)/shard_map/ppermute | solution.py:320
  40.9 1.6 %shard_map.71 = (f32[32,4,512]{2,1,0:T(4,128)S(1)}, f32[512,768]{1,0:T(8,128)}) custom-call(f32[64,768]{1,0:T(8,128)S(1)} %copy-done.2, f32[64,768]{1,0:T(8,128)S(1)} %collective-permute-done.refs_0_.other_ref, f32[400,256]{1,0:T(8,128)S(1)} %shard_map.69.refs_0_, f32[400,256]{1,0:T(8,128)S(1)} %collective-permute-done.2.refs_1_, ...), custom_call_target="tpu_custom_call" | custom-call | flops 301989888 | bytes 3145728 | tf_op jit(solution)/shard_map/pallas_call | solution.py:179
  42.5 4.8 %collective-permute-start.8 = (f32[512,768]{1,0:T(8,128)}, f32[512,768]{1,0:T(8,128)}, u32[]{:S(2)}, u32[]{:S(2)}) collective-permute-start(f32[512,768]{1,0:T(8,128)} %get-tuple-element.5.panel_ref), channel_id=1, source_target_pairs={{0,32},{32,0},{64,96},{96,64},{128,160},{160,128},{192,224},{224,1... | collective-permute-start | bytes 4718600 | tf_op jit(solution)/shard_map/ppermute | solution.py:325
  47.3 20.1 %all_to_all.10 = f32[32,4,512]{2,1,0:T(4,128)} all-to-all(f32[32,4,512]{2,1,0:T(4,128)S(1)} %get-tuple-element.4), channel_id=1, replica_groups=mesh['row'=16,'col'=32] {'col'}, dimensions={0} | all-to-all | bytes 524288 | tf_op jit(solution)/shard_map/all_to_all | solution.py:328
  67.4 1.0 reduce_sum.9
  68.4 3.1 %collective-permute-start.7 = (f32[2,512]{1,0:T(2,128)S(1)}, f32[2,512]{1,0:T(2,128)S(1)}, u32[]{:S(2)}, u32[]{:S(2)}) collective-permute-start(f32[2,512]{1,0:T(2,128)S(1)} %get-tuple-element.6), channel_id=1, source_target_pairs={{0,32},{32,0},{64,96},{96,64},{128,160},{160,128},{192,224},{224,1... | collective-permute-start | bytes 12296 | tf_op jit(solution)/shard_map/ppermute | solution.py:329
  71.6 0.7 slice.14._
  72.2 0.1 collective-permute-done.7.other_ref
  72.4 1.9 %shard_map.72 = f32[2,1024]{1,0:T(2,128)S(1)} custom-call(f32[2,512]{1,0:T(2,128)S(1)} %get-tuple-element.7.residual_ref, f32[2,512]{1,0:T(2,128)S(1)} %collective-permute-done.7.other_ref, f32[2,512,512]{2,1,0:T(8,128)S(1)} %copy-done, f32[512,512]{1,0:T(8,128)S(1)} %copy-done.1, f32[8,128]{1,0:T(8,128)S(1)} %slice.14._), custom_call_target="tpu_custom_call" | custom-call | flops 150994944 | bytes 3145728 | tf_op jit(solution)/shard_map/pallas_call | solution.py:235
  74.2 0.1 broadcast_in_dim.3
  74.3 16.0 %all_to_all.11 = f32[32,2,1024]{2,1,0:T(2,128)S(1)} all-to-all(f32[32,2,1024]{2,1,0:T(2,128)S(1)} %broadcast_in_dim.3), channel_id=1, replica_groups=mesh['row'=16,'col'=32] {'col'}, dimensions={0} | all-to-all | bytes 524288 | tf_op jit(solution)/shard_map/all_to_all | solution.py:331
  90.3 0.2 reshape.7.found_ref
  90.5 0.1 shard_map.73
  90.6 5.5 %collective-permute-start.9 = (f32[32,2,32]{2,1,0:T(2,128)S(1)}, f32[32,2,32]{2,1,0:T(2,128)S(1)}, u32[]{:S(2)}, u32[]{:S(2)}) collective-permute-start(f32[32,2,32]{2,1,0:T(2,128)S(1)} %shard_map.73), channel_id=1, source_target_pairs={{0,0},{1,1},{2,32},{3,33},{4,64},{5,65},{6,96},{7,97},{8,128},{9,1... | collective-permute-start | bytes 24584 | tf_op jit(solution)/shard_map/ppermute | solution.py:335
  96.1 2.8 %shard_map.74 = f32[64,768]{1,0:T(8,128)} custom-call(f32[64,768]{1,0:T(8,128)S(1)} %copy-done.2, f32[64,1024]{1,0:T(8,128)S(1)} %reshape.7.found_ref, f32[512,768]{1,0:T(8,128)} %get-tuple-element.5.panel_ref, f32[512,768]{1,0:T(8,128)} %collective-permute-done.8.other_ref), custom_call_target="tpu_custom_call" | custom-call | flops 1811939328 | bytes 3145728 | tf_op jit(solution)/shard_map/pallas_call | solution.py:272
  99.0 5.4 %collective-permute-done.9 = f32[32,2,32]{2,1,0:T(2,128)S(1)} collective-permute-done((f32[32,2,32]{2,1,0:T(2,128)S(1)}, f32[32,2,32]{2,1,0:T(2,128)S(1)}, u32[]{:S(2)}, u32[]{:S(2)}) %collective-permute-start.9) | collective-permute-done | bytes 8224 | tf_op jit(solution)/shard_map/ppermute | solution.py:335
  104.4 0.6 copy.8
  (13 shorter events, 0.0 us)
Async XLA Ops:
  0.6 40.3 %copy-start.2 = (f32[64,768]{1,0:T(8,128)S(1)}, f32[64,768]{1,0:T(8,128)}, u32[]{:S(2)}) copy-start(f32[64,768]{1,0:T(8,128)} %solved_ref.3) | copy-start | bytes 589828
  0.6 1.0 copy-start.3
  1.6 0.8 copy-start.4
  2.5 13.2 %collective-permute-start.1 = (f32[200,256]{1,0:T(8,128)S(1)}, f32[200,256]{1,0:T(8,128)S(1)}, u32[]{:S(2)}, u32[]{:S(2)}) collective-permute-start(f32[200,256]{1,0:T(8,128)S(1)} %shard_map.68.one_ref), channel_id=1, source_target_pairs={{0,32},{32,0},{64,96},{96,64},{128,160},{160,128},{192,224},{224,1... | collective-permute-start | bytes 614408 | tf_op jit(solution)/shard_map/ppermute | solution.py:314
  5.1 17.8 %collective-permute-start.3 = (f32[200,256]{1,0:T(8,128)S(1)}, f32[200,256]{1,0:T(8,128)S(1)}, u32[]{:S(2)}, u32[]{:S(2)}) collective-permute-start(f32[200,256]{1,0:T(8,128)S(1)} %shard_map.68.one_ref), channel_id=1, source_target_pairs={{0,128},{32,416},{64,192},{96,480},{128,256},{160,32},{192,320},{2... | collective-permute-start | bytes 614408 | tf_op jit(solution)/shard_map/ppermute | solution.py:315
  15.8 9.3 %collective-permute-start.4 = (f32[200,256]{1,0:T(8,128)S(1)}, f32[200,256]{1,0:T(8,128)S(1)}, u32[]{:S(2)}, u32[]{:S(2)}) collective-permute-start(f32[200,256]{1,0:T(8,128)S(1)} %collective-permute-done.1.two_ref), channel_id=1, source_target_pairs={{0,128},{32,416},{64,192},{96,480},{128,256},{160,32},{192,320},{2... | collective-permute-start | bytes 614408 | tf_op jit(solution)/shard_map/ppermute | solution.py:316
  18.0 5.0 %collective-permute-start = (f32[64,768]{1,0:T(8,128)}, f32[64,768]{1,0:T(8,128)S(1)}, u32[]{:S(2)}, u32[]{:S(2)}) collective-permute-start(f32[64,768]{1,0:T(8,128)} %solved_ref.3), channel_id=1, source_target_pairs={{0,32},{32,0},{64,96},{96,64},{128,160},{160,128},{192,224},{224,1... | collective-permute-start | bytes 589832 | tf_op jit(solution)/shard_map/ppermute | solution.py:319
  21.0 19.9 %collective-permute-start.2 = (f32[400,256]{1,0:T(8,128)S(1)}, f32[400,256]{1,0:T(8,128)S(1)}, u32[]{:S(2)}, u32[]{:S(2)}) collective-permute-start(f32[400,256]{1,0:T(8,128)S(1)} %shard_map.69.refs_0_), channel_id=1, source_target_pairs={{0,64},{32,480},{64,128},{96,32},{128,192},{160,96},{192,256},{224... | collective-permute-start | bytes 1228808 | tf_op jit(solution)/shard_map/ppermute | solution.py:318
  25.0 47.3 %copy-start.1 = (f32[512,512]{1,0:T(8,128)S(1)}, f32[512,512]{1,0:T(8,128)}, u32[]{:S(2)}) copy-start(f32[512,512]{1,0:T(8,128)} %coupling_ref.1) | copy-start | bytes 3145732
  25.6 46.8 %copy-start = (f32[2,512,512]{2,1,0:T(8,128)S(1)}, f32[2,512,512]{2,1,0:T(8,128)}, u32[]{:S(2)}) copy-start(f32[2,512,512]{2,1,0:T(8,128)} %inverses_ref.1) | copy-start | bytes 6291460
  25.6 15.3 %collective-permute-start.5 = (f32[400,256]{1,0:T(8,128)S(1)}, f32[400,256]{1,0:T(8,128)S(1)}, u32[]{:S(2)}, u32[]{:S(2)}) collective-permute-start(f32[400,256]{1,0:T(8,128)S(1)} %shard_map.70.refs_2_), channel_id=1, source_target_pairs={{0,64},{32,480},{64,128},{96,32},{128,192},{160,96},{192,256},{224... | collective-permute-start | bytes 1228808 | tf_op jit(solution)/shard_map/ppermute | solution.py:322
  29.5 11.4 %collective-permute-start.6 = (f32[200,256]{1,0:T(8,128)S(1)}, f32[200,256]{1,0:T(8,128)S(1)}, u32[]{:S(2)}, u32[]{:S(2)}) collective-permute-start(f32[200,256]{1,0:T(8,128)S(1)} %collective-permute-done.4.two_ref), channel_id=1, source_target_pairs={{0,128},{32,416},{64,192},{96,480},{128,256},{160,32},{192,320},{2... | collective-permute-start | bytes 614408 | tf_op jit(solution)/shard_map/ppermute | solution.py:320
  42.5 29.0 %collective-permute-start.8 = (f32[512,768]{1,0:T(8,128)}, f32[512,768]{1,0:T(8,128)}, u32[]{:S(2)}, u32[]{:S(2)}) collective-permute-start(f32[512,768]{1,0:T(8,128)} %get-tuple-element.5.panel_ref), channel_id=1, source_target_pairs={{0,32},{32,0},{64,96},{96,64},{128,160},{160,128},{192,224},{224,1... | collective-permute-start | bytes 4718600 | tf_op jit(solution)/shard_map/ppermute | solution.py:325
  68.4 3.9 %collective-permute-start.7 = (f32[2,512]{1,0:T(2,128)S(1)}, f32[2,512]{1,0:T(2,128)S(1)}, u32[]{:S(2)}, u32[]{:S(2)}) collective-permute-start(f32[2,512]{1,0:T(2,128)S(1)} %get-tuple-element.6), channel_id=1, source_target_pairs={{0,32},{32,0},{64,96},{96,64},{128,160},{160,128},{192,224},{224,1... | collective-permute-start | bytes 12296 | tf_op jit(solution)/shard_map/ppermute | solution.py:329
  90.6 13.7 %collective-permute-start.9 = (f32[32,2,32]{2,1,0:T(2,128)S(1)}, f32[32,2,32]{2,1,0:T(2,128)S(1)}, u32[]{:S(2)}, u32[]{:S(2)}) collective-permute-start(f32[32,2,32]{2,1,0:T(2,128)S(1)} %shard_map.73), channel_id=1, source_target_pairs={{0,0},{1,1},{2,32},{3,33},{4,64},{5,65},{6,96},{7,97},{8,128},{9,1... | collective-permute-start | bytes 24584 | tf_op jit(solution)/shard_map/ppermute | solution.py:335

commit v13 on v12

--- a/solution.py
+++ b/solution.py
@@ -12,6 +12,7 @@
 COLS = 32
 TAIL = 8
 LANES = 256
+GROUPS = 3
 MIB = 1024 * 1024
 
 
@@ -131,67 +132,133 @@
     return pl.BlockSpec(memory_space=pl.ANY)
 
 
-def reduce_panel(solved, solved_other, pairs, last):
+def unit_rows(place, part):
+    core = position()[1]
+    first = jnp.where(core == 0, HALF_RING - 1 - place, place) * part
+    return [pl.multiple_of(first + k * HALF_RING * part, part) for k in range(2)]
+
+
+def block_rows(ref, base, part, k):
+    return [ref[base + (2 * g + k) * part : base + (2 * g + k + 1) * part] for g in range(GROUPS)]
+
+
+def block_window(ref, base, part, k, count):
+    base += 2 * part * GROUPS
+    per = part // TAIL
+    return [
+        ref[base : base + TAIL, (k * per + g) * count : (k * per + g + 1) * count]
+        for g in range(per)
+    ]
+
+
+def spread_window(window, rows):
+    (plane, core), col = position(), lax.axis_index("col")
+    count = window.shape[1]
+    spread = jnp.concatenate([window] * (2 * rows // count), axis=1)
+    lane = lax.broadcasted_iota(jnp.int32, spread.shape, 1)
+    mine = 2 * ((col // 2 % CORES) ^ core) + col % 2
+    mine = jnp.where(plane == col // (2 * CORES), mine, -1)
+    return jnp.where(lane // count == mine, spread, 0.0)
+
+
+def reduce_early(solved, solved_other, blocks, part):
     rows, width = solved.shape
-    groups = width // LANES
-    block = last.shape[0]
-    part = (block - TAIL) // (2 * groups)
-    side = HALF_RING * part
-    unknowns = 2 * side
+    unknowns = 2 * HALF_RING * part
+    count = rows // 2
+    arrays = list({id(array): array for array, _, _ in blocks}.values())
+    index = {id(array): i for i, array in enumerate(arrays)}
+    missing = [place for place in range(HALF_RING) if place not in {p for _, _, p in blocks}]
+
+    def body(solved_ref, other_ref, *refs):
+        *array_refs, total_ref, panel, window = refs
+        for array, base, place in blocks:
+            ref = array_refs[index[id(array)]]
+            for k, start in enumerate(unit_rows(place, part)):
+                for g, value in enumerate(block_rows(ref, base, part, k)):
+                    panel[pl.ds(start, part), g * LANES : (g + 1) * LANES] = value
+                for g, value in enumerate(block_window(ref, base, part, k, count)):
+                    window[pl.ds(start + g * TAIL, TAIL)] = value
+        for place in missing:
+            for start in unit_rows(place, part):
+                panel[pl.ds(start, part)] = jnp.zeros((part, width), jnp.float32)
+                window[pl.ds(start, part)] = jnp.zeros((part, count), jnp.float32)
+        solved_pair = jnp.concatenate([solved_ref[...], other_ref[...]], axis=0)
+        total = rounded_dot(halves(panel[...]), halves(solved_pair), ((1,), (1,)))
+        total_ref[...] = spread_window(window[...], rows) - total
+
+    return kernel_call(
+        body,
+        [
+            jax.ShapeDtypeStruct((unknowns, 2 * rows), jnp.float32),
+            jax.ShapeDtypeStruct((unknowns, width), jnp.float32),
+        ],
+        [in_vmem()] * (2 + len(arrays)),
+        [in_vmem()] * 2,
+        scratch=[pltpu.VMEM((unknowns, count), jnp.float32)],
+        mib=32,
+        flops=12 * rows * unknowns * width,
+        moved=8 * unknowns * width,
+    )(solved, solved_other, *arrays)
+
+
+def reduce_late(solved, solved_other, total, panel, array, places, part):
+    rows, width = solved.shape
+    unknowns = total.shape[0]
     each = rows // COLS
     count = rows // 2
-
-    def body(solved_ref, other_ref, *refs):
-        *pair_refs, last_ref, out_ref, panel, window, partial = refs
-        (plane, core), col = position(), lax.axis_index("col")
-
-        def put(place, ref, at):
-            base = at * block
-            first = jnp.where(core == 0, HALF_RING - 1 - place, place) * part
-            for k in range(2):
-                start = pl.multiple_of(first + k * side, part)
-                for g in range(groups):
-                    row = base + (2 * g + k) * part
-                    panel[pl.ds(start, part), g * LANES : (g + 1) * LANES] = ref[row : row + part]
-                for g in range(part // TAIL):
-                    lanes = (k * (part // TAIL) + g) * count
-                    window[pl.ds(start + g * TAIL, TAIL)] = ref[
-                        base + block - TAIL : base + block, lanes : lanes + count
-                    ]
-
-        put(0, pair_refs[0], 0)
-        for step, ref in enumerate(pair_refs[1:], start=1):
-            put(2 * step, ref, 0)
-            put(2 * step - 1, ref, 1)
-        put(HALF_RING - 1, last_ref, 0)
+    block = array.shape[0] // len(places)
+    runs = 2 * len(places)
+
+    def body(solved_ref, other_ref, total_ref, _, ref, out_ref, panel_ref, held, window, sums, sems):
+        starts = [start for place in places for start in unit_rows(place, part)]
+        for i in range(runs):
+            at, k = i // 2 * block, i % 2
+            for g, value in enumerate(block_rows(ref, at, part, k)):
+                held[i * part : (i + 1) * part, g * LANES : (g + 1) * LANES] = value
+            for g, value in enumerate(block_window(ref, at, part, k, count)):
+                window[i * part + g * TAIL : i * part + (g + 1) * TAIL] = value
+        copies = [
+            pltpu.make_async_copy(
+                held.at[i * part : (i + 1) * part], panel_ref.at[pl.ds(start, part)], sems.at[i]
+            )
+            for i, start in enumerate(starts)
+        ]
+        for copy in copies:
+            copy.start()
         solved_pair = jnp.concatenate([solved_ref[...], other_ref[...]], axis=0)
-        total = rounded_dot(halves(panel[...]), halves(solved_pair), ((1,), (1,)))
-        spread = jnp.concatenate([window[...]] * (2 * rows // count), axis=1)
-        lane = lax.broadcasted_iota(jnp.int32, spread.shape, 1)
-        mine = 2 * ((col // 2 % CORES) ^ core) + col % 2
-        mine = jnp.where(plane == col // (2 * CORES), mine, -1)
-        partial[...] = (jnp.where(lane // count == mine, spread, 0.0) - total).T
+        late = rounded_dot(halves(held[...]), halves(solved_pair), ((1,), (1,)))
+        late = spread_window(window[...], rows) - late
+        sums[...] = total_ref[...]
+        for i, start in enumerate(starts):
+            sums[pl.ds(start, part)] = late[i * part : (i + 1) * part]
+        partial = sums[...].T
         for member in range(COLS):
             at = member * each
             out_ref[member, :each] = partial[at : at + each]
             out_ref[member, each:] = partial[rows + at : rows + at + each]
-
-    return kernel_call(
-        body,
-        [
+        for copy in copies:
+            copy.wait()
+
+    return pl.pallas_call(
+        body,
+        out_shape=[
             jax.ShapeDtypeStruct((COLS, 2 * each, unknowns), jnp.float32),
-            jax.ShapeDtypeStruct((unknowns, width), jnp.float32),
+            jax.ShapeDtypeStruct(panel.shape, panel.dtype),
         ],
-        [in_vmem()] * (3 + len(pairs)),
-        [in_vmem()] * 2,
-        scratch=[
-            pltpu.VMEM((unknowns, count), jnp.float32),
-            pltpu.VMEM((2 * rows, unknowns), jnp.float32),
+        in_specs=[in_vmem()] * 3 + [anywhere(), in_vmem()],
+        out_specs=[in_vmem(), anywhere()],
+        scratch_shapes=[
+            pltpu.VMEM((runs * part, width), jnp.float32),
+            pltpu.VMEM((runs * part, count), jnp.float32),
+            pltpu.VMEM((unknowns, 2 * rows), jnp.float32),
+            pltpu.SemaphoreType.DMA((runs,)),
         ],
-        mib=32,
-        flops=12 * rows * unknowns * width,
-        moved=8 * unknowns * width,
-    )(solved, solved_other, *pairs, last)
+        input_output_aliases={3: 1},
+        compiler_params=pltpu.CompilerParams(vmem_limit_bytes=32 * MIB),
+        cost_estimate=pl.CostEstimate(
+            flops=12 * rows * runs * part * width, bytes_accessed=8 * unknowns * width, transcendentals=0
+        ),
+    )(solved, solved_other, total, panel, array)
 
 
 def panel_solve(residual, residual_other, inverses, coupling, arrival):
@@ -320,7 +387,11 @@
     four = lax.ppermute(two_other, "row", apart(2))
     two = join(two_own, two_other, (solved_other,))
     three = lax.ppermute(two, "row", apart(1))
-    partial, panel = reduce_panel(solved, solved_other, [both, one, two, three], four)
+    part, block = factor.shape[1], own.shape[0]
+    early = [(both, 0, 0), (one, 0, 2), (one, block, 1), (two, 0, 4), (two, block, 3)]
+    early += [(three, 0, 6), (three, block, 5)]
+    total, panel = reduce_early(solved, solved_other, early, part)
+    partial, panel = reduce_late(solved, solved_other, total, panel, four, (HALF_RING - 1,), part)
 
     panel_other = lax.ppermute(panel, "row", core_swap())
 

time: 106 us -> 105 us (level)
  waiting for transfers between devices: 14.8 us -> 13.1 us
  Pallas kernels: 7.66 us -> 8.79 us
    ppermute x1, waiting for transfers between devices: 7.26 us -> 3.82 us  [shards(): four = lax.ppermute(two_other, 'row', apart(2))]
    ppermute x1, waiting for transfers between devices: 0.01 us -> 1.69 us  [shards(): three = lax.ppermute(two, 'row', apart(1))]
    pallas_call x1 -> x2, Pallas kernels: 1.59 us -> 2.72 us  [the longest x1 1.73 us: reduce_early(): kernel_call(body, [jax.ShapeDtypeStruct((unknowns, 2 * rows), jnp.float32...]
  transfers between devices with their start and end apart: 10 -> 10, of which waited for: 4 -> 5; matrix products, arithmetic and copies ran while one was open for 2% -> 2% of each run, Pallas kernels for 4% -> 5%
where the time goes in v13:
time: 105 us; the launch traced here: 104 us
  starting transfers between devices  41.2 us (39%)
  blocking collectives  36.1 us (34%)
  waiting for transfers between devices  13.1 us (12%)
  Pallas kernels  8.79 us (8%)
  local copies, waits for them, and re-layouts  3.29 us (3%)
    all_to_all x1, blocking collectives, shards(): residual = jnp.sum(lax.all_to_all(partial, 'col', 0, 0, tiled=True), axis=0)  20.1 us
    all_to_all x1, blocking collectives, shards(): lax.all_to_all(jnp.broadcast_to(found, (COLS,) + found.shape), 'col', 0,...  16 us
    ppermute x1, starting transfers between devices, shards(): two_own = lax.ppermute(own, 'row', apart(2))  10.7 us
    ppermute x1, starting transfers between devices, shards(): owned = lax.ppermute(cut(gathered, part), ('row', 'col'), work_to_window())  5.5 us
    ppermute x1, waiting for transfers between devices, shards(): owned = lax.ppermute(cut(gathered, part), ('row', 'col'), work_to_window())  5.38 us
    ppermute x1, starting transfers between devices, shards(): panel_other = lax.ppermute(panel, 'row', core_swap())  4.92 us
    ppermute x1, starting transfers between devices, shards(): four = lax.ppermute(two_other, 'row', apart(2))  4.12 us
    ppermute x1, waiting for transfers between devices, shards(): four = lax.ppermute(two_other, 'row', apart(2))  3.82 us
  transfers between devices with their start and end apart: 10, of which 5 were waited for; matrix products, arithmetic and copies ran while one was open for 2% of the time, Pallas kernels for 5%

profile of v13, /device:TPU:13, one launch (start us, length us, event | category | flops | bytes accessed | tf_op | source)
XLA Modules:
  0.0 104.4 jit_solution(17719624265203482066)
XLA Ops:
  0.7 1.0 copy-done.3
  1.6 0.8 copy-done.4
  2.4 0.2 shard_map.68.one_ref
  2.5 2.6 %collective-permute-start.1 = (f32[200,256]{1,0:T(8,128)S(1)}, f32[200,256]{1,0:T(8,128)S(1)}, u32[]{:S(2)}, u32[]{:S(2)}) collective-permute-start(f32[200,256]{1,0:T(8,128)S(1)} %shard_map.68.one_ref), channel_id=1, source_target_pairs={{0,32},{32,0},{64,96},{96,64},{128,160},{160,128},{192,224},{224,1... | collective-permute-start | bytes 614408 | tf_op jit(solution)/shard_map/ppermute | solution.py:381
  5.1 10.7 %collective-permute-start.3 = (f32[200,256]{1,0:T(8,128)S(1)}, f32[200,256]{1,0:T(8,128)S(1)}, u32[]{:S(2)}, u32[]{:S(2)}) collective-permute-start(f32[200,256]{1,0:T(8,128)S(1)} %shard_map.68.one_ref), channel_id=1, source_target_pairs={{0,128},{32,416},{64,192},{96,480},{128,256},{160,32},{192,320},{2... | collective-permute-start | bytes 614408 | tf_op jit(solution)/shard_map/ppermute | solution.py:382
  15.8 2.2 %collective-permute-start.4 = (f32[200,256]{1,0:T(8,128)S(1)}, f32[200,256]{1,0:T(8,128)S(1)}, u32[]{:S(2)}, u32[]{:S(2)}) collective-permute-start(f32[200,256]{1,0:T(8,128)S(1)} %collective-permute-done.1.two_ref), channel_id=1, source_target_pairs={{0,128},{32,416},{64,192},{96,480},{128,256},{160,32},{192,320},{2... | collective-permute-start | bytes 614408 | tf_op jit(solution)/shard_map/ppermute | solution.py:383
  18.0 2.5 %collective-permute-start = (f32[64,768]{1,0:T(8,128)}, f32[64,768]{1,0:T(8,128)S(1)}, u32[]{:S(2)}, u32[]{:S(2)}) collective-permute-start(f32[64,768]{1,0:T(8,128)} %solved_ref.5), channel_id=1, source_target_pairs={{0,32},{32,0},{64,96},{96,64},{128,160},{160,128},{192,224},{224,1... | collective-permute-start | bytes 589832 | tf_op jit(solution)/shard_map/ppermute | solution.py:386
  20.5 0.5 shard_map.69.refs_0_
  21.0 1.9 %collective-permute-start.2 = (f32[400,256]{1,0:T(8,128)S(1)}, f32[400,256]{1,0:T(8,128)S(1)}, u32[]{:S(2)}, u32[]{:S(2)}) collective-permute-start(f32[400,256]{1,0:T(8,128)S(1)} %shard_map.69.refs_0_), channel_id=1, source_target_pairs={{0,64},{32,480},{64,128},{96,32},{128,192},{160,96},{192,256},{224... | collective-permute-start | bytes 1228808 | tf_op jit(solution)/shard_map/ppermute | solution.py:385
  23.0 2.1 %collective-permute-done.4.two_ref = f32[200,256]{1,0:T(8,128)S(1)} collective-permute-done((f32[200,256]{1,0:T(8,128)S(1)}, f32[200,256]{1,0:T(8,128)S(1)}, u32[]{:S(2)}, u32[]{:S(2)}) %collective-permute-start.4) | collective-permute-done | bytes 204832 | tf_op jit(solution)/shard_map/ppermute | solution.py:383
  25.0 0.5 shard_map.70.refs_2_
  25.6 3.8 %collective-permute-start.5 = (f32[400,256]{1,0:T(8,128)S(1)}, f32[400,256]{1,0:T(8,128)S(1)}, u32[]{:S(2)}, u32[]{:S(2)}) collective-permute-start(f32[400,256]{1,0:T(8,128)S(1)} %shard_map.70.refs_2_), channel_id=1, source_target_pairs={{0,64},{32,480},{64,128},{96,32},{128,192},{160,96},{192,256},{224... | collective-permute-start | bytes 1228808 | tf_op jit(solution)/shard_map/ppermute | solution.py:389
  29.4 4.1 %collective-permute-start.6 = (f32[200,256]{1,0:T(8,128)S(1)}, f32[200,256]{1,0:T(8,128)S(1)}, u32[]{:S(2)}, u32[]{:S(2)}) collective-permute-start(f32[200,256]{1,0:T(8,128)S(1)} %collective-permute-done.4.two_ref), channel_id=1, source_target_pairs={{0,128},{32,416},{64,192},{96,480},{128,256},{160,32},{192,320},{2... | collective-permute-start | bytes 614408 | tf_op jit(solution)/shard_map/ppermute | solution.py:387
  33.5 1.7 %collective-permute-done.5.refs_3_ = f32[400,256]{1,0:T(8,128)S(1)} collective-permute-done((f32[400,256]{1,0:T(8,128)S(1)}, f32[400,256]{1,0:T(8,128)S(1)}, u32[]{:S(2)}, u32[]{:S(2)}) %collective-permute-start.5) | collective-permute-done | bytes 409632 | tf_op jit(solution)/shard_map/ppermute | solution.py:389
  35.2 1.7 %shard_map.71 = (f32[512,128]{1,0:T(8,128)S(1)}, f32[512,768]{1,0:T(8,128)}) custom-call(f32[64,768]{1,0:T(8,128)S(1)} %copy-done.2, f32[64,768]{1,0:T(8,128)S(1)} %collective-permute-done.refs_0_.other_ref, f32[400,256]{1,0:T(8,128)S(1)} %shard_map.69.refs_0_, f32[400,256]{1,0:T(8,128)S(1)} %collective-permute-done.2.refs_1_, ...), custom_call_target="tpu_custom_call" | custom-call | flops 301989888 | bytes 3145728 | tf_op jit(solution)/shard_map/pallas_call | solution.py:189
  36.9 3.8 %collective-permute-done.6.ref = f32[200,256]{1,0:T(8,128)S(1)} collective-permute-done((f32[200,256]{1,0:T(8,128)S(1)}, f32[200,256]{1,0:T(8,128)S(1)}, u32[]{:S(2)}, u32[]{:S(2)}) %collective-permute-start.6) | collective-permute-done | bytes 204832 | tf_op jit(solution)/shard_map/ppermute | solution.py:387
  40.7 1.0 shard_map.72
  41.7 4.9 %collective-permute-start.8 = (f32[512,768]{1,0:T(8,128)}, f32[512,768]{1,0:T(8,128)}, u32[]{:S(2)}, u32[]{:S(2)}) collective-permute-start(f32[512,768]{1,0:T(8,128)} %get-tuple-element.9.panel_ref), channel_id=1, source_target_pairs={{0,32},{32,0},{64,96},{96,64},{128,160},{160,128},{192,224},{224,1... | collective-permute-start | bytes 4718600 | tf_op jit(solution)/shard_map/ppermute | solution.py:396
  46.7 20.1 %all_to_all.10 = f32[32,4,512]{2,1,0:T(4,128)} all-to-all(f32[32,4,512]{2,1,0:T(4,128)S(1)} %get-tuple-element.8), channel_id=1, replica_groups=mesh['row'=16,'col'=32] {'col'}, dimensions={0} | all-to-all | bytes 524288 | tf_op jit(solution)/shard_map/all_to_all | solution.py:399
  66.8 1.0 reduce_sum.9
  67.8 3.1 %collective-permute-start.7 = (f32[2,512]{1,0:T(2,128)S(1)}, f32[2,512]{1,0:T(2,128)S(1)}, u32[]{:S(2)}, u32[]{:S(2)}) collective-permute-start(f32[2,512]{1,0:T(2,128)S(1)} %get-tuple-element.10), channel_id=1, source_target_pairs={{0,32},{32,0},{64,96},{96,64},{128,160},{160,128},{192,224},{224,1... | collective-permute-start | bytes 12296 | tf_op jit(solution)/shard_map/ppermute | solution.py:400
  70.9 0.7 slice.14._
  71.6 0.1 collective-permute-done.7.other_ref
  71.7 1.9 %shard_map.73 = f32[2,1024]{1,0:T(2,128)S(1)} custom-call(f32[2,512]{1,0:T(2,128)S(1)} %get-tuple-element.11.residual_ref, f32[2,512]{1,0:T(2,128)S(1)} %collective-permute-done.7.other_ref, f32[2,512,512]{2,1,0:T(8,128)S(1)} %copy-done, f32[512,512]{1,0:T(8,128)S(1)} %copy-done.1, f32[8,128]{1,0:T(8,128)S(1)} %slice.14._), custom_call_target="tpu_custom_call" | custom-call | flops 150994944 | bytes 3145728 | tf_op jit(solution)/shard_map/pallas_call | solution.py:302
  73.6 0.1 broadcast_in_dim.3
  73.7 16.0 %all_to_all.11 = f32[32,2,1024]{2,1,0:T(2,128)S(1)} all-to-all(f32[32,2,1024]{2,1,0:T(2,128)S(1)} %broadcast_in_dim.3), channel_id=1, replica_groups=mesh['row'=16,'col'=32] {'col'}, dimensions={0} | all-to-all | bytes 524288 | tf_op jit(solution)/shard_map/all_to_all | solution.py:402
  89.7 0.2 reshape.7.found_ref
  89.9 0.1 shard_map.74
  90.0 5.5 %collective-permute-start.9 = (f32[32,2,32]{2,1,0:T(2,128)S(1)}, f32[32,2,32]{2,1,0:T(2,128)S(1)}, u32[]{:S(2)}, u32[]{:S(2)}) collective-permute-start(f32[32,2,32]{2,1,0:T(2,128)S(1)} %shard_map.74), channel_id=1, source_target_pairs={{0,0},{1,1},{2,32},{3,33},{4,64},{5,65},{6,96},{7,97},{8,128},{9,1... | collective-permute-start | bytes 24584 | tf_op jit(solution)/shard_map/ppermute | solution.py:406
  95.5 2.8 %shard_map.75 = f32[64,768]{1,0:T(8,128)} custom-call(f32[64,768]{1,0:T(8,128)S(1)} %copy-done.2, f32[64,1024]{1,0:T(8,128)S(1)} %reshape.7.found_ref, f32[512,768]{1,0:T(8,128)} %get-tuple-element.9.panel_ref, f32[512,768]{1,0:T(8,128)} %collective-permute-done.8.other_ref), custom_call_target="tpu_custom_call" | custom-call | flops 1811939328 | bytes 3145728 | tf_op jit(solution)/shard_map/pallas_call | solution.py:339
  98.4 5.4 %collective-permute-done.9 = f32[32,2,32]{2,1,0:T(2,128)S(1)} collective-permute-done((f32[32,2,32]{2,1,0:T(2,128)S(1)}, f32[32,2,32]{2,1,0:T(2,128)S(1)}, u32[]{:S(2)}, u32[]{:S(2)}) %collective-permute-start.9) | collective-permute-done | bytes 8224 | tf_op jit(solution)/shard_map/ppermute | solution.py:406
  103.8 0.6 copy.10
  (14 shorter events, 0.0 us)
Async XLA Ops:
  0.6 34.6 %copy-start.2 = (f32[64,768]{1,0:T(8,128)S(1)}, f32[64,768]{1,0:T(8,128)}, u32[]{:S(2)}) copy-start(f32[64,768]{1,0:T(8,128)} %solved_ref.5) | copy-start | bytes 589828
  0.6 1.0 copy-start.3
  1.6 0.8 copy-start.4
  2.5 13.2 %collective-permute-start.1 = (f32[200,256]{1,0:T(8,128)S(1)}, f32[200,256]{1,0:T(8,128)S(1)}, u32[]{:S(2)}, u32[]{:S(2)}) collective-permute-start(f32[200,256]{1,0:T(8,128)S(1)} %shard_map.68.one_ref), channel_id=1, source_target_pairs={{0,32},{32,0},{64,96},{96,64},{128,160},{160,128},{192,224},{224,1... | collective-permute-start | bytes 614408 | tf_op jit(solution)/shard_map/ppermute | solution.py:381
  5.1 17.8 %collective-permute-start.3 = (f32[200,256]{1,0:T(8,128)S(1)}, f32[200,256]{1,0:T(8,128)S(1)}, u32[]{:S(2)}, u32[]{:S(2)}) collective-permute-start(f32[200,256]{1,0:T(8,128)S(1)} %shard_map.68.one_ref), channel_id=1, source_target_pairs={{0,128},{32,416},{64,192},{96,480},{128,256},{160,32},{192,320},{2... | collective-permute-start | bytes 614408 | tf_op jit(solution)/shard_map/ppermute | solution.py:382
  15.8 9.3 %collective-permute-start.4 = (f32[200,256]{1,0:T(8,128)S(1)}, f32[200,256]{1,0:T(8,128)S(1)}, u32[]{:S(2)}, u32[]{:S(2)}) collective-permute-start(f32[200,256]{1,0:T(8,128)S(1)} %collective-permute-done.1.two_ref), channel_id=1, source_target_pairs={{0,128},{32,416},{64,192},{96,480},{128,256},{160,32},{192,320},{2... | collective-permute-start | bytes 614408 | tf_op jit(solution)/shard_map/ppermute | solution.py:383
  18.0 5.0 %collective-permute-start = (f32[64,768]{1,0:T(8,128)}, f32[64,768]{1,0:T(8,128)S(1)}, u32[]{:S(2)}, u32[]{:S(2)}) collective-permute-start(f32[64,768]{1,0:T(8,128)} %solved_ref.5), channel_id=1, source_target_pairs={{0,32},{32,0},{64,96},{96,64},{128,160},{160,128},{192,224},{224,1... | collective-permute-start | bytes 589832 | tf_op jit(solution)/shard_map/ppermute | solution.py:386
  21.0 12.5 %collective-permute-start.2 = (f32[400,256]{1,0:T(8,128)S(1)}, f32[400,256]{1,0:T(8,128)S(1)}, u32[]{:S(2)}, u32[]{:S(2)}) collective-permute-start(f32[400,256]{1,0:T(8,128)S(1)} %shard_map.69.refs_0_), channel_id=1, source_target_pairs={{0,64},{32,480},{64,128},{96,32},{128,192},{160,96},{192,256},{224... | collective-permute-start | bytes 1228808 | tf_op jit(solution)/shard_map/ppermute | solution.py:385
  25.6 9.6 %collective-permute-start.5 = (f32[400,256]{1,0:T(8,128)S(1)}, f32[400,256]{1,0:T(8,128)S(1)}, u32[]{:S(2)}, u32[]{:S(2)}) collective-permute-start(f32[400,256]{1,0:T(8,128)S(1)} %shard_map.70.refs_2_), channel_id=1, source_target_pairs={{0,64},{32,480},{64,128},{96,32},{128,192},{160,96},{192,256},{224... | collective-permute-start | bytes 1228808 | tf_op jit(solution)/shard_map/ppermute | solution.py:389
  29.4 11.4 %collective-permute-start.6 = (f32[200,256]{1,0:T(8,128)S(1)}, f32[200,256]{1,0:T(8,128)S(1)}, u32[]{:S(2)}, u32[]{:S(2)}) collective-permute-start(f32[200,256]{1,0:T(8,128)S(1)} %collective-permute-done.4.two_ref), channel_id=1, source_target_pairs={{0,128},{32,416},{64,192},{96,480},{128,256},{160,32},{192,320},{2... | collective-permute-start | bytes 614408 | tf_op jit(solution)/shard_map/ppermute | solution.py:387
  40.7 31.0 %copy-start = (f32[2,512,512]{2,1,0:T(8,128)S(1)}, f32[2,512,512]{2,1,0:T(8,128)}, u32[]{:S(2)}) copy-start(f32[2,512,512]{2,1,0:T(8,128)} %inverses_ref.1) | copy-start | bytes 6291460
  40.7 31.0 %copy-start.1 = (f32[512,512]{1,0:T(8,128)S(1)}, f32[512,512]{1,0:T(8,128)}, u32[]{:S(2)}) copy-start(f32[512,512]{1,0:T(8,128)} %coupling_ref.1) | copy-start | bytes 3145732
  41.7 29.2 %collective-permute-start.8 = (f32[512,768]{1,0:T(8,128)}, f32[512,768]{1,0:T(8,128)}, u32[]{:S(2)}, u32[]{:S(2)}) collective-permute-start(f32[512,768]{1,0:T(8,128)} %get-tuple-element.9.panel_ref), channel_id=1, source_target_pairs={{0,32},{32,0},{64,96},{96,64},{128,160},{160,128},{192,224},{224,1... | collective-permute-start | bytes 4718600 | tf_op jit(solution)/shard_map/ppermute | solution.py:396
  67.8 3.9 %collective-permute-start.7 = (f32[2,512]{1,0:T(2,128)S(1)}, f32[2,512]{1,0:T(2,128)S(1)}, u32[]{:S(2)}, u32[]{:S(2)}) collective-permute-start(f32[2,512]{1,0:T(2,128)S(1)} %get-tuple-element.10), channel_id=1, source_target_pairs={{0,32},{32,0},{64,96},{96,64},{128,160},{160,128},{192,224},{224,1... | collective-permute-start | bytes 12296 | tf_op jit(solution)/shard_map/ppermute | solution.py:400
  90.0 13.7 %collective-permute-start.9 = (f32[32,2,32]{2,1,0:T(2,128)S(1)}, f32[32,2,32]{2,1,0:T(2,128)S(1)}, u32[]{:S(2)}, u32[]{:S(2)}) collective-permute-start(f32[32,2,32]{2,1,0:T(2,128)S(1)} %shard_map.74), channel_id=1, source_target_pairs={{0,0},{1,1},{2,32},{3,33},{4,64},{5,65},{6,96},{7,97},{8,128},{9,1... | collective-permute-start | bytes 24584 | tf_op jit(solution)/shard_map/ppermute | solution.py:406

commit v14 on v13

--- a/solution.py
+++ b/solution.py
@@ -105,6 +105,40 @@
     )(factor, rhs_window)
 
 
+def anywhere():
+    return pl.BlockSpec(memory_space=pl.ANY)
+
+
+def in_hbm():
+    return pl.BlockSpec(memory_space=pltpu.MemorySpace.HBM)
+
+
+def with_window(factor, rhs_window):
+    panels, part, width = factor.shape
+    rows = panels * part
+    groups = width // LANES
+
+    def body(factor_ref, window_ref, out_ref):
+        count = window_ref.shape[0]
+        for k in range(panels):
+            turned = window_ref[:, k].T
+            for g in range(part // TAIL):
+                at = (k * (part // TAIL) + g) * count
+                out_ref[groups * rows :, at : at + count] = turned[g * TAIL : (g + 1) * TAIL]
+            for g in range(groups):
+                at = g * rows + k * part
+                out_ref[at : at + part] = factor_ref[k, :, g * LANES : (g + 1) * LANES]
+
+    return kernel_call(
+        body,
+        jax.ShapeDtypeStruct((groups * rows + TAIL, LANES), factor.dtype),
+        [in_vmem()] * 2,
+        in_vmem(),
+        mib=16,
+        moved=8 * factor.size,
+    )(factor, rhs_window)
+
+
 def join(one, two, arrivals=()):
     def body(one_ref, two_ref, *refs):
         out_ref, sems = refs[-2:]
@@ -130,6 +164,20 @@
 
 def anywhere():
     return pl.BlockSpec(memory_space=pl.ANY)
+
+
+def after(block, arrivals):
+    def body(*refs):
+        del refs
+
+    return pl.pallas_call(
+        body,
+        out_shape=jax.ShapeDtypeStruct(block.shape, block.dtype),
+        in_specs=[anywhere()] * (1 + len(arrivals)),
+        out_specs=anywhere(),
+        input_output_aliases={0: 0},
+        compiler_params=pltpu.CompilerParams(vmem_limit_bytes=MIB),
+    )(block, *arrivals)
 
 
 def unit_rows(place, part):
@@ -384,14 +432,15 @@
     both = join(own, other)
     one = lax.ppermute(both, "row", apart(1))
     solved_other = lax.ppermute(solved, "row", core_swap())
+    three_own = lax.ppermute(two_own, "row", apart(1))
+    two_other = after(two_other, (solved_other,))
     four = lax.ppermute(two_other, "row", apart(2))
-    two = join(two_own, two_other, (solved_other,))
-    three = lax.ppermute(two, "row", apart(1))
+    three_other = lax.ppermute(two_other, "row", apart(1))
     part, block = factor.shape[1], own.shape[0]
-    early = [(both, 0, 0), (one, 0, 2), (one, block, 1), (two, 0, 4), (two, block, 3)]
-    early += [(three, 0, 6), (three, block, 5)]
+    early = [(both, 0, 0), (one, 0, 2), (one, block, 1), (two_own, 0, 4), (two_other, 0, 3)]
+    early += [(four, 0, HALF_RING - 1), (three_own, 0, 6)]
     total, panel = reduce_early(solved, solved_other, early, part)
-    partial, panel = reduce_late(solved, solved_other, total, panel, four, (HALF_RING - 1,), part)
+    partial, panel = reduce_late(solved, solved_other, total, panel, three_other, (5,), part)
 
     panel_other = lax.ppermute(panel, "row", core_swap())
 

time: 105 us -> 105 us (level)
  the two profiles are of different devices: /device:TPU:13 before, /device:TPU:68 now
where the time goes in v14:
time: 105 us
  starting transfers between devices  39.8 us (38%)
  blocking collectives  38.5 us (37%)
  waiting for transfers between devices  12.8 us (12%)
  Pallas kernels  8.34 us (8%)
  local copies, waits for them, and re-layouts  3.3 us (3%)
    all_to_all x1, blocking collectives, shards(): residual = jnp.sum(lax.all_to_all(partial, 'col', 0, 0, tiled=True), axis=0)  21.5 us
    all_to_all x1, blocking collectives, shards(): lax.all_to_all(jnp.broadcast_to(found, (COLS,) + found.shape), 'col', 0,...  17 us
    ppermute x1, starting transfers between devices, shards(): owned = lax.ppermute(cut(gathered, part), ('row', 'col'), work_to_window())  6.71 us
    ppermute x1, waiting for transfers between devices, shards(): owned = lax.ppermute(cut(gathered, part), ('row', 'col'), work_to_window())  6.47 us
    ppermute x1, starting transfers between devices, shards(): two_other = lax.ppermute(other, 'row', apart(2))  6.4 us
    ppermute x1, starting transfers between devices, shards(): two_own = lax.ppermute(own, 'row', apart(2))  6.09 us
    ppermute x1, waiting for transfers between devices, shards(): four = lax.ppermute(two_other, 'row', apart(2))  5.89 us
    ppermute x1, starting transfers between devices, shards(): four = lax.ppermute(two_other, 'row', apart(2))  4.23 us
  transfers between devices with their start and end apart: 11, of which 3 were waited for; matrix products, arithmetic and copies ran while one was open for 2% of the time, Pallas kernels for 5%

profile of v14, /device:TPU:68, one launch (start us, length us, event | category | flops | bytes accessed | tf_op | source)
XLA Modules:
  0.0 104.6 jit_solution(13833754296809051269)
XLA Ops:
  0.6 0.0 copy-start.2
  0.7 1.0 copy-done.3
  1.6 0.8 copy-done.4
  2.4 0.2 shard_map.68.one_ref
  2.5 1.9 %collective-permute-start.1 = (f32[200,256]{1,0:T(8,128)S(1)}, f32[200,256]{1,0:T(8,128)S(1)}, u32[]{:S(2)}, u32[]{:S(2)}) collective-permute-start(f32[200,256]{1,0:T(8,128)S(1)} %shard_map.68.one_ref), channel_id=1, source_target_pairs={{0,32},{32,0},{64,96},{96,64},{128,160},{160,128},{192,224},{224,1... | collective-permute-start | bytes 614408 | tf_op jit(solution)/shard_map/ppermute | solution.py:429
  4.4 6.1 %collective-permute-start.3 = (f32[200,256]{1,0:T(8,128)S(1)}, f32[200,256]{1,0:T(8,128)S(1)}, u32[]{:S(2)}, u32[]{:S(2)}) collective-permute-start(f32[200,256]{1,0:T(8,128)S(1)} %shard_map.68.one_ref), channel_id=1, source_target_pairs={{0,128},{32,416},{64,192},{96,480},{128,256},{160,32},{192,320},{2... | collective-permute-start | bytes 614408 | tf_op jit(solution)/shard_map/ppermute | solution.py:430
  10.5 0.0 collective-permute-done.1.two_ref
  10.6 6.4 %collective-permute-start.4 = (f32[200,256]{1,0:T(8,128)S(1)}, f32[200,256]{1,0:T(8,128)S(1)}, u32[]{:S(2)}, u32[]{:S(2)}) collective-permute-start(f32[200,256]{1,0:T(8,128)S(1)} %collective-permute-done.1.two_ref), channel_id=1, source_target_pairs={{0,128},{32,416},{64,192},{96,480},{128,256},{160,32},{192,320},{2... | collective-permute-start | bytes 614408 | tf_op jit(solution)/shard_map/ppermute | solution.py:431
  17.0 0.5 shard_map.69.refs_0_
  17.5 3.4 %collective-permute-start.2 = (f32[400,256]{1,0:T(8,128)S(1)}, f32[400,256]{1,0:T(8,128)S(1)}, u32[]{:S(2)}, u32[]{:S(2)}) collective-permute-start(f32[400,256]{1,0:T(8,128)S(1)} %shard_map.69.refs_0_), channel_id=1, source_target_pairs={{0,64},{32,480},{64,128},{96,32},{128,192},{160,96},{192,256},{224... | collective-permute-start | bytes 1228808 | tf_op jit(solution)/shard_map/ppermute | solution.py:433
  20.9 1.9 %collective-permute-start = (f32[64,768]{1,0:T(8,128)}, f32[64,768]{1,0:T(8,128)S(1)}, u32[]{:S(2)}, u32[]{:S(2)}) collective-permute-start(f32[64,768]{1,0:T(8,128)} %solved_ref.5), channel_id=1, source_target_pairs={{0,32},{32,0},{64,96},{96,64},{128,160},{160,128},{192,224},{224,1... | collective-permute-start | bytes 589832 | tf_op jit(solution)/shard_map/ppermute | solution.py:434
  22.8 3.4 %collective-permute-start.6 = (f32[200,256]{1,0:T(8,128)S(1)}, f32[200,256]{1,0:T(8,128)S(1)}, u32[]{:S(2)}, u32[]{:S(2)}) collective-permute-start(f32[200,256]{1,0:T(8,128)S(1)} %collective-permute-done.3.refs_2_), channel_id=1, source_target_pairs={{0,64},{32,480},{64,128},{96,32},{128,192},{160,96},{192,256},{224... | collective-permute-start | bytes 614408 | tf_op jit(solution)/shard_map/ppermute | solution.py:435
  26.3 4.2 %collective-permute-start.5 = (f32[200,256]{1,0:T(8,128)S(1)}, f32[200,256]{1,0:T(8,128)S(1)}, u32[]{:S(2)}, u32[]{:S(2)}) collective-permute-start(f32[200,256]{1,0:T(8,128)S(1)} %shard_map.70.refs_3_), channel_id=1, source_target_pairs={{0,128},{32,416},{64,192},{96,480},{128,256},{160,32},{192,320},{2... | collective-permute-start | bytes 614408 | tf_op jit(solution)/shard_map/ppermute | solution.py:437
  30.5 1.9 %collective-permute-start.7 = (f32[200,256]{1,0:T(8,128)S(1)}, f32[200,256]{1,0:T(8,128)S(1)}, u32[]{:S(2)}, u32[]{:S(2)}) collective-permute-start(f32[200,256]{1,0:T(8,128)S(1)} %shard_map.70.refs_3_), channel_id=1, source_target_pairs={{0,64},{32,480},{64,128},{96,32},{128,192},{160,96},{192,256},{224... | collective-permute-start | bytes 614408 | tf_op jit(solution)/shard_map/ppermute | solution.py:438
  32.4 5.9 %collective-permute-done.5.refs_4_ = f32[200,256]{1,0:T(8,128)S(1)} collective-permute-done((f32[200,256]{1,0:T(8,128)S(1)}, f32[200,256]{1,0:T(8,128)S(1)}, u32[]{:S(2)}, u32[]{:S(2)}) %collective-permute-start.5) | collective-permute-done | bytes 204832 | tf_op jit(solution)/shard_map/ppermute | solution.py:437
  38.3 1.8 %shard_map.71 = (f32[512,128]{1,0:T(8,128)S(1)}, f32[512,768]{1,0:T(8,128)}) custom-call(f32[64,768]{1,0:T(8,128)S(1)} %copy-done.2, f32[64,768]{1,0:T(8,128)S(1)} %collective-permute-done.refs_1_.other_ref, f32[400,256]{1,0:T(8,128)S(1)} %shard_map.69.refs_0_, f32[400,256]{1,0:T(8,128)S(1)} %collective-permute-done.2.refs_1_, ...), custom_call_target="tpu_custom_call" | custom-call | flops 301989888 | bytes 3145728 | tf_op jit(solution)/shard_map/pallas_call | solution.py:237
  40.1 1.0 shard_map.72
  41.1 1.9 %collective-permute-start.9 = (f32[512,768]{1,0:T(8,128)}, f32[512,768]{1,0:T(8,128)}, u32[]{:S(2)}, u32[]{:S(2)}) collective-permute-start(f32[512,768]{1,0:T(8,128)} %get-tuple-element.9.panel_ref), channel_id=1, source_target_pairs={{0,32},{32,0},{64,96},{96,64},{128,160},{160,128},{192,224},{224,1... | collective-permute-start | bytes 4718600 | tf_op jit(solution)/shard_map/ppermute | solution.py:445
  43.1 21.5 %all_to_all.10 = f32[32,4,512]{2,1,0:T(4,128)} all-to-all(f32[32,4,512]{2,1,0:T(4,128)S(1)} %get-tuple-element.8), channel_id=1, replica_groups=mesh['row'=16,'col'=32] {'col'}, dimensions={0} | all-to-all | bytes 524288 | tf_op jit(solution)/shard_map/all_to_all | solution.py:448
  64.6 1.0 reduce_sum.9
  65.6 1.9 %collective-permute-start.8 = (f32[2,512]{1,0:T(2,128)S(1)}, f32[2,512]{1,0:T(2,128)S(1)}, u32[]{:S(2)}, u32[]{:S(2)}) collective-permute-start(f32[2,512]{1,0:T(2,128)S(1)} %get-tuple-element.10), channel_id=1, source_target_pairs={{0,32},{32,0},{64,96},{96,64},{128,160},{160,128},{192,224},{224,1... | collective-permute-start | bytes 12296 | tf_op jit(solution)/shard_map/ppermute | solution.py:449
  67.6 0.7 slice.14._
  68.3 0.4 collective-permute-done.8.other_ref
  68.7 1.9 %shard_map.73 = f32[2,1024]{1,0:T(2,128)S(1)} custom-call(f32[2,512]{1,0:T(2,128)S(1)} %get-tuple-element.11.residual_ref, f32[2,512]{1,0:T(2,128)S(1)} %collective-permute-done.8.other_ref, f32[2,512,512]{2,1,0:T(8,128)S(1)} %copy-done, f32[512,512]{1,0:T(8,128)S(1)} %copy-done.1, f32[8,128]{1,0:T(8,128)S(1)} %slice.14._), custom_call_target="tpu_custom_call" | custom-call | flops 150994944 | bytes 3145728 | tf_op jit(solution)/shard_map/pallas_call | solution.py:350
  70.6 0.1 broadcast_in_dim.3
  70.7 17.0 %all_to_all.11 = f32[32,2,1024]{2,1,0:T(2,128)S(1)} all-to-all(f32[32,2,1024]{2,1,0:T(2,128)S(1)} %broadcast_in_dim.3), channel_id=1, replica_groups=mesh['row'=16,'col'=32] {'col'}, dimensions={0} | all-to-all | bytes 524288 | tf_op jit(solution)/shard_map/all_to_all | solution.py:451
  87.6 0.2 reshape.7.found_ref
  87.8 0.1 shard_map.74
  87.9 6.7 %collective-permute-start.10 = (f32[32,2,32]{2,1,0:T(2,128)S(1)}, f32[32,2,32]{2,1,0:T(2,128)S(1)}, u32[]{:S(2)}, u32[]{:S(2)}) collective-permute-start(f32[32,2,32]{2,1,0:T(2,128)S(1)} %shard_map.74), channel_id=1, source_target_pairs={{0,0},{1,1},{2,32},{3,33},{4,64},{5,65},{6,96},{7,97},{8,128},{9,1... | collective-permute-start | bytes 24584 | tf_op jit(solution)/shard_map/ppermute | solution.py:455
  94.7 2.8 %shard_map.75 = f32[64,768]{1,0:T(8,128)} custom-call(f32[64,768]{1,0:T(8,128)S(1)} %copy-done.2, f32[64,1024]{1,0:T(8,128)S(1)} %reshape.7.found_ref, f32[512,768]{1,0:T(8,128)} %get-tuple-element.9.panel_ref, f32[512,768]{1,0:T(8,128)} %collective-permute-done.9.other_ref), custom_call_target="tpu_custom_call" | custom-call | flops 1811939328 | bytes 3145728 | tf_op jit(solution)/shard_map/pallas_call | solution.py:387
  97.5 6.5 %collective-permute-done.10 = f32[32,2,32]{2,1,0:T(2,128)S(1)} collective-permute-done((f32[32,2,32]{2,1,0:T(2,128)S(1)}, f32[32,2,32]{2,1,0:T(2,128)S(1)}, u32[]{:S(2)}, u32[]{:S(2)}) %collective-permute-start.10) | collective-permute-done | bytes 8224 | tf_op jit(solution)/shard_map/ppermute | solution.py:455
  104.0 0.6 copy.12
  (16 shorter events, 0.0 us)
Async XLA Ops:
  0.6 37.7 %copy-start.2 = (f32[64,768]{1,0:T(8,128)S(1)}, f32[64,768]{1,0:T(8,128)}, u32[]{:S(2)}) copy-start(f32[64,768]{1,0:T(8,128)} %solved_ref.5) | copy-start | bytes 589828
  0.6 1.0 copy-start.3
  1.6 0.8 copy-start.4
  2.5 8.0 %collective-permute-start.1 = (f32[200,256]{1,0:T(8,128)S(1)}, f32[200,256]{1,0:T(8,128)S(1)}, u32[]{:S(2)}, u32[]{:S(2)}) collective-permute-start(f32[200,256]{1,0:T(8,128)S(1)} %shard_map.68.one_ref), channel_id=1, source_target_pairs={{0,32},{32,0},{64,96},{96,64},{128,160},{160,128},{192,224},{224,1... | collective-permute-start | bytes 614408 | tf_op jit(solution)/shard_map/ppermute | solution.py:429
  4.4 18.4 %collective-permute-start.3 = (f32[200,256]{1,0:T(8,128)S(1)}, f32[200,256]{1,0:T(8,128)S(1)}, u32[]{:S(2)}, u32[]{:S(2)}) collective-permute-start(f32[200,256]{1,0:T(8,128)S(1)} %shard_map.68.one_ref), channel_id=1, source_target_pairs={{0,128},{32,416},{64,192},{96,480},{128,256},{160,32},{192,320},{2... | collective-permute-start | bytes 614408 | tf_op jit(solution)/shard_map/ppermute | solution.py:430
  10.6 15.7 %collective-permute-start.4 = (f32[200,256]{1,0:T(8,128)S(1)}, f32[200,256]{1,0:T(8,128)S(1)}, u32[]{:S(2)}, u32[]{:S(2)}) collective-permute-start(f32[200,256]{1,0:T(8,128)S(1)} %collective-permute-done.1.two_ref), channel_id=1, source_target_pairs={{0,128},{32,416},{64,192},{96,480},{128,256},{160,32},{192,320},{2... | collective-permute-start | bytes 614408 | tf_op jit(solution)/shard_map/ppermute | solution.py:431
  17.5 20.8 %collective-permute-start.2 = (f32[400,256]{1,0:T(8,128)S(1)}, f32[400,256]{1,0:T(8,128)S(1)}, u32[]{:S(2)}, u32[]{:S(2)}) collective-permute-start(f32[400,256]{1,0:T(8,128)S(1)} %shard_map.69.refs_0_), channel_id=1, source_target_pairs={{0,64},{32,480},{64,128},{96,32},{128,192},{160,96},{192,256},{224... | collective-permute-start | bytes 1228808 | tf_op jit(solution)/shard_map/ppermute | solution.py:433
  20.9 5.3 %collective-permute-start = (f32[64,768]{1,0:T(8,128)}, f32[64,768]{1,0:T(8,128)S(1)}, u32[]{:S(2)}, u32[]{:S(2)}) collective-permute-start(f32[64,768]{1,0:T(8,128)} %solved_ref.5), channel_id=1, source_target_pairs={{0,32},{32,0},{64,96},{96,64},{128,160},{160,128},{192,224},{224,1... | collective-permute-start | bytes 589832 | tf_op jit(solution)/shard_map/ppermute | solution.py:434
  22.8 9.6 %collective-permute-start.6 = (f32[200,256]{1,0:T(8,128)S(1)}, f32[200,256]{1,0:T(8,128)S(1)}, u32[]{:S(2)}, u32[]{:S(2)}) collective-permute-start(f32[200,256]{1,0:T(8,128)S(1)} %collective-permute-done.3.refs_2_), channel_id=1, source_target_pairs={{0,64},{32,480},{64,128},{96,32},{128,192},{160,96},{192,256},{224... | collective-permute-start | bytes 614408 | tf_op jit(solution)/shard_map/ppermute | solution.py:435
  26.3 12.1 %collective-permute-start.5 = (f32[200,256]{1,0:T(8,128)S(1)}, f32[200,256]{1,0:T(8,128)S(1)}, u32[]{:S(2)}, u32[]{:S(2)}) collective-permute-start(f32[200,256]{1,0:T(8,128)S(1)} %shard_map.70.refs_3_), channel_id=1, source_target_pairs={{0,128},{32,416},{64,192},{96,480},{128,256},{160,32},{192,320},{2... | collective-permute-start | bytes 614408 | tf_op jit(solution)/shard_map/ppermute | solution.py:437
  30.5 9.6 %collective-permute-start.7 = (f32[200,256]{1,0:T(8,128)S(1)}, f32[200,256]{1,0:T(8,128)S(1)}, u32[]{:S(2)}, u32[]{:S(2)}) collective-permute-start(f32[200,256]{1,0:T(8,128)S(1)} %shard_map.70.refs_3_), channel_id=1, source_target_pairs={{0,64},{32,480},{64,128},{96,32},{128,192},{160,96},{192,256},{224... | collective-permute-start | bytes 614408 | tf_op jit(solution)/shard_map/ppermute | solution.py:438
  40.1 28.6 %copy-start = (f32[2,512,512]{2,1,0:T(8,128)S(1)}, f32[2,512,512]{2,1,0:T(8,128)}, u32[]{:S(2)}) copy-start(f32[2,512,512]{2,1,0:T(8,128)} %inverses_ref.1) | copy-start | bytes 6291460
  40.1 28.6 %copy-start.1 = (f32[512,512]{1,0:T(8,128)S(1)}, f32[512,512]{1,0:T(8,128)}, u32[]{:S(2)}) copy-start(f32[512,512]{1,0:T(8,128)} %coupling_ref.1) | copy-start | bytes 3145732
  41.1 26.4 %collective-permute-start.9 = (f32[512,768]{1,0:T(8,128)}, f32[512,768]{1,0:T(8,128)}, u32[]{:S(2)}, u32[]{:S(2)}) collective-permute-start(f32[512,768]{1,0:T(8,128)} %get-tuple-element.9.panel_ref), channel_id=1, source_target_pairs={{0,32},{32,0},{64,96},{96,64},{128,160},{160,128},{192,224},{224,1... | collective-permute-start | bytes 4718600 | tf_op jit(solution)/shard_map/ppermute | solution.py:445
  65.6 3.1 %collective-permute-start.8 = (f32[2,512]{1,0:T(2,128)S(1)}, f32[2,512]{1,0:T(2,128)S(1)}, u32[]{:S(2)}, u32[]{:S(2)}) collective-permute-start(f32[2,512]{1,0:T(2,128)S(1)} %get-tuple-element.10), channel_id=1, source_target_pairs={{0,32},{32,0},{64,96},{96,64},{128,160},{160,128},{192,224},{224,1... | collective-permute-start | bytes 12296 | tf_op jit(solution)/shard_map/ppermute | solution.py:449
  87.9 16.0 %collective-permute-start.10 = (f32[32,2,32]{2,1,0:T(2,128)S(1)}, f32[32,2,32]{2,1,0:T(2,128)S(1)}, u32[]{:S(2)}, u32[]{:S(2)}) collective-permute-start(f32[32,2,32]{2,1,0:T(2,128)S(1)} %shard_map.74), channel_id=1, source_target_pairs={{0,0},{1,1},{2,32},{3,33},{4,64},{5,65},{6,96},{7,97},{8,128},{9,1... | collective-permute-start | bytes 24584 | tf_op jit(solution)/shard_map/ppermute | solution.py:455

commit v15 on v14

--- a/solution.py
+++ b/solution.py
@@ -249,21 +249,21 @@
     )(solved, solved_other, *arrays)
 
 
-def reduce_late(solved, solved_other, total, panel, array, places, part):
+def reduce_late(solved, solved_other, total, panel, arrays, places, part):
     rows, width = solved.shape
     unknowns = total.shape[0]
     each = rows // COLS
     count = rows // 2
-    block = array.shape[0] // len(places)
     runs = 2 * len(places)
 
-    def body(solved_ref, other_ref, total_ref, _, ref, out_ref, panel_ref, held, window, sums, sems):
+    def body(solved_ref, other_ref, total_ref, _, *refs):
+        *array_refs, out_ref, panel_ref, held, window, sums, sems = refs
         starts = [start for place in places for start in unit_rows(place, part)]
         for i in range(runs):
-            at, k = i // 2 * block, i % 2
-            for g, value in enumerate(block_rows(ref, at, part, k)):
+            ref, k = array_refs[i // 2], i % 2
+            for g, value in enumerate(block_rows(ref, 0, part, k)):
                 held[i * part : (i + 1) * part, g * LANES : (g + 1) * LANES] = value
-            for g, value in enumerate(block_window(ref, at, part, k, count)):
+            for g, value in enumerate(block_window(ref, 0, part, k, count)):
                 window[i * part + g * TAIL : i * part + (g + 1) * TAIL] = value
         copies = [
             pltpu.make_async_copy(
@@ -293,7 +293,7 @@
             jax.ShapeDtypeStruct((COLS, 2 * each, unknowns), jnp.float32),
             jax.ShapeDtypeStruct(panel.shape, panel.dtype),
         ],
-        in_specs=[in_vmem()] * 3 + [anywhere(), in_vmem()],
+        in_specs=[in_vmem()] * 3 + [anywhere()] + [in_vmem()] * len(arrays),
         out_specs=[in_vmem(), anywhere()],
         scratch_shapes=[
             pltpu.VMEM((runs * part, width), jnp.float32),
@@ -306,7 +306,7 @@
         cost_estimate=pl.CostEstimate(
             flops=12 * rows * runs * part * width, bytes_accessed=8 * unknowns * width, transcendentals=0
         ),
-    )(solved, solved_other, total, panel, array)
+    )(solved, solved_other, total, panel, *arrays)
 
 
 def panel_solve(residual, residual_other, inverses, coupling, arrival):
@@ -438,9 +438,12 @@
     three_other = lax.ppermute(two_other, "row", apart(1))
     part, block = factor.shape[1], own.shape[0]
     early = [(both, 0, 0), (one, 0, 2), (one, block, 1), (two_own, 0, 4), (two_other, 0, 3)]
-    early += [(four, 0, HALF_RING - 1), (three_own, 0, 6)]
+    early += [(three_own, 0, 6)]
     total, panel = reduce_early(solved, solved_other, early, part)
-    partial, panel = reduce_late(solved, solved_other, total, panel, three_other, (5,), part)
+    late = [four, three_other]
+    partial, panel = reduce_late(
+        solved, solved_other, total, panel, late, (HALF_RING - 1, 5), part
+    )
 
     panel_other = lax.ppermute(panel, "row", core_swap())
 

time: 105 us -> 107 us (1.019)
  the two profiles are of different devices: /device:TPU:68 before, /device:TPU:13 now
where the time goes in v15:
time: 107 us
  starting transfers between devices  49.3 us (46%)
  blocking collectives  36.1 us (34%)
  Pallas kernels  8.46 us (8%)
  waiting for transfers between devices  7.58 us (7%)
  local copies, waits for them, and re-layouts  3.3 us (3%)
    all_to_all x1, blocking collectives, shards(): residual = jnp.sum(lax.all_to_all(partial, 'col', 0, 0, tiled=True), axis=0)  20.1 us
    all_to_all x1, blocking collectives, shards(): lax.all_to_all(jnp.broadcast_to(found, (COLS,) + found.shape), 'col', 0,...  16 us
    ppermute x1, starting transfers between devices, shards(): two_own = lax.ppermute(own, 'row', apart(2))  10.7 us
    ppermute x1, starting transfers between devices, shards(): owned = lax.ppermute(cut(gathered, part), ('row', 'col'), work_to_window())  9.07 us
    ppermute x1, starting transfers between devices, shards(): panel_other = lax.ppermute(panel, 'row', core_swap())  5.52 us
    ppermute x1, starting transfers between devices, shards(): four = lax.ppermute(two_other, 'row', apart(2))  5.01 us
    ppermute x1, starting transfers between devices, shards(): solved_other = lax.ppermute(solved, 'row', core_swap())  3.93 us
    ppermute x1, starting transfers between devices, shards(): three_own = lax.ppermute(two_own, 'row', apart(1))  3.39 us
  transfers between devices with their start and end apart: 11, of which 4 were waited for; matrix products, arithmetic and copies ran while one was open for 2% of the time, Pallas kernels for 5%

profile of v15, /device:TPU:13, one launch (start us, length us, event | category | flops | bytes accessed | tf_op | source)
XLA Modules:
  0.0 106.6 jit_solution(3373813063127873187)
XLA Ops:
  0.6 0.0 copy-start.2
  0.7 1.0 copy-done.3
  1.6 0.8 copy-done.4
  2.4 0.2 shard_map.68.one_ref
  2.5 2.6 %collective-permute-start.1 = (f32[200,256]{1,0:T(8,128)S(1)}, f32[200,256]{1,0:T(8,128)S(1)}, u32[]{:S(2)}, u32[]{:S(2)}) collective-permute-start(f32[200,256]{1,0:T(8,128)S(1)} %shard_map.68.one_ref), channel_id=1, source_target_pairs={{0,32},{32,0},{64,96},{96,64},{128,160},{160,128},{192,224},{224,1... | collective-permute-start | bytes 614408 | tf_op jit(solution)/shard_map/ppermute | solution.py:429
  5.1 10.7 %collective-permute-start.3 = (f32[200,256]{1,0:T(8,128)S(1)}, f32[200,256]{1,0:T(8,128)S(1)}, u32[]{:S(2)}, u32[]{:S(2)}) collective-permute-start(f32[200,256]{1,0:T(8,128)S(1)} %shard_map.68.one_ref), channel_id=1, source_target_pairs={{0,128},{32,416},{64,192},{96,480},{128,256},{160,32},{192,320},{2... | collective-permute-start | bytes 614408 | tf_op jit(solution)/shard_map/ppermute | solution.py:430
  15.8 0.5 shard_map.69.refs_0_
  16.3 2.2 %collective-permute-start.2 = (f32[400,256]{1,0:T(8,128)S(1)}, f32[400,256]{1,0:T(8,128)S(1)}, u32[]{:S(2)}, u32[]{:S(2)}) collective-permute-start(f32[400,256]{1,0:T(8,128)S(1)} %shard_map.69.refs_0_), channel_id=1, source_target_pairs={{0,64},{32,480},{64,128},{96,32},{128,192},{160,96},{192,256},{224... | collective-permute-start | bytes 1228808 | tf_op jit(solution)/shard_map/ppermute | solution.py:433
  18.5 1.9 %collective-permute-start.4 = (f32[200,256]{1,0:T(8,128)S(1)}, f32[200,256]{1,0:T(8,128)S(1)}, u32[]{:S(2)}, u32[]{:S(2)}) collective-permute-start(f32[200,256]{1,0:T(8,128)S(1)} %collective-permute-done.1.two_ref), channel_id=1, source_target_pairs={{0,128},{32,416},{64,192},{96,480},{128,256},{160,32},{192,320},{2... | collective-permute-start | bytes 614408 | tf_op jit(solution)/shard_map/ppermute | solution.py:431
  20.5 3.9 %collective-permute-start = (f32[64,768]{1,0:T(8,128)}, f32[64,768]{1,0:T(8,128)S(1)}, u32[]{:S(2)}, u32[]{:S(2)}) collective-permute-start(f32[64,768]{1,0:T(8,128)} %solved_ref.5), channel_id=1, source_target_pairs={{0,32},{32,0},{64,96},{96,64},{128,160},{160,128},{192,224},{224,1... | collective-permute-start | bytes 589832 | tf_op jit(solution)/shard_map/ppermute | solution.py:434
  24.4 3.4 %collective-permute-start.5 = (f32[200,256]{1,0:T(8,128)S(1)}, f32[200,256]{1,0:T(8,128)S(1)}, u32[]{:S(2)}, u32[]{:S(2)}) collective-permute-start(f32[200,256]{1,0:T(8,128)S(1)} %collective-permute-done.3.refs_2_), channel_id=1, source_target_pairs={{0,64},{32,480},{64,128},{96,32},{128,192},{160,96},{192,256},{224... | collective-permute-start | bytes 614408 | tf_op jit(solution)/shard_map/ppermute | solution.py:435
  27.8 2.6 %collective-permute-done.4.refs_0_ = f32[200,256]{1,0:T(8,128)S(1)} collective-permute-done((f32[200,256]{1,0:T(8,128)S(1)}, f32[200,256]{1,0:T(8,128)S(1)}, u32[]{:S(2)}, u32[]{:S(2)}) %collective-permute-start.4) | collective-permute-done | bytes 204832 | tf_op jit(solution)/shard_map/ppermute | solution.py:431
  30.4 1.9 %collective-permute-start.7 = (f32[200,256]{1,0:T(8,128)S(1)}, f32[200,256]{1,0:T(8,128)S(1)}, u32[]{:S(2)}, u32[]{:S(2)}) collective-permute-start(f32[200,256]{1,0:T(8,128)S(1)} %shard_map.70.refs_3_), channel_id=1, source_target_pairs={{0,64},{32,480},{64,128},{96,32},{128,192},{160,96},{192,256},{224... | collective-permute-start | bytes 614408 | tf_op jit(solution)/shard_map/ppermute | solution.py:438
  32.4 5.0 %collective-permute-start.6 = (f32[200,256]{1,0:T(8,128)S(1)}, f32[200,256]{1,0:T(8,128)S(1)}, u32[]{:S(2)}, u32[]{:S(2)}) collective-permute-start(f32[200,256]{1,0:T(8,128)S(1)} %shard_map.70.refs_3_), channel_id=1, source_target_pairs={{0,128},{32,416},{64,192},{96,480},{128,256},{160,32},{192,320},{2... | collective-permute-start | bytes 614408 | tf_op jit(solution)/shard_map/ppermute | solution.py:437
  37.4 1.7 %shard_map.71 = (f32[512,128]{1,0:T(8,128)S(1)}, f32[512,768]{1,0:T(8,128)}) custom-call(f32[64,768]{1,0:T(8,128)S(1)} %copy-done.2, f32[64,768]{1,0:T(8,128)S(1)} %collective-permute-done.refs_1_.other_ref, f32[400,256]{1,0:T(8,128)S(1)} %shard_map.69.refs_0_, f32[400,256]{1,0:T(8,128)S(1)} %collective-permute-done.2.refs_1_, ...), custom_call_target="tpu_custom_call" | custom-call | flops 301989888 | bytes 3145728 | tf_op jit(solution)/shard_map/pallas_call | solution.py:237
  39.2 3.1 %collective-permute-done.6.refs_0_ = f32[200,256]{1,0:T(8,128)S(1)} collective-permute-done((f32[200,256]{1,0:T(8,128)S(1)}, f32[200,256]{1,0:T(8,128)S(1)}, u32[]{:S(2)}, u32[]{:S(2)}) %collective-permute-start.6) | collective-permute-done | bytes 204832 | tf_op jit(solution)/shard_map/ppermute | solution.py:437
  42.3 1.2 %shard_map.72 = (f32[32,4,512]{2,1,0:T(4,128)S(1)}, f32[512,768]{1,0:T(8,128)}) custom-call(f32[64,768]{1,0:T(8,128)S(1)} %copy-done.2, f32[64,768]{1,0:T(8,128)S(1)} %collective-permute-done.refs_1_.other_ref, f32[512,128]{1,0:T(8,128)S(1)} %get-tuple-element.6.total_ref, f32[512,768]{1,0:T(8,128)} %get-tuple-element.7._, ...), custom_call_target="tpu_custom_call", output_to_operand_aliasing={{1}: (3, {})} | custom-call | flops 75497472 | bytes 3145728 | tf_op jit(solution)/shard_map/pallas_call | solution.py:290
  43.4 5.5 %collective-permute-start.9 = (f32[512,768]{1,0:T(8,128)}, f32[512,768]{1,0:T(8,128)}, u32[]{:S(2)}, u32[]{:S(2)}) collective-permute-start(f32[512,768]{1,0:T(8,128)} %get-tuple-element.9.panel_ref), channel_id=1, source_target_pairs={{0,32},{32,0},{64,96},{96,64},{128,160},{160,128},{192,224},{224,1... | collective-permute-start | bytes 4718600 | tf_op jit(solution)/shard_map/ppermute | solution.py:448
  49.0 20.1 %all_to_all.10 = f32[32,4,512]{2,1,0:T(4,128)} all-to-all(f32[32,4,512]{2,1,0:T(4,128)S(1)} %get-tuple-element.8), channel_id=1, replica_groups=mesh['row'=16,'col'=32] {'col'}, dimensions={0} | all-to-all | bytes 524288 | tf_op jit(solution)/shard_map/all_to_all | solution.py:451
  69.1 1.0 reduce_sum.9
  70.1 3.1 %collective-permute-start.8 = (f32[2,512]{1,0:T(2,128)S(1)}, f32[2,512]{1,0:T(2,128)S(1)}, u32[]{:S(2)}, u32[]{:S(2)}) collective-permute-start(f32[2,512]{1,0:T(2,128)S(1)} %get-tuple-element.10), channel_id=1, source_target_pairs={{0,32},{32,0},{64,96},{96,64},{128,160},{160,128},{192,224},{224,1... | collective-permute-start | bytes 12296 | tf_op jit(solution)/shard_map/ppermute | solution.py:452
  73.2 0.7 slice.14._
  73.9 0.1 collective-permute-done.8.other_ref
  74.0 1.9 %shard_map.73 = f32[2,1024]{1,0:T(2,128)S(1)} custom-call(f32[2,512]{1,0:T(2,128)S(1)} %get-tuple-element.11.residual_ref, f32[2,512]{1,0:T(2,128)S(1)} %collective-permute-done.8.other_ref, f32[2,512,512]{2,1,0:T(8,128)S(1)} %copy-done, f32[512,512]{1,0:T(8,128)S(1)} %copy-done.1, f32[8,128]{1,0:T(8,128)S(1)} %slice.14._), custom_call_target="tpu_custom_call" | custom-call | flops 150994944 | bytes 3145728 | tf_op jit(solution)/shard_map/pallas_call | solution.py:350
  75.9 0.1 broadcast_in_dim.3
  76.0 16.0 %all_to_all.11 = f32[32,2,1024]{2,1,0:T(2,128)S(1)} all-to-all(f32[32,2,1024]{2,1,0:T(2,128)S(1)} %broadcast_in_dim.3), channel_id=1, replica_groups=mesh['row'=16,'col'=32] {'col'}, dimensions={0} | all-to-all | bytes 524288 | tf_op jit(solution)/shard_map/all_to_all | solution.py:454
  92.0 0.2 reshape.7.found_ref
  92.2 0.1 shard_map.74
  92.3 9.1 %collective-permute-start.10 = (f32[32,2,32]{2,1,0:T(2,128)S(1)}, f32[32,2,32]{2,1,0:T(2,128)S(1)}, u32[]{:S(2)}, u32[]{:S(2)}) collective-permute-start(f32[32,2,32]{2,1,0:T(2,128)S(1)} %shard_map.74), channel_id=1, source_target_pairs={{0,0},{1,1},{2,32},{3,33},{4,64},{5,65},{6,96},{7,97},{8,128},{9,1... | collective-permute-start | bytes 24584 | tf_op jit(solution)/shard_map/ppermute | solution.py:458
  101.4 2.8 %shard_map.75 = f32[64,768]{1,0:T(8,128)} custom-call(f32[64,768]{1,0:T(8,128)S(1)} %copy-done.2, f32[64,1024]{1,0:T(8,128)S(1)} %reshape.7.found_ref, f32[512,768]{1,0:T(8,128)} %get-tuple-element.9.panel_ref, f32[512,768]{1,0:T(8,128)} %collective-permute-done.9.other_ref), custom_call_target="tpu_custom_call" | custom-call | flops 1811939328 | bytes 3145728 | tf_op jit(solution)/shard_map/pallas_call | solution.py:387
  104.2 1.7 %collective-permute-done.10 = f32[32,2,32]{2,1,0:T(2,128)S(1)} collective-permute-done((f32[32,2,32]{2,1,0:T(2,128)S(1)}, f32[32,2,32]{2,1,0:T(2,128)S(1)}, u32[]{:S(2)}, u32[]{:S(2)}) %collective-permute-start.10) | collective-permute-done | bytes 8224 | tf_op jit(solution)/shard_map/ppermute | solution.py:458
  106.0 0.6 copy.12
  (16 shorter events, 0.0 us)
Async XLA Ops:
  0.6 36.8 %copy-start.2 = (f32[64,768]{1,0:T(8,128)S(1)}, f32[64,768]{1,0:T(8,128)}, u32[]{:S(2)}) copy-start(f32[64,768]{1,0:T(8,128)} %solved_ref.5) | copy-start | bytes 589828
  0.6 1.0 copy-start.3
  1.6 0.8 copy-start.4
  2.5 13.2 %collective-permute-start.1 = (f32[200,256]{1,0:T(8,128)S(1)}, f32[200,256]{1,0:T(8,128)S(1)}, u32[]{:S(2)}, u32[]{:S(2)}) collective-permute-start(f32[200,256]{1,0:T(8,128)S(1)} %shard_map.68.one_ref), channel_id=1, source_target_pairs={{0,32},{32,0},{64,96},{96,64},{128,160},{160,128},{192,224},{224,1... | collective-permute-start | bytes 614408 | tf_op jit(solution)/shard_map/ppermute | solution.py:429
  5.1 19.3 %collective-permute-start.3 = (f32[200,256]{1,0:T(8,128)S(1)}, f32[200,256]{1,0:T(8,128)S(1)}, u32[]{:S(2)}, u32[]{:S(2)}) collective-permute-start(f32[200,256]{1,0:T(8,128)S(1)} %shard_map.68.one_ref), channel_id=1, source_target_pairs={{0,128},{32,416},{64,192},{96,480},{128,256},{160,32},{192,320},{2... | collective-permute-start | bytes 614408 | tf_op jit(solution)/shard_map/ppermute | solution.py:430
  16.3 21.1 %collective-permute-start.2 = (f32[400,256]{1,0:T(8,128)S(1)}, f32[400,256]{1,0:T(8,128)S(1)}, u32[]{:S(2)}, u32[]{:S(2)}) collective-permute-start(f32[400,256]{1,0:T(8,128)S(1)} %shard_map.69.refs_0_), channel_id=1, source_target_pairs={{0,64},{32,480},{64,128},{96,32},{128,192},{160,96},{192,256},{224... | collective-permute-start | bytes 1228808 | tf_op jit(solution)/shard_map/ppermute | solution.py:433
  18.5 11.9 %collective-permute-start.4 = (f32[200,256]{1,0:T(8,128)S(1)}, f32[200,256]{1,0:T(8,128)S(1)}, u32[]{:S(2)}, u32[]{:S(2)}) collective-permute-start(f32[200,256]{1,0:T(8,128)S(1)} %collective-permute-done.1.two_ref), channel_id=1, source_target_pairs={{0,128},{32,416},{64,192},{96,480},{128,256},{160,32},{192,320},{2... | collective-permute-start | bytes 614408 | tf_op jit(solution)/shard_map/ppermute | solution.py:431
  20.5 7.4 %collective-permute-start = (f32[64,768]{1,0:T(8,128)}, f32[64,768]{1,0:T(8,128)S(1)}, u32[]{:S(2)}, u32[]{:S(2)}) collective-permute-start(f32[64,768]{1,0:T(8,128)} %solved_ref.5), channel_id=1, source_target_pairs={{0,32},{32,0},{64,96},{96,64},{128,160},{160,128},{192,224},{224,1... | collective-permute-start | bytes 589832 | tf_op jit(solution)/shard_map/ppermute | solution.py:434
  24.4 13.0 %collective-permute-start.5 = (f32[200,256]{1,0:T(8,128)S(1)}, f32[200,256]{1,0:T(8,128)S(1)}, u32[]{:S(2)}, u32[]{:S(2)}) collective-permute-start(f32[200,256]{1,0:T(8,128)S(1)} %collective-permute-done.3.refs_2_), channel_id=1, source_target_pairs={{0,64},{32,480},{64,128},{96,32},{128,192},{160,96},{192,256},{224... | collective-permute-start | bytes 614408 | tf_op jit(solution)/shard_map/ppermute | solution.py:435
  30.4 8.7 %collective-permute-start.7 = (f32[200,256]{1,0:T(8,128)S(1)}, f32[200,256]{1,0:T(8,128)S(1)}, u32[]{:S(2)}, u32[]{:S(2)}) collective-permute-start(f32[200,256]{1,0:T(8,128)S(1)} %shard_map.70.refs_3_), channel_id=1, source_target_pairs={{0,64},{32,480},{64,128},{96,32},{128,192},{160,96},{192,256},{224... | collective-permute-start | bytes 614408 | tf_op jit(solution)/shard_map/ppermute | solution.py:438
  32.4 9.9 %collective-permute-start.6 = (f32[200,256]{1,0:T(8,128)S(1)}, f32[200,256]{1,0:T(8,128)S(1)}, u32[]{:S(2)}, u32[]{:S(2)}) collective-permute-start(f32[200,256]{1,0:T(8,128)S(1)} %shard_map.70.refs_3_), channel_id=1, source_target_pairs={{0,128},{32,416},{64,192},{96,480},{128,256},{160,32},{192,320},{2... | collective-permute-start | bytes 614408 | tf_op jit(solution)/shard_map/ppermute | solution.py:437
  42.3 31.8 %copy-start = (f32[2,512,512]{2,1,0:T(8,128)S(1)}, f32[2,512,512]{2,1,0:T(8,128)}, u32[]{:S(2)}) copy-start(f32[2,512,512]{2,1,0:T(8,128)} %inverses_ref.1) | copy-start | bytes 6291460
  42.3 31.8 %copy-start.1 = (f32[512,512]{1,0:T(8,128)S(1)}, f32[512,512]{1,0:T(8,128)}, u32[]{:S(2)}) copy-start(f32[512,512]{1,0:T(8,128)} %coupling_ref.1) | copy-start | bytes 3145732
  43.4 29.8 %collective-permute-start.9 = (f32[512,768]{1,0:T(8,128)}, f32[512,768]{1,0:T(8,128)}, u32[]{:S(2)}, u32[]{:S(2)}) collective-permute-start(f32[512,768]{1,0:T(8,128)} %get-tuple-element.9.panel_ref), channel_id=1, source_target_pairs={{0,32},{32,0},{64,96},{96,64},{128,160},{160,128},{192,224},{224,1... | collective-permute-start | bytes 4718600 | tf_op jit(solution)/shard_map/ppermute | solution.py:448
  70.1 3.9 %collective-permute-start.8 = (f32[2,512]{1,0:T(2,128)S(1)}, f32[2,512]{1,0:T(2,128)S(1)}, u32[]{:S(2)}, u32[]{:S(2)}) collective-permute-start(f32[2,512]{1,0:T(2,128)S(1)} %get-tuple-element.10), channel_id=1, source_target_pairs={{0,32},{32,0},{64,96},{96,64},{128,160},{160,128},{192,224},{224,1... | collective-permute-start | bytes 12296 | tf_op jit(solution)/shard_map/ppermute | solution.py:452
  92.3 13.7 %collective-permute-start.10 = (f32[32,2,32]{2,1,0:T(2,128)S(1)}, f32[32,2,32]{2,1,0:T(2,128)S(1)}, u32[]{:S(2)}, u32[]{:S(2)}) collective-permute-start(f32[32,2,32]{2,1,0:T(2,128)S(1)} %shard_map.74), channel_id=1, source_target_pairs={{0,0},{1,1},{2,32},{3,33},{4,64},{5,65},{6,96},{7,97},{8,128},{9,1... | collective-permute-start | bytes 24584 | tf_op jit(solution)/shard_map/ppermute | solution.py:458

commit v16 on v14

--- a/solution.py
+++ b/solution.py
@@ -438,9 +438,9 @@
     three_other = lax.ppermute(two_other, "row", apart(1))
     part, block = factor.shape[1], own.shape[0]
     early = [(both, 0, 0), (one, 0, 2), (one, block, 1), (two_own, 0, 4), (two_other, 0, 3)]
-    early += [(four, 0, HALF_RING - 1), (three_own, 0, 6)]
+    early += [(three_other, 0, 5), (three_own, 0, 6)]
     total, panel = reduce_early(solved, solved_other, early, part)
-    partial, panel = reduce_late(solved, solved_other, total, panel, three_other, (5,), part)
+    partial, panel = reduce_late(solved, solved_other, total, panel, four, (HALF_RING - 1,), part)
 
     panel_other = lax.ppermute(panel, "row", core_swap())
 

time: 105 us -> 106 us (level)
    ppermute x1, waiting for transfers between devices: 0.01 us -> 1.84 us  [shards(): three_other = lax.ppermute(two_other, 'row', apart(1))]
  transfers between devices with their start and end apart: 11 -> 11, of which waited for: 3 -> 4; matrix products, arithmetic and copies ran while one was open for 2% -> 2% of each run, Pallas kernels for 5% -> 5%
where the time goes in v16:
time: 106 us; the launch traced here: 105 us
  starting transfers between devices  40.1 us (38%)
  blocking collectives  38.5 us (36%)
  waiting for transfers between devices  13.3 us (13%)
  Pallas kernels  8.3 us (8%)
  local copies, waits for them, and re-layouts  3.3 us (3%)
    all_to_all x1, blocking collectives, shards(): residual = jnp.sum(lax.all_to_all(partial, 'col', 0, 0, tiled=True), axis=0)  21.5 us
    all_to_all x1, blocking collectives, shards(): lax.all_to_all(jnp.broadcast_to(found, (COLS,) + found.shape), 'col', 0,...  17 us
    ppermute x1, starting transfers between devices, shards(): owned = lax.ppermute(cut(gathered, part), ('row', 'col'), work_to_window())  7.06 us
    ppermute x1, starting transfers between devices, shards(): two_other = lax.ppermute(other, 'row', apart(2))  6.4 us
    ppermute x1, waiting for transfers between devices, shards(): owned = lax.ppermute(cut(gathered, part), ('row', 'col'), work_to_window())  6.11 us
    ppermute x1, starting transfers between devices, shards(): two_own = lax.ppermute(own, 'row', apart(2))  6.09 us
    ppermute x1, waiting for transfers between devices, shards(): four = lax.ppermute(two_other, 'row', apart(2))  4.9 us
    ppermute x1, starting transfers between devices, shards(): four = lax.ppermute(two_other, 'row', apart(2))  3.44 us
  transfers between devices with their start and end apart: 11, of which 4 were waited for; matrix products, arithmetic and copies ran while one was open for 2% of the time, Pallas kernels for 5%

profile of v16, /device:TPU:68, one launch (start us, length us, event | category | flops | bytes accessed | tf_op | source)
XLA Modules:
  0.0 105.4 jit_solution(16987445596849980354)
XLA Ops:
  0.6 0.0 copy-start.2
  0.7 1.0 copy-done.3
  1.6 0.8 copy-done.4
  2.4 0.2 shard_map.68.one_ref
  2.5 1.9 %collective-permute-start.1 = (f32[200,256]{1,0:T(8,128)S(1)}, f32[200,256]{1,0:T(8,128)S(1)}, u32[]{:S(2)}, u32[]{:S(2)}) collective-permute-start(f32[200,256]{1,0:T(8,128)S(1)} %shard_map.68.one_ref), channel_id=1, source_target_pairs={{0,32},{32,0},{64,96},{96,64},{128,160},{160,128},{192,224},{224,1... | collective-permute-start | bytes 614408 | tf_op jit(solution)/shard_map/ppermute | solution.py:429
  4.4 6.1 %collective-permute-start.3 = (f32[200,256]{1,0:T(8,128)S(1)}, f32[200,256]{1,0:T(8,128)S(1)}, u32[]{:S(2)}, u32[]{:S(2)}) collective-permute-start(f32[200,256]{1,0:T(8,128)S(1)} %shard_map.68.one_ref), channel_id=1, source_target_pairs={{0,128},{32,416},{64,192},{96,480},{128,256},{160,32},{192,320},{2... | collective-permute-start | bytes 614408 | tf_op jit(solution)/shard_map/ppermute | solution.py:430
  10.6 6.4 %collective-permute-start.4 = (f32[200,256]{1,0:T(8,128)S(1)}, f32[200,256]{1,0:T(8,128)S(1)}, u32[]{:S(2)}, u32[]{:S(2)}) collective-permute-start(f32[200,256]{1,0:T(8,128)S(1)} %collective-permute-done.1.two_ref), channel_id=1, source_target_pairs={{0,128},{32,416},{64,192},{96,480},{128,256},{160,32},{192,320},{2... | collective-permute-start | bytes 614408 | tf_op jit(solution)/shard_map/ppermute | solution.py:431
  17.0 0.5 shard_map.69.refs_0_
  17.5 3.4 %collective-permute-start.2 = (f32[400,256]{1,0:T(8,128)S(1)}, f32[400,256]{1,0:T(8,128)S(1)}, u32[]{:S(2)}, u32[]{:S(2)}) collective-permute-start(f32[400,256]{1,0:T(8,128)S(1)} %shard_map.69.refs_0_), channel_id=1, source_target_pairs={{0,64},{32,480},{64,128},{96,32},{128,192},{160,96},{192,256},{224... | collective-permute-start | bytes 1228808 | tf_op jit(solution)/shard_map/ppermute | solution.py:433
  20.9 1.9 %collective-permute-start = (f32[64,768]{1,0:T(8,128)}, f32[64,768]{1,0:T(8,128)S(1)}, u32[]{:S(2)}, u32[]{:S(2)}) collective-permute-start(f32[64,768]{1,0:T(8,128)} %solved_ref.5), channel_id=1, source_target_pairs={{0,32},{32,0},{64,96},{96,64},{128,160},{160,128},{192,224},{224,1... | collective-permute-start | bytes 589832 | tf_op jit(solution)/shard_map/ppermute | solution.py:434
  22.8 3.4 %collective-permute-start.6 = (f32[200,256]{1,0:T(8,128)S(1)}, f32[200,256]{1,0:T(8,128)S(1)}, u32[]{:S(2)}, u32[]{:S(2)}) collective-permute-start(f32[200,256]{1,0:T(8,128)S(1)} %collective-permute-done.3.refs_2_), channel_id=1, source_target_pairs={{0,64},{32,480},{64,128},{96,32},{128,192},{160,96},{192,256},{224... | collective-permute-start | bytes 614408 | tf_op jit(solution)/shard_map/ppermute | solution.py:435
  26.3 2.7 %collective-permute-start.5 = (f32[200,256]{1,0:T(8,128)S(1)}, f32[200,256]{1,0:T(8,128)S(1)}, u32[]{:S(2)}, u32[]{:S(2)}) collective-permute-start(f32[200,256]{1,0:T(8,128)S(1)} %shard_map.70.refs_3_), channel_id=1, source_target_pairs={{0,64},{32,480},{64,128},{96,32},{128,192},{160,96},{192,256},{224... | collective-permute-start | bytes 614408 | tf_op jit(solution)/shard_map/ppermute | solution.py:438
  29.0 3.4 %collective-permute-start.7 = (f32[200,256]{1,0:T(8,128)S(1)}, f32[200,256]{1,0:T(8,128)S(1)}, u32[]{:S(2)}, u32[]{:S(2)}) collective-permute-start(f32[200,256]{1,0:T(8,128)S(1)} %shard_map.70.refs_3_), channel_id=1, source_target_pairs={{0,128},{32,416},{64,192},{96,480},{128,256},{160,32},{192,320},{2... | collective-permute-start | bytes 614408 | tf_op jit(solution)/shard_map/ppermute | solution.py:437
  32.4 1.8 %collective-permute-done.5.refs_4_ = f32[200,256]{1,0:T(8,128)S(1)} collective-permute-done((f32[200,256]{1,0:T(8,128)S(1)}, f32[200,256]{1,0:T(8,128)S(1)}, u32[]{:S(2)}, u32[]{:S(2)}) %collective-permute-start.5) | collective-permute-done | bytes 204832 | tf_op jit(solution)/shard_map/ppermute | solution.py:438
  34.3 1.7 %shard_map.71 = (f32[512,128]{1,0:T(8,128)S(1)}, f32[512,768]{1,0:T(8,128)}) custom-call(f32[64,768]{1,0:T(8,128)S(1)} %copy-done.2, f32[64,768]{1,0:T(8,128)S(1)} %collective-permute-done.refs_1_.other_ref, f32[400,256]{1,0:T(8,128)S(1)} %shard_map.69.refs_0_, f32[400,256]{1,0:T(8,128)S(1)} %collective-permute-done.2.refs_1_, ...), custom_call_target="tpu_custom_call" | custom-call | flops 301989888 | bytes 3145728 | tf_op jit(solution)/shard_map/pallas_call | solution.py:237
  36.0 4.9 %collective-permute-done.7.ref = f32[200,256]{1,0:T(8,128)S(1)} collective-permute-done((f32[200,256]{1,0:T(8,128)S(1)}, f32[200,256]{1,0:T(8,128)S(1)}, u32[]{:S(2)}, u32[]{:S(2)}) %collective-permute-start.7) | collective-permute-done | bytes 204832 | tf_op jit(solution)/shard_map/ppermute | solution.py:437
  40.9 1.0 shard_map.72
  41.9 1.9 %collective-permute-start.9 = (f32[512,768]{1,0:T(8,128)}, f32[512,768]{1,0:T(8,128)}, u32[]{:S(2)}, u32[]{:S(2)}) collective-permute-start(f32[512,768]{1,0:T(8,128)} %get-tuple-element.9.panel_ref), channel_id=1, source_target_pairs={{0,32},{32,0},{64,96},{96,64},{128,160},{160,128},{192,224},{224,1... | collective-permute-start | bytes 4718600 | tf_op jit(solution)/shard_map/ppermute | solution.py:445
  43.9 21.5 %all_to_all.10 = f32[32,4,512]{2,1,0:T(4,128)} all-to-all(f32[32,4,512]{2,1,0:T(4,128)S(1)} %get-tuple-element.8), channel_id=1, replica_groups=mesh['row'=16,'col'=32] {'col'}, dimensions={0} | all-to-all | bytes 524288 | tf_op jit(solution)/shard_map/all_to_all | solution.py:448
  65.4 1.0 reduce_sum.9
  66.4 1.9 %collective-permute-start.8 = (f32[2,512]{1,0:T(2,128)S(1)}, f32[2,512]{1,0:T(2,128)S(1)}, u32[]{:S(2)}, u32[]{:S(2)}) collective-permute-start(f32[2,512]{1,0:T(2,128)S(1)} %get-tuple-element.10), channel_id=1, source_target_pairs={{0,32},{32,0},{64,96},{96,64},{128,160},{160,128},{192,224},{224,1... | collective-permute-start | bytes 12296 | tf_op jit(solution)/shard_map/ppermute | solution.py:449
  68.4 0.7 slice.14._
  69.1 0.4 collective-permute-done.8.other_ref
  69.5 1.9 %shard_map.73 = f32[2,1024]{1,0:T(2,128)S(1)} custom-call(f32[2,512]{1,0:T(2,128)S(1)} %get-tuple-element.11.residual_ref, f32[2,512]{1,0:T(2,128)S(1)} %collective-permute-done.8.other_ref, f32[2,512,512]{2,1,0:T(8,128)S(1)} %copy-done, f32[512,512]{1,0:T(8,128)S(1)} %copy-done.1, f32[8,128]{1,0:T(8,128)S(1)} %slice.14._), custom_call_target="tpu_custom_call" | custom-call | flops 150994944 | bytes 3145728 | tf_op jit(solution)/shard_map/pallas_call | solution.py:350
  71.4 0.1 broadcast_in_dim.3
  71.5 17.0 %all_to_all.11 = f32[32,2,1024]{2,1,0:T(2,128)S(1)} all-to-all(f32[32,2,1024]{2,1,0:T(2,128)S(1)} %broadcast_in_dim.3), channel_id=1, replica_groups=mesh['row'=16,'col'=32] {'col'}, dimensions={0} | all-to-all | bytes 524288 | tf_op jit(solution)/shard_map/all_to_all | solution.py:451
  88.4 0.2 reshape.7.found_ref
  88.6 0.1 shard_map.74
  88.7 7.1 %collective-permute-start.10 = (f32[32,2,32]{2,1,0:T(2,128)S(1)}, f32[32,2,32]{2,1,0:T(2,128)S(1)}, u32[]{:S(2)}, u32[]{:S(2)}) collective-permute-start(f32[32,2,32]{2,1,0:T(2,128)S(1)} %shard_map.74), channel_id=1, source_target_pairs={{0,0},{1,1},{2,32},{3,33},{4,64},{5,65},{6,96},{7,97},{8,128},{9,1... | collective-permute-start | bytes 24584 | tf_op jit(solution)/shard_map/ppermute | solution.py:455
  95.8 2.8 %shard_map.75 = f32[64,768]{1,0:T(8,128)} custom-call(f32[64,768]{1,0:T(8,128)S(1)} %copy-done.2, f32[64,1024]{1,0:T(8,128)S(1)} %reshape.7.found_ref, f32[512,768]{1,0:T(8,128)} %get-tuple-element.9.panel_ref, f32[512,768]{1,0:T(8,128)} %collective-permute-done.9.other_ref), custom_call_target="tpu_custom_call" | custom-call | flops 1811939328 | bytes 3145728 | tf_op jit(solution)/shard_map/pallas_call | solution.py:387
  98.7 6.1 %collective-permute-done.10 = f32[32,2,32]{2,1,0:T(2,128)S(1)} collective-permute-done((f32[32,2,32]{2,1,0:T(2,128)S(1)}, f32[32,2,32]{2,1,0:T(2,128)S(1)}, u32[]{:S(2)}, u32[]{:S(2)}) %collective-permute-start.10) | collective-permute-done | bytes 8224 | tf_op jit(solution)/shard_map/ppermute | solution.py:455
  104.8 0.6 copy.12
  (16 shorter events, 0.0 us)
Async XLA Ops:
  0.6 33.7 %copy-start.2 = (f32[64,768]{1,0:T(8,128)S(1)}, f32[64,768]{1,0:T(8,128)}, u32[]{:S(2)}) copy-start(f32[64,768]{1,0:T(8,128)} %solved_ref.5) | copy-start | bytes 589828
  0.6 1.0 copy-start.3
  1.6 0.8 copy-start.4
  2.5 8.0 %collective-permute-start.1 = (f32[200,256]{1,0:T(8,128)S(1)}, f32[200,256]{1,0:T(8,128)S(1)}, u32[]{:S(2)}, u32[]{:S(2)}) collective-permute-start(f32[200,256]{1,0:T(8,128)S(1)} %shard_map.68.one_ref), channel_id=1, source_target_pairs={{0,32},{32,0},{64,96},{96,64},{128,160},{160,128},{192,224},{224,1... | collective-permute-start | bytes 614408 | tf_op jit(solution)/shard_map/ppermute | solution.py:429
  4.4 18.4 %collective-permute-start.3 = (f32[200,256]{1,0:T(8,128)S(1)}, f32[200,256]{1,0:T(8,128)S(1)}, u32[]{:S(2)}, u32[]{:S(2)}) collective-permute-start(f32[200,256]{1,0:T(8,128)S(1)} %shard_map.68.one_ref), channel_id=1, source_target_pairs={{0,128},{32,416},{64,192},{96,480},{128,256},{160,32},{192,320},{2... | collective-permute-start | bytes 614408 | tf_op jit(solution)/shard_map/ppermute | solution.py:430
  10.6 15.7 %collective-permute-start.4 = (f32[200,256]{1,0:T(8,128)S(1)}, f32[200,256]{1,0:T(8,128)S(1)}, u32[]{:S(2)}, u32[]{:S(2)}) collective-permute-start(f32[200,256]{1,0:T(8,128)S(1)} %collective-permute-done.1.two_ref), channel_id=1, source_target_pairs={{0,128},{32,416},{64,192},{96,480},{128,256},{160,32},{192,320},{2... | collective-permute-start | bytes 614408 | tf_op jit(solution)/shard_map/ppermute | solution.py:431
  17.5 16.8 %collective-permute-start.2 = (f32[400,256]{1,0:T(8,128)S(1)}, f32[400,256]{1,0:T(8,128)S(1)}, u32[]{:S(2)}, u32[]{:S(2)}) collective-permute-start(f32[400,256]{1,0:T(8,128)S(1)} %shard_map.69.refs_0_), channel_id=1, source_target_pairs={{0,64},{32,480},{64,128},{96,32},{128,192},{160,96},{192,256},{224... | collective-permute-start | bytes 1228808 | tf_op jit(solution)/shard_map/ppermute | solution.py:433
  20.9 5.3 %collective-permute-start = (f32[64,768]{1,0:T(8,128)}, f32[64,768]{1,0:T(8,128)S(1)}, u32[]{:S(2)}, u32[]{:S(2)}) collective-permute-start(f32[64,768]{1,0:T(8,128)} %solved_ref.5), channel_id=1, source_target_pairs={{0,32},{32,0},{64,96},{96,64},{128,160},{160,128},{192,224},{224,1... | collective-permute-start | bytes 589832 | tf_op jit(solution)/shard_map/ppermute | solution.py:434
  22.8 9.6 %collective-permute-start.6 = (f32[200,256]{1,0:T(8,128)S(1)}, f32[200,256]{1,0:T(8,128)S(1)}, u32[]{:S(2)}, u32[]{:S(2)}) collective-permute-start(f32[200,256]{1,0:T(8,128)S(1)} %collective-permute-done.3.refs_2_), channel_id=1, source_target_pairs={{0,64},{32,480},{64,128},{96,32},{128,192},{160,96},{192,256},{224... | collective-permute-start | bytes 614408 | tf_op jit(solution)/shard_map/ppermute | solution.py:435
  26.3 8.0 %collective-permute-start.5 = (f32[200,256]{1,0:T(8,128)S(1)}, f32[200,256]{1,0:T(8,128)S(1)}, u32[]{:S(2)}, u32[]{:S(2)}) collective-permute-start(f32[200,256]{1,0:T(8,128)S(1)} %shard_map.70.refs_3_), channel_id=1, source_target_pairs={{0,64},{32,480},{64,128},{96,32},{128,192},{160,96},{192,256},{224... | collective-permute-start | bytes 614408 | tf_op jit(solution)/shard_map/ppermute | solution.py:438
  29.0 12.0 %collective-permute-start.7 = (f32[200,256]{1,0:T(8,128)S(1)}, f32[200,256]{1,0:T(8,128)S(1)}, u32[]{:S(2)}, u32[]{:S(2)}) collective-permute-start(f32[200,256]{1,0:T(8,128)S(1)} %shard_map.70.refs_3_), channel_id=1, source_target_pairs={{0,128},{32,416},{64,192},{96,480},{128,256},{160,32},{192,320},{2... | collective-permute-start | bytes 614408 | tf_op jit(solution)/shard_map/ppermute | solution.py:437
  40.9 28.6 %copy-start = (f32[2,512,512]{2,1,0:T(8,128)S(1)}, f32[2,512,512]{2,1,0:T(8,128)}, u32[]{:S(2)}) copy-start(f32[2,512,512]{2,1,0:T(8,128)} %inverses_ref.1) | copy-start | bytes 6291460
  40.9 28.6 %copy-start.1 = (f32[512,512]{1,0:T(8,128)S(1)}, f32[512,512]{1,0:T(8,128)}, u32[]{:S(2)}) copy-start(f32[512,512]{1,0:T(8,128)} %coupling_ref.1) | copy-start | bytes 3145732
  41.9 26.4 %collective-permute-start.9 = (f32[512,768]{1,0:T(8,128)}, f32[512,768]{1,0:T(8,128)}, u32[]{:S(2)}, u32[]{:S(2)}) collective-permute-start(f32[512,768]{1,0:T(8,128)} %get-tuple-element.9.panel_ref), channel_id=1, source_target_pairs={{0,32},{32,0},{64,96},{96,64},{128,160},{160,128},{192,224},{224,1... | collective-permute-start | bytes 4718600 | tf_op jit(solution)/shard_map/ppermute | solution.py:445
  66.4 3.1 %collective-permute-start.8 = (f32[2,512]{1,0:T(2,128)S(1)}, f32[2,512]{1,0:T(2,128)S(1)}, u32[]{:S(2)}, u32[]{:S(2)}) collective-permute-start(f32[2,512]{1,0:T(2,128)S(1)} %get-tuple-element.10), channel_id=1, source_target_pairs={{0,32},{32,0},{64,96},{96,64},{128,160},{160,128},{192,224},{224,1... | collective-permute-start | bytes 12296 | tf_op jit(solution)/shard_map/ppermute | solution.py:449
  88.7 16.0 %collective-permute-start.10 = (f32[32,2,32]{2,1,0:T(2,128)S(1)}, f32[32,2,32]{2,1,0:T(2,128)S(1)}, u32[]{:S(2)}, u32[]{:S(2)}) collective-permute-start(f32[32,2,32]{2,1,0:T(2,128)S(1)} %shard_map.74), channel_id=1, source_target_pairs={{0,0},{1,1},{2,32},{3,33},{4,64},{5,65},{6,96},{7,97},{8,128},{9,1... | collective-permute-start | bytes 24584 | tf_op jit(solution)/shard_map/ppermute | solution.py:455
